TPU v7x, 32 devices: a whole 2x2x4 slice. The times are simulated.
32 devices in a mesh: seq: 8 (over z, x), shard: 4 (over y, core).
Axes of the slice: x: 2, y: 2, z: 4, core: 2. Of those that a mesh axis runs over, the one named last changes fastest.
Arguments:
- tokens: bfloat16 [4, 2048, 2048], P('shard', 'seq'), may hold values from -6 to 6
- in_weight: bfloat16 [2048, 8512], P('shard'), may hold values from -0.125 to 0.125
- out_weight: bfloat16 [2048, 4096], P('shard'), may hold values from -0.09375 to 0.09375
- pre_gain: float32 [2048], replicated, may hold values from 0.1 to 1.9
- conv_kernel: float32 [4, 4352], replicated, may hold values from -3 to 3
- conv_bias: float32 [4352], replicated, may hold values from -3 to 3
- step_bias: float32 [64], replicated, may hold values from -11 to -4
- decay_log: float32 [64], replicated, may hold values from 0 to 2
- skip_gain: float32 [64], replicated, may hold values from 0.5 to 1.5
- gate_gain: float32 [4096], replicated, may hold values from 0.1 to 1.9
- segments: int32 [4, 2048], P('shard'), may hold values from 0 to 3, never falling along the last dimension, each value on 1 to 1024 neighbouring positions
- cotangent: bfloat16 [4, 2048, 2048], P('shard', 'seq'), may hold values from -6 to 6
Outputs:
- block_output: bfloat16 [4, 2048, 2048], P('shard', 'seq')
- token_gradient: float32 [4, 2048, 2048], P('shard', 'seq')
- in_weight_gradient: float32 [2048, 8512], P('shard')
- out_weight_gradient: float32 [2048, 4096], P('shard')
- pre_gain_gradient: float32 [2048], replicated
- conv_kernel_gradient: float32 [4, 4352], replicated
- conv_bias_gradient: float32 [4352], replicated
- step_bias_gradient: float32 [64], replicated
- decay_log_gradient: float32 [64], replicated
- skip_gain_gradient: float32 [64], replicated
- gate_gain_gradient: float32 [4096], replicated
Inputs may be any that keep to these rules, and one draw needn't show every extreme that they name: `segments`: along each sequence the numbers never fall; a document is a run of equal numbers, 1 to 1024 tokens long, and one document in each sequence has exactly 1024 tokens.
All inputs are finite; a program needn't handle non-finite values.
Results may differ from a plain program's by a relative error of at most 0.015.
Values may be sent and summed in bfloat16 or wider, within the bound.
No kernel may reach another device: no remote copies, remote signals or barrier semaphores. Data moves between devices by JAX's collectives and lax.ppermute only.
A program may use at most 448 MiB of HBM per device.

v0:
```python
from functools import partial

import jax
import jax.numpy as jnp
from jax import lax
from jax.sharding import PartitionSpec as P

BLOCK = 256


epsilon = 1e-05
highest = lax.Precision.HIGHEST


def rms_scale(values):
    return lax.rsqrt(jnp.mean(values * values, axis=-1, keepdims=True) + epsilon)


def causal_conv(inputs, kernel, offset, segment):
    length = inputs.shape[0]
    result = offset[None, :] + kernel[0][None, :] * inputs
    for delay_steps in range(1, kernel.shape[0]):
        shifted = jnp.concatenate(
            [
                jnp.zeros((delay_steps, inputs.shape[1]), inputs.dtype),
                inputs[: length - delay_steps],
            ],
            axis=0,
        )
        earlier = jnp.concatenate(
            [jnp.full((delay_steps,), -1, jnp.int32), segment[: length - delay_steps]], axis=0
        )
        same_doc = (earlier == segment).astype(inputs.dtype)
        result = result + kernel[delay_steps][None, :] * shifted * same_doc[:, None]
    return result


def block_terms(block, decay_rates):
    inputs_x, step_sizes, keys_b, queries_c, segment = block
    block_rows = inputs_x.shape[0]
    cumulative = jnp.cumsum(step_sizes * decay_rates[None, :], axis=0)
    position = lax.iota(jnp.int32, block_rows)
    allowed = ((position[:, None] >= position[None, :]) & (segment[:, None] == segment[None, :]))[
        :, :, None
    ]
    log_gaps = jnp.where(allowed, cumulative[:, None, :] - cumulative[None, :, :], 0.0)
    affinity = jnp.einsum("tn,sn->ts", queries_c, keys_b, precision=highest)
    weights = jnp.where(allowed, jnp.exp(log_gaps), 0.0) * affinity[:, :, None]
    scaled = inputs_x * step_sizes[:, :, None]
    local_out = jnp.einsum("tsk,skp->tkp", weights, scaled, precision=highest)
    tail_weight = jnp.where(
        (segment == segment[block_rows - 1])[:, None],
        jnp.exp(cumulative[block_rows - 1][None, :] - cumulative),
        0.0,
    )
    state_add = jnp.einsum(
        "sn,skp->knp", keys_b, scaled * tail_weight[:, :, None], precision=highest
    )
    return (local_out, state_add, cumulative)


def mix_sequence(inputs_x, step_sizes, keys_b, queries_c, decay_rates, segment, mapper):
    length, head_count, head_dim = inputs_x.shape
    block_count = length // BLOCK
    blocks = (
        inputs_x.reshape(block_count, BLOCK, head_count, head_dim),
        step_sizes.reshape(block_count, BLOCK, head_count),
        keys_b.reshape(block_count, BLOCK, -1),
        queries_c.reshape(block_count, BLOCK, -1),
        segment.reshape(block_count, BLOCK),
    )
    local_out, state_add, cumulative = mapper(partial(block_terms, decay_rates=decay_rates), blocks)
    running = jnp.cumsum(cumulative[:, BLOCK - 1, :], axis=0)
    before = jnp.concatenate([jnp.zeros((1, head_count), running.dtype), running[:-1]], axis=0)
    block_ends = blocks[4][:, BLOCK - 1]
    prior_end = jnp.concatenate([jnp.full((1,), -1, jnp.int32), block_ends[:-1]], axis=0)
    block_index = lax.iota(jnp.int32, block_count)
    linked = (
        (block_index[:, None] > block_index[None, :]) & (prior_end[:, None] == block_ends[None, :])
    )[:, :, None]
    carried = jnp.where(
        linked, jnp.exp(jnp.where(linked, before[:, None, :] - running[None, :, :], 0.0)), 0.0
    )
    entering = jnp.einsum("cdk,dknp->cknp", carried, state_add, precision=highest)
    reach_weight = jnp.where(
        (blocks[4] == prior_end[:, None])[:, :, None], jnp.exp(cumulative), 0.0
    )
    state_out = (
        jnp.einsum("ctn,cknp->ctkp", blocks[3], entering, precision=highest)
        * reach_weight[:, :, :, None]
    )
    return (local_out + state_out).reshape(length, head_count, head_dim)


def spread_map(function, blocks):
    return jax.vmap(function)(blocks)


def input_norm(values, gain):
    return values * rms_scale(values) * gain[None, :]


def gated_norm(mixed, gate_values, gain):
    gated = mixed * jax.nn.silu(gate_values)
    return gated * rms_scale(gated) * gain[None, :]


def body(
    tokens,
    in_weight,
    out_weight,
    pre_gain,
    conv_kernel,
    conv_bias,
    step_bias,
    decay_log,
    skip_gain,
    gate_gain,
    segments,
    cotangent,
):
    groups = lax.axis_size("seq")
    seq_place = lax.axis_index("seq")
    head_count = step_bias.shape[0]
    inner_width = gate_gain.shape[0]
    channels = conv_bias.shape[0]
    state_width = (channels - inner_width) // 2
    head_dim = inner_width // head_count
    local_heads = head_count // groups
    local_width = local_heads * head_dim
    first_head = seq_place * local_heads
    segment = segments[0]
    series = tokens[0].astype(jnp.float32)
    upstream = cotangent[0]
    full_in, full_out = (
        lax.all_gather(in_weight, "shard", axis=0, tiled=True),
        lax.all_gather(out_weight, "shard", axis=0, tiled=True),
    )
    normed, norm_pull = jax.vjp(input_norm, series, pre_gain)
    normed_low = normed.astype(jnp.bfloat16)
    projected = jnp.dot(normed_low, full_in, preferred_element_type=jnp.float32)
    gate_values = projected[:, :inner_width]
    packed = projected[:, inner_width:].astype(jnp.bfloat16)
    value_tokens = packed[:, :inner_width]
    shared = packed[:, inner_width:channels]
    step_tokens = packed[:, channels:]
    value_heads, step_heads = (
        lax.all_to_all(value_tokens, "seq", split_axis=1, concat_axis=0, tiled=True),
        lax.all_to_all(step_tokens, "seq", split_axis=1, concat_axis=0, tiled=True),
    )
    shared_all = lax.all_gather(shared, "seq", axis=0, tiled=True)

    def local_mixer(
        value_in, shared_in, step_in, kernel, offset, step_offsets, decay_logs, skip_gains
    ):
        channel_start = first_head * head_dim
        kernel_own = lax.dynamic_slice_in_dim(kernel, channel_start, local_width, 1)
        offset_own = lax.dynamic_slice_in_dim(offset, channel_start, local_width, 0)
        value_conv = jax.nn.silu(causal_conv(value_in, kernel_own, offset_own, segment))
        shared_conv = jax.nn.silu(
            causal_conv(shared_in, kernel[:, inner_width:], offset[inner_width:], segment)
        )
        step_sizes = jax.nn.softplus(
            step_in + lax.dynamic_slice_in_dim(step_offsets, first_head, local_heads, 0)[None, :]
        )
        decay_rates = -jnp.exp(lax.dynamic_slice_in_dim(decay_logs, first_head, local_heads, 0))
        inputs_x = value_conv.reshape(-1, local_heads, head_dim)
        result = mix_sequence(
            inputs_x,
            step_sizes,
            shared_conv[:, :state_width],
            shared_conv[:, state_width:],
            decay_rates,
            segment,
            spread_map,
        )
        result = (
            result
            + lax.dynamic_slice_in_dim(skip_gains, first_head, local_heads, 0)[None, :, None]
            * inputs_x
        )
        return result.reshape(-1, local_width)

    mixed, mixer_pull = jax.vjp(
        local_mixer,
        value_heads.astype(jnp.float32),
        shared_all.astype(jnp.float32),
        step_heads.astype(jnp.float32),
        conv_kernel,
        conv_bias,
        step_bias,
        decay_log,
        skip_gain,
    )
    mixed_tokens = lax.all_to_all(
        mixed.astype(jnp.bfloat16), "seq", split_axis=0, concat_axis=1, tiled=True
    )
    normed_out, gate_pull = jax.vjp(
        gated_norm, mixed_tokens.astype(jnp.float32), gate_values, gate_gain
    )
    normed_out_low = normed_out.astype(jnp.bfloat16)
    branch = jnp.einsum("ti,di->td", normed_out_low, full_out, preferred_element_type=jnp.float32)
    block_output = (series + branch).astype(jnp.bfloat16)[None]
    out_grad = jnp.dot(upstream, full_out, preferred_element_type=jnp.float32)
    mixed_grad, gate_grad, gate_gain_gradient = gate_pull(out_grad)
    mixed_grad_heads = lax.all_to_all(
        mixed_grad.astype(jnp.bfloat16), "seq", split_axis=1, concat_axis=0, tiled=True
    )
    (
        value_grad,
        shared_grad,
        step_grad,
        kernel_gradient,
        conv_bias_gradient,
        step_bias_gradient,
        decay_log_gradient,
        skip_gain_gradient,
    ) = mixer_pull(mixed_grad_heads.astype(jnp.float32))
    value_grad_tokens, step_grad_tokens = (
        lax.all_to_all(
            value_grad.astype(jnp.bfloat16), "seq", split_axis=0, concat_axis=1, tiled=True
        ),
        lax.all_to_all(
            step_grad.astype(jnp.bfloat16), "seq", split_axis=0, concat_axis=1, tiled=True
        ),
    )
    shared_grad_tokens = lax.psum_scatter(
        shared_grad.astype(jnp.bfloat16), "seq", scatter_dimension=0, tiled=True
    )
    projected_grad = jnp.concatenate(
        [gate_grad.astype(jnp.bfloat16), value_grad_tokens, shared_grad_tokens, step_grad_tokens],
        axis=1,
    )
    normed_grad = jnp.einsum(
        "te,de->td", projected_grad, full_in, preferred_element_type=jnp.float32
    )
    series_grad, pre_gain_gradient = norm_pull(normed_grad)
    token_gradient = (upstream.astype(jnp.float32) + series_grad)[None]
    in_part = jnp.einsum(
        "tr,te->re", normed_low, projected_grad, preferred_element_type=jnp.float32
    )
    out_part = jnp.einsum("tr,ti->ri", upstream, normed_out_low, preferred_element_type=jnp.float32)
    term_rows = lax.psum_scatter(
        jnp.concatenate([in_part, out_part], axis=1).astype(jnp.bfloat16),
        "shard",
        scatter_dimension=0,
        tiled=True,
    )
    summed = lax.psum(term_rows, "seq").astype(jnp.float32)
    in_columns = projected_grad.shape[1]
    in_weight_gradient = summed[:, :in_columns]
    out_weight_gradient = summed[:, in_columns:]
    small_total = lax.psum(
        (
            pre_gain_gradient,
            kernel_gradient,
            conv_bias_gradient,
            step_bias_gradient,
            decay_log_gradient,
            skip_gain_gradient,
            gate_gain_gradient,
        ),
        ("seq", "shard"),
    )
    return (
        block_output,
        token_gradient,
        in_weight_gradient,
        out_weight_gradient,
        small_total[0],
        small_total[1],
        small_total[2],
        small_total[3],
        small_total[4],
        small_total[5],
        small_total[6],
    )


def solution(mesh):
    placed = (
        P("shard", "seq", None),
        P("shard", None),
        P("shard", None),
        P(),
        P(),
        P(),
        P(),
        P(),
        P(),
        P(),
        P("shard", None),
        P("shard", "seq", None),
    )
    return jax.shard_map(
        body,
        mesh=mesh,
        in_specs=placed,
        out_specs=(
            P("shard", "seq", None),
            P("shard", "seq", None),
            P("shard", None),
            P("shard", None),
            P(),
            P(),
            P(),
            P(),
            P(),
            P(),
            P(),
        ),
        check_vma=False,
    )
```

profile of v0, /device:TPU:1, one launch (start us, length us, event | category | flops | bytes accessed | tf_op | source)
XLA Modules:
  0.0 1723.1 jit_solution(4257422666736850310)
XLA Ops:
  9.2 214.2 %all-gather.4.cloned.1.call-done = bf16[2048,8512]{0,1:T(8,128)(2,1)} async-done(((bf16[512,8512]{0,1:T(8,128)(2,1)}), bf16[2048,8512]{0,1:T(8,128)(2,1)}) %all-gather.4.cloned.1.call-update) | async-done | bytes 34865168 | tf_op jit(solution)/shard_map/all_gather | solution.py:136
  223.4 18.7 %fusion.190 = (bf16[256,8512]{0,1:T(8,128)(2,1)S(1)}, f32[256,8512]{0,1:T(8,128)}) fusion(bf16[2048,8512]{0,1:T(8,128)(2,1)} %all-gather.4.cloned.1.call-done, bf16[1,256,2048]{2,1,0:T(8,128)(2,1)S(1)} %copy-done.23, f32[2048]{0:T(1024)S(1)} %copy-done.48, f32[256]{0:T(256)S(1)} %fusion.171), kind=kOutput, calls=%fused_computation.248 | convolution fusion | flops 8929755136 | bytes 48997376 | tf_op jit(solution)/shard_map/dot_general | solution.py:141
  273.3 19.4 %all-gather.6.cloned.1.call-done = bf16[2048,256]{0,1:T(8,128)(2,1)} async-done(((bf16[256,256]{0,1:T(8,128)(2,1)}), bf16[2048,256]{0,1:T(8,128)(2,1)}) %all-gather.6.cloned.1.call-update) | async-done | bytes 1048592 | tf_op jit(solution)/shard_map/all_gather | solution.py:151
  327.3 7.1 reshape.437
  357.3 20.9 %bitcast_add_fusion.1 = f32[8,256,8,64]{1,3,2,0:T(8,128)} fusion(f32[8,256,8,64]{1,3,2,0:T(8,128)S(1)} %bitcast.274, f32[8,256,8]{1,2,0:T(8,128)S(1)} %get-tuple-element.105, f32[8,256,256]{2,1,0:T(8,128)S(1)} %copy-done.25, f32[8,256,8]{1,2,0:T(8,128)S(1)} %get-tuple-element.106, pred[8,256,256]{2,1,0:T(8,128)(4,1)S(1)} %copy-done.30, ...), kind=kOutput, calls=%fused_computation.50 | convolution fusion | flops 3241148416 | bytes 15400960 | tf_op jit(solution)/shard_map/jvp(vmap(tsk,skp->tkp))/dot_general | solution.py:50
  378.2 6.9 copy.264
  385.1 7.6 reshape.435
  397.3 58.5 %all_to_all.93 = bf16[8,256,512]{2,1,0:T(8,128)(2,1)S(1)} all-to-all(bf16[8,256,512]{2,1,0:T(8,128)(2,1)S(1)} %bitcast.283), channel_id=1, replica_groups=mesh['seq'=8,'shard'=4] {'seq'}, dimensions={0} | all-to-all | bytes 4194304 | tf_op jit(solution)/shard_map/all_to_all | solution.py:195
  470.6 15.8 multiply_reduce_fusion
  495.7 51.5 %all_to_all.94 = bf16[256,8,512]{2,0,1:T(8,128)(2,1)} all-to-all(bf16[256,8,512]{2,0,1:T(8,128)(2,1)S(1)} %copy.224), channel_id=1, replica_groups=mesh['seq'=8,'shard'=4] {'seq'}, dimensions={1} | all-to-all | bytes 4194304 | tf_op jit(solution)/shard_map/all_to_all | solution.py:206
  570.1 7.9 fusion.91
  578.0 8.0 fusion.90
  586.0 16.9 fusion.11
  603.0 13.9 multiply_reduce_fusion.5
  632.9 6.9 copy.271
  639.8 7.5 reshape.436
  647.3 8.1 multiply_reduce_fusion.4
  684.5 19.8 %reduce-window.16 = f32[8,8,2,128]{3,1,2,0:T(8,128)S(1)} reduce-window(f32[8,8,2,128]{3,1,2,0:T(8,128)S(1)} %add_bitcast_fusion, f32[]{:T(128)} %constant.42.clone.1), window={size=1x1x1x128 pad=0_0x0_0x0_0x0_127}, to_apply=%region_17.18 | reduce-window | flops 2080768 | bytes 131076 | tf_op jit(solution)/shard_map/reduce-window.2
  705.5 16.5 all-to-all-done.4
  722.0 7.1 all-to-all-start.5
  729.1 11.0 convert_bitcast_fusion
  744.1 16.3 reduce-scatter.3.cloned.1.call-done
  760.5 19.8 %convolution_convert_fusion = bf16[2048,8512]{0,1:T(8,128)(2,1)} fusion(bf16[256,64]{0,1:T(8,128)(2,1)S(1)} %bitcast.296, bf16[256,256]{0,1:T(8,128)(2,1)} %reduce-scatter.3.cloned.1.call-done, bf16[256,4096]{0,1:T(8,128)(2,1)} %bitcast.288, bf16[256,4096]{0,1:T(8,128)(2,1)} %get-tuple-element.111, bf16[1,256,2048]{2,1,0:T(8,128)(2,1)S(1)} %copy-done.24, ...), kind=kOutput, calls=%fused_computation.1 | convolution fusion | flops 8962441216 | bytes 40281088 | tf_op jit(solution)/shard_map/tr,te->re/dot_general | solution.py:239
  780.2 44.7 %pad_maximum_fusion = bf16[2048,12608]{0,1:T(8,128)(2,1)} fusion(bf16[2048,4096]{0,1:T(8,128)(2,1)} %convert_bitcast_fusion, bf16[2048,8512]{0,1:T(8,128)(2,1)} %convolution_convert_fusion), kind=kLoop, calls=%fused_computation | loop fusion | flops 103284736 | bytes 103284736 | tf_op jit(solution)/shard_map/concatenate | solution.py:244
  825.0 352.4 %reduce-scatter.5.cloned.1.call-done = bf16[512,12608]{0,1:T(8,128)(2,1)} async-done(((bf16[2048,12608]{0,1:T(8,128)(2,1)}), bf16[512,12608]{0,1:T(8,128)(2,1)}) %reduce-scatter.5.cloned.1.call-update) | async-done | bytes 12910608 | tf_op jit(solution)/shard_map/reduce_scatter | solution.py:243
  1177.8 13.2 fusion.46
  1192.5 18.2 %fusion.50 = (f32[2048]{0:T(1024)S(1)}, f32[256]{0:T(256)S(1)}, f32[256,2048]{1,0:T(8,128)}) fusion(bf16[1,256,2048]{2,1,0:T(8,128)(2,1)S(1)} %copy-done.24, f32[256]{0:T(256)S(1)} %copy-done.54, f32[2048]{0:T(1024)S(1)} %copy-done.49, bf16[2048,8512]{0,1:T(8,128)(2,1)} %all-gather.4.cloned.1.call-done, bf16[256,64]{0,1:T(8,128)(2,1)S(1)} %bitcast.297, ...), kind=kOutput, calls=%fused_computation.91 | convolution fusion | flops 8946579456 | bytes 42387456 | tf_op jit(solution)/shard_map/te,de->td/dot_general | solution.py:234
  1214.3 43.3 %all-reduce.30 = (f32[2048]{0:T(1024)}, f32[4352]{0:T(1024)}, f32[64]{0:T(128)}, f32[64]{0:T(128)}, f32[64]{0:T(128)}, /*index=5*/f32[4096]{0:T(1024)}) all-reduce(f32[2048]{0:T(1024)S(1)} %get-tuple-element.75, f32[4352]{0:T(1024)S(1)} %fusion.170, ...), channel_id=1, replica_groups=mesh['seq'=8,'shard'=4] {'seq','shard'}, use_global_device_ids=true, to_apply=%region_23.24 | all-reduce | flops 10688 | bytes 85504 | tf_op jit(solution)/shard_map/psum | solution.py:253
  1257.6 331.1 %all-reduce.34.cloned.1.call-done = bf16[512,12608]{0,1:T(8,128)(2,1)} async-done(((bf16[512,12608]{0,1:T(8,128)(2,1)}), bf16[512,12608]{0,1:T(8,128)(2,1)}) %all-reduce.34.cloned.1.call-update) | async-done | bytes 12910608 | tf_op jit(solution)/shard_map/psum | solution.py:249
  1595.5 8.9 copy.251
  1604.4 10.5 slice.189
  1614.9 99.4 %all-reduce.36.cloned.1.call-done = f32[4,4352]{1,0:T(4,128)} async-done(((f32[4,4352]{1,0:T(4,128)}), f32[4,4352]{1,0:T(4,128)}) %all-reduce.36.cloned.1.call-update) | async-done | bytes 69648 | tf_op jit(solution)/shard_map/psum | solution.py:253
  (273 shorter events, 205.5 us)
Async XLA Ops:
  7.2 216.2 %copy-start.48 = (f32[2048]{0:T(1024)S(1)}, f32[2048]{0:T(1024)}, u32[]{:S(2)}) copy-start(f32[2048]{0:T(1024)} %param.15) | copy-start | bytes 24580
  7.2 216.2 %all-gather.4.cloned.1.call-start = ((), (), s32[]{:S(2)}) async-start(), calls=%async_computation.8 | async-start | bytes 43581440 | tf_op jit(solution)/shard_map/all_gather | solution.py:136
  7.9 284.8 %all-gather.6.cloned.1.call-start = ((), (), s32[]{:S(2)}) async-start(), calls=%async_computation.9 | async-start | bytes 1179648 | tf_op jit(solution)/shard_map/all_gather | solution.py:151
  9.2 232.9 %copy-start.53 = (f32[256]{0:T(256)}, f32[256]{0:T(256)S(1)}, u32[]{:S(2)}) copy-start(f32[256]{0:T(256)S(1)} %fusion.171) | copy-start | bytes 3076
  244.9 225.6 %all-gather.8.cloned.1.call-start = ((), (), s32[]{:S(2)}) async-start(), calls=%async_computation.10 | async-start | bytes 20971520 | tf_op jit(solution)/shard_map/all_gather | solution.py:137
  249.4 10.8 all-to-all-start.1
  260.1 34.1 %copy-start.28 = (bf16[256,8,8]{0,2,1:T(8,128)(2,1)}, bf16[256,8,8]{0,2,1:T(8,128)(2,1)S(1)}, u32[]{:S(2)}) copy-start(bf16[256,8,8]{0,2,1:T(8,128)(2,1)S(1)} %all-to-all-done.1) | copy-start | bytes 98308
  260.1 60.2 %all-to-all-start = ((bf16[256,8,512]{2,0,1:T(8,128)(2,1)}), bf16[256,8,512]{2,0,1:T(8,128)(2,1)S(1)}, u32[]{:S(2)}, u32[]{:S(2)}) async-start(bf16[256,8,512]{2,0,1:T(8,128)(2,1)} %copy.205), calls=%async_computation | async-start | bytes 4194304 | tf_op jit(solution)/shard_map/all_to_all | solution.py:148
  264.9 29.7 %copy-start.59 = (f32[8]{0:T(128)}, f32[8]{0:T(128)S(1)}, u32[]{:S(2)}) copy-start(f32[8]{0:T(128)S(1)} %fusion.173) | copy-start | bytes 100
  265.1 29.5 %copy-start.51 = (f32[8]{0:T(128)}, f32[8]{0:T(128)S(1)}, u32[]{:S(2)}) copy-start(f32[8]{0:T(128)S(1)} %dynamic_slice.17) | copy-start | bytes 100
  266.3 28.5 %copy-start.38 = (f32[1,256]{1,0:T(1,128)}, f32[1,256]{1,0:T(1,128)S(1)}, u32[]{:S(2)}) copy-start(f32[1,256]{1,0:T(1,128)S(1)} %get-tuple-element.128) | copy-start | bytes 3076
  266.3 28.5 %copy-start.40 = (f32[1,256]{1,0:T(1,128)}, f32[1,256]{1,0:T(1,128)S(1)}, u32[]{:S(2)}) copy-start(f32[1,256]{1,0:T(1,128)S(1)} %get-tuple-element.130) | copy-start | bytes 3076
  266.3 28.5 %copy-start.42 = (f32[1,256]{1,0:T(1,128)}, f32[1,256]{1,0:T(1,128)S(1)}, u32[]{:S(2)}) copy-start(f32[1,256]{1,0:T(1,128)S(1)} %get-tuple-element.131) | copy-start | bytes 3076
  266.3 28.5 %copy-start.44 = (f32[1,256]{1,0:T(1,128)}, f32[1,256]{1,0:T(1,128)S(1)}, u32[]{:S(2)}) copy-start(f32[1,256]{1,0:T(1,128)S(1)} %get-tuple-element.129) | copy-start | bytes 3076
  266.4 28.1 %copy-start.35 = (pred[8,256]{1,0:T(8,128)(4,1)}, pred[8,256]{1,0:T(8,128)(4,1)S(1)}, u32[]{:S(2)}) copy-start(pred[8,256]{1,0:T(8,128)(4,1)S(1)} %get-tuple-element.133) | copy-start | bytes 6148
  470.5 15.8 copy-start.4
  470.5 15.8 copy-start.7
  664.8 57.2 %all-to-all-start.4 = ((bf16[8,256,512]{2,1,0:T(8,128)(2,1)}), bf16[8,256,512]{2,1,0:T(8,128)(2,1)}, u32[]{:S(2)}, u32[]{:S(2)}) async-start(bf16[8,256,512]{2,1,0:T(8,128)(2,1)} %bitcast.279), calls=%async_computation.4 | async-start | bytes 4194304 | tf_op jit(solution)/shard_map/all_to_all | solution.py:220
  669.1 91.3 %reduce-scatter.3.cloned.1.call-start = ((), (), s32[]{:S(2)}) async-start(), calls=%async_computation.11 | async-start | bytes 1179648 | tf_op jit(solution)/shard_map/reduce_scatter | solution.py:227
  680.1 24.5 %copy-start.29 = (bf16[256,8,8]{0,2,1:T(8,128)(2,1)S(1)}, bf16[256,8,8]{0,2,1:T(8,128)(2,1)}, u32[]{:S(2)}) copy-start(bf16[256,8,8]{0,2,1:T(8,128)(2,1)} %copy-done.28) | copy-start | bytes 98308
  680.1 24.5 %copy-start.52 = (f32[8]{0:T(128)S(1)}, f32[8]{0:T(128)}, u32[]{:S(2)}) copy-start(f32[8]{0:T(128)} %copy-done.51) | copy-start | bytes 100
  680.1 24.5 %copy-start.60 = (f32[8]{0:T(128)S(1)}, f32[8]{0:T(128)}, u32[]{:S(2)}) copy-start(f32[8]{0:T(128)} %copy-done.59) | copy-start | bytes 100
  680.1 49.0 %copy-start.22 = (bf16[1,256,2048]{2,1,0:T(8,128)(2,1)S(1)}, bf16[1,256,2048]{2,1,0:T(8,128)(2,1)}, u32[]{:S(2)}) copy-start(bf16[1,256,2048]{2,1,0:T(8,128)(2,1)} %param.23) | copy-start | bytes 3145732
  722.0 22.1 %all-to-all-start.5 = ((bf16[8,256,8]{1,2,0:T(8,128)(2,1)}), bf16[8,256,8]{1,2,0:T(8,128)(2,1)S(1)}, u32[]{:S(2)}, u32[]{:S(2)}) async-start(bf16[8,256,8]{1,2,0:T(8,128)(2,1)} %get-tuple-element.102), calls=%async_computation.6 | async-start | bytes 65536 | tf_op jit(solution)/shard_map/all_to_all | solution.py:223
  729.1 448.3 %reduce-scatter.5.cloned.1.call-start = ((), (), s32[]{:S(2)}) async-start(), calls=%async_computation.12 | async-start | bytes 64552960 | tf_op jit(solution)/shard_map/reduce_scatter | solution.py:243
  740.1 20.4 %copy-start.24 = (bf16[1,256,2048]{2,1,0:T(8,128)(2,1)S(1)}, bf16[1,256,2048]{2,1,0:T(8,128)(2,1)}, u32[]{:S(2)}) copy-start(bf16[1,256,2048]{2,1,0:T(8,128)(2,1)} %param.12) | copy-start | bytes 3145732
  740.1 20.4 %copy-start.49 = (f32[2048]{0:T(1024)S(1)}, f32[2048]{0:T(1024)}, u32[]{:S(2)}) copy-start(f32[2048]{0:T(1024)} %param.15) | copy-start | bytes 24580
  740.1 20.4 %copy-start.54 = (f32[256]{0:T(256)S(1)}, f32[256]{0:T(256)}, u32[]{:S(2)}) copy-start(f32[256]{0:T(256)} %copy-done.53) | copy-start | bytes 3076
  825.0 763.7 %all-reduce.34.cloned.1.call-start = ((), (), s32[]{:S(2)}) async-start(), calls=%async_computation.13 | async-start | bytes 25821184 | tf_op jit(solution)/shard_map/psum | solution.py:249
  1177.5 14.9 copy-start.63
  1177.5 536.8 %all-reduce.36.cloned.1.call-start = ((), (), s32[]{:S(2)}) async-start(), calls=%async_computation.14 | async-start | bytes 139264 | tf_op jit(solution)/shard_map/psum | solution.py:253
  1192.4 18.2 %copy-start.47 = (f32[256]{0:T(256)S(1)}, f32[256]{0:T(256)}, u32[]{:S(2)}) copy-start(f32[256]{0:T(256)} %copy-done.46) | copy-start | bytes 3076
  (46 other events, 256.2 us)
Sparse Core Ops, SparseCore 0:
  9.6 213.7 all-gather.3
  245.0 47.6 all-gather.5
  294.3 117.4 all-gather.7
  680.3 80.1 reduce-scatter.2
  825.1 352.2 reduce-scatter.4
  1181.3 407.3 all-reduce.33
  1595.8 118.5 all-reduce.35
where the time goes:
time: 1730 us; the launch traced here: 1720 us
  waiting for transfers between devices  1060 us (61%)
  matrix products  212 us (12%)
  blocking collectives  153 us (9%)
  other arithmetic  140 us (8%)
  local copies, waits for them, and re-layouts  123 us (7%)
  starting transfers between devices  21.8 us (1%)
    reduce_scatter x1, waiting for transfers between devices, body(): lax.psum_scatter(jnp.concatenate([in_part, out_part], axis=1).astype(jnp....  352 us
    psum x1, waiting for transfers between devices, body(): summed = lax.psum(term_rows, 'seq').astype(jnp.float32)  331 us
    all_gather x1, waiting for transfers between devices, body(): lax.all_gather(in_weight, 'shard', axis=0, tiled=True)  214 us
    psum x1, waiting for transfers between devices, body(): lax.psum((pre_gain_gradient, kernel_gradient, conv_bias_gradient, step_bi...  99.4 us
    all_to_all x1, blocking collectives, body(): lax.all_to_all(mixed.astype(jnp.bfloat16), 'seq', split_axis=0, concat_ax...  58.5 us
    dot_general x3, matrix products, block_terms(): local_out = jnp.einsum('tsk,skp->tkp', weights, scaled, precision=highest)  51.7 us
    all_to_all x1, blocking collectives, body(): lax.all_to_all(mixed_grad.astype(jnp.bfloat16), 'seq', split_axis=1, conc...  51.5 us
    concatenate x1, other arithmetic, body(): jnp.concatenate([in_part, out_part], axis=1).astype(jnp.bfloat16)  44.7 us
  transfers between devices with their start and end apart: 11, of which 9 were waited for; matrix products, arithmetic and copies ran while one was open for 14% of the time, Pallas kernels for 0%

commit v1 on v0

v1 whole, which is shorter than its diff:
```python
from functools import partial

import jax
import jax.numpy as jnp
from jax import lax
from jax.sharding import PartitionSpec as P

BLOCK = 256
HALO = 16
epsilon = 1e-05
highest = lax.Precision.HIGHEST
f32 = jnp.float32
bf16 = jnp.bfloat16
AXES = ("seq", "shard")


class Slice:
    def __init__(self, mesh):
        self.seq = mesh.shape["seq"]
        self.shard = mesh.shape["shard"]
        self.Y = self.shard // 2
        self.X = self.Y
        self.Z = self.seq // self.X
        self.TP = 2 * self.X

    def place(self):
        s, k = lax.axis_index("seq"), lax.axis_index("shard")
        self.z, self.x = s // self.X, s % self.X
        self.y, self.c = k // 2, k % 2
        self.j = self.x * 2 + self.c

    def move(self, a, target):
        pairs = []
        for z in range(self.Z):
            for x in range(self.X):
                for y in range(self.Y):
                    for c in range(2):
                        to = target(z, x, y, c)
                        if to is None:
                            continue
                        tz, tx, ty, tc = to
                        if not 0 <= tz < self.Z:
                            continue
                        src = (z * self.X + x) * self.shard + y * 2 + c
                        dst = (tz * self.X + tx % self.X) * self.shard + (ty % self.Y) * 2 + tc
                        pairs.append((src, dst))
        return lax.ppermute(a, AXES, pairs)

    def swap_core(self, a):
        return self.move(a, lambda z, x, y, c: (z, x, y, 1 - c))

    def shift_x(self, a, d):
        return self.move(a, lambda z, x, y, c: (z, x + d, y, c))

    def shift_y(self, a, d):
        return self.move(a, lambda z, x, y, c: (z, x, y + d, c))

    def shift_z(self, a, d):
        return self.move(a, lambda z, x, y, c: (z + d, x, y, c))

    def swap_z(self, a):
        return self.move(a, lambda z, x, y, c: (z ^ 1, x, y, c))

    def by_core(self, own, other):
        first = self.c == 0
        return jnp.where(first, own, other), jnp.where(first, other, own)

    def gather_tp(self, a):
        parts = [a] + [self.shift_x(a, d) for d in range(1, self.X)]
        buf = jnp.stack(parts)
        buf = self.true_x(parts)
        lo, hi = self.by_core(buf, self.swap_core(buf))
        return jnp.stack([lo, hi])

    def true_x(self, parts):
        rows = []
        for tx in range(self.X):
            pick = parts[0]
            for d in range(1, self.X):
                pick = jnp.where((self.x - d) % self.X == tx, parts[d], pick)
            rows.append(pick)
        return jnp.stack(rows)

    def scatter_tp(self, a):
        keep, send = self.by_core(a[0], a[1])
        total = (keep.astype(f32) + self.swap_core(send).astype(f32)).astype(bf16)
        acc = lax.dynamic_index_in_dim(total, self.x, 0, False).astype(f32)
        for d in range(1, self.X):
            part = lax.dynamic_index_in_dim(total, (self.x + d) % self.X, 0, False)
            acc = acc + self.shift_x(part, d).astype(f32)
        return acc

    def sum_tp(self, a):
        total = a
        for dx in range(self.X):
            for dc in range(2):
                if dx or dc:
                    total = total + self.move(a, lambda z, x, y, c: (z, x + dx, y, c ^ dc))
        return total

    def own_first(self, a):
        width = a.shape[-1] // self.Y
        parts = [
            lax.dynamic_slice_in_dim(a, ((self.y - i) % self.Y) * width, width, a.ndim - 1)
            for i in range(self.Y)
        ]
        return jnp.concatenate(parts, axis=-1)

    def fetch_rows(self, half):
        n = half.shape[0]
        shared = (n // 3 + 15) // 16 * 16
        direct = n - 2 * shared
        even = self.z % 2 == 0
        full = [half]
        for d in range(1, self.Y):
            b0, b1 = half[direct : direct + shared], half[direct + shared :]
            r = self.shift_y(jnp.where(even, b0, b1), d)
            straight = self.shift_y(half[:direct], d)
            o = self.swap_z(r)
            full += [straight, jnp.where(even, r, o), jnp.where(even, o, r)]
        return jnp.concatenate(full, axis=0)

    def columns(self, local, pick):
        own = pick(local, self.j)
        other = self.swap_core(pick(local, self.x * 2 + 1 - self.c))
        lo, hi = self.by_core(own, other)
        return self.fetch_rows(jnp.concatenate([lo, hi], axis=0))

    def reduce_gradient(self, part):
        rows = part.shape[0] // self.shard
        p = part.reshape(self.Y, 2, rows, part.shape[1])
        acc = p[0].astype(f32)
        for i in range(1, self.Y):
            acc = acc + self.shift_y(p[i], -i).astype(f32)
        acc = acc.astype(bf16)
        keep, send = self.by_core(acc[0], acc[1])
        lo, hi = self.by_core(keep, self.swap_core(send))
        q = jnp.stack([lo, hi])
        half = self.Z // 2
        for step in range(half - 1):
            r = self.move(
                q,
                lambda z, x, y, c: (z + 1, x, y, c)
                if z == step
                else ((z - 1, x, y, c) if z == self.Z - 1 - step else None),
            )
            q = (q.astype(f32) + r.astype(f32)).astype(bf16)
        r = self.move(
            q,
            lambda z, x, y, c: (z + 1, x, y, c)
            if z == half - 1
            else ((z - 1, x, y, c) if z == half else None),
        )
        q = (q.astype(f32) + r.astype(f32)).astype(bf16)
        for step in range(half - 1):
            a, b = half - 1 - step, half + step
            r = self.move(
                q,
                lambda z, x, y, c: (z - 1, x, y, c)
                if z == a
                else ((z + 1, x, y, c) if z == b else None),
            )
            q = jnp.where((self.z == a - 1) | (self.z == b + 1), r, q)
        return [q] + [self.shift_x(q, d) for d in range(1, self.X)]

    def sum_small(self, v, over_tp):
        def ordered(a, n, own, shift):
            buf = jnp.zeros((n,) + a.shape, a.dtype)
            buf = lax.dynamic_update_index_in_dim(buf, a, own, 0)
            for d in range(1, n):
                buf = lax.dynamic_update_index_in_dim(buf, shift(a, d), (own - d) % n, 0)
            return buf

        def turn_z(a, d):
            return self.move(a, lambda z, x, y, c: ((z + d) % self.Z, x, y, c))

        v = jnp.sum(ordered(v, self.Z, self.z, turn_z), axis=0)
        v = jnp.sum(ordered(v, self.Y, self.y, self.shift_y), axis=0)
        v = ordered(v, self.X, self.x, self.shift_x)
        v = ordered(v, 2, self.c, lambda a, d: self.swap_core(a))
        return jnp.sum(v, axis=(0, 1)) if over_tp else v


def silu_slope(v):
    g = jax.nn.sigmoid(v)
    return g * (1.0 + v * (1.0 - g))


def low_dot(a, b, dims):
    return lax.dot_general(a.astype(bf16), b.astype(bf16), dims, preferred_element_type=f32)


def mm(a, b):
    return low_dot(a, b, (((a.ndim - 1,), (0,)), ((), ())))


def intra_forward(keys, queries, cum, seg, xs):
    pos = lax.iota(jnp.int32, BLOCK)
    allowed = (pos[:, None] >= pos[None, :])[None] & (seg[:, :, None] == seg[:, None, :])
    gram = jnp.einsum("btn,bsn->bts", queries.astype(bf16), keys.astype(bf16), preferred_element_type=f32)
    ct = cum.transpose(0, 2, 1)
    gaps = jnp.where(allowed[:, None], ct[:, :, :, None] - ct[:, :, None, :], -1e30)
    weights = (jnp.exp(gaps) * gram[:, None]).astype(bf16)
    return jnp.einsum("bhts,bshp->bthp", weights, xs.astype(bf16), preferred_element_type=f32)


def intra_backward(keys, queries, cum, step, seg, x, d_out):
    pos = lax.iota(jnp.int32, BLOCK)
    allowed = (pos[:, None] >= pos[None, :])[None] & (seg[:, :, None] == seg[:, None, :])
    gram = jnp.einsum("btn,bsn->bts", queries.astype(bf16), keys.astype(bf16), preferred_element_type=f32)
    ct = cum.transpose(0, 2, 1)
    gaps = jnp.where(allowed[:, None], ct[:, :, :, None] - ct[:, :, None, :], -1e30)
    decay = jnp.exp(gaps)
    e = jnp.einsum("bthp,bshp->bhts", d_out.astype(bf16), x.astype(bf16), preferred_element_type=f32)
    st = step.transpose(0, 2, 1)
    le = decay * e * st[:, :, None, :]
    zsum = jnp.sum(le, axis=1)
    m = le * gram[:, None]
    across = (jnp.sum(m, axis=3) - jnp.sum(m, axis=2)).transpose(0, 2, 1)
    dxs = jnp.einsum(
        "bhts,bthp->bshp", (decay * gram[:, None]).astype(bf16), d_out.astype(bf16), preferred_element_type=f32
    )
    zl = zsum.astype(bf16)
    d_queries = jnp.einsum("bts,bsn->btn", zl, keys.astype(bf16), preferred_element_type=f32)
    d_keys = jnp.einsum("bts,btn->bsn", zl, queries.astype(bf16), preferred_element_type=f32)
    return dxs, across, d_keys, d_queries


def body(
    g,
    tokens,
    in_weight,
    out_weight,
    pre_gain,
    conv_kernel,
    conv_bias,
    step_bias,
    decay_log,
    skip_gain,
    gate_gain,
    segments,
    cotangent,
):
    g.place()
    heads = step_bias.shape[0]
    inner = gate_gain.shape[0]
    channels = conv_bias.shape[0]
    shared = channels - inner
    state = shared // 2
    taps = conv_kernel.shape[0]
    hd = inner // heads
    HL = heads // g.TP
    HW = HL * hd
    SW = shared // g.TP
    own_len = tokens.shape[1]
    width = tokens.shape[2]
    T = own_len * g.X
    nb = T // BLOCK
    NB = 2 * nb
    j = g.j

    series = tokens[0].astype(f32)
    scale = lax.rsqrt(jnp.mean(series * series, axis=-1, keepdims=True) + epsilon)
    normed = g.own_first((series * scale * pre_gain[None, :]).astype(bf16))
    n_all = g.gather_tp(normed).reshape(2, T, width)
    halo = g.shift_z(n_all[:, T - HALO :], 1)
    n_ext = jnp.concatenate([halo, n_all], axis=1).reshape(2 * (HALO + T), width)
    n_all = n_all.reshape(2 * T, width)
    cot_all = g.gather_tp(g.own_first(cotangent[0])).reshape(2 * T, width)

    def pick_packed(w, jj):
        a = lax.dynamic_slice_in_dim(w, inner + HW * jj, HW, 1)
        return jnp.concatenate([a, w[:, inner * 2 :]], axis=1)

    def pick_gate(w, jj):
        return lax.dynamic_slice_in_dim(w, HW * jj, HW, 1)

    w_packed = g.columns(in_weight, pick_packed)
    w_gate = g.columns(in_weight, pick_gate)
    w_out = g.columns(out_weight, pick_gate)

    s_lo, s_hi = g.by_core(segments, g.swap_core(segments))
    seg_all = jnp.concatenate([s_lo, s_hi], axis=0)
    start = g.z * T
    seg_pad = jnp.concatenate([jnp.full((2, HALO), -1, jnp.int32), seg_all], axis=1)
    seg_ext = lax.dynamic_slice_in_dim(seg_pad, start, T + HALO, 1)
    seg = seg_ext[:, HALO:]
    same = [
        (seg_ext[:, HALO - k : HALO - k + T] == seg).astype(f32)[:, :, None] for k in range(taps)
    ]
    seg_b = seg.reshape(NB, BLOCK)
    block_end = seg_b[:, BLOCK - 1]
    prior_end = seg_ext.reshape(2, T + HALO)[:, HALO - 1 :][:, : T : BLOCK].reshape(NB)

    packed = mm(n_ext, w_packed).astype(bf16).reshape(2, HALO + T, HW + shared + heads)

    def own_channels(a):
        x_part = lax.dynamic_slice_in_dim(a, HW * j, HW, a.ndim - 1)
        return jnp.concatenate([x_part, a[..., inner:]], axis=-1)

    kernel_own = own_channels(conv_kernel)
    bias_own = own_channels(conv_bias)
    CW = HW + shared
    conv_in = packed[:, :, :CW].astype(f32)
    pre = bias_own[None, None, :]
    for k in range(taps):
        pre = pre + kernel_own[k] * conv_in[:, HALO - k : HALO - k + T] * same[k]
    act = jax.nn.silu(pre)
    x = act[:, :, :HW].astype(bf16).reshape(NB, BLOCK, HW)
    keys = act[:, :, HW : HW + state].astype(bf16).reshape(NB, BLOCK, state)
    queries = act[:, :, HW + state :].astype(bf16).reshape(NB, BLOCK, state)

    def own_heads(a):
        return lax.dynamic_slice_in_dim(a, HL * j, HL, a.ndim - 1)

    raw = own_heads(packed[:, HALO:, CW:]).astype(f32) + own_heads(step_bias)
    step = jax.nn.softplus(raw).reshape(NB, BLOCK, HL)
    rate = jnp.exp(own_heads(decay_log))
    skip = own_heads(skip_gain)
    log_decay = -rate * step
    pos = lax.iota(jnp.int32, BLOCK)
    lower = (pos[:, None] >= pos[None, :]).astype(f32)
    cum = jnp.einsum("ts,bsh->bth", lower, log_decay, precision=highest)
    cum_end = cum[:, BLOCK - 1, :]
    reach = jnp.where((seg_b == prior_end[:, None])[:, :, None], jnp.exp(cum), 0.0)
    tail = jnp.where(
        (seg_b == block_end[:, None])[:, :, None], jnp.exp(cum_end[:, None, :] - cum), 0.0
    )
    carry = jnp.where((prior_end == block_end)[:, None], jnp.exp(cum_end), 0.0)

    def spread(a):
        return jnp.repeat(a, hd, axis=-1)

    def per_head(a):
        return a.reshape(a.shape[:-1] + (HL, hd)).sum(axis=-1)

    xf = x.astype(f32)
    step_wide = spread(step)
    xs = xf * step_wide
    tail_wide = spread(tail)
    reach_wide = spread(reach)
    xst = (xs * tail_wide).astype(bf16)
    s_block = jnp.einsum("bsn,bsi->bni", keys, xst, preferred_element_type=f32).reshape(
        2, nb, state, HW
    )
    carry_b = carry.reshape(2, nb, HL)
    carry_wide = spread(carry_b)[:, :, None, :]

    def exchange(cur, direction):
        cc = jnp.prod(carry_b, axis=1)
        d = 1
        while d < g.Z // 2:
            r = g.shift_z(cur.astype(bf16), direction * d).astype(f32)
            cur = cur + spread(cc)[:, None, :] * r
            if 2 * d < g.Z // 2:
                cc = cc * g.shift_z(cc, direction * d)
            d *= 2
        return g.shift_z(cur.astype(bf16), direction).astype(f32)

    s_range = s_block[:, 0]
    for b in range(1, nb):
        s_range = s_block[:, b] + carry_wide[:, b] * s_range
    enter = [exchange(s_range, 1)]
    for b in range(nb - 1):
        enter.append(s_block[:, b] + carry_wide[:, b] * enter[b])
    enter = jnp.stack(enter, axis=1).astype(bf16).reshape(NB, state, HW)

    y_local = intra_forward(keys, queries, cum, seg_b, xs.reshape(NB, BLOCK, HL, hd)).reshape(
        NB, BLOCK, HW
    )
    from_state = (
        jnp.einsum("btn,bni->bti", queries, enter, preferred_element_type=f32) * reach_wide
    )
    skip_wide = spread(skip)
    mixed = (y_local + from_state + skip_wide * xf).astype(bf16).astype(f32)

    gate = mm(n_all, w_gate).reshape(NB, BLOCK, HW)
    out_grad = mm(cot_all, w_out).reshape(NB, BLOCK, HW)
    gain_own = lax.dynamic_slice_in_dim(gate_gain, HW * j, HW, 0)
    gate_act = jax.nn.silu(gate)
    gated = mixed * gate_act
    lifted = out_grad * gain_own
    sums = jnp.stack([jnp.sum(gated * gated, axis=-1), jnp.sum(gated * lifted, axis=-1)])
    sums = g.sum_tp(sums) / inner
    r = lax.rsqrt(sums[0] + epsilon)[:, :, None]
    normed_out = (gated * r * gain_own).astype(bf16).reshape(2 * T, HW)
    gated_grad = r * lifted - gated * (r * r * r) * sums[1][:, :, None]
    gain_grad = jnp.sum(out_grad * gated * r, axis=(0, 1))
    d_out = (gated_grad * gate_act).astype(bf16)
    gate_grad = (gated_grad * mixed * silu_slope(gate)).astype(bf16).reshape(2 * T, HW)

    rows_first = (((0,), (0,)), ((), ()))
    rows_last = (((1,), (1,)), ((), ()))
    out_part = low_dot(cot_all, normed_out, rows_first).astype(bf16)
    gate_part = low_dot(n_all, gate_grad, rows_first).astype(bf16)
    out_sum = g.reduce_gradient(out_part)
    gate_sum = g.reduce_gradient(gate_part)
    branch = low_dot(normed_out, w_out, rows_last).astype(bf16)
    branch = g.own_first_back(g.scatter_tp(branch.reshape(2, g.X, own_len, width)))
    block_output = (series + branch).astype(bf16)[None]

    d_f = d_out.astype(f32)
    d_reach = (d_f * reach_wide).astype(bf16)
    de_block = jnp.einsum("btn,bti->bni", queries, d_reach, preferred_element_type=f32).reshape(
        2, nb, state, HW
    )
    d_range = de_block[:, nb - 1]
    for b in range(nb - 2, -1, -1):
        d_range = de_block[:, b] + carry_wide[:, b] * d_range
    leave = [exchange(d_range, -1)]
    for b in range(nb - 1, 0, -1):
        leave.insert(0, de_block[:, b] + carry_wide[:, b] * leave[0])
    leave = jnp.stack(leave, axis=1).astype(bf16).reshape(NB, state, HW)
    dxs, across, d_keys, d_queries = intra_backward(
        keys,
        queries,
        cum,
        step,
        seg_b,
        x.reshape(NB, BLOCK, HL, hd),
        d_out.reshape(NB, BLOCK, HL, hd),
    )
    key_leave = (
        jnp.einsum("bsn,bni->bsi", keys, leave, preferred_element_type=f32) * tail_wide
    )
    dxs = dxs.reshape(NB, BLOCK, HW) + key_leave
    d_keys = d_keys + jnp.einsum("bsi,bni->bsn", xst, leave, preferred_element_type=f32)
    d_queries = d_queries + jnp.einsum("bti,bni->btn", d_reach, enter, preferred_element_type=f32)
    x_grad = skip_wide * d_f + step_wide * dxs
    came_in = per_head(d_f * from_state)
    goes_out = per_head(xs * key_leave)
    through = carry * per_head(jnp.sum(enter.astype(f32) * leave.astype(f32), axis=1))
    decay_grad = (
        jnp.einsum("ts,bth->bsh", lower, across + came_in, precision=highest)
        + jnp.einsum("ts,bsh->bth", lower - jnp.eye(BLOCK, dtype=f32), goes_out, precision=highest)
        + through[:, None, :]
    )
    step_grad = per_head(xf * dxs) - rate * decay_grad
    decay_log_grad = -rate * jnp.sum(step * decay_grad, axis=(0, 1))
    skip_grad = jnp.sum(per_head(d_f * xf), axis=(0, 1))
    raw_grad = step_grad.reshape(2, T, HL) * jax.nn.sigmoid(raw)
    step_bias_grad = jnp.sum(raw_grad, axis=(0, 1))

    both = jnp.concatenate([d_keys, d_queries], axis=-1).astype(bf16).reshape(2, T, shared)
    both_sum = lax.dynamic_slice_in_dim(both, SW * j, SW, 2).astype(f32)
    for dx in range(g.X):
        for dc in range(2):
            if dx or dc:
                jj = (g.x + dx) % g.X * 2 + (g.c ^ dc)
                part = lax.dynamic_slice_in_dim(both, SW * jj, SW, 2)
                part = g.move(part, lambda z, x, y, c: (z, x + dx, y, c ^ dc))
                both_sum = both_sum + part.astype(f32)

    def own_shared(a):
        return lax.dynamic_slice_in_dim(a, HW + SW * j, SW, a.ndim - 1)

    def conv_back(grad, pre_own, kernel, values):
        cg = grad * silu_slope(pre_own)
        back = 0.0
        kg = []
        for k in range(taps):
            m = cg * same[k]
            kg.append(jnp.sum(m * values[:, HALO - k : HALO - k + T], axis=(0, 1)))
            back = back + jnp.pad(kernel[k] * m, ((0, 0), (HALO - k, k), (0, 0)))
        return back.astype(bf16), jnp.stack(kg), jnp.sum(cg, axis=(0, 1))

    x_back, x_kg, x_bg = conv_back(
        x_grad.reshape(2, T, HW), pre[:, :, :HW], kernel_own[:, :HW], conv_in[:, :, :HW]
    )
    s_back, s_kg, s_bg = conv_back(
        both_sum, own_shared(pre), own_shared(kernel_own), own_shared(conv_in)
    )
    raw_low = jnp.pad(raw_grad, ((0, 0), (HALO, 0), (0, 0))).astype(bf16)
    tail_back = jnp.concatenate([s_back, raw_low], axis=-1)
    x_back = x_back.reshape(2 * (HALO + T), HW)
    tail_back = tail_back.reshape(2 * (HALO + T), SW + HL)
    x_part = low_dot(n_ext, x_back, rows_first).astype(bf16)
    tail_part = low_dot(n_ext, tail_back, rows_first).astype(bf16)
    x_sum = g.reduce_gradient(x_part)
    tail_sum = g.reduce_gradient(tail_part)

    w_tail = jnp.concatenate(
        [
            lax.dynamic_slice_in_dim(w_packed, HW + SW * j, SW, 1),
            lax.dynamic_slice_in_dim(w_packed, CW + HL * j, HL, 1),
        ],
        axis=1,
    )
    packed_back = jnp.concatenate([x_back, tail_back], axis=1)
    w_back = jnp.concatenate([w_packed[:, :HW], w_tail], axis=1)
    n_grad_ext = low_dot(packed_back, w_back, rows_last).reshape(2, HALO + T, width)
    n_grad = n_grad_ext[:, HALO:] + low_dot(gate_grad, w_gate, rows_last).reshape(2, T, width)
    spill = g.shift_z(n_grad_ext[:, :HALO].astype(bf16), -1).astype(f32)
    n_grad = n_grad + jnp.pad(spill, ((0, 0), (T - HALO, 0), (0, 0)))
    n_grad = g.own_first_back(
        g.scatter_tp(n_grad.astype(bf16).reshape(2, g.X, own_len, width))
    )
    pre_grad = jnp.sum(n_grad * series * scale, axis=0)
    lifted_n = n_grad * pre_gain[None, :]
    token_gradient = (
        cotangent[0].astype(f32)
        + scale * lifted_n
        - series * scale**3 * jnp.mean(series * lifted_n, axis=-1, keepdims=True)
    )[None]

    k_all = jnp.concatenate([x_kg, s_kg], axis=1)
    b_all = jnp.concatenate([x_bg, s_bg])
    small = jnp.concatenate(
        [gain_grad, k_all.reshape(-1), b_all, step_bias_grad, decay_log_grad, skip_grad]
    )
    n_small = small.shape[0]
    small = jnp.pad(small, (0, -n_small % 1024)).reshape(-1, 128)
    small = g.sum_small(small, False)
    small = small.transpose(1, 0, 2, 3).reshape(g.TP, -1)[:, :n_small]
    pre_total = g.sum_small(pre_grad.reshape(-1, 128), True).reshape(-1)
    at = 0
    gain_total = small[:, :HW].reshape(-1)
    at = HW
    kt = small[:, at : at + taps * (HW + SW)].reshape(g.TP, taps, HW + SW).transpose(1, 0, 2)
    at += taps * (HW + SW)
    kernel_total = jnp.concatenate(
        [kt[:, :, :HW].reshape(taps, -1), kt[:, :, HW:].reshape(taps, -1)], axis=1
    )
    bt = small[:, at : at + HW + SW]
    at += HW + SW
    bias_total = jnp.concatenate([bt[:, :HW].reshape(-1), bt[:, HW:].reshape(-1)])
    step_total = small[:, at : at + HL].reshape(-1)
    decay_total = small[:, at + HL : at + 2 * HL].reshape(-1)
    skip_total = small[:, at + 2 * HL : at + 3 * HL].reshape(-1)

    def place(sums, first, size):
        parts = g.true_x([q[:, :, first : first + size] for q in sums])
        return [parts[tx, tc] for tx in range(g.X) for tc in range(2)]

    columns = (
        place(gate_sum, 0, HW)
        + place(x_sum, 0, HW)
        + place(tail_sum, 0, SW)
        + place(tail_sum, SW, HL)
    )
    in_weight_gradient = jnp.concatenate(columns, axis=1).astype(f32)
    out_weight_gradient = jnp.concatenate(place(out_sum, 0, HW), axis=1).astype(f32)
    return (
        block_output,
        token_gradient,
        in_weight_gradient,
        out_weight_gradient,
        pre_total,
        kernel_total,
        bias_total,
        step_total,
        decay_total,
        skip_total,
        gain_total,
    )


def own_first_back(self, a):
    width = a.shape[-1] // self.Y
    parts = []
    for t in range(self.Y):
        parts.append(
            lax.dynamic_slice_in_dim(a, ((self.y - t) % self.Y) * width, width, a.ndim - 1)
        )
    return jnp.concatenate(parts, axis=-1)


Slice.own_first_back = own_first_back


def solution(mesh):
    placed = (
        P("shard", "seq", None),
        P("shard", None),
        P("shard", None),
        P(),
        P(),
        P(),
        P(),
        P(),
        P(),
        P(),
        P("shard", None),
        P("shard", "seq", None),
    )
    return jax.shard_map(
        partial(body, Slice(mesh)),
        mesh=mesh,
        in_specs=placed,
        out_specs=(
            P("shard", "seq", None),
            P("shard", "seq", None),
            P("shard", None),
            P("shard", None),
            P(),
            P(),
            P(),
            P(),
            P(),
            P(),
            P(),
        ),
        check_vma=False,
    )
```

time: 1730 us -> 1090 us (0.63)
  waiting for transfers between devices: 1060 us -> 471 us
  blocking collectives: 153 us -> 0 us
  matrix products: 212 us -> 126 us
  local copies, waits for them, and re-layouts: 123 us -> 201 us
  starting transfers between devices: 21.8 us -> 92.7 us
  other arithmetic: 140 us -> 181 us
    ppermute x0 -> x69, waiting for transfers between devices: none -> 471 us  [move(): return lax.ppermute(a, AXES, pairs)]
    psum x2 -> x0, waiting for transfers between devices: 431 us -> none  [the longest x1 331 us: body(): summed = lax.psum(term_rows, 'seq').astype(jnp.float32)]
    reduce_scatter x2 -> x0, waiting for transfers between devices: 369 us -> none  [the longest x1 352 us: body(): lax.psum_scatter(jnp.concatenate([in_part, out_part], axis=1).astype(jnp....]
    all_gather x3 -> x0, waiting for transfers between devices: 234 us -> none  [the longest x1 214 us: body(): lax.all_gather(in_weight, 'shard', axis=0, tiled=True)]
    all_to_all x2 -> x0, blocking collectives: 110 us -> none  [the longest x1 58.5 us: body(): lax.all_to_all(mixed.astype(jnp.bfloat16), 'seq', split_axis=0, concat_ax...]
    ppermute x0 -> x69, starting transfers between devices: none -> 92.7 us  [move(): return lax.ppermute(a, AXES, pairs)]
    dot_general x20 -> x25, matrix products: 209 us -> 126 us  [the longest x10 76.2 us: low_dot(): lax.dot_general(a.astype(bf16), b.astype(bf16), dims, preferred_element_t...]
    psum x1 -> x0, blocking collectives: 43.3 us -> none  [body(): lax.psum((pre_gain_gradient, kernel_gradient, conv_bias_gradient, step_bi...]
  transfers between devices with their start and end apart: 11 -> 69, of which waited for: 9 -> 28; matrix products, arithmetic and copies ran while one was open for 14% -> 32% of each run, Pallas kernels for 0% -> 0%
where the time goes in v1:
time: 1090 us; the launch traced here: 1080 us
  waiting for transfers between devices  471 us (43%)
  local copies, waits for them, and re-layouts  201 us (18%)
  other arithmetic  181 us (17%)
  matrix products  126 us (12%)
  starting transfers between devices  92.7 us (9%)
    ppermute x69, waiting for transfers between devices, move(): return lax.ppermute(a, AXES, pairs)  471 us
    ppermute x69, starting transfers between devices, move(): return lax.ppermute(a, AXES, pairs)  92.7 us
    dot_general x10, matrix products, low_dot(): lax.dot_general(a.astype(bf16), b.astype(bf16), dims, preferred_element_t...  76.2 us
    unnamed x252, local copies, waits for them, and re-layouts  43.4 us
  transfers between devices with their start and end apart: 69, of which 28 were waited for; matrix products, arithmetic and copies ran while one was open for 32% of the time, Pallas kernels for 0%

profile of v1, /device:TPU:1, one launch (start us, length us, event | category | flops | bytes accessed | tf_op | source)
XLA Modules:
  0.0 1075.6 jit_solution(12951694085987235412)
XLA Ops:
  34.7 22.5 %collective-permute-done = bf16[256,2048]{1,0:T(8,128)(2,1)} collective-permute-done((bf16[256,2048]{1,0:T(8,128)(2,1)}, bf16[256,2048]{1,0:T(8,128)(2,1)}, u32[]{:S(2)}, u32[]{:S(2)}) %collective-permute-start) | collective-permute-done | bytes 1048608 | tf_op jit(solution)/shard_map/ppermute | solution.py:47
  90.9 24.1 %collective-permute-done.11 = bf16[320,1024]{1,0:T(8,128)(2,1)} collective-permute-done((bf16[320,1024]{1,0:T(8,128)(2,1)}, bf16[320,1024]{1,0:T(8,128)(2,1)}, u32[]{:S(2)}, u32[]{:S(2)}) %collective-permute-start.11) | collective-permute-done | bytes 655392 | tf_op jit(solution)/shard_map/ppermute | solution.py:47
  121.4 28.3 %collective-permute-done.12 = bf16[352,1024]{1,0:T(8,128)(2,1)S(1)} collective-permute-done((bf16[352,1024]{1,0:T(8,128)(2,1)}, bf16[352,1024]{1,0:T(8,128)(2,1)S(1)}, u32[]{:S(2)}, u32[]{:S(2)}) %collective-permute-start.12) | collective-permute-done | bytes 720928 | tf_op jit(solution)/shard_map/ppermute | solution.py:47
  157.7 13.0 %collective-permute-done.5 = bf16[352,1344]{1,0:T(8,128)(2,1)} collective-permute-done((bf16[352,1344]{1,0:T(8,128)(2,1)}, bf16[352,1344]{1,0:T(8,128)(2,1)}, u32[]{:S(2)}, u32[]{:S(2)}) %collective-permute-start.5) | collective-permute-done | bytes 946208 | tf_op jit(solution)/shard_map/ppermute | solution.py:47
  192.7 8.8 fusion.41
  206.9 9.7 concatenate.116
  222.1 7.1 convolution_convert_fusion
  235.1 8.0 multiply_convert_fusion.3
  276.6 8.5 multiply_convert_fusion.6
  333.7 12.0 %multiply_reduce_fusion.4 = (f32[4,256]{1,0:T(4,128)S(1)}, f32[4,256]{1,0:T(4,128)S(1)}, bf16[4,256,1024]{2,1,0:T(8,128)(2,1)}, f32[4,256,1024]{2,1,0:T(8,128)}) fusion(f32[4,256,1024]{2,1,0:T(8,128)} %fusion.41, f32[1024]{0:T(1024)S(1)} %copy-done.90, f32[4,256,1024]{2,1,0:T(8,128)S(1)} %bitcast.466, f32[1024]{0:T(1024)S(1)} %mul.704, ...), kind=kOutput, calls=%fused_computation.95 | convolution fusion | flops 4310693888 | bytes 31473664 | tf_op jit(solution)/shard_map/dot_general | solution.py:190
  355.1 7.7 fusion.31
  384.3 12.2 %multiply_reduce_fusion = (f32[4,16,256]{2,1,0:T(8,128)}, f32[4,16,256]{2,1,0:T(8,128)}, bf16[4,256,256]{2,1,0:T(8,128)(2,1)S(1)}) fusion(f32[4,256,256]{2,1,0:T(8,128)} %copy-done.53, f32[4,16,256]{2,1,0:T(8,128)} %copy.379, bf16[4,256,16,64]{1,3,2,0:T(8,128)(2,1)} %bitcast.521, bf16[4,256,16,64]{1,0,3,2:T(4,128)(2,1)} %reshape.487, ...), kind=kOutput, calls=%fused_computation.3 | convolution fusion | flops 570130432 | bytes 6291456 | tf_op jit(solution)/shard_map/bthp,bshp->bhts/dot_general | solution.py:214
  400.1 7.4 convolution_convert_fusion.3
  421.7 7.6 convolution_convert_fusion.1
  435.6 10.6 collective-permute-done.26
  447.6 14.0 %fusion.29 = (f32[4,256,1024]{2,1,0:T(8,128)}, f32[4,256,1024]{2,1,0:T(8,128)}, f32[4,256,1024]{2,1,0:T(8,128)}, f32[4,256,1024]{2,1,0:T(8,128)}) fusion(bf16[4,256,1024]{2,1,0:T(8,128)(2,1)S(1)} %get-tuple-element.112, f32[4,256,1024]{2,1,0:T(8,128)} %copy.355, f32[1024]{0:T(1024)S(1)} %mul.704, f32[4,256,1024]{2,1,0:T(8,128)} %copy.374, ...), kind=kOutput, calls=%fused_computation.50 | convolution fusion | flops 277872640 | bytes 45355008 | tf_op jit(solution)/shard_map/bsn,bni->bsi/dot_general | solution.py:424
  467.0 14.9 %fusion.35 = (f32[1024]{0:T(1024)S(1)}, f32[1024]{0:T(1024)}, f32[1024]{0:T(1024)}, f32[1024]{0:T(1024)}, f32[1024]{0:T(1024)}, /*index=5*/f32[2,512,1024]{1,2,0:T(8,128)S(1)}) fusion(f32[2,528,1280]{1,2,0:T(8,128)} %copy-done, f32[2,512]{1,0:T(2,128)S(1)} %get-tuple-element.136, f32[2,512]{1,0:T(2,128)S(1)} %get-tuple-element.249, ...), kind=kLoop, calls=%fused_computation.60 | loop fusion | flops 20966400 | bytes 29392896 | tf_op jit(solution)/shard_map/reduce_sum | solution.py:463
  491.5 9.6 bitcast_convert_fusion
  550.1 7.6 fusion.21
  569.9 65.2 %collective-permute-done.66 = f32[56,128]{1,0:T(8,128)S(1)} collective-permute-done((f32[56,128]{1,0:T(8,128)S(1)}, f32[56,128]{1,0:T(8,128)S(1)}, u32[]{:S(2)}, u32[]{:S(2)}) %collective-permute-start.66) | collective-permute-done | bytes 28704 | tf_op jit(solution)/shard_map/ppermute | solution.py:47
  643.8 9.8 fusion.3
  673.7 13.9 %collective-permute-done.49 = bf16[2,512,80]{2,1,0:T(8,128)(2,1)S(1)} collective-permute-done((bf16[2,512,80]{2,1,0:T(8,128)(2,1)S(1)}, bf16[2,512,80]{2,1,0:T(8,128)(2,1)S(1)}, u32[]{:S(2)}, u32[]{:S(2)}) %collective-permute-start.49) | collective-permute-done | bytes 163872 | tf_op jit(solution)/shard_map/ppermute | solution.py:47
  719.6 36.5 %collective-permute-done.35 = bf16[2,512,1024]{2,1,0:T(8,128)(2,1)S(1)} collective-permute-done((bf16[2,512,1024]{2,1,0:T(8,128)(2,1)S(1)}, bf16[2,512,1024]{2,1,0:T(8,128)(2,1)S(1)}, u32[]{:S(2)}, u32[]{:S(2)}) %collective-permute-start.35) | collective-permute-done | bytes 2097184 | tf_op jit(solution)/shard_map/ppermute | solution.py:47
  758.9 42.1 %collective-permute-done.53 = bf16[2,512,1024]{2,1,0:T(8,128)(2,1)S(1)} collective-permute-done((bf16[2,512,1024]{2,1,0:T(8,128)(2,1)S(1)}, bf16[2,512,1024]{2,1,0:T(8,128)(2,1)S(1)}, u32[]{:S(2)}, u32[]{:S(2)}) %collective-permute-start.53) | collective-permute-done | bytes 2097184 | tf_op jit(solution)/shard_map/ppermute | solution.py:47
  808.3 37.7 %collective-permute-done.41 = bf16[2,512,1024]{2,1,0:T(8,128)(2,1)S(1)} collective-permute-done((bf16[2,512,1024]{2,1,0:T(8,128)(2,1)S(1)}, bf16[2,512,1024]{2,1,0:T(8,128)(2,1)S(1)}, u32[]{:S(2)}, u32[]{:S(2)}) %collective-permute-start.41) | collective-permute-done | bytes 2097184 | tf_op jit(solution)/shard_map/ppermute | solution.py:47
  862.4 39.4 %collective-permute-done.59 = f32[16,128]{1,0:T(8,128)S(1)} collective-permute-done((f32[16,128]{1,0:T(8,128)S(1)}, f32[16,128]{1,0:T(8,128)S(1)}, u32[]{:S(2)}, u32[]{:S(2)}) %collective-permute-start.59) | collective-permute-done | bytes 8224 | tf_op jit(solution)/shard_map/ppermute | solution.py:47
  912.9 33.8 %collective-permute-done.55 = bf16[2,512,1024]{2,1,0:T(8,128)(2,1)} collective-permute-done((bf16[2,512,1024]{2,1,0:T(8,128)(2,1)}, bf16[2,512,1024]{2,1,0:T(8,128)(2,1)}, u32[]{:S(2)}, u32[]{:S(2)}) %collective-permute-start.55) | collective-permute-done | bytes 2097184 | tf_op jit(solution)/shard_map/ppermute | solution.py:47
  955.1 8.6 collective-permute-start.62
  965.2 26.5 %collective-permute-done.43 = bf16[2,512,1024]{2,1,0:T(8,128)(2,1)} collective-permute-done((bf16[2,512,1024]{2,1,0:T(8,128)(2,1)}, bf16[2,512,1024]{2,1,0:T(8,128)(2,1)}, u32[]{:S(2)}, u32[]{:S(2)}) %collective-permute-start.43) | collective-permute-done | bytes 2097184 | tf_op jit(solution)/shard_map/ppermute | solution.py:47
  1006.8 38.1 %collective-permute-done.44 = bf16[2,512,1024]{2,1,0:T(8,128)(2,1)S(1)} collective-permute-done((bf16[2,512,1024]{2,1,0:T(8,128)(2,1)S(1)}, bf16[2,512,1024]{2,1,0:T(8,128)(2,1)S(1)}, u32[]{:S(2)}, u32[]{:S(2)}) %collective-permute-start.44) | collective-permute-done | bytes 2097184 | tf_op jit(solution)/shard_map/ppermute | solution.py:47
  1048.2 14.2 %concatenate.137 = bf16[512,8512]{1,0:T(8,128)(2,1)} concatenate(bf16[512,1024]{1,0:T(8,128)(2,1)S(1)} %get-tuple-element.195, bf16[512,1024]{1,0:T(8,128)(2,1)S(1)} %get-tuple-element.194, bf16[512,1024]{1,0:T(8,128)(2,1)} %get-tuple-element.193, bf16[512,1024]{1,0:T(8,128)(2,1)S(1)} %get-tuple-element.192, bf16[512,1024]{1,0:T(8,128)(2,1)} %get-tuple-element.191, ...), dimensions={1} | concatenate | bytes 17432576 | tf_op jit(solution)/shard_map/concatenate | solution.py:541
  1062.3 13.0 %copy.399 = f32[512,8512]{0,1:T(8,128)} copy(bf16[512,8512]{1,0:T(8,128)(2,1)} %concatenate.137) | data formatting | bytes 26148864
  (658 shorter events, 460.0 us)
Async XLA Ops:
  6.9 72.8 %collective-permute-start.3 = (bf16[512,1344]{0,1:T(8,128)(2,1)}, bf16[512,1344]{0,1:T(8,128)(2,1)}, u32[]{:S(2)}, u32[]{:S(2)}) collective-permute-start(bf16[512,1344]{0,1:T(8,128)(2,1)} %pad_maximum_fusion.8), channel_id=1, source_target_pairs={{0,1},{1,0},{2,3},{3,2},{4,5},{5,4},{6,7},{7,6},{8,9},{9,8},{10,11... | collective-permute-start | bytes 4128776 | tf_op jit(solution)/shard_map/ppermute | solution.py:47
  13.3 43.8 %collective-permute-start = (bf16[256,2048]{1,0:T(8,128)(2,1)}, bf16[256,2048]{1,0:T(8,128)(2,1)}, u32[]{:S(2)}, u32[]{:S(2)}) collective-permute-start(bf16[256,2048]{1,0:T(8,128)(2,1)} %pad_maximum_fusion.10), channel_id=1, source_target_pairs={{0,4},{1,5},{2,6},{3,7},{4,0},{5,1},{6,2},{7,3},{8,12},{9,13},{10,... | collective-permute-start | bytes 3145736 | tf_op jit(solution)/shard_map/ppermute | solution.py:47
  15.9 47.3 %collective-permute-start.16 = (bf16[512,1024]{1,0:T(8,128)(2,1)}, bf16[512,1024]{1,0:T(8,128)(2,1)}, u32[]{:S(2)}, u32[]{:S(2)}) collective-permute-start(bf16[512,1024]{1,0:T(8,128)(2,1)} %constant_dynamic-slice_fusion.9), channel_id=1, source_target_pairs={{0,1},{1,0},{2,3},{3,2},{4,5},{5,4},{6,7},{7,6},{8,9},{9,8},{10,11... | collective-permute-start | bytes 3145736 | tf_op jit(solution)/shard_map/ppermute | solution.py:47
  25.8 46.6 %collective-permute-start.10 = (bf16[512,1024]{1,0:T(8,128)(2,1)}, bf16[512,1024]{1,0:T(8,128)(2,1)}, u32[]{:S(2)}, u32[]{:S(2)}) collective-permute-start(bf16[512,1024]{1,0:T(8,128)(2,1)} %copy.412), channel_id=1, source_target_pairs={{0,1},{1,0},{2,3},{3,2},{4,5},{5,4},{6,7},{7,6},{8,9},{9,8},{10,11... | collective-permute-start | bytes 3145736 | tf_op jit(solution)/shard_map/ppermute | solution.py:47
  62.6 118.9 %collective-permute-start.1 = (bf16[2,256,2048]{2,1,0:T(8,128)(2,1)}, bf16[2,256,2048]{2,1,0:T(8,128)(2,1)}, u32[]{:S(2)}, u32[]{:S(2)}) collective-permute-start(bf16[2,256,2048]{2,1,0:T(8,128)(2,1)} %pad_maximum_fusion.2), channel_id=1, source_target_pairs={{0,1},{1,0},{2,3},{3,2},{4,5},{5,4},{6,7},{7,6},{8,9},{9,8},{10,11... | collective-permute-start | bytes 6291464 | tf_op jit(solution)/shard_map/ppermute | solution.py:47
  72.2 44.1 %collective-permute-start.18 = (bf16[352,1024]{1,0:T(8,128)(2,1)}, bf16[352,1024]{1,0:T(8,128)(2,1)}, u32[]{:S(2)}, u32[]{:S(2)}) collective-permute-start(bf16[352,1024]{1,0:T(8,128)(2,1)} %slice_select_fusion.1), channel_id=1, source_target_pairs={{0,2},{1,3},{2,0},{3,1},{4,6},{5,7},{6,4},{7,5},{8,10},{9,11},{10,... | collective-permute-start | bytes 2162696 | tf_op jit(solution)/shard_map/ppermute | solution.py:47
  85.1 64.6 %collective-permute-start.4 = (bf16[320,1344]{1,0:T(8,128)(2,1)}, bf16[320,1344]{1,0:T(8,128)(2,1)}, u32[]{:S(2)}, u32[]{:S(2)}) collective-permute-start(bf16[320,1344]{1,0:T(8,128)(2,1)} %copy.338), channel_id=1, source_target_pairs={{0,2},{1,3},{2,0},{3,1},{4,6},{5,7},{6,4},{7,5},{8,10},{9,11},{10,... | collective-permute-start | bytes 2580488 | tf_op jit(solution)/shard_map/ppermute | solution.py:47
  89.6 60.1 %collective-permute-start.12 = (bf16[352,1024]{1,0:T(8,128)(2,1)}, bf16[352,1024]{1,0:T(8,128)(2,1)S(1)}, u32[]{:S(2)}, u32[]{:S(2)}) collective-permute-start(bf16[352,1024]{1,0:T(8,128)(2,1)} %slice_select_fusion.2), channel_id=1, source_target_pairs={{0,2},{1,3},{2,0},{3,1},{4,6},{5,7},{6,4},{7,5},{8,10},{9,11},{10,... | collective-permute-start | bytes 2162696 | tf_op jit(solution)/shard_map/ppermute | solution.py:47
  115.0 55.6 %collective-permute-start.5 = (bf16[352,1344]{1,0:T(8,128)(2,1)}, bf16[352,1344]{1,0:T(8,128)(2,1)}, u32[]{:S(2)}, u32[]{:S(2)}) collective-permute-start(bf16[352,1344]{1,0:T(8,128)(2,1)} %copy.339), channel_id=1, source_target_pairs={{0,2},{1,3},{2,0},{3,1},{4,6},{5,7},{6,4},{7,5},{8,10},{9,11},{10,... | collective-permute-start | bytes 2838536 | tf_op jit(solution)/shard_map/ppermute | solution.py:47
  116.3 58.3 %collective-permute-start.19 = (bf16[352,1024]{1,0:T(8,128)(2,1)}, bf16[352,1024]{1,0:T(8,128)(2,1)S(1)}, u32[]{:S(2)}, u32[]{:S(2)}) collective-permute-start(bf16[352,1024]{1,0:T(8,128)(2,1)} %collective-permute-done.18), channel_id=1, source_target_pairs={{0,8},{1,9},{2,10},{3,11},{4,12},{5,13},{6,14},{7,15},{8,0},{9,1},... | collective-permute-start | bytes 2162696 | tf_op jit(solution)/shard_map/ppermute | solution.py:47
  383.0 46.2 %collective-permute-start.25 = (bf16[2,128,1024]{2,1,0:T(8,128)(2,1)}, bf16[2,128,1024]{2,1,0:T(8,128)(2,1)}, u32[]{:S(2)}, u32[]{:S(2)}) collective-permute-start(bf16[2,128,1024]{2,1,0:T(8,128)(2,1)} %fusion.89), channel_id=1, source_target_pairs={{8,0},{9,1},{10,2},{11,3},{12,4},{13,5},{14,6},{15,7},{16,8},{17,9... | collective-permute-start | bytes 1572872 | tf_op jit(solution)/shard_map/ppermute | solution.py:47
  409.9 292.2 %collective-permute-start.23 = (bf16[2,256,2048]{2,1,0:T(8,128)(2,1)}, bf16[2,256,2048]{2,1,0:T(8,128)(2,1)}, u32[]{:S(2)}, u32[]{:S(2)}) collective-permute-start(bf16[2,256,2048]{2,1,0:T(8,128)(2,1)} %bitcast.42), channel_id=1, source_target_pairs={{0,1},{1,0},{2,3},{3,2},{4,5},{5,4},{6,7},{7,6},{8,9},{9,8},{10,11... | collective-permute-start | bytes 6291464 | tf_op jit(solution)/shard_map/ppermute | solution.py:47
  419.7 279.5 %collective-permute-start.33 = (bf16[2,512,1024]{2,1,0:T(8,128)(2,1)}, bf16[2,512,1024]{2,1,0:T(8,128)(2,1)}, u32[]{:S(2)}, u32[]{:S(2)}) collective-permute-start(bf16[2,512,1024]{2,1,0:T(8,128)(2,1)} %bitcast.89), channel_id=1, source_target_pairs={{0,2},{1,3},{2,0},{3,1},{4,6},{5,7},{6,4},{7,5},{8,10},{9,11},{10,... | collective-permute-start | bytes 6291464 | tf_op jit(solution)/shard_map/ppermute | solution.py:47
  542.6 163.3 %collective-permute-start.51 = (bf16[2,512,1024]{2,1,0:T(8,128)(2,1)}, bf16[2,512,1024]{2,1,0:T(8,128)(2,1)}, u32[]{:S(2)}, u32[]{:S(2)}) collective-permute-start(bf16[2,512,1024]{2,1,0:T(8,128)(2,1)} %bitcast.134), channel_id=1, source_target_pairs={{0,2},{1,3},{2,0},{3,1},{4,6},{5,7},{6,4},{7,5},{8,10},{9,11},{10,... | collective-permute-start | bytes 6291464 | tf_op jit(solution)/shard_map/ppermute | solution.py:47
  544.0 167.2 %collective-permute-start.39 = (bf16[2,512,1024]{2,1,0:T(8,128)(2,1)}, bf16[2,512,1024]{2,1,0:T(8,128)(2,1)}, u32[]{:S(2)}, u32[]{:S(2)}) collective-permute-start(bf16[2,512,1024]{2,1,0:T(8,128)(2,1)} %bitcast.102), channel_id=1, source_target_pairs={{0,2},{1,3},{2,0},{3,1},{4,6},{5,7},{6,4},{7,5},{8,10},{9,11},{10,... | collective-permute-start | bytes 6291464 | tf_op jit(solution)/shard_map/ppermute | solution.py:47
  568.5 66.5 %collective-permute-start.66 = (f32[56,128]{1,0:T(8,128)S(1)}, f32[56,128]{1,0:T(8,128)S(1)}, u32[]{:S(2)}, u32[]{:S(2)}) collective-permute-start(f32[56,128]{1,0:T(8,128)S(1)} %reduce_sum.334), channel_id=1, source_target_pairs={{0,2},{1,3},{2,0},{3,1},{4,6},{5,7},{6,4},{7,5},{8,10},{9,11},{10,... | collective-permute-start | bytes 86024 | tf_op jit(solution)/shard_map/ppermute | solution.py:47
  704.8 53.1 %collective-permute-start.24 = (bf16[256,2048]{1,0:T(8,128)(2,1)S(1)}, bf16[256,2048]{1,0:T(8,128)(2,1)S(1)}, u32[]{:S(2)}, u32[]{:S(2)}) collective-permute-start(bf16[256,2048]{1,0:T(8,128)(2,1)S(1)} %dynamic-slice_bitcast_fusion.3), channel_id=1, source_target_pairs={{0,4},{1,5},{2,6},{3,7},{4,0},{5,1},{6,2},{7,3},{8,12},{9,13},{10,... | collective-permute-start | bytes 3145736 | tf_op jit(solution)/shard_map/ppermute | solution.py:47
  709.8 46.3 %collective-permute-start.35 = (bf16[2,512,1024]{2,1,0:T(8,128)(2,1)S(1)}, bf16[2,512,1024]{2,1,0:T(8,128)(2,1)S(1)}, u32[]{:S(2)}, u32[]{:S(2)}) collective-permute-start(bf16[2,512,1024]{2,1,0:T(8,128)(2,1)S(1)} %pad_maximum_fusion.5), channel_id=1, source_target_pairs={{0,8},{1,9},{2,10},{3,11},{4,12},{5,13},{6,14},{7,15},{24,16},{25,... | collective-permute-start | bytes 6291464 | tf_op jit(solution)/shard_map/ppermute | solution.py:47
  714.7 86.3 %collective-permute-start.53 = (bf16[2,512,1024]{2,1,0:T(8,128)(2,1)S(1)}, bf16[2,512,1024]{2,1,0:T(8,128)(2,1)S(1)}, u32[]{:S(2)}, u32[]{:S(2)}) collective-permute-start(bf16[2,512,1024]{2,1,0:T(8,128)(2,1)S(1)} %pad_maximum_fusion.7), channel_id=1, source_target_pairs={{0,8},{1,9},{2,10},{3,11},{4,12},{5,13},{6,14},{7,15},{24,16},{25,... | collective-permute-start | bytes 6291464 | tf_op jit(solution)/shard_map/ppermute | solution.py:47
  718.2 127.8 %collective-permute-start.41 = (bf16[2,512,1024]{2,1,0:T(8,128)(2,1)S(1)}, bf16[2,512,1024]{2,1,0:T(8,128)(2,1)S(1)}, u32[]{:S(2)}, u32[]{:S(2)}) collective-permute-start(bf16[2,512,1024]{2,1,0:T(8,128)(2,1)S(1)} %pad_maximum_fusion.6), channel_id=1, source_target_pairs={{0,8},{1,9},{2,10},{3,11},{4,12},{5,13},{6,14},{7,15},{24,16},{25,... | collective-permute-start | bytes 6291464 | tf_op jit(solution)/shard_map/ppermute | solution.py:47
  757.1 93.3 %collective-permute-start.36 = (bf16[2,512,1024]{2,1,0:T(8,128)(2,1)S(1)}, bf16[2,512,1024]{2,1,0:T(8,128)(2,1)S(1)}, u32[]{:S(2)}, u32[]{:S(2)}) collective-permute-start(bf16[2,512,1024]{2,1,0:T(8,128)(2,1)S(1)} %add_convert_fusion.6), channel_id=1, source_target_pairs={{8,16},{9,17},{10,18},{11,19},{12,20},{13,21},{14,22},{15,23},{16,... | collective-permute-start | bytes 6291464 | tf_op jit(solution)/shard_map/ppermute | solution.py:47
  802.1 55.0 %collective-permute-start.54 = (bf16[2,512,1024]{2,1,0:T(8,128)(2,1)S(1)}, bf16[2,512,1024]{2,1,0:T(8,128)(2,1)S(1)}, u32[]{:S(2)}, u32[]{:S(2)}) collective-permute-start(bf16[2,512,1024]{2,1,0:T(8,128)(2,1)S(1)} %add_convert_fusion.2), channel_id=1, source_target_pairs={{8,16},{9,17},{10,18},{11,19},{12,20},{13,21},{14,22},{15,23},{16,... | collective-permute-start | bytes 6291464 | tf_op jit(solution)/shard_map/ppermute | solution.py:47
  803.7 57.2 %collective-permute-start.57 = (f32[16,128]{1,0:T(8,128)S(1)}, f32[16,128]{1,0:T(8,128)S(1)}, u32[]{:S(2)}, u32[]{:S(2)}) collective-permute-start(f32[16,128]{1,0:T(8,128)S(1)} %bitcast.545), channel_id=1, source_target_pairs={{0,8},{1,9},{2,10},{3,11},{4,12},{5,13},{6,14},{7,15},{8,16},{9,17... | collective-permute-start | bytes 24584 | tf_op jit(solution)/shard_map/ppermute | solution.py:47
  807.0 55.3 %collective-permute-start.58 = (f32[16,128]{1,0:T(8,128)S(1)}, f32[16,128]{1,0:T(8,128)S(1)}, u32[]{:S(2)}, u32[]{:S(2)}) collective-permute-start(f32[16,128]{1,0:T(8,128)S(1)} %bitcast.546), channel_id=1, source_target_pairs={{0,16},{1,17},{2,18},{3,19},{4,20},{5,21},{6,22},{7,23},{8,24},{9,... | collective-permute-start | bytes 24584 | tf_op jit(solution)/shard_map/ppermute | solution.py:47
  848.3 54.9 %collective-permute-start.42 = (bf16[2,512,1024]{2,1,0:T(8,128)(2,1)}, bf16[2,512,1024]{2,1,0:T(8,128)(2,1)}, u32[]{:S(2)}, u32[]{:S(2)}) collective-permute-start(bf16[2,512,1024]{2,1,0:T(8,128)(2,1)} %add_convert_fusion.4), channel_id=1, source_target_pairs={{8,16},{9,17},{10,18},{11,19},{12,20},{13,21},{14,22},{15,23},{16,... | collective-permute-start | bytes 6291464 | tf_op jit(solution)/shard_map/ppermute | solution.py:47
  853.3 56.2 %collective-permute-start.37 = (bf16[2,512,1024]{2,1,0:T(8,128)(2,1)}, bf16[2,512,1024]{2,1,0:T(8,128)(2,1)}, u32[]{:S(2)}, u32[]{:S(2)}) collective-permute-start(bf16[2,512,1024]{2,1,0:T(8,128)(2,1)} %add_convert_fusion.5), channel_id=1, source_target_pairs={{8,0},{9,1},{10,2},{11,3},{12,4},{13,5},{14,6},{15,7},{16,24},{17,... | collective-permute-start | bytes 6291464 | tf_op jit(solution)/shard_map/ppermute | solution.py:47
  857.1 44.8 %collective-permute-start.59 = (f32[16,128]{1,0:T(8,128)S(1)}, f32[16,128]{1,0:T(8,128)S(1)}, u32[]{:S(2)}, u32[]{:S(2)}) collective-permute-start(f32[16,128]{1,0:T(8,128)S(1)} %bitcast.547), channel_id=1, source_target_pairs={{0,24},{1,25},{2,26},{3,27},{4,28},{5,29},{6,30},{7,31},{8,0},{9,1... | collective-permute-start | bytes 24584 | tf_op jit(solution)/shard_map/ppermute | solution.py:47
  860.8 85.9 %collective-permute-start.55 = (bf16[2,512,1024]{2,1,0:T(8,128)(2,1)}, bf16[2,512,1024]{2,1,0:T(8,128)(2,1)}, u32[]{:S(2)}, u32[]{:S(2)}) collective-permute-start(bf16[2,512,1024]{2,1,0:T(8,128)(2,1)} %add_convert_fusion.1), channel_id=1, source_target_pairs={{8,0},{9,1},{10,2},{11,3},{12,4},{13,5},{14,6},{15,7},{16,24},{17,... | collective-permute-start | bytes 6291464 | tf_op jit(solution)/shard_map/ppermute | solution.py:47
  908.2 83.5 %collective-permute-start.43 = (bf16[2,512,1024]{2,1,0:T(8,128)(2,1)}, bf16[2,512,1024]{2,1,0:T(8,128)(2,1)}, u32[]{:S(2)}, u32[]{:S(2)}) collective-permute-start(bf16[2,512,1024]{2,1,0:T(8,128)(2,1)} %add_convert_fusion.3), channel_id=1, source_target_pairs={{8,0},{9,1},{10,2},{11,3},{12,4},{13,5},{14,6},{15,7},{16,24},{17,... | collective-permute-start | bytes 6291464 | tf_op jit(solution)/shard_map/ppermute | solution.py:47
  911.3 82.8 %collective-permute-start.38 = (bf16[2,512,1024]{2,1,0:T(8,128)(2,1)S(1)}, bf16[2,512,1024]{2,1,0:T(8,128)(2,1)}, u32[]{:S(2)}, u32[]{:S(2)}) collective-permute-start(bf16[2,512,1024]{2,1,0:T(8,128)(2,1)S(1)} %broadcast_select_fusion.2), channel_id=1, source_target_pairs={{0,4},{1,5},{2,6},{3,7},{4,0},{5,1},{6,2},{7,3},{8,12},{9,13},{10,... | collective-permute-start | bytes 6291464 | tf_op jit(solution)/shard_map/ppermute | solution.py:47
  949.9 50.2 %collective-permute-start.56 = (bf16[2,512,1024]{2,1,0:T(8,128)(2,1)}, bf16[2,512,1024]{2,1,0:T(8,128)(2,1)}, u32[]{:S(2)}, u32[]{:S(2)}) collective-permute-start(bf16[2,512,1024]{2,1,0:T(8,128)(2,1)} %broadcast_select_fusion), channel_id=1, source_target_pairs={{0,4},{1,5},{2,6},{3,7},{4,0},{5,1},{6,2},{7,3},{8,12},{9,13},{10,... | collective-permute-start | bytes 6291464 | tf_op jit(solution)/shard_map/ppermute | solution.py:47
  993.5 51.4 %collective-permute-start.44 = (bf16[2,512,1024]{2,1,0:T(8,128)(2,1)S(1)}, bf16[2,512,1024]{2,1,0:T(8,128)(2,1)S(1)}, u32[]{:S(2)}, u32[]{:S(2)}) collective-permute-start(bf16[2,512,1024]{2,1,0:T(8,128)(2,1)S(1)} %broadcast_select_fusion.1), channel_id=1, source_target_pairs={{0,4},{1,5},{2,6},{3,7},{4,0},{5,1},{6,2},{7,3},{8,12},{9,13},{10,... | collective-permute-start | bytes 6291464 | tf_op jit(solution)/shard_map/ppermute | solution.py:47
  (157 other events, 1480.6 us)

commit v2 on v1

v2 whole, which is shorter than its diff:
```python
from functools import partial

import jax
import jax.numpy as jnp
import numpy as np
from jax import lax
from jax.experimental import pallas as pl
from jax.experimental.pallas import tpu as pltpu
from jax.sharding import PartitionSpec as P

BLOCK = 256
HALO = 16
epsilon = 1e-05
highest = lax.Precision.HIGHEST
f32 = jnp.float32
bf16 = jnp.bfloat16
AXES = ("seq", "shard")


class Slice:
    def __init__(self, mesh):
        self.seq = mesh.shape["seq"]
        self.shard = mesh.shape["shard"]
        self.Y = self.shard // 2
        self.X = self.Y
        self.Z = self.seq // self.X
        self.TP = 2 * self.X

    def place(self):
        s, k = lax.axis_index("seq"), lax.axis_index("shard")
        self.z, self.x = s // self.X, s % self.X
        self.y, self.c = k // 2, k % 2
        self.j = self.x * 2 + self.c

    def move(self, a, target):
        pairs = []
        for z in range(self.Z):
            for x in range(self.X):
                for y in range(self.Y):
                    for c in range(2):
                        to = target(z, x, y, c)
                        if to is None:
                            continue
                        tz, tx, ty, tc = to
                        if not 0 <= tz < self.Z:
                            continue
                        src = (z * self.X + x) * self.shard + y * 2 + c
                        dst = (tz * self.X + tx % self.X) * self.shard + (ty % self.Y) * 2 + tc
                        pairs.append((src, dst))
        return lax.ppermute(a, AXES, pairs)

    def swap_core(self, a):
        return self.move(a, lambda z, x, y, c: (z, x, y, 1 - c))

    def shift_x(self, a, d):
        return self.move(a, lambda z, x, y, c: (z, x + d, y, c))

    def shift_y(self, a, d):
        return self.move(a, lambda z, x, y, c: (z, x, y + d, c))

    def shift_z(self, a, d):
        return self.move(a, lambda z, x, y, c: (z + d, x, y, c))

    def swap_z(self, a):
        return self.move(a, lambda z, x, y, c: (z ^ 1, x, y, c))

    def by_core(self, own, other):
        first = self.c == 0
        return jnp.where(first, own, other), jnp.where(first, other, own)

    def own_first(self, a):
        width = a.shape[-1] // self.Y
        parts = [
            lax.dynamic_slice_in_dim(a, ((self.y - i) % self.Y) * width, width, a.ndim - 1)
            for i in range(self.Y)
        ]
        return jnp.concatenate(parts, axis=-1)

    def own_first_back(self, a):
        width = a.shape[-1] // self.Y
        parts = [
            lax.dynamic_slice_in_dim(a, ((self.y - t) % self.Y) * width, width, a.ndim - 1)
            for t in range(self.Y)
        ]
        return jnp.concatenate(parts, axis=-1)

    def cut(self, a, axis, i, n):
        size = a.shape[axis] // n
        return lax.slice_in_dim(a, i * size, (i + 1) * size, axis=axis)


    def fetch_task(self, half, axis, out):
        n, m = half.shape
        shared = (n // 3 + 15) // 16 * 16
        direct = n - 2 * shared
        odd = self.z % 2
        sent = yield [lax.dynamic_slice_in_dim(half, direct + odd * shared, shared, 0)]
        got = yield [self.shift_y(sent[0], d) for d in range(1, self.Y)]
        sent = yield [half[:direct]] + got
        done = yield [self.shift_y(sent[0], d) for d in range(1, self.Y)] + [
            self.swap_z(r) for r in sent[1:]
        ]
        pieces = [(half, None, (n, m), (0, 0))]
        for d in range(1, self.Y):
            at = (lambda r: (r, d * m)) if axis else (lambda r: (d * n + r, 0))
            r, o = got[d - 1], done[self.Y - 2 + d]
            pieces += [
                (done[d - 1], None, (direct, m), at(0)),
                (r, None, (shared, m), at(direct + odd * shared)),
                (o, None, (shared, m), at(direct + (1 - odd) * shared)),
            ]
        shape = (n, m * self.Y) if axis else (n * self.Y, m)
        out["w"] = assemble(pieces, shape)

    def direct_task(self, half, shares, out):
        n, m = half.shape
        edges = [n * sum(shares[:i]) // sum(shares) // 16 * 16 for i in range(len(shares) + 1)]
        pieces = [(half, None, (n, m), (0, 0))]
        for a, b in zip(edges[:-1], edges[1:]):
            sent = yield [half[a:b]]
            got = yield [self.shift_y(sent[0], d) for d in range(1, self.Y)]
            for d, r in enumerate(got):
                pieces.append((r, None, (b - a, m), ((d + 1) * n + a, 0)))
        out["w"] = assemble(pieces, (n * self.Y, m))

    def gather_task(self, a, last, out):
        rows, F = a.shape
        length = self.X * rows + (0 if last is None else last.shape[0])
        sent = yield [a] + ([] if last is None else [last])
        got = yield [self.shift_x(sent[0], d) for d in range(1, self.X)] + [
            self.swap_core(sent[0])
        ] + [
            self.move(s, lambda z, x, y, c: (z + 1, t, y, c) if x == self.X - 1 else None)
            for s in sent[1:]
            for t in range(self.X)
        ]
        far = got[: self.X - 1]
        send = list(far)
        if last is not None:
            send.append(sum(got[self.X + 1 :], got[self.X]))
        if send:
            sent = yield send
            done = yield [self.swap_core(s) for s in sent]
        pieces = []
        for d in range(self.X):
            at = (self.x - d) % self.X * rows
            mine = a if d == 0 else sent[d - 1]
            other = got[self.X - 1] if d == 0 else done[d - 1]
            pieces.append((mine[None], None, (1, rows, F), (self.c, at, 0)))
            pieces.append((other[None], None, (1, rows, F), (1 - self.c, at, 0)))
        if last is not None:
            n = last.shape[0]
            pieces.append((sent[-1][None], None, (1, n, F), (self.c, self.X * rows, 0)))
            pieces.append((done[-1][None], None, (1, n, F), (1 - self.c, self.X * rows, 0)))
        out["all"] = assemble(pieces, (2, length, F))

    def y_task(self, send, own, out):
        sent = yield send
        got = yield [self.shift_y(p, -i - 1) for i, p in enumerate(sent)]
        acc = own()
        for r in got:
            acc = acc + r.astype(f32)
        out["q"] = acc.astype(bf16)

    def sum_z(self, q):
        groups = [[z * self.X + x for z in range(self.Z)] for x in range(self.X)]
        return lax.psum(q, "seq", axis_index_groups=groups)

    def spread_task(self, q, axis, out):
        keep, send = self.by_core(self.cut(q, axis, 0, 2), self.cut(q, axis, 1, 2))
        keep, send = yield [keep, send]
        moves = [(d, e) for d in range(self.X) for e in range(2) if d or e]
        got = yield [
            self.move((keep, send)[e], lambda z, x, y, c: (z, x + d, y, c ^ e)) for d, e in moves
        ]
        out["done"] = dict(zip(moves, got))
        out["done"][0, 0] = keep

    def scatter_task(self, a, out):
        keep, send = self.by_core(a[0], a[1])
        sent = yield [send]
        got = yield [self.swap_core(sent[0])]
        total = (keep.astype(f32) + got[0].astype(f32)).astype(bf16)
        parts = [
            lax.dynamic_index_in_dim(total, (self.x + d) % self.X, 0, False) for d in range(self.X)
        ]
        sent = yield parts[1:]
        got = yield [self.shift_x(p, d + 1) for d, p in enumerate(sent)]
        acc = parts[0].astype(f32)
        for r in got:
            acc = acc + r.astype(f32)
        out["sum"] = acc

    def gradient_task(self, send, own_part, axis, out):
        half = self.Z // 2
        sent = yield send
        got = yield [self.shift_y(p, -i - 1) for i, p in enumerate(sent)]
        acc = own_part()
        for r in got:
            acc = acc + r.astype(f32)
        q = acc.astype(bf16)
        for step in range(half - 1):
            (q,) = yield [q]
            got = yield [
                self.move(
                    q,
                    lambda z, x, y, c: (z + 1, x, y, c)
                    if z == step
                    else ((z - 1, x, y, c) if z == self.Z - 1 - step else None),
                )
            ]
            q = (q.astype(f32) + got[0].astype(f32)).astype(bf16)
        (q,) = yield [q]
        got = yield [
            self.move(
                q,
                lambda z, x, y, c: (z + 1, x, y, c)
                if z == half - 1
                else ((z - 1, x, y, c) if z == half else None),
            )
        ]
        q = (q.astype(f32) + got[0].astype(f32)).astype(bf16)
        for step in range(half - 1):
            a, b = half - 1 - step, half + step
            (q,) = yield [q]
            got = yield [
                self.move(
                    q,
                    lambda z, x, y, c: (z - 1, x, y, c)
                    if z == a
                    else ((z + 1, x, y, c) if z == b else None),
                )
            ]
            q = jnp.where((self.z == a - 1) | (self.z == b + 1), got[0], q)
        keep, send = self.by_core(self.cut(q, axis, 0, 2), self.cut(q, axis, 1, 2))
        keep, send = yield [keep, send]
        moves = [(d, e) for d in range(self.X) for e in range(2) if d or e]
        got = yield [
            self.move((keep, send)[e], lambda z, x, y, c: (z, x + d, y, c ^ e)) for d, e in moves
        ]
        out["done"] = dict(zip(moves, got))
        out["done"][0, 0] = keep

    def state_task(self, cur, cc, spread, direction, out):
        d = 1
        while d < self.Z // 2:
            send = [cur.astype(bf16)] + ([cc] if 2 * d < self.Z // 2 else [])
            sent = yield send
            got = yield [self.shift_z(a, direction * d) for a in sent]
            cur = cur + spread(cc)[:, None, :] * got[0].astype(f32)
            if len(got) > 1:
                cc = cc * got[1]
            d *= 2
        sent = yield [cur.astype(bf16)]
        got = yield [self.shift_z(sent[0], direction)]
        out["state"] = got[0].astype(f32)

    def small_task(self, v, over_tp, out):
        def turn_z(a, d):
            return self.move(a, lambda z, x, y, c: ((z + d) % self.Z, x, y, c))

        def turn_group(a, d):
            dx, dc = d // 2, d % 2
            return self.move(a, lambda z, x, y, c: (z, x + dx, y, c ^ dc))

        def from_group(d):
            return ((self.x - d // 2) % self.X) * 2 + (self.c ^ (d % 2))

        rounds = [
            (self.Z, lambda d: (self.z - d) % self.Z, turn_z),
            (self.Y, lambda d: (self.y - d) % self.Y, self.shift_y),
            (self.TP, from_group, turn_group),
        ]
        for i, (n, source, shift) in enumerate(rounds):
            sent = yield [v]
            got = yield [shift(sent[0], d) for d in range(1, n)]
            buf = jnp.zeros((n,) + v.shape, v.dtype)
            for d, r in enumerate([v] + got):
                buf = lax.dynamic_update_index_in_dim(buf, r, source(d), 0)
            v = jnp.sum(buf, axis=0) if i < 2 else buf
        out["sum"] = jnp.sum(v, axis=0) if over_tp else v

    def sum_tp_task(self, a, out):
        moves = [(dx, dc) for dx in range(self.X) for dc in range(2) if dx or dc]
        sent = yield [a]
        got = yield [
            self.move(sent[0], lambda z, x, y, c: (z, x + dx, y, c ^ dc)) for dx, dc in moves
        ]
        total = a
        for r in got:
            total = total + r
        out["sum"] = total

    def chunks_task(self, both, SW, out):
        moves = [(dx, dc) for dx in range(self.X) for dc in range(2)]
        parts = []
        for dx, dc in moves:
            jj = (self.x + dx) % self.X * 2 + (self.c ^ dc)
            parts.append(lax.dynamic_slice_in_dim(both, SW * jj, SW, 2))
        sent = yield parts[1:]
        got = yield [
            self.move(p, lambda z, x, y, c: (z, x + dx, y, c ^ dc))
            for p, (dx, dc) in zip(sent, moves[1:])
        ]
        total = parts[0].astype(f32)
        for r in got:
            total = total + r.astype(f32)
        out["sum"] = total

    def one_task(self, arrays, send, out):
        sent = yield arrays
        out["got"] = yield [send(a) for a in sent]


def fence(arrays):
    flat, tree = jax.tree.flatten(arrays)
    return jax.tree.unflatten(tree, lax.optimization_barrier(tuple(flat)))


class Stages:
    def __init__(self):
        self.tasks = []

    def add(self, task, *args):
        out = {}
        gen = task(*args, out)
        self.tasks.append([gen, next(gen), None])
        return out

    def settle(self, live):
        flying = [t for t in self.tasks if t[2] is not None]
        got, live = fence(([t[2] for t in flying], live))
        for t, r in zip(flying, got):
            t[2] = None
            try:
                t[1] = t[0].send(r)
            except StopIteration:
                self.tasks.remove(t)
        return live

    def launch(self, live):
        ready, live = fence(([t[1] for t in self.tasks], live))
        for t, a in zip(self.tasks, ready):
            t[2] = t[0].send(a)
        return live

    def tick(self, live):
        return self.launch(self.settle(live))


def low_dot(a, b, dims):
    return lax.dot_general(a.astype(bf16), b.astype(bf16), dims, preferred_element_type=f32)


def silu_slope(v):
    g = jax.nn.sigmoid(v)
    return g * (1.0 + v * (1.0 - g))


NT = (((1,), (1,)), ((), ()))
TN = (((0,), (0,)), ((), ()))
NN = (((1,), (0,)), ((), ()))
GH = 4
LANES = 256
FAR = -1e30
VMEM_LIMIT = 40 * 1024 * 1024


def bdot(a, b, dims):
    return lax.dot_general(a.astype(bf16), b.astype(bf16), dims, preferred_element_type=f32)


def fdot(a, b, dims):
    return lax.dot_general(a, b, dims, precision=highest, preferred_element_type=f32)


def wide(fac):
    low = lax.broadcasted_iota(jnp.int32, (fac.shape[0], 128), 1) < 64
    pairs = [jnp.where(low, fac[:, i : i + 1], fac[:, i + 1 : i + 2]) for i in (0, 2)]
    return jnp.concatenate(pairs, axis=1)


def head_sum(v):
    lane = lax.broadcasted_iota(jnp.int32, (LANES, 128), 0) // 64
    head = lax.broadcasted_iota(jnp.int32, (LANES, 128), 1)
    return bdot(v, (lane == head).astype(bf16), NN)[:, :GH]


def triangle(strict_lower=False, upper=False):
    r = lax.broadcasted_iota(jnp.int32, (BLOCK, BLOCK), 0)
    t = lax.broadcasted_iota(jnp.int32, (BLOCK, BLOCK), 1)
    keep = t >= r if upper else (t < r if strict_lower else t <= r)
    return keep.astype(f32)


def sigmoid(v):
    return 0.5 * jnp.tanh(0.5 * v) + 0.5


def turned(rows):
    pad = jnp.zeros((120, 128), f32)
    parts = []
    for i in range(rows.shape[1] // 128):
        square = jnp.concatenate([rows[:, i * 128 : (i + 1) * 128], pad], axis=0)
        parts.append(square.T[:, :8])
    return jnp.concatenate(parts, axis=0)


def turn_body(rows, out):
    out[0] = turned(rows[0])


def softplus(v):
    u = jnp.exp(-jnp.abs(v))
    w = 1.0 + u
    log1p = jnp.where(w == 1.0, u, jnp.log(w) * u / jnp.where(w == 1.0, 1.0, w - 1.0))
    return jnp.maximum(v, 0.0) + log1p


def call(kernel, grid, ins, outs, scratch=(), flops=0, name=None):
    arrays = [a for a, _, _ in ins]
    total = sum(a.size * a.dtype.itemsize for a in arrays)
    total += sum(int(np.prod(s)) * jnp.dtype(d).itemsize for s, d, _, _ in outs)
    return pl.pallas_call(
        kernel,
        grid=grid,
        in_specs=[pl.BlockSpec(b, m) for _, b, m in ins],
        out_specs=[pl.BlockSpec(b, m) for _, _, b, m in outs],
        out_shape=[jax.ShapeDtypeStruct(s, d) for s, d, _, _ in outs],
        scratch_shapes=list(scratch),
        compiler_params=pltpu.CompilerParams(vmem_limit_bytes=VMEM_LIMIT),
        cost_estimate=pl.CostEstimate(flops=flops, bytes_accessed=total, transcendentals=0),
        name=name,
    )(*arrays)


def conv_kernel_body(
    nb, pk, dt, sel, hp, marks, kern, bias, x_out, bc_out, s_out, step_out, cum_out, row_out, v_scr, keys_scr
):
    T = nb * BLOCK
    v_scr[:HALO, :] = pk[0, T:, :].astype(f32)
    v_scr[HALO:, :] = pk[0, :T, :].astype(f32)
    pre = bias[...] + kern[0:1, :] * v_scr[HALO : HALO + T, :]
    for k in range(1, 4):
        pre = pre + kern[k : k + 1, :] * (v_scr[HALO - k : HALO - k + T, :] * marks[0, :, k - 1 : k])
    act = pre * sigmoid(pre)
    chunk = pl.program_id(1)

    @pl.when(chunk == 0)
    def _():
        bc_out[...] = act.astype(bf16)
        keys_scr[...] = act[:, : keys_scr.shape[1]].astype(bf16)

    @pl.when(chunk > 0)
    def _():
        x_out[...] = act.astype(bf16)
        raw = bdot(dt[0, :T, :], sel[0], NN)[:, :GH] + hp[0, 0:1, :]
        step = softplus(raw)
        step_out[0, 0] = step
        tri = triangle()
        for b in range(nb):
            rows = slice(b * BLOCK, (b + 1) * BLOCK)
            st = step[rows]
            cum = fdot(tri, -hp[0, 1:2, :] * st, NN)
            cum_out[0, 0, rows, :] = cum
            padded = jnp.concatenate([cum, jnp.zeros((BLOCK, 128 - GH), f32)], axis=1)
            row_out[0, 0, b] = padded.T[:GH]
            tail = jnp.exp(cum[BLOCK - 1 :, :] - cum) * marks[0, rows, 3:4]
            xst = act[rows] * wide(st * tail)
            s_out[0, b] = bdot(keys_scr[rows, :], xst, TN)


def gaps_mask(seg_col, seg_row, transposed):
    r = lax.broadcasted_iota(jnp.int32, (BLOCK, BLOCK), 0)
    t = lax.broadcasted_iota(jnp.int32, (BLOCK, BLOCK), 1)
    order = t >= r if transposed else r >= t
    return jnp.where(order & (seg_col == seg_row), 0.0, FAR)


HALF = BLOCK // 2


def intra_forward_body(x, bc, cum, row, step, marks, flags, hp, y_out, gram, mask):
    @pl.when(pl.program_id(1) == 0)
    def _():
        n = bc.shape[1] // 2
        gram[...] = bdot(bc[:, n:], bc[:, :n], NT)
        mask[...] = gaps_mask(marks[0, :, 6:7], flags[0, 6:7, :], False)

    xf = x[...].astype(f32)
    xs = (xf * wide(step[0, 0])).astype(bf16)
    low = lax.broadcasted_iota(jnp.int32, (HALF, 128), 1) < 64
    c = cum[0, 0]
    for half in range(2):
        rows = slice(half * HALF, (half + 1) * HALF)
        reachable = (half + 1) * HALF
        g = gram[rows, :reachable]
        m = mask[rows, :reachable]
        parts = []
        for i in range(GH):
            d = c[rows, i : i + 1] - row[0, 0, 0, i : i + 1, :reachable] + m
            p = (jnp.exp(d) * g).astype(bf16)
            pair = i // 2 * 128
            parts.append(bdot(p, xs[:reachable, pair : pair + 128], NN))
        y = jnp.concatenate(
            [jnp.where(low, parts[0], parts[1]), jnp.where(low, parts[2], parts[3])], axis=1
        )
        y_out[rows, :] = (y + wide(hp[0, 2:3, :]) * xf[rows]).astype(bf16)


def reach_of(cum, marks):
    return jnp.exp(jnp.minimum(cum, 0.0)) * marks[:, 4:5]


def join_body(nb, y, bc, enter, cum, marks, gate, og, gain, mixed_out, sums_out):
    n = bc.shape[1] // 2
    ones = jnp.ones((16, LANES), bf16)
    first = lax.broadcasted_iota(jnp.int32, (8, BLOCK), 0) == 0
    for b in range(nb):
        rows = slice(b * BLOCK, (b + 1) * BLOCK)
        reach = wide(reach_of(cum[0, 0, rows, :], marks[0, rows, :]))
        state = bdot(bc[rows, n:], enter[0, b], NN) * reach
        mixed = (y[rows, :].astype(f32) + state).astype(bf16)
        mixed_out[rows, :] = mixed
        gv = gate[0, rows, :].astype(f32)
        gated = mixed.astype(f32) * (gv * sigmoid(gv))
        lifted = og[rows, :].astype(f32) * gain[...]
        ss = bdot(ones, gated * gated, NT)[:8]
        sg = bdot(ones, gated * lifted, NT)[:8]
        both = jnp.where(first, ss, sg)

        @pl.when(pl.program_id(1) == 0)
        def _(both=both, rows=rows):
            sums_out[0, :, rows] = both

        @pl.when(pl.program_id(1) > 0)
        def _(both=both, rows=rows):
            sums_out[0, :, rows] += both


def gates_body(
    nb, inner, mixed, gate, og, sums, gain, bc, cum, marks, no_out, gg_out, do_out, gain_out, de_out
):
    n = bc.shape[1] // 2
    T = nb * BLOCK
    total = turned(sums[0]) / inner
    part = None
    for b in range(nb):
        rows = slice(b * BLOCK, (b + 1) * BLOCK)
        gv = gate[0, rows, :].astype(f32)
        sg = sigmoid(gv)
        act = gv * sg
        mx = mixed[rows, :].astype(f32)
        ogv = og[rows, :].astype(f32)
        r = lax.rsqrt(total[rows, 0:1] + epsilon)
        gr = mx * act * r
        no_out[rows, :] = (gr * gain[...]).astype(bf16)
        p = jnp.sum(ogv * gr, axis=0, keepdims=True)
        part = p if part is None else part + p
        grad = r * (ogv * gain[...]) - gr * (r * r * total[rows, 1:2])
        d_out = (grad * act).astype(bf16)
        do_out[rows, :] = d_out
        gg_out[0, rows, :] = (grad * mx * (sg * (1.0 + gv * (1.0 - sg)))).astype(bf16)
        dr = d_out.astype(f32) * wide(reach_of(cum[0, 0, rows, :], marks[0, rows, :]))
        de_out[0, b] = bdot(bc[rows, n:], dr, TN)
    gg_out[0, T:, :] = jnp.zeros((HALO, LANES), bf16)

    @pl.when(pl.program_id(1) == 0)
    def _():
        gain_out[...] = part

    @pl.when(pl.program_id(1) > 0)
    def _():
        gain_out[...] += part


def input_grad_body(gg, xb, tb, wg, wx, wt, out):
    total = bdot(gg[...], wg[...], NN) + bdot(xb[...], wx[...], NN) + bdot(tb[...], wt[...], NN)
    out[...] = total.astype(bf16)


def intra_backward_body(
    x, bc, do, cum, row, step, enter, marks, flags, dxs_out, dec_out, dbc_out, gram, mask, zt, dq
):
    n = bc.shape[1] // 2
    keys, queries = bc[:, :n], bc[:, n:]
    g_id = pl.program_id(1)

    @pl.when(g_id == 0)
    def _():
        gram[...] = bdot(keys, queries, NT)
        mask[...] = gaps_mask(marks[0, :, 6:7], flags[0, 6:7, :], True)
        zt[...] = jnp.zeros_like(zt)
        dq[...] = jnp.zeros_like(dq)

    low = lax.broadcasted_iota(jnp.int32, (BLOCK, 128), 1) < 64
    c = cum[0, 0]
    st = step[0, 0]
    row_sums = [None] * GH
    col_sums = []
    dxs = [[], []]
    for i in range(GH):
        pair = i // 2 * 128
        mine = low if i % 2 == 0 else ~low
        dop = do[:, pair : pair + 128]
        xm = jnp.where(mine, x[:, pair : pair + 128].astype(f32), 0.0).astype(bf16)
        cols = []
        for half in range(2):
            rows = slice(half * HALF, (half + 1) * HALF)
            after = slice(half * HALF, BLOCK)
            e = bdot(xm[rows], dop[after], NT)
            d = row[0, 0, 0, i : i + 1, after] - c[rows, i : i + 1] + mask[rows, after]
            decay = jnp.exp(d)
            le = decay * e * st[rows, i : i + 1]
            zt[rows, after] += le
            gr = gram[rows, after]
            m = le * gr
            total = jnp.sum(m, axis=0, keepdims=True)
            if half == 0:
                row_sums[i] = total
            else:
                row_sums[i] = row_sums[i] + jnp.concatenate([jnp.zeros((1, HALF), f32), total], axis=1)
            cols.append(jnp.sum(m, axis=1, keepdims=True))
            dxs[half].append(bdot((decay * gr).astype(bf16), dop[after], NN))
        col_sums.append(jnp.concatenate(cols, axis=0))
    for half in range(2):
        p = dxs[half]
        lo = low[:HALF]
        dxs_out[half * HALF : (half + 1) * HALF, :] = jnp.concatenate(
            [jnp.where(lo, p[0], p[1]), jnp.where(lo, p[2], p[3])], axis=1
        ).astype(bf16)
    dof = do[...].astype(f32)
    rw = wide(reach_of(c, marks[0]))
    from_state = bdot(queries, enter[0], NN) * rw
    came = head_sum(dof * from_state)
    upper = triangle(upper=True)
    rows4 = jnp.concatenate(row_sums + [jnp.zeros((16 - GH, BLOCK), f32)], axis=0)
    cols4 = jnp.concatenate(col_sums, axis=1)
    dec_out[0, 0] = fdot(upper, rows4, NT)[:, :GH] + fdot(upper, came - cols4, NN)
    dq[...] += bdot(dof * rw, enter[0], NT)

    @pl.when(g_id == pl.num_programs(1) - 1)
    def _():
        z = zt[...].astype(bf16)
        dbc_out[:, :n] = bdot(z, queries, NN)
        dbc_out[:, n:] = dq[...] + bdot(z, keys, TN)


def finish_body(
    nb, pk, x, do, dxl, bc, leave, enter, cum, step, dec, dt, sel, hp, marks, kern, bias,
    back_out, kg_out, sm_out, raw_out, dk_out, v_scr, m_scr,
):
    T = nb * BLOCK
    n = bc.shape[1] // 2
    g_id = pl.program_id(1)
    v_scr[:HALO, :] = pk[0, T:, :].astype(f32)
    v_scr[HALO:, :] = pk[0, :T, :].astype(f32)
    pre = bias[...] + kern[0:1, :] * v_scr[HALO : HALO + T, :]
    for k in range(1, 4):
        pre = pre + kern[k : k + 1, :] * (v_scr[HALO - k : HALO - k + T, :] * marks[0, :, k - 1 : k])
    sg = sigmoid(pre)
    slope = sg * (1.0 + pre * (1.0 - sg))
    raw = bdot(dt[0, :T, :], sel[0], NN)[:, :GH] + hp[0, 0:1, :]
    rate = hp[0, 1:2, :]
    skip = wide(hp[0, 2:3, :])
    strict = triangle(strict_lower=True)
    sums = [0.0, 0.0, 0.0]
    m_scr[:HALO, :] = jnp.zeros((HALO, LANES), f32)
    m_scr[HALO + T :, :] = jnp.zeros((HALO, LANES), f32)
    grads = []
    for b in range(nb):
        rows = slice(b * BLOCK, (b + 1) * BLOCK)
        c = cum[0, 0, rows, :]
        st = step[0, 0, rows, :]
        end = c[BLOCK - 1 :, :]
        tail = wide(jnp.exp(end - c) * marks[0, rows, 3:4])
        stw = wide(st)
        keys = bc[rows, :n]
        lv = leave[0, b]
        kl = bdot(keys, lv, NN) * tail
        dxs = dxl[rows, :].astype(f32) + kl
        dof = do[rows, :].astype(f32)
        xf = x[rows, :].astype(f32)
        xs = xf * stw
        grads.append(skip * dof + stw * dxs)
        out4 = head_sum(xs * kl)
        direct = head_sum(xf * dxs)
        sums[2] = sums[2] + jnp.sum(head_sum(dof * xf), axis=0, keepdims=True)
        dk = bdot(xs * tail, lv, NT)

        @pl.when(g_id == 0)
        def _(dk=dk, rows=rows):
            dk_out[rows, :] = dk

        @pl.when(g_id > 0)
        def _(dk=dk, rows=rows):
            dk_out[rows, :] += dk

        both = jnp.sum(enter[0, b].astype(f32) * lv.astype(f32), axis=0, keepdims=True)
        both = jnp.concatenate([both, jnp.zeros((15, LANES), f32)], axis=0)
        through = head_sum(both)[:1] * jnp.exp(end) * marks[0, b * BLOCK : b * BLOCK + 1, 5:6]
        decay = dec[0, 0, rows, :] + fdot(strict, out4, NN) + through
        sums[1] = sums[1] - rate * jnp.sum(st * decay, axis=0, keepdims=True)
        rg = (direct - rate * decay) * sigmoid(raw[rows])
        sums[0] = sums[0] + jnp.sum(rg, axis=0, keepdims=True)
        raw_out[0, 0, rows, :] = rg
    cg = jnp.concatenate(grads, axis=0) * slope
    sm_out[0, 0] = jnp.concatenate(sums + [jnp.zeros((5, GH), f32)], axis=0)
    kgs = []
    back = None
    for k in range(4):
        m = cg if k == 0 else cg * marks[0, :, k - 1 : k]
        kgs.append(jnp.sum(m * v_scr[HALO - k : HALO - k + T, :], axis=0, keepdims=True))
        m_scr[HALO : HALO + T, :] = m
        part = kern[k : k + 1, :] * m_scr[k : k + T + HALO, :]
        back = part if back is None else back + part
    kgs.append(jnp.sum(cg, axis=0, keepdims=True))
    kg_out[0] = jnp.concatenate(kgs + [jnp.zeros((3, LANES), f32)], axis=0)
    back = back.astype(bf16)
    back_out[0, :T, :] = back[HALO:]
    back_out[0, T:, :] = back[:HALO]

def offsets(index, starts, sizes, steps):
    window = []
    for s, n, step in zip(starts, sizes, steps):
        if not isinstance(s, int):
            s = pl.multiple_of(index[s[0]], step)
        window.append(pl.ds(s, n))
    return tuple(window)


def tabled(moves):
    table = []

    def entry(v):
        if isinstance(v, (int, np.integer)):
            return int(v)
        table.append(jnp.asarray(v, jnp.int32))
        return (len(table) - 1,)

    moves = [tuple(tuple(entry(v) for v in part) for part in m) for m in moves]
    table = table or [jnp.zeros((), jnp.int32)]
    return moves, jnp.stack(table)


def assemble(pieces, shape):
    arrays = [p[0] for p in pieces]
    zero = (0,) * len(shape)
    moves, table = tabled([(zero if s is None else s, at) for _, s, _, at in pieces])
    steps = (1,) * (len(shape) - 2) + (16, 128)

    n = len(arrays)

    def kernel(index, *refs):
        out, held, sems = refs[n], refs[n + 1 : -1], refs[-1]
        loads, stores = [], []
        for i, (source, _) in enumerate(moves):
            window = offsets(index, source, pieces[i][2], steps)
            loads.append(pltpu.make_async_copy(refs[i].at[window], held[i], sems.at[0, i]))
            loads[-1].start()
        for i, (_, target) in enumerate(moves):
            loads[i].wait()
            window = offsets(index, target, pieces[i][2], steps)
            stores.append(pltpu.make_async_copy(held[i], out.at[window], sems.at[1, i]))
            stores[-1].start()
        for c in stores:
            c.wait()

    size = 4 * int(np.prod(shape))
    return pl.pallas_call(
        kernel,
        in_specs=[pl.BlockSpec(memory_space=pltpu.SMEM)]
        + [pl.BlockSpec(memory_space=pl.ANY)] * len(arrays),
        out_specs=pl.BlockSpec(memory_space=pl.ANY),
        out_shape=jax.ShapeDtypeStruct(shape, arrays[0].dtype),
        scratch_shapes=[pltpu.VMEM(p[2], p[0].dtype) for p in pieces]
        + [pltpu.SemaphoreType.DMA((2, n))],
        compiler_params=pltpu.CompilerParams(vmem_limit_bytes=VMEM_LIMIT),
        cost_estimate=pl.CostEstimate(flops=0, bytes_accessed=size, transcendentals=0),
        name="assemble",
    )(table, *arrays)


def place(pieces, moves, shape, buf):
    spots, table = tabled([(s, at) for _, s, _, at in moves])
    n = len(pieces)

    def kernel(index, *refs):
        out, wide_refs, sems = refs[-n - 2], refs[-n - 1 : -1], refs[-1]
        copies = []
        for i in range(n):
            wide_refs[i][...] = refs[i][...].astype(f32)
            for k, (source, target) in enumerate(spots):
                if moves[k][0] != i:
                    continue
                sizes = moves[k][2]
                copies.append(
                    pltpu.make_async_copy(
                        wide_refs[i].at[offsets(index, source, sizes, (8, 128))],
                        out.at[offsets(index, target, sizes, (8, 128))],
                        sems.at[k],
                    )
                )
                copies[-1].start()
        for c in copies:
            c.wait()

    size = sum(6 * p.size for p in pieces)
    extra = [] if buf is None else [buf]
    return pl.pallas_call(
        kernel,
        in_specs=[pl.BlockSpec(memory_space=pltpu.SMEM)]
        + [pl.BlockSpec(memory_space=pltpu.VMEM)] * n
        + [pl.BlockSpec(memory_space=pl.ANY)] * len(extra),
        out_specs=pl.BlockSpec(memory_space=pl.ANY),
        out_shape=jax.ShapeDtypeStruct(shape, f32),
        scratch_shapes=[pltpu.VMEM(p.shape, f32) for p in pieces]
        + [pltpu.SemaphoreType.DMA((len(moves),))],
        input_output_aliases={} if buf is None else {1 + n: 0},
        compiler_params=pltpu.CompilerParams(vmem_limit_bytes=VMEM_LIMIT),
        cost_estimate=pl.CostEstimate(flops=0, bytes_accessed=size, transcendentals=0),
        name="place",
    )(table, *pieces, *extra)


def body(
    g,
    tokens,
    in_weight,
    out_weight,
    pre_gain,
    conv_kernel,
    conv_bias,
    step_bias,
    decay_log,
    skip_gain,
    gate_gain,
    segments,
    cotangent,
):
    g.place()
    heads = step_bias.shape[0]
    inner = gate_gain.shape[0]
    channels = conv_bias.shape[0]
    shared = channels - inner
    state = shared // 2
    taps = conv_kernel.shape[0]
    hd = inner // heads
    HL = heads // g.TP
    HW = HL * hd
    SW = shared // g.TP
    CW = HW + shared
    own_len = tokens.shape[1]
    width = tokens.shape[2]
    own_d = in_weight.shape[0]
    T = own_len * g.X
    TE = T + HALO
    nb = T // BLOCK
    NB = 2 * nb
    G = HW // LANES
    KW = HW + shared + 128
    j = g.j
    other_j = g.x * 2 + 1 - g.c

    w_t = in_weight.T
    rest = jnp.pad(w_t[2 * inner :], ((0, KW - CW - heads), (0, 0)))
    far = g.swap_core(lax.dynamic_slice_in_dim(w_t, inner + HW * other_j, HW, 0))
    far_rest = g.swap_core(rest)
    n_rest = KW - HW
    half_packed = assemble(
        [
            (w_t, (inner + HW * j, 0), (HW, own_d), (0, g.c * own_d)),
            (rest, None, (n_rest, own_d), (HW, g.c * own_d)),
            (far, None, (HW, own_d), (0, (1 - g.c) * own_d)),
            (far_rest, None, (n_rest, own_d), (HW, (1 - g.c) * own_d)),
        ],
        (KW, 2 * own_d),
    )

    series = tokens[0].astype(f32)
    scale = lax.rsqrt(jnp.mean(series * series, axis=-1, keepdims=True) + epsilon)
    normed = g.own_first((series * scale * pre_gain[None, :]).astype(bf16))

    stages = Stages()
    at_n = stages.add(g.gather_task, normed, normed[own_len - HALO :])
    at_packed = stages.add(g.fetch_task, half_packed, 1)
    in_weight, out_weight, cotangent = stages.launch([in_weight, out_weight, cotangent])
    w_t = in_weight.T
    far_gate = g.swap_core(lax.dynamic_slice_in_dim(w_t, HW * other_j, HW, 0))
    far_out = g.swap_core(lax.dynamic_slice_in_dim(out_weight, HW * other_j, HW, 1))
    at_cot = stages.add(g.gather_task, g.own_first(cotangent[0]), None)
    half_gate = assemble(
        [
            (w_t, (HW * j, 0), (HW, own_d), (0, g.c * own_d)),
            (far_gate, None, (HW, own_d), (0, (1 - g.c) * own_d)),
        ],
        (HW, 2 * own_d),
    )
    half_out = assemble(
        [
            (out_weight, (0, HW * j), (own_d, HW), (g.c * own_d, 0)),
            (far_out, None, (own_d, HW), ((1 - g.c) * own_d, 0)),
        ],
        (2 * own_d, HW),
    )

    s_lo, s_hi = g.by_core(segments, g.swap_core(segments))
    seg_all = jnp.concatenate([s_lo, s_hi], axis=0)
    seg_pad = jnp.concatenate([jnp.full((2, HALO), -1, jnp.int32), seg_all], axis=1)
    seg_ext = lax.dynamic_slice_in_dim(seg_pad, g.z * T, T + HALO, 1)
    seg = seg_ext[:, HALO:]
    ends = [seg[:, (b + 1) * BLOCK - 1 : (b + 1) * BLOCK] for b in range(nb)]
    begins = [seg_ext[:, HALO - 1 + b * BLOCK : HALO + b * BLOCK] for b in range(nb)]
    block_end = jnp.concatenate(ends, axis=1)
    prior_end = jnp.concatenate(begins, axis=1)
    carry_flag = (prior_end == block_end).astype(f32)

    def across(cols):
        return jnp.concatenate([jnp.broadcast_to(v, (2, BLOCK)) for v in cols], axis=1)

    end_row, prior_row = across(ends), across(begins)
    flags = [(seg_ext[:, HALO - k : HALO - k + T] == seg) for k in range(1, taps)]
    flags += [seg == end_row, seg == prior_row, end_row == prior_row, seg, jnp.zeros_like(seg)]
    flags = jnp.stack([v.astype(f32) for v in flags], axis=1)

    def own_channels(a):
        x_part = lax.dynamic_slice_in_dim(a, HW * j, HW, a.ndim - 1)
        return jnp.concatenate([x_part, a[..., inner:]], axis=-1)

    def own_heads(a):
        return lax.dynamic_slice_in_dim(a, HL * j, HL, a.ndim - 1)

    kernel_own = own_channels(conv_kernel)
    bias_own = own_channels(conv_bias)[None, :]
    rate = jnp.exp(own_heads(decay_log))
    hp = jnp.stack([own_heads(step_bias), rate, own_heads(skip_gain)]).reshape(3, G, GH)
    hp = jnp.pad(hp.transpose(1, 0, 2), ((0, 0), (0, 5), (0, 0)))
    ids = HL * j + GH * lax.broadcasted_iota(jnp.int32, (G, 128, 128), 0)
    lane = lax.broadcasted_iota(jnp.int32, (G, 128, 128), 2)
    sel = (lax.broadcasted_iota(jnp.int32, (G, 128, 128), 1) == ids + lane) & (lane < GH)
    sel = sel.astype(bf16)
    gain_own = lax.dynamic_slice_in_dim(gate_gain, HW * j, HW, 0)[None, :]
    (marks,) = call(
        turn_body,
        (2,),
        [(flags, (1, 8, T), lambda s: (s, 0, 0))],
        [((2, T, 8), f32, (1, T, 8), lambda s: (s, 0, 0))],
        name="turn",
    )
    held = stages.settle([half_gate, half_out, marks, flags, kernel_own, bias_own, hp, sel, gain_own])
    half_gate, half_out, marks, flags, kernel_own, bias_own, hp, sel, gain_own = held
    stages.launch([])
    half_gate, half_out = stages.settle([half_gate, half_out])
    n_ext = at_n["all"].reshape(2 * TE, width)
    w_packed = at_packed["w"]
    at_gate = stages.add(g.fetch_task, half_gate, 1)
    n_ext, w_packed, half_out = stages.launch([n_ext, w_packed, half_out])

    packed = low_dot(n_ext, w_packed, NT).astype(bf16)
    (packed,) = stages.settle([packed])
    at_out = stages.add(g.direct_task, half_out, [4, 6, 6])
    (packed,) = stages.launch([packed])
    packed = packed.reshape(2, TE, KW)
    marks_b = marks.reshape(NB, BLOCK, 8)

    def seq_block(b):
        return lax.div(b, nb), lax.rem(b, nb)

    def late(c):
        return jnp.maximum(c - 1, 0)

    def shared_first(c):
        return jnp.where(c == 0, G, c - 1)

    dt_block = CW // 128
    x, bc, s_block, step, cum, row = call(
        partial(conv_kernel_body, nb),
        (2, G + 1),
        [
            (packed, (1, TE, LANES), lambda s, c: (s, 0, shared_first(c))),
            (packed, (1, TE, 128), lambda s, c: (s, 0, dt_block)),
            (sel, (1, 128, 128), lambda s, c: (late(c), 0, 0)),
            (hp, (1, 8, GH), lambda s, c: (late(c), 0, 0)),
            (marks, (1, T, 8), lambda s, c: (s, 0, 0)),
            (kernel_own, (taps, LANES), lambda s, c: (0, shared_first(c))),
            (bias_own, (1, LANES), lambda s, c: (0, shared_first(c))),
        ],
        [
            ((2 * T, HW), bf16, (T, LANES), lambda s, c: (s, late(c))),
            ((2 * T, shared), bf16, (T, shared), lambda s, c: (s, 0)),
            ((2, nb, state, HW), f32, (1, nb, state, LANES), lambda s, c: (s, 0, 0, late(c))),
            ((2, G, T, GH), f32, (1, 1, T, GH), lambda s, c: (s, late(c), 0, 0)),
            ((2, G, T, GH), f32, (1, 1, T, GH), lambda s, c: (s, late(c), 0, 0)),
            ((2, G, nb, GH, BLOCK), f32, (1, 1, nb, GH, BLOCK), lambda s, c: (s, late(c), 0, 0, 0)),
        ],
        [pltpu.VMEM((TE, LANES), f32), pltpu.VMEM((T, state), bf16)],
        flops=2 * T * HW * state * 20,
        name="convolve",
    )

    end = jnp.exp(row[..., BLOCK - 1]).transpose(0, 2, 1, 3).reshape(2, nb, HL)
    carry_b = end * carry_flag[:, :, None]

    def spread(a):
        return jnp.repeat(a, hd, axis=-1)

    carry_wide = spread(carry_b)[:, :, None, :]
    carry_range = jnp.prod(carry_b, axis=1)
    s_range = s_block[:, 0]
    for b in range(1, nb):
        s_range = s_block[:, b] + carry_wide[:, b] * s_range
    s_range, x, bc, cum, row, step = stages.settle([s_range, x, bc, cum, row, step])
    at_enter = stages.add(g.state_task, s_range, carry_range, spread, 1)
    x, bc, cum, row, step = stages.launch([x, bc, cum, row, step])

    def tile(a):
        return (a, (BLOCK, LANES), lambda b, k: (b, k))

    def whole(a):
        return (a, (BLOCK, a.shape[1]), lambda b, k: (b, 0))

    def small_tile(a):
        def at(b, k):
            s, m = seq_block(b)
            return s, k, m, 0

        return (a, (1, 1, BLOCK, GH), at)

    def row_tile(b, k):
        s, m = seq_block(b)
        return s, k, m, 0, 0

    def flag_tile(b, k):
        s, m = seq_block(b)
        return s, 0, m

    pair_flops = 2 * 2 * T * BLOCK * HW
    (y_local,) = call(
        intra_forward_body,
        (NB, G),
        [
            tile(x),
            whole(bc),
            small_tile(cum),
            (row, (1, 1, 1, GH, BLOCK), row_tile),
            small_tile(step),
            (marks_b, (1, BLOCK, 8), lambda b, k: (b, 0, 0)),
            (flags, (1, 8, BLOCK), flag_tile),
            (hp, (1, 8, GH), lambda b, k: (k, 0, 0)),
        ],
        [((2 * T, HW), bf16, (BLOCK, LANES), lambda b, k: (b, k))],
        [pltpu.VMEM((BLOCK, BLOCK), f32)] * 2,
        flops=pair_flops * 8,
        name="intra_forward",
    )
    (y_local,) = stages.settle([y_local])
    w_gate = at_gate["w"]
    n_ext, w_gate = stages.launch([n_ext, w_gate])
    gate = low_dot(n_ext, w_gate, NT).astype(bf16)
    (gate,) = stages.settle([gate])
    while "state" not in at_enter or "w" not in at_out:
        stages.launch([])
        stages.settle([])
    enter = [at_enter["state"]]
    for b in range(nb - 1):
        enter.append(s_block[:, b] + carry_wide[:, b] * enter[b])
    enter = jnp.stack(enter, axis=1).astype(bf16)
    w_out = at_out["w"]
    cot_all = at_cot["all"].reshape(2 * T, width)
    out_grad = low_dot(cot_all, w_out, NN).astype(bf16)
    gate = gate.reshape(2, TE, HW)

    def seq_tile(a):
        return (a, (T, LANES), lambda s, k: (s, k))

    def seq_small(a):
        return (a, (1, 1, T, GH), lambda s, k: (s, k, 0, 0))

    def seq_state(a):
        return (a, (1, nb, state, LANES), lambda s, k: (s, 0, 0, k))

    def seq_whole(a):
        return (a, (1,) + a.shape[1:], lambda s, k: (s, 0, 0))

    def lane_tile(a):
        return (a, (a.shape[0], LANES), lambda s, k: (0, k))

    bc_seq = (bc, (T, shared), lambda s, k: (s, 0))
    main_tile = (gate, (1, T, LANES), lambda s, k: (s, 0, k))
    mixed, sums = call(
        partial(join_body, nb),
        (2, G),
        [
            seq_tile(y_local),
            bc_seq,
            seq_state(enter),
            seq_small(cum),
            seq_whole(marks),
            main_tile,
            seq_tile(out_grad),
            lane_tile(gain_own),
        ],
        [
            ((2 * T, HW), bf16, (T, LANES), lambda s, k: (s, k)),
            ((2, 8, T), f32, (1, 8, T), lambda s, k: (s, 0, 0)),
        ],
        flops=pair_flops,
        name="join",
    )
    at_sums = stages.add(g.sum_tp_task, sums)
    stages.launch([])
    stages.settle([])

    def turn(spec):
        a, block, at = spec
        return (a, block, lambda k, s: at(s, k))

    normed_out, gate_grad, d_out, gain_grad, de_block = call(
        partial(gates_body, nb, inner),
        (G, 2),
        [
            turn(v)
            for v in [
                seq_tile(mixed),
                main_tile,
                seq_tile(out_grad),
                seq_whole(at_sums["sum"]),
                lane_tile(gain_own),
                bc_seq,
                seq_small(cum),
                seq_whole(marks),
            ]
        ],
        [
            ((2 * T, HW), bf16, (T, LANES), lambda k, s: (s, k)),
            ((2, TE, HW), bf16, (1, TE, LANES), lambda k, s: (s, 0, k)),
            ((2 * T, HW), bf16, (T, LANES), lambda k, s: (s, k)),
            ((1, HW), f32, (1, LANES), lambda k, s: (0, k)),
            ((2, nb, state, HW), f32, (1, nb, state, LANES), lambda k, s: (s, 0, 0, k)),
        ],
        flops=pair_flops,
        name="gates",
    )
    gate_grad = gate_grad.reshape(2 * TE, HW)

    def far_rows(f, n):
        return [f(i).astype(bf16) for i in range(1, n)]

    def out_part(i):
        return low_dot(g.cut(cot_all, 1, i, g.Y), normed_out, TN)

    def in_part(a, i):
        return low_dot(a, g.cut(n_ext, 1, i, g.Y), TN)

    d_range = de_block[:, nb - 1]
    for b in range(nb - 2, -1, -1):
        d_range = de_block[:, b] + carry_wide[:, b] * d_range
    at_leave = stages.add(g.state_task, d_range, carry_range, spread, -1)
    at_outy = stages.add(g.y_task, far_rows(out_part, g.Y), lambda: out_part(0))
    x, d_out, normed_out, gate_grad = stages.launch([x, d_out, normed_out, gate_grad])
    dxs, dec, dbc = call(
        intra_backward_body,
        (NB, G),
        [
            tile(x),
            whole(bc),
            tile(d_out),
            small_tile(cum),
            (row, (1, 1, 1, GH, BLOCK), row_tile),
            small_tile(step),
            (
                enter.reshape(NB, state, HW),
                (1, state, LANES),
                lambda b, k: (b, 0, k),
            ),
            (marks_b, (1, BLOCK, 8), lambda b, k: (b, 0, 0)),
            (flags, (1, 8, BLOCK), flag_tile),
        ],
        [
            ((2 * T, HW), bf16, (BLOCK, LANES), lambda b, k: (b, k)),
            ((2, G, T, GH), f32) + small_tile(cum)[1:],
            ((2 * T, shared), f32, (BLOCK, shared), lambda b, k: (b, 0)),
        ],
        [pltpu.VMEM((BLOCK, BLOCK), f32)] * 3 + [pltpu.VMEM((BLOCK, state), f32)],
        flops=pair_flops * 16,
        name="intra_backward",
    )
    gate_far = far_rows(lambda i: in_part(gate_grad, i), g.Y)
    dxs, gate_far, normed_out = stages.settle([dxs, gate_far, normed_out])
    out_sum = g.sum_z(at_outy["q"])
    at_gatey = stages.add(g.y_task, gate_far, lambda: in_part(gate_grad, 0))
    dxs, normed_out, gate_grad = stages.launch([dxs, normed_out, gate_grad])
    branch = low_dot(normed_out, w_out, NT).astype(bf16)
    dxs, branch = stages.settle([dxs, branch])
    gate_sum = g.sum_z(at_gatey["q"])
    at_branch = stages.add(g.scatter_task, branch.reshape(2, g.X, own_len, width))
    while "state" not in at_leave:
        stages.launch([])
        stages.settle([])
    leave = [at_leave["state"]]
    for b in range(nb - 1, 0, -1):
        leave.insert(0, de_block[:, b] + carry_wide[:, b] * leave[0])
    leave = jnp.stack(leave, axis=1).astype(bf16)
    leave, dxs = stages.launch([leave, dxs])

    x_back, kg, sm, raw_grad, d_keys = call(
        partial(finish_body, nb),
        (2, G),
        [
            (packed, (1, TE, LANES), lambda s, k: (s, 0, k)),
            seq_tile(x),
            seq_tile(d_out),
            seq_tile(dxs),
            bc_seq,
            seq_state(leave),
            seq_state(enter),
            seq_small(cum),
            seq_small(step),
            seq_small(dec),
            (packed, (1, TE, 128), lambda s, k: (s, 0, dt_block)),
            (sel, (1, 128, 128), lambda s, k: (k, 0, 0)),
            (hp, (1, 8, GH), lambda s, k: (k, 0, 0)),
            seq_whole(marks),
            lane_tile(kernel_own),
            lane_tile(bias_own),
        ],
        [
            ((2, TE, HW), bf16, (1, TE, LANES), lambda s, k: (s, 0, k)),
            ((2, 8, HW), f32, (1, 8, LANES), lambda s, k: (s, 0, k)),
            ((2, G, 8, GH), f32, (1, 1, 8, GH), lambda s, k: (s, k, 0, 0)),
            ((2, G, T, GH), f32, (1, 1, T, GH), lambda s, k: (s, k, 0, 0)),
            ((2 * T, state), f32, (T, state), lambda s, k: (s, 0)),
        ],
        [pltpu.VMEM((TE, LANES), f32), pltpu.VMEM((HALO + TE, LANES), f32)],
        flops=pair_flops * 16,
        name="finish",
    )
    x_back = x_back.reshape(2 * TE, HW)
    cols = min(HW, 512)
    NC = HW // cols

    def x_cut(k):
        return lax.slice_in_dim(x_back, k * cols, (k + 1) * cols, axis=1)

    def x_task(k):
        return (
            g.gradient_task,
            far_rows(lambda i: in_part(x_cut(k), i), g.Y),
            lambda: in_part(x_cut(k), 0),
            1,
        )

    kg = jnp.sum(kg, axis=0)
    x_kg, x_bg = kg[:taps], kg[taps]
    sm = jnp.sum(sm, axis=0)[:, :3].transpose(1, 0, 2).reshape(3, HL)

    both = jnp.concatenate([dbc[:, :state] + d_keys, dbc[:, state:]], axis=-1)
    both = both.astype(bf16).reshape(2, T, shared)
    task = x_task(0)
    task, both, x_back = stages.settle([task[1], both, x_back])
    task = (g.gradient_task, task, lambda: in_part(x_cut(0), 0), 1)
    at_xs = [stages.add(*task)]
    at_both = stages.add(g.chunks_task, both, SW)
    x_back, raw_grad = stages.launch([x_back, raw_grad])
    later = [x_task(k) for k in range(1, NC)]
    later_far, raw_grad = stages.settle([[t[1] for t in later], raw_grad])
    for k in range(1, NC):
        at_xs.append(
            stages.add(g.gradient_task, later_far[k - 1], lambda k=k: in_part(x_cut(k), 0), 1)
        )
    (raw_grad,) = stages.launch([raw_grad])
    both_sum = at_both["sum"]

    def own_shared(a):
        return lax.dynamic_slice_in_dim(a, HW + SW * j, SW, a.ndim - 1)

    sh_in = own_shared(packed).astype(f32)
    sh_in = jnp.concatenate([sh_in[:, T:], sh_in[:, :T]], axis=1)
    sh_kernel = own_shared(kernel_own)
    sh_pre = own_shared(bias_own)[None]
    same = [None] + [marks[:, :, k - 1 : k] for k in range(1, taps)]
    moved = [sh_in[:, HALO - k : HALO - k + T] for k in range(taps)]
    for k in range(taps):
        moved[k] = moved[k] if k == 0 else moved[k] * same[k]
        sh_pre = sh_pre + sh_kernel[k] * moved[k]
    cg = both_sum * silu_slope(sh_pre)
    s_back = 0.0
    s_kg = []
    for k in range(taps):
        m = cg if k == 0 else cg * same[k]
        s_kg.append(jnp.sum(cg * moved[k], axis=(0, 1)))
        s_back = s_back + jnp.pad(sh_kernel[k] * m, ((0, 0), (HALO - k, k), (0, 0)))
    s_kg, s_bg = jnp.stack(s_kg), jnp.sum(cg, axis=(0, 1))
    s_back = jnp.concatenate([s_back[:, HALO:], s_back[:, :HALO]], axis=1)
    raw_low = raw_grad.transpose(0, 2, 1, 3).reshape(2, T, HL)
    raw_low = jnp.pad(raw_low, ((0, 0), (0, HALO), (0, 0)))
    tail_w = SW + HL
    pad_w = 128 - tail_w
    tail_back = jnp.concatenate([s_back, raw_low, jnp.zeros((2, TE, pad_w), f32)], axis=-1)
    tail_back = tail_back.astype(bf16).reshape(2 * TE, 128)
    tail_cut = tail_back[:, :tail_w]
    w_tail = jnp.concatenate(
        [
            lax.dynamic_slice_in_dim(w_packed, HW + SW * j, SW, 0),
            lax.dynamic_slice_in_dim(w_packed, CW + HL * j, HL, 0),
            jnp.zeros((pad_w, width), bf16),
        ],
        axis=0,
    )
    k_all = jnp.concatenate([x_kg, s_kg], axis=1)
    b_all = jnp.concatenate([x_bg, s_bg])
    small = jnp.concatenate([gain_grad.reshape(-1), k_all.reshape(-1), b_all, sm.reshape(-1)])
    n_small = small.shape[0]
    small = jnp.pad(small, (0, -n_small % 1024)).reshape(-1, 128)
    tail_far = far_rows(lambda i: in_part(tail_cut, i), g.Y)
    tail_far, small = stages.settle([tail_far, small])
    at_tail = stages.add(g.gradient_task, tail_far, lambda: in_part(tail_cut, 0), 1)
    at_small = stages.add(g.small_task, small, False)
    x_back, tail_back, gate_grad = stages.launch([x_back, tail_back, gate_grad])

    NW = 512
    (n_grad,) = call(
        input_grad_body,
        (width // NW,),
        [
            (gate_grad, (2 * TE, HW), lambda n: (0, 0)),
            (x_back, (2 * TE, HW), lambda n: (0, 0)),
            (tail_back, (2 * TE, 128), lambda n: (0, 0)),
            (w_gate, (HW, NW), lambda n: (0, n)),
            (w_packed, (HW, NW), lambda n: (0, n)),
            (w_tail, (128, NW), lambda n: (0, n)),
        ],
        [((2 * TE, width), bf16, (2 * TE, NW), lambda n: (0, n))],
        flops=2 * 2 * TE * width * (2 * HW + 128),
        name="input_grad",
    )
    n_grad = n_grad.reshape(2, TE, width)
    (n_grad,) = stages.settle([n_grad])
    at_spill = stages.add(g.one_task, [n_grad[:, T:]], lambda a: g.shift_z(a, -1))
    at_gates = stages.add(g.spread_task, gate_sum, 1)
    (n_grad,) = stages.launch([n_grad])
    (n_grad,) = stages.settle([n_grad])
    last = n_grad[:, T - HALO : T].astype(f32) + at_spill["got"][0].astype(f32)
    n_grad = jnp.concatenate([n_grad[:, : T - HALO], last.astype(bf16)], axis=1)
    at_ngrad = stages.add(g.scatter_task, n_grad.reshape(2, g.X, own_len, width))
    at_outs = stages.add(g.spread_task, out_sum, 0)
    stages.launch([])

    in_shape = (2 * inner + shared + heads, own_d)
    out_shape = (own_d, inner)
    dest = {(d, e): (g.x - d) % g.X * 2 + (g.c ^ e) for d in range(g.X) for e in range(2)}

    def place_rows(done, first, buf):
        keys = list(done)
        moves = [
            (i, (0, 0), done[k].shape, (first + HW * dest[k], 0)) for i, k in enumerate(keys)
        ]
        return place([done[k] for k in keys], moves, in_shape, buf)

    in_buf = place_rows(at_gates["done"], 0, None)
    (in_buf,) = stages.settle([in_buf])
    stages.launch([])
    keys = list(at_outs["done"])
    moves = [(i, (0, 0), (own_d, HW), (0, HW * dest[k])) for i, k in enumerate(keys)]
    out_weight_gradient = place([at_outs["done"][k] for k in keys], moves, out_shape, None)
    (out_weight_gradient,) = stages.settle([out_weight_gradient])
    while "sum" not in at_ngrad:
        stages.launch([])
        stages.settle([])
    stages.launch([])
    n_grad = g.own_first_back(at_ngrad["sum"])
    pre_grad = jnp.sum(n_grad * series * scale, axis=0)
    lifted_n = n_grad * pre_gain[None, :]
    token_gradient = (
        cotangent[0].astype(f32)
        + scale * lifted_n
        - series * scale**3 * jnp.mean(series * lifted_n, axis=-1, keepdims=True)
    )[None]
    block_output = (series + g.own_first_back(at_branch["sum"])).astype(bf16)[None]
    at_pre = stages.add(g.small_task, pre_grad.reshape(-1, 128), True)
    flying = {"x": list(enumerate(at_xs)), "tail": True}
    while stages.tasks or flying["x"] or flying["tail"]:
        if stages.tasks:
            (in_buf,) = stages.settle([in_buf])
            if stages.tasks:
                stages.launch([])
        for k, a in list(flying["x"]):
            if "done" in a:
                in_buf = place_rows(a["done"], inner + k * cols, in_buf)
                flying["x"].remove((k, a))
        if flying["tail"] and "done" in at_tail:
            keys = list(at_tail["done"])
            moves = []
            for i, k in enumerate(keys):
                moves.append((i, (0, 0), (SW, own_d), (2 * inner + SW * dest[k], 0)))
                moves.append((i, (SW, 0), (HL, own_d), (2 * inner + shared + HL * dest[k], 0)))
            in_buf = place([at_tail["done"][k] for k in keys], moves, in_shape, in_buf)
            flying["tail"] = False
    in_weight_gradient = in_buf.T

    small = at_small["sum"].reshape(g.TP, -1)[:, :n_small]
    pre_total = at_pre["sum"].reshape(-1)
    gain_total = small[:, :HW].reshape(-1)
    at = HW
    kt = small[:, at : at + taps * (HW + SW)].reshape(g.TP, taps, HW + SW).transpose(1, 0, 2)
    at += taps * (HW + SW)
    kernel_total = jnp.concatenate(
        [kt[:, :, :HW].reshape(taps, -1), kt[:, :, HW:].reshape(taps, -1)], axis=1
    )
    bt = small[:, at : at + HW + SW]
    at += HW + SW
    bias_total = jnp.concatenate([bt[:, :HW].reshape(-1), bt[:, HW:].reshape(-1)])
    step_total = small[:, at : at + HL].reshape(-1)
    decay_total = small[:, at + HL : at + 2 * HL].reshape(-1)
    skip_total = small[:, at + 2 * HL : at + 3 * HL].reshape(-1)
    return (
        block_output,
        token_gradient,
        in_weight_gradient,
        out_weight_gradient,
        pre_total,
        kernel_total,
        bias_total,
        step_total,
        decay_total,
        skip_total,
        gain_total,
    )


def solution(mesh):
    placed = (
        P("shard", "seq", None),
        P("shard", None),
        P("shard", None),
        P(),
        P(),
        P(),
        P(),
        P(),
        P(),
        P(),
        P("shard", None),
        P("shard", "seq", None),
    )
    results = (P("shard", "seq", None),) * 2 + (P("shard", None),) * 2 + (P(),) * 7
    return jax.shard_map(
        partial(body, Slice(mesh)),
        mesh=mesh,
        in_specs=placed,
        out_specs=results,
        check_vma=False,
    )
```

time: 1090 us -> 849 us (0.78)
  Pallas kernels: 0 us -> 167 us
  waiting for transfers between devices: 471 us -> 338 us
  local copies, waits for them, and re-layouts: 201 us -> 80.2 us
  other arithmetic: 181 us -> 78.5 us
  matrix products: 126 us -> 62.7 us
  between operations: 3.27 us -> 16.6 us
    ppermute x69 -> x81, waiting for transfers between devices: 471 us -> 236 us  [move(): return lax.ppermute(a, AXES, pairs)]
    pallas_call x0 -> x21, Pallas kernels: none -> 167 us  [the longest x8 129 us: call(): pl.pallas_call(kernel, grid=grid, in_specs=[pl.BlockSpec(b, m) for _, b,...]
    psum x0 -> x1, waiting for transfers between devices: none -> 101 us  [sum_z(): return lax.psum(q, 'seq', axis_index_groups=groups)]
    dot_general x15 -> x0, matrix products: 50 us -> none  [the longest x1 14 us: body(): jnp.einsum('bsn,bni->bsi', keys, leave, preferred_element_type=f32)]
    reshape x12 -> x1, local copies, waits for them, and re-layouts: 36 us -> 0.08 us  [body(): end = jnp.exp(row[..., BLOCK - 1]).transpose(0, 2, 1, 3).reshape(2, nb, HL)]
    reduce_sum x15 -> x8, other arithmetic: 37.1 us -> 3.05 us  [the longest x1 1.79 us: body(): s_kg.append(jnp.sum(cg * moved[k], axis=(0, 1)))]
    another operation x24 -> x13, other arithmetic: 29.7 us -> 2.94 us  [the longest x8 13.4 us: true_x(): return jnp.stack(rows)]
    concatenate x5 -> x2, local copies, waits for them, and re-layouts: 26.8 us -> 0.69 us  [the longest x1 0.62 us: body(): jnp.concatenate([s_back, raw_low, jnp.zeros((2, TE, pad_w), f32)], axis=-1)]
  transfers between devices with their start and end apart: 69 -> 82, of which waited for: 28 -> 30; matrix products, arithmetic and copies ran while one was open for 32% -> 15% of each run, Pallas kernels for 0% -> 16%
where the time goes in v2:
time: 849 us; the launch traced here: 843 us
  waiting for transfers between devices  338 us (40%)
  Pallas kernels  167 us (20%)
  starting transfers between devices  99.8 us (12%)
  local copies, waits for them, and re-layouts  80.2 us (9%)
  other arithmetic  78.5 us (9%)
  matrix products  62.7 us (7%)
  between operations  16.6 us (2%)
    ppermute x81, waiting for transfers between devices, move(): return lax.ppermute(a, AXES, pairs)  236 us
    pallas_call x8, Pallas kernels, call(): pl.pallas_call(kernel, grid=grid, in_specs=[pl.BlockSpec(b, m) for _, b,...  129 us
    psum x1, waiting for transfers between devices, sum_z(): return lax.psum(q, 'seq', axis_index_groups=groups)  101 us
    ppermute x81, starting transfers between devices, move(): return lax.ppermute(a, AXES, pairs)  99.8 us
    dot_general x14, matrix products, low_dot(): lax.dot_general(a.astype(bf16), b.astype(bf16), dims, preferred_element_t...  62.7 us
    unnamed x279, local copies, waits for them, and re-layouts  38 us
    pallas_call x8, Pallas kernels, assemble(): pl.pallas_call(kernel, in_specs=[pl.BlockSpec(memory_space=pltpu.SMEM)] +...  19.2 us
    pallas_call x5, Pallas kernels, place(): pl.pallas_call(kernel, in_specs=[pl.BlockSpec(memory_space=pltpu.SMEM)] +...  18.7 us
  transfers between devices with their start and end apart: 82, of which 30 were waited for; matrix products, arithmetic and copies ran while one was open for 15% of the time, Pallas kernels for 16%

profile of v2, /device:TPU:1, one launch (start us, length us, event | category | flops | bytes accessed | tf_op | source)
XLA Modules:
  0.0 842.8 jit_solution(16550890609717743947)
XLA Ops:
  69.1 15.9 %collective-permute-done.12.refs_1_ = bf16[448,1024]{1,0:T(8,128)(2,1)} collective-permute-done((bf16[448,1024]{1,0:T(8,128)(2,1)}, bf16[448,1024]{1,0:T(8,128)(2,1)}, u32[]{:S(2)}, u32[]{:S(2)}) %collective-permute-start.12) | collective-permute-done | bytes 917536 | tf_op jit(solution)/shard_map/ppermute | solution.py:50
  96.1 7.1 convolution_convert_fusion
  113.7 22.8 %convolve.1 = (bf16[1024,1024]{1,0:T(8,128)(2,1)S(1)}, bf16[1024,256]{1,0:T(8,128)(2,1)S(1)}, f32[2,2,128,1024]{3,2,1,0:T(8,128)S(1)}, f32[2,4,512,4]{3,2,1,0:T(...) custom-call(bf16[2,528,1408]{2,1,0:T(8,128)(2,1)S(1)} %bitcast.310, ...), custom_call_target="tpu_custom_call" | custom-call | flops 2684354560 | bytes 11052544 | tf_op jit(solution)/shard_map/convolve/pallas_call | solution.py:424
  163.3 10.3 %intra_forward.1.y = bf16[1024,1024]{1,0:T(8,128)(2,1)S(1)} custom-call(bf16[1024,1024]{1,0:T(8,128)(2,1)S(1)} %copy-done.57, bf16[1024,256]{1,0:T(8,128)(2,1)S(1)} %get-tuple-element.288.bc, f32[2,4,512,4]{3,2,1,0:T(8,128)S(1)} %copy-done.9, f32[2,4,2,4,256]{4,3,2,1,0:T(4,128)S(1)} %get-tuple-element.290.row, f32[2,4,512,4]{3,2,1,0:T(8,128)S(1)} %copy-done.61, ...), custom_call_target="tpu_custom_call" | custom-call | flops 4294967296 | bytes 4981248 | tf_op jit(solution)/shard_map/intra_forward/pallas_call | solution.py:424
  180.0 4.9 convolution_convert_fusion.1
  186.8 8.2 collective-permute-done.23.refs_3_
  196.9 8.4 %convolution_convert_fusion.4.og = bf16[1024,1024]{1,0:T(8,128)(2,1)S(1)} fusion(bf16[1024,2048]{1,0:T(8,128)(2,1)} %bitcast.302, bf16[2048,1024]{1,0:T(8,128)(2,1)S(1)} %assemble.15), kind=kOutput, calls=%fused_computation.52 | convolution fusion | flops 4296015872 | bytes 10485760 | tf_op jit(solution)/shard_map/dot_general | solution.py:352
  205.4 8.9 %join.1 = (bf16[1024,1024]{1,0:T(8,128)(2,1)S(1)}, f32[2,8,512]{2,1,0:T(8,128)S(1)}) custom-call(bf16[1024,1024]{1,0:T(8,128)(2,1)S(1)} %copy-done.25, bf16[1024,256]{1,0:T(8,128)(2,1)S(1)} %get-tuple-element.288.bc, bf16[2,2,128,1024]{3,2,1,0:T(8,128)(2,1)S(1)} %maximum_convert_fusion.enter, f32[2,4,512,4]{3,2,1,0:T(8,128)S(1)} %copy-done.9, ...), custom_call_target="tpu_custom_call" | custom-call | flops 536870912 | bytes 10162176 | tf_op jit(solution)/shard_map/join/pallas_call | solution.py:424
  215.7 5.8 collective-permute-start.27
  225.9 12.6 %gates.1 = (bf16[1024,1024]{1,0:T(8,128)(2,1)S(1)}, bf16[2,528,1024]{2,1,0:T(8,128)(2,1)}, bf16[1024,1024]{1,0:T(8,128)(2,1)S(1)}, f32[1,1024]{1,0:T(1,128)S(1)}, f32[2,2,128,1024]{3,2,1,0:T(8,128)S(1)}) custom-call(bf16[1024,1024]{1,0:T(8,128)(2,1)S(1)} %copy-done.27, bf16[2,528,1024]{2,1,0:T(8,128)(2,1)} %bitcast.295, ...), custom_call_target="tpu_custom_call" | custom-call | flops 536870912 | bytes 15474688 | tf_op jit(solution)/shard_map/gates/pallas_call | solution.py:424
  238.8 6.6 fusion.22
  250.2 36.0 %intra_backward.1 = (bf16[1024,1024]{1,0:T(8,128)(2,1)S(1)}, f32[2,4,512,4]{3,2,1,0:T(8,128)S(1)}, f32[1024,256]{1,0:T(8,128)S(1)}) custom-call(bf16[1024,1024]{1,0:T(8,128)(2,1)S(1)} %copy-done.58, bf16[1024,256]{1,0:T(8,128)(2,1)S(1)} %get-tuple-element.288.bc, bf16[1024,1024]{1,0:T(8,128)(2,1)S(1)} %copy-done.50, f32[2,4,512,4]{3,2,1,0:T(8,128)S(1)} %copy-done.10, ...), custom_call_target="tpu_custom_call" | custom-call | flops 8589934592 | bytes 9240576 | tf_op jit(solution)/shard_map/intra_backward/pallas_call | solution.py:424
  299.9 4.9 convolution_convert_fusion.2
  304.8 4.5 fusion.25
  313.0 26.7 %collective-permute-done.31 = bf16[1024,1024]{1,0:T(8,128)(2,1)} collective-permute-done((bf16[1024,1024]{1,0:T(8,128)(2,1)}, bf16[1024,1024]{1,0:T(8,128)(2,1)}, u32[]{:S(2)}, u32[]{:S(2)}) %collective-permute-start.31) | collective-permute-done | bytes 2097184 | tf_op jit(solution)/shard_map/ppermute | solution.py:50
  344.3 25.9 %finish.1 = (bf16[2,528,1024]{2,1,0:T(8,128)(2,1)}, f32[2,8,1024]{2,1,0:T(8,128)S(1)}, f32[2,4,8,4]{3,2,1,0:T(8,128)S(1)}, f32[2,4,512,4]{3,2,1,0:T(8,128)S(1)}, f32[1024,128]{1,0:T(8,128)S(1)}) custom-call(bf16[2,528,1408]{2,1,0:T(8,128)(2,1)} %bitcast.313, bf16[1024,1024]{1,0:T(8,128)(2,1)S(1)} %copy-done.59, bf16[1024,1024]{1,0:T(8,128)(2,1)S(1)} %copy-done.51, ...), custom_call_target="tpu_custom_call" | custom-call | flops 8589934592 | bytes 18065920 | tf_op jit(solution)/shard_map/finish/pallas_call | solution.py:424
  371.2 5.0 add_convert_fusion.1
  401.5 21.6 %collective-permute-done.33 = bf16[256,2048]{1,0:T(8,128)(2,1)S(1)} collective-permute-done((bf16[256,2048]{1,0:T(8,128)(2,1)S(1)}, bf16[256,2048]{1,0:T(8,128)(2,1)S(1)}, u32[]{:S(2)}, u32[]{:S(2)}) %collective-permute-start.33) | collective-permute-done | bytes 1048608 | tf_op jit(solution)/shard_map/ppermute | solution.py:50
  443.0 101.4 %all-reduce.12.cloned.1.call-done = (bf16[1024,1024]{1,0:T(8,128)(2,1)}, bf16[1024,1024]{1,0:T(8,128)(2,1)}) async-done(((bf16[1024,1024]{1,0:T(8,128)(2,1)}, bf16[1024,1024]{1,0:T(8,128)(2,1)}), (bf16[1024,1024]{1,0:T(8,128)(2,1)}, bf16[1024,1024]{1,0:T(8,128)(2,1)})) %all-reduce.12.cloned.1.call-update) | async-done | bytes 4194320 | tf_op jit(solution)/shard_map/psum | solution.py:167
  555.2 4.6 collective-permute-start.41
  559.9 12.6 %input_grad.1 = bf16[1056,2048]{1,0:T(8,128)(2,1)S(1)} custom-call(bf16[1056,1024]{1,0:T(8,128)(2,1)S(1)} %bitcast.318, bf16[1056,1024]{1,0:T(8,128)(2,1)S(1)} %bitcast.323, bf16[1056,128]{1,0:T(8,128)(2,1)S(1)} %maximum_maximum_fusion.1.tb, bf16[1024,2048]{1,0:T(8,128)(2,1)S(1)} %copy-done.19, bf16[1408,2048]{1,0:T(8,128)(2,1)} %copy-done.12, ...), custom_call_target="tpu_custom_call" | custom-call | flops 9412018176 | bytes 19406848 | tf_op jit(solution)/shard_map/input_grad/pallas_call | solution.py:424
  604.9 19.3 %collective-permute-done.46 = bf16[512,1024]{1,0:T(8,128)(2,1)} collective-permute-done((bf16[512,1024]{1,0:T(8,128)(2,1)}, bf16[512,1024]{1,0:T(8,128)(2,1)}, u32[]{:S(2)}, u32[]{:S(2)}) %collective-permute-start.46) | collective-permute-done | bytes 1048608 | tf_op jit(solution)/shard_map/ppermute | solution.py:50
  624.3 20.6 %collective-permute-done.52.refs_1_ = bf16[1024,512]{1,0:T(8,128)(2,1)} collective-permute-done((bf16[1024,512]{1,0:T(8,128)(2,1)S(1)}, bf16[1024,512]{1,0:T(8,128)(2,1)}, u32[]{:S(2)}, u32[]{:S(2)}) %collective-permute-start.52) | collective-permute-done | bytes 1048608 | tf_op jit(solution)/shard_map/ppermute | solution.py:50
  653.3 5.2 broadcast_select_fusion.1
  661.0 23.6 %collective-permute-done.61 = f32[56,128]{1,0:T(8,128)S(1)} collective-permute-done((f32[56,128]{1,0:T(8,128)S(1)}, f32[56,128]{1,0:T(8,128)S(1)}, u32[]{:S(2)}, u32[]{:S(2)}) %collective-permute-start.61) | collective-permute-done | bytes 28704 | tf_op jit(solution)/shard_map/ppermute | solution.py:50
  697.4 5.1 place.5.refs_4_
  702.5 22.8 %collective-permute-done.57 = bf16[512,1024]{1,0:T(8,128)(2,1)} collective-permute-done((bf16[512,1024]{1,0:T(8,128)(2,1)}, bf16[512,1024]{1,0:T(8,128)(2,1)}, u32[]{:S(2)}, u32[]{:S(2)}) %collective-permute-start.57) | collective-permute-done | bytes 1048608 | tf_op jit(solution)/shard_map/ppermute | solution.py:50
  725.3 12.9 %collective-permute-done.64.refs_1_ = bf16[512,1024]{1,0:T(8,128)(2,1)} collective-permute-done((bf16[512,1024]{1,0:T(8,128)(2,1)S(1)}, bf16[512,1024]{1,0:T(8,128)(2,1)}, u32[]{:S(2)}, u32[]{:S(2)}) %collective-permute-start.64) | collective-permute-done | bytes 1048608 | tf_op jit(solution)/shard_map/ppermute | solution.py:50
  758.6 5.5 place.6
  764.7 9.2 %collective-permute-done.67.refs_1_ = bf16[512,512]{1,0:T(8,128)(2,1)} collective-permute-done((bf16[512,512]{1,0:T(8,128)(2,1)S(1)}, bf16[512,512]{1,0:T(8,128)(2,1)}, u32[]{:S(2)}, u32[]{:S(2)}) %collective-permute-start.67) | collective-permute-done | bytes 524320 | tf_op jit(solution)/shard_map/ppermute | solution.py:50
  774.0 22.4 %collective-permute-done.70 = bf16[256,2048]{1,0:T(8,128)(2,1)} collective-permute-done((bf16[256,2048]{1,0:T(8,128)(2,1)}, bf16[256,2048]{1,0:T(8,128)(2,1)}, u32[]{:S(2)}, u32[]{:S(2)}) %collective-permute-start.70) | collective-permute-done | bytes 1048608 | tf_op jit(solution)/shard_map/ppermute | solution.py:50
  802.0 7.0 collective-permute-start.72
  (664 shorter events, 317.8 us)
Async XLA Ops:
  7.2 537.2 %all-reduce.12.cloned.1.call-start = ((), (), s32[]{:S(2)}) async-start(), calls=%async_computation | async-start | bytes 8388608 | tf_op jit(solution)/shard_map/psum | solution.py:167
  31.3 25.6 %collective-permute-start.3 = (bf16[256,2048]{1,0:T(8,128)(2,1)}, bf16[256,2048]{1,0:T(8,128)(2,1)}, u32[]{:S(2)}, u32[]{:S(2)}) collective-permute-start(bf16[256,2048]{1,0:T(8,128)(2,1)} %get-tuple-element.232), channel_id=1, source_target_pairs={{0,1},{1,0},{2,3},{3,2},{4,5},{5,4},{6,7},{7,6},{8,9},{9,8},{10,11... | collective-permute-start | bytes 3145736 | tf_op jit(solution)/shard_map/ppermute | solution.py:50
  31.7 25.8 %collective-permute-start.2 = (bf16[256,2048]{1,0:T(8,128)(2,1)}, bf16[256,2048]{1,0:T(8,128)(2,1)}, u32[]{:S(2)}, u32[]{:S(2)}) collective-permute-start(bf16[256,2048]{1,0:T(8,128)(2,1)} %get-tuple-element.232), channel_id=1, source_target_pairs={{0,4},{1,5},{2,6},{3,7},{4,0},{5,1},{6,2},{7,3},{8,12},{9,13},{10,... | collective-permute-start | bytes 3145736 | tf_op jit(solution)/shard_map/ppermute | solution.py:50
  57.5 27.5 %collective-permute-start.10 = (bf16[256,2048]{1,0:T(8,128)(2,1)}, bf16[256,2048]{1,0:T(8,128)(2,1)}, u32[]{:S(2)}, u32[]{:S(2)}) collective-permute-start(bf16[256,2048]{1,0:T(8,128)(2,1)} %collective-permute-done.2), channel_id=1, source_target_pairs={{0,1},{1,0},{2,3},{3,2},{4,5},{5,4},{6,7},{7,6},{8,9},{9,8},{10,11... | collective-permute-start | bytes 3145736 | tf_op jit(solution)/shard_map/ppermute | solution.py:50
  58.6 26.4 %collective-permute-start.15 = (bf16[256,2048]{1,0:T(8,128)(2,1)}, bf16[256,2048]{1,0:T(8,128)(2,1)}, u32[]{:S(2)}, u32[]{:S(2)}) collective-permute-start(bf16[256,2048]{1,0:T(8,128)(2,1)} %get-tuple-element.246), channel_id=1, source_target_pairs={{0,1},{1,0},{2,3},{3,2},{4,5},{5,4},{6,7},{7,6},{8,9},{9,8},{10,11... | collective-permute-start | bytes 3145736 | tf_op jit(solution)/shard_map/ppermute | solution.py:50
  58.6 26.3 %collective-permute-start.14 = (bf16[256,2048]{1,0:T(8,128)(2,1)}, bf16[256,2048]{1,0:T(8,128)(2,1)}, u32[]{:S(2)}, u32[]{:S(2)}) collective-permute-start(bf16[256,2048]{1,0:T(8,128)(2,1)} %get-tuple-element.246), channel_id=1, source_target_pairs={{0,4},{1,5},{2,6},{3,7},{4,0},{5,1},{6,2},{7,3},{8,12},{9,13},{10,... | collective-permute-start | bytes 3145736 | tf_op jit(solution)/shard_map/ppermute | solution.py:50
  110.7 33.4 %collective-permute-start.20 = (bf16[256,1024]{1,0:T(8,128)(2,1)}, bf16[256,1024]{1,0:T(8,128)(2,1)}, u32[]{:S(2)}, u32[]{:S(2)}) collective-permute-start(bf16[256,1024]{1,0:T(8,128)(2,1)} %slice.276), channel_id=1, source_target_pairs={{0,2},{1,3},{2,0},{3,1},{4,6},{5,7},{6,4},{7,5},{8,10},{9,11},{10,... | collective-permute-start | bytes 1572872 | tf_op jit(solution)/shard_map/ppermute | solution.py:50
  112.2 32.0 %collective-permute-start.18 = (bf16[320,1024]{1,0:T(8,128)(2,1)}, bf16[320,1024]{1,0:T(8,128)(2,1)}, u32[]{:S(2)}, u32[]{:S(2)}) collective-permute-start(bf16[320,1024]{1,0:T(8,128)(2,1)} %slice.275), channel_id=1, source_target_pairs={{0,2},{1,3},{2,0},{3,1},{4,6},{5,7},{6,4},{7,5},{8,10},{9,11},{10,... | collective-permute-start | bytes 1966088 | tf_op jit(solution)/shard_map/ppermute | solution.py:50
  112.2 32.0 %collective-permute-start.19 = (bf16[352,1024]{1,0:T(8,128)(2,1)}, bf16[352,1024]{1,0:T(8,128)(2,1)}, u32[]{:S(2)}, u32[]{:S(2)}) collective-permute-start(bf16[352,1024]{1,0:T(8,128)(2,1)} %collective-permute-done.17.refs_2_), channel_id=1, source_target_pairs={{0,8},{1,9},{2,10},{3,11},{4,12},{5,13},{6,14},{7,15},{8,0},{9,1},... | collective-permute-start | bytes 2162696 | tf_op jit(solution)/shard_map/ppermute | solution.py:50
  146.0 27.7 %collective-permute-start.21 = (bf16[384,1024]{1,0:T(8,128)(2,1)}, bf16[384,1024]{1,0:T(8,128)(2,1)}, u32[]{:S(2)}, u32[]{:S(2)}) collective-permute-start(bf16[384,1024]{1,0:T(8,128)(2,1)} %get-tuple-element.285), channel_id=1, source_target_pairs={{0,2},{1,3},{2,0},{3,1},{4,6},{5,7},{6,4},{7,5},{8,10},{9,11},{10,... | collective-permute-start | bytes 2359304 | tf_op jit(solution)/shard_map/ppermute | solution.py:50
  245.4 47.4 %collective-permute-start.29 = (bf16[1024,1024]{1,0:T(8,128)(2,1)}, bf16[1024,1024]{1,0:T(8,128)(2,1)}, u32[]{:S(2)}, u32[]{:S(2)}) collective-permute-start(bf16[1024,1024]{1,0:T(8,128)(2,1)} %fusion.22), channel_id=1, source_target_pairs={{0,2},{1,3},{2,0},{3,1},{4,6},{5,7},{6,4},{7,5},{8,10},{9,11},{10,... | collective-permute-start | bytes 6291464 | tf_op jit(solution)/shard_map/ppermute | solution.py:50
  248.7 41.7 %collective-permute-start.28 = (bf16[2,128,1024]{2,1,0:T(8,128)(2,1)S(1)}, bf16[2,128,1024]{2,1,0:T(8,128)(2,1)S(1)}, u32[]{:S(2)}, u32[]{:S(2)}) collective-permute-start(bf16[2,128,1024]{2,1,0:T(8,128)(2,1)S(1)} %fusion.55), channel_id=1, source_target_pairs={{8,0},{9,1},{10,2},{11,3},{12,4},{13,5},{14,6},{15,7},{16,8},{17,9... | collective-permute-start | bytes 1572872 | tf_op jit(solution)/shard_map/ppermute | solution.py:50
  293.1 46.5 %collective-permute-start.31 = (bf16[1024,1024]{1,0:T(8,128)(2,1)}, bf16[1024,1024]{1,0:T(8,128)(2,1)}, u32[]{:S(2)}, u32[]{:S(2)}) collective-permute-start(bf16[1024,1024]{1,0:T(8,128)(2,1)} %convolution_convert_fusion.3), channel_id=1, source_target_pairs={{0,2},{1,3},{2,0},{3,1},{4,6},{5,7},{6,4},{7,5},{8,10},{9,11},{10,... | collective-permute-start | bytes 6291464 | tf_op jit(solution)/shard_map/ppermute | solution.py:50
  342.3 39.5 %collective-permute-start.32 = (bf16[2,256,2048]{2,1,0:T(8,128)(2,1)}, bf16[2,256,2048]{2,1,0:T(8,128)(2,1)}, u32[]{:S(2)}, u32[]{:S(2)}) collective-permute-start(bf16[2,256,2048]{2,1,0:T(8,128)(2,1)} %bitcast.57), channel_id=1, source_target_pairs={{0,1},{1,0},{2,3},{3,2},{4,5},{5,4},{6,7},{7,6},{8,9},{9,8},{10,11... | collective-permute-start | bytes 6291464 | tf_op jit(solution)/shard_map/ppermute | solution.py:50
  388.7 34.4 %collective-permute-start.33 = (bf16[256,2048]{1,0:T(8,128)(2,1)S(1)}, bf16[256,2048]{1,0:T(8,128)(2,1)S(1)}, u32[]{:S(2)}, u32[]{:S(2)}) collective-permute-start(bf16[256,2048]{1,0:T(8,128)(2,1)S(1)} %dynamic-slice_bitcast_fusion.3), channel_id=1, source_target_pairs={{0,4},{1,5},{2,6},{3,7},{4,0},{5,1},{6,2},{7,3},{8,12},{9,13},{10,... | collective-permute-start | bytes 3145736 | tf_op jit(solution)/shard_map/ppermute | solution.py:50
  388.8 34.3 %collective-permute-start.34 = (bf16[512,1024]{1,0:T(8,128)(2,1)S(1)}, bf16[512,1024]{1,0:T(8,128)(2,1)S(1)}, u32[]{:S(2)}, u32[]{:S(2)}) collective-permute-start(bf16[512,1024]{1,0:T(8,128)(2,1)S(1)} %convolution_convert_fusion.6), channel_id=1, source_target_pairs={{0,2},{1,3},{2,0},{3,1},{4,6},{5,7},{6,4},{7,5},{8,10},{9,11},{10,... | collective-permute-start | bytes 3145736 | tf_op jit(solution)/shard_map/ppermute | solution.py:50
  433.2 114.1 %collective-permute-start.39 = (bf16[512,1024]{1,0:T(8,128)(2,1)}, bf16[512,1024]{1,0:T(8,128)(2,1)}, u32[]{:S(2)}, u32[]{:S(2)}) collective-permute-start(bf16[512,1024]{1,0:T(8,128)(2,1)} %convolution_convert_fusion.5), channel_id=1, source_target_pairs={{0,2},{1,3},{2,0},{3,1},{4,6},{5,7},{6,4},{7,5},{8,10},{9,11},{10,... | collective-permute-start | bytes 3145736 | tf_op jit(solution)/shard_map/ppermute | solution.py:50
  433.2 114.0 %collective-permute-start.38 = (bf16[512,1024]{1,0:T(8,128)(2,1)}, bf16[512,1024]{1,0:T(8,128)(2,1)}, u32[]{:S(2)}, u32[]{:S(2)}) collective-permute-start(bf16[512,1024]{1,0:T(8,128)(2,1)} %add_convert_fusion.7), channel_id=1, source_target_pairs={{0,8},{1,9},{2,10},{3,11},{4,12},{5,13},{6,14},{7,15},{24,16},{25,... | collective-permute-start | bytes 3145736 | tf_op jit(solution)/shard_map/ppermute | solution.py:50
  593.7 30.5 %collective-permute-start.53 = (bf16[1024,512]{1,0:T(8,128)(2,1)}, bf16[1024,512]{1,0:T(8,128)(2,1)S(1)}, u32[]{:S(2)}, u32[]{:S(2)}) collective-permute-start(bf16[1024,512]{1,0:T(8,128)(2,1)} %get-tuple-element.393), channel_id=1, source_target_pairs={{0,5},{1,4},{2,7},{3,6},{4,1},{5,0},{6,3},{7,2},{8,13},{9,12},{10,... | collective-permute-start | bytes 3145736 | tf_op jit(solution)/shard_map/ppermute | solution.py:50
  598.1 26.1 %collective-permute-start.51 = (bf16[1024,512]{1,0:T(8,128)(2,1)}, bf16[1024,512]{1,0:T(8,128)(2,1)}, u32[]{:S(2)}, u32[]{:S(2)}) collective-permute-start(bf16[1024,512]{1,0:T(8,128)(2,1)} %get-tuple-element.393), channel_id=1, source_target_pairs={{0,1},{1,0},{2,3},{3,2},{4,5},{5,4},{6,7},{7,6},{8,9},{9,8},{10,11... | collective-permute-start | bytes 3145736 | tf_op jit(solution)/shard_map/ppermute | solution.py:50
  598.1 26.1 %collective-permute-start.46 = (bf16[512,1024]{1,0:T(8,128)(2,1)}, bf16[512,1024]{1,0:T(8,128)(2,1)}, u32[]{:S(2)}, u32[]{:S(2)}) collective-permute-start(bf16[512,1024]{1,0:T(8,128)(2,1)} %get-tuple-element.388), channel_id=1, source_target_pairs={{8,0},{9,1},{10,2},{11,3},{12,4},{13,5},{14,6},{15,7},{16,24},{17,... | collective-permute-start | bytes 3145736 | tf_op jit(solution)/shard_map/ppermute | solution.py:50
  601.1 43.8 %collective-permute-start.52 = (bf16[1024,512]{1,0:T(8,128)(2,1)S(1)}, bf16[1024,512]{1,0:T(8,128)(2,1)}, u32[]{:S(2)}, u32[]{:S(2)}) collective-permute-start(bf16[1024,512]{1,0:T(8,128)(2,1)S(1)} %get-tuple-element.394.refs_3_), channel_id=1, source_target_pairs={{0,4},{1,5},{2,6},{3,7},{4,0},{5,1},{6,2},{7,3},{8,12},{9,13},{10,... | collective-permute-start | bytes 3145736 | tf_op jit(solution)/shard_map/ppermute | solution.py:50
  658.5 79.8 %collective-permute-start.62 = (bf16[2,256,2048]{2,1,0:T(8,128)(2,1)}, bf16[2,256,2048]{2,1,0:T(8,128)(2,1)}, u32[]{:S(2)}, u32[]{:S(2)}) collective-permute-start(bf16[2,256,2048]{2,1,0:T(8,128)(2,1)} %bitcast.92), channel_id=1, source_target_pairs={{0,1},{1,0},{2,3},{3,2},{4,5},{5,4},{6,7},{7,6},{8,9},{9,8},{10,11... | collective-permute-start | bytes 6291464 | tf_op jit(solution)/shard_map/ppermute | solution.py:50
  658.9 32.0 %collective-permute-start.56 = (bf16[512,512]{1,0:T(8,128)(2,1)}, bf16[512,512]{1,0:T(8,128)(2,1)S(1)}, u32[]{:S(2)}, u32[]{:S(2)}) collective-permute-start(bf16[512,512]{1,0:T(8,128)(2,1)} %get-tuple-element.403), channel_id=1, source_target_pairs={{0,5},{1,4},{2,7},{3,6},{4,1},{5,0},{6,3},{7,2},{8,13},{9,12},{10,... | collective-permute-start | bytes 1572872 | tf_op jit(solution)/shard_map/ppermute | solution.py:50
  658.9 32.2 %collective-permute-start.54 = (bf16[512,512]{1,0:T(8,128)(2,1)}, bf16[512,512]{1,0:T(8,128)(2,1)}, u32[]{:S(2)}, u32[]{:S(2)}) collective-permute-start(bf16[512,512]{1,0:T(8,128)(2,1)} %get-tuple-element.403), channel_id=1, source_target_pairs={{0,1},{1,0},{2,3},{3,2},{4,5},{5,4},{6,7},{7,6},{8,9},{9,8},{10,11... | collective-permute-start | bytes 1572872 | tf_op jit(solution)/shard_map/ppermute | solution.py:50
  659.0 33.4 %collective-permute-start.55 = (bf16[512,512]{1,0:T(8,128)(2,1)S(1)}, bf16[512,512]{1,0:T(8,128)(2,1)}, u32[]{:S(2)}, u32[]{:S(2)}) collective-permute-start(bf16[512,512]{1,0:T(8,128)(2,1)S(1)} %get-tuple-element.404.refs_3_), channel_id=1, source_target_pairs={{0,4},{1,5},{2,6},{3,7},{4,0},{5,1},{6,2},{7,3},{8,12},{9,13},{10,... | collective-permute-start | bytes 1572872 | tf_op jit(solution)/shard_map/ppermute | solution.py:50
  690.3 35.0 %collective-permute-start.65 = (bf16[512,1024]{1,0:T(8,128)(2,1)}, bf16[512,1024]{1,0:T(8,128)(2,1)}, u32[]{:S(2)}, u32[]{:S(2)}) collective-permute-start(bf16[512,1024]{1,0:T(8,128)(2,1)} %get-tuple-element.409), channel_id=1, source_target_pairs={{0,5},{1,4},{2,7},{3,6},{4,1},{5,0},{6,3},{7,2},{8,13},{9,12},{10,... | collective-permute-start | bytes 3145736 | tf_op jit(solution)/shard_map/ppermute | solution.py:50
  690.9 34.4 %collective-permute-start.63 = (bf16[512,1024]{1,0:T(8,128)(2,1)}, bf16[512,1024]{1,0:T(8,128)(2,1)}, u32[]{:S(2)}, u32[]{:S(2)}) collective-permute-start(bf16[512,1024]{1,0:T(8,128)(2,1)} %get-tuple-element.409), channel_id=1, source_target_pairs={{0,1},{1,0},{2,3},{3,2},{4,5},{5,4},{6,7},{7,6},{8,9},{9,8},{10,11... | collective-permute-start | bytes 3145736 | tf_op jit(solution)/shard_map/ppermute | solution.py:50
  691.1 34.2 %collective-permute-start.57 = (bf16[512,1024]{1,0:T(8,128)(2,1)}, bf16[512,1024]{1,0:T(8,128)(2,1)}, u32[]{:S(2)}, u32[]{:S(2)}) collective-permute-start(bf16[512,1024]{1,0:T(8,128)(2,1)} %add_convert_fusion.2), channel_id=1, source_target_pairs={{8,0},{9,1},{10,2},{11,3},{12,4},{13,5},{14,6},{15,7},{16,24},{17,... | collective-permute-start | bytes 3145736 | tf_op jit(solution)/shard_map/ppermute | solution.py:50
  692.4 45.8 %collective-permute-start.64 = (bf16[512,1024]{1,0:T(8,128)(2,1)S(1)}, bf16[512,1024]{1,0:T(8,128)(2,1)}, u32[]{:S(2)}, u32[]{:S(2)}) collective-permute-start(bf16[512,1024]{1,0:T(8,128)(2,1)S(1)} %get-tuple-element.410.refs_3_), channel_id=1, source_target_pairs={{0,4},{1,5},{2,6},{3,7},{4,0},{5,1},{6,2},{7,3},{8,12},{9,13},{10,... | collective-permute-start | bytes 3145736 | tf_op jit(solution)/shard_map/ppermute | solution.py:50
  752.2 44.1 %collective-permute-start.70 = (bf16[256,2048]{1,0:T(8,128)(2,1)}, bf16[256,2048]{1,0:T(8,128)(2,1)}, u32[]{:S(2)}, u32[]{:S(2)}) collective-permute-start(bf16[256,2048]{1,0:T(8,128)(2,1)} %dynamic-slice_bitcast_fusion), channel_id=1, source_target_pairs={{0,4},{1,5},{2,6},{3,7},{4,0},{5,1},{6,2},{7,3},{8,12},{9,13},{10,... | collective-permute-start | bytes 3145736 | tf_op jit(solution)/shard_map/ppermute | solution.py:50
  799.8 26.2 %collective-permute-start.73 = (f32[16,128]{1,0:T(8,128)S(1)}, f32[16,128]{1,0:T(8,128)S(1)}, u32[]{:S(2)}, u32[]{:S(2)}) collective-permute-start(f32[16,128]{1,0:T(8,128)S(1)} %bitcast.350), channel_id=1, source_target_pairs={{0,24},{1,25},{2,26},{3,27},{4,28},{5,29},{6,30},{7,31},{8,0},{9,1... | collective-permute-start | bytes 24584 | tf_op jit(solution)/shard_map/ppermute | solution.py:50
  (191 other events, 1952.3 us)
Sparse Core Ops, SparseCore 0:
  376.3 168.0 all-reduce.11

commit v3 on v2

--- a/solution.py
+++ b/solution.py
@@ -22,47 +22,45 @@
         self.seq = mesh.shape["seq"]
         self.shard = mesh.shape["shard"]
         self.Y = self.shard // 2
-        self.X = self.Y
-        self.Z = self.seq // self.X
-        self.TP = 2 * self.X
+        self.W = 4
+        self.Z = self.seq // self.W
+        self.TP = 2 * self.W
 
     def place(self):
         s, k = lax.axis_index("seq"), lax.axis_index("shard")
-        self.z, self.x = s // self.X, s % self.X
+        self.z, self.w = s // self.W, s % self.W
         self.y, self.c = k // 2, k % 2
-        self.j = self.x * 2 + self.c
+        self.j = self.w * 2 + self.c
 
     def move(self, a, target):
         pairs = []
         for z in range(self.Z):
-            for x in range(self.X):
+            for w in range(self.W):
                 for y in range(self.Y):
                     for c in range(2):
-                        to = target(z, x, y, c)
-                        if to is None:
+                        to = target(z, w, y, c)
+                        if to is None or not 0 <= to[0] < self.Z:
                             continue
-                        tz, tx, ty, tc = to
-                        if not 0 <= tz < self.Z:
-                            continue
-                        src = (z * self.X + x) * self.shard + y * 2 + c
-                        dst = (tz * self.X + tx % self.X) * self.shard + (ty % self.Y) * 2 + tc
+                        tz, tw, ty, tc = to
+                        src = (z * self.W + w) * self.shard + y * 2 + c
+                        dst = (tz * self.W + tw) * self.shard + (ty % self.Y) * 2 + tc
                         pairs.append((src, dst))
         return lax.ppermute(a, AXES, pairs)
 
-    def swap_core(self, a):
-        return self.move(a, lambda z, x, y, c: (z, x, y, 1 - c))
-
-    def shift_x(self, a, d):
-        return self.move(a, lambda z, x, y, c: (z, x + d, y, c))
+    def flip(self, a, d, e=0):
+        return self.move(a, lambda z, w, y, c: (z, w ^ d, y, c ^ e))
+
+    def bit(self, d, e):
+        return self.c if e else (self.w // d) % 2
+
+    def flip_core(self, a):
+        return self.flip(a, 0, 1)
 
     def shift_y(self, a, d):
-        return self.move(a, lambda z, x, y, c: (z, x, y + d, c))
+        return self.move(a, lambda z, w, y, c: (z, w, y + d, c))
 
     def shift_z(self, a, d):
-        return self.move(a, lambda z, x, y, c: (z + d, x, y, c))
-
-    def swap_z(self, a):
-        return self.move(a, lambda z, x, y, c: (z ^ 1, x, y, c))
+        return self.move(a, lambda z, w, y, c: (z + d, w, y, c))
 
     def by_core(self, own, other):
         first = self.c == 0
@@ -89,124 +87,102 @@
         return lax.slice_in_dim(a, i * size, (i + 1) * size, axis=axis)
 
 
-    def fetch_task(self, half, axis, out):
-        n, m = half.shape
-        shared = (n // 3 + 15) // 16 * 16
-        direct = n - 2 * shared
-        odd = self.z % 2
-        sent = yield [lax.dynamic_slice_in_dim(half, direct + odd * shared, shared, 0)]
-        got = yield [self.shift_y(sent[0], d) for d in range(1, self.Y)]
-        sent = yield [half[:direct]] + got
-        done = yield [self.shift_y(sent[0], d) for d in range(1, self.Y)] + [
-            self.swap_z(r) for r in sent[1:]
-        ]
-        pieces = [(half, None, (n, m), (0, 0))]
-        for d in range(1, self.Y):
-            at = (lambda r: (r, d * m)) if axis else (lambda r: (d * n + r, 0))
-            r, o = got[d - 1], done[self.Y - 2 + d]
-            pieces += [
-                (done[d - 1], None, (direct, m), at(0)),
-                (r, None, (shared, m), at(direct + odd * shared)),
-                (o, None, (shared, m), at(direct + (1 - odd) * shared)),
-            ]
-        shape = (n, m * self.Y) if axis else (n * self.Y, m)
-        out["w"] = assemble(pieces, shape)
-
-    def direct_task(self, half, shares, out):
+    def direct_task(self, half, shares, axis, out):
         n, m = half.shape
         edges = [n * sum(shares[:i]) // sum(shares) // 16 * 16 for i in range(len(shares) + 1)]
         pieces = [(half, None, (n, m), (0, 0))]
         for a, b in zip(edges[:-1], edges[1:]):
-            sent = yield [half[a:b]]
+            sent = yield [half[a:b] if len(shares) > 1 else half]
             got = yield [self.shift_y(sent[0], d) for d in range(1, self.Y)]
             for d, r in enumerate(got):
-                pieces.append((r, None, (b - a, m), ((d + 1) * n + a, 0)))
-        out["w"] = assemble(pieces, (n * self.Y, m))
+                at = (a, (d + 1) * m) if axis else ((d + 1) * n + a, 0)
+                pieces.append((r, None, (b - a, m), at))
+        out["w"] = assemble(pieces, (n, m * self.Y) if axis else (n * self.Y, m))
 
     def gather_task(self, a, last, out):
         rows, F = a.shape
-        length = self.X * rows + (0 if last is None else last.shape[0])
+        half = rows // 2
         sent = yield [a] + ([] if last is None else [last])
-        got = yield [self.shift_x(sent[0], d) for d in range(1, self.X)] + [
-            self.swap_core(sent[0])
-        ] + [
-            self.move(s, lambda z, x, y, c: (z + 1, t, y, c) if x == self.X - 1 else None)
+        got = yield [self.flip(sent[0], 1), self.flip(sent[0], 2)] + [
+            self.move(s, lambda z, w, y, c: (z + 1, t, y, c) if w == self.W - 1 else None)
             for s in sent[1:]
-            for t in range(self.X)
+            for t in range(2)
         ]
-        far = got[: self.X - 1]
-        send = list(far)
-        if last is not None:
-            send.append(sum(got[self.X + 1 :], got[self.X]))
-        if send:
-            sent = yield send
-            done = yield [self.swap_core(s) for s in sent]
-        pieces = []
-        for d in range(self.X):
-            at = (self.x - d) % self.X * rows
-            mine = a if d == 0 else sent[d - 1]
-            other = got[self.X - 1] if d == 0 else done[d - 1]
-            pieces.append((mine[None], None, (1, rows, F), (self.c, at, 0)))
-            pieces.append((other[None], None, (1, rows, F), (1 - self.c, at, 0)))
+        r1, r2 = got[:2]
+        n = 0
+        up, across = r1[:half], r2[half:]
         if last is not None:
             n = last.shape[0]
-            pieces.append((sent[-1][None], None, (1, n, F), (self.c, self.X * rows, 0)))
-            pieces.append((done[-1][None], None, (1, n, F), (1 - self.c, self.X * rows, 0)))
-        out["all"] = assemble(pieces, (2, length, F))
-
-    def y_task(self, send, own, out):
-        sent = yield send
-        got = yield [self.shift_y(p, -i - 1) for i, p in enumerate(sent)]
-        acc = own()
-        for r in got:
-            acc = acc + r.astype(f32)
-        out["q"] = acc.astype(bf16)
-
-    def sum_z(self, q):
-        groups = [[z * self.X + x for z in range(self.Z)] for x in range(self.X)]
-        return lax.psum(q, "seq", axis_index_groups=groups)
-
-    def spread_task(self, q, axis, out):
-        keep, send = self.by_core(self.cut(q, axis, 0, 2), self.cut(q, axis, 1, 2))
-        keep, send = yield [keep, send]
-        moves = [(d, e) for d in range(self.X) for e in range(2) if d or e]
-        got = yield [
-            self.move((keep, send)[e], lambda z, x, y, c: (z, x + d, y, c ^ e)) for d, e in moves
+            edge = got[2] + got[3]
+            up = jnp.concatenate([up, edge], axis=0)
+        sent = yield [up, across, jnp.stack([a, r1, r2])]
+        up, across, others = yield [
+            self.flip(sent[0], 2),
+            self.flip(sent[1], 1),
+            self.flip_core(sent[2]),
         ]
-        out["done"] = dict(zip(moves, got))
-        out["done"][0, 0] = keep
-
-    def scatter_task(self, a, out):
+        far = jnp.concatenate([up[:half], across], axis=0)
+        if last is not None:
+            edge = jnp.where(self.w < 2, edge, up[half:])
+            far = jnp.concatenate([far, edge], axis=0)
+        (far,) = yield [far]
+        (far_other,) = yield [self.flip_core(far)]
+        pieces = []
+        for i, (d, mine) in enumerate(((0, a), (1, r1), (2, r2))):
+            at = (self.w ^ d) * rows
+            pieces.append((mine[None], None, (1, rows, F), (self.c, at, 0)))
+            pieces.append((others, (i, 0, 0), (1, rows, F), (1 - self.c, at, 0)))
+        length = self.W * rows
+        for c, part in ((self.c, far[None]), (1 - self.c, far_other[None])):
+            pieces.append((part, (0, 0, 0), (1, rows, F), (c, (self.w ^ 3) * rows, 0)))
+            if n:
+                pieces.append((part, (0, rows, 0), (1, n, F), (c, length, 0)))
+        out["all"] = assemble(pieces, (2, length + n, F))
+
+    def scatter_task(self, a, order, out):
         keep, send = self.by_core(a[0], a[1])
         sent = yield [send]
-        got = yield [self.swap_core(sent[0])]
+        got = yield [self.flip(sent[0], 0, 1)]
         total = (keep.astype(f32) + got[0].astype(f32)).astype(bf16)
-        parts = [
-            lax.dynamic_index_in_dim(total, (self.x + d) % self.X, 0, False) for d in range(self.X)
-        ]
-        sent = yield parts[1:]
-        got = yield [self.shift_x(p, d + 1) for d, p in enumerate(sent)]
-        acc = parts[0].astype(f32)
-        for r in got:
-            acc = acc + r.astype(f32)
-        out["sum"] = acc
-
-    def gradient_task(self, send, own_part, axis, out):
+
+        def part(d):
+            return lax.dynamic_index_in_dim(total, self.w ^ d, 0, False)
+
+        d1, d2 = order
+        sent = yield [jnp.stack([part(d1), part(3)])]
+        got = yield [self.flip(sent[0], d1)]
+        mine = part(0).astype(f32) + got[0][0].astype(f32)
+        pass_on = (part(d2).astype(f32) + got[0][1].astype(f32)).astype(bf16)
+        sent = yield [pass_on]
+        got = yield [self.flip(sent[0], d2)]
+        out["sum"] = mine + got[0].astype(f32)
+
+    def gradient_task(self, send, own_part, axis, order, out):
         half = self.Z // 2
+        over_group = order is None
+        halvings = [(0, 1), (1, 0), (2, 0)]
         sent = yield send
         got = yield [self.shift_y(p, -i - 1) for i, p in enumerate(sent)]
         acc = own_part()
         for r in got:
             acc = acc + r.astype(f32)
         q = acc.astype(bf16)
+        if over_group:
+            for d, e in halvings:
+                n = q.shape[0] // 2
+                b = self.bit(d, e)
+                keep = lax.dynamic_slice_in_dim(q, b * n, n, 0)
+                (send,) = yield [lax.dynamic_slice_in_dim(q, (1 - b) * n, n, 0)]
+                (got,) = yield [self.flip(send, d, e)]
+                q = (keep.astype(f32) + got.astype(f32)).astype(bf16)
         for step in range(half - 1):
             (q,) = yield [q]
             got = yield [
                 self.move(
                     q,
-                    lambda z, x, y, c: (z + 1, x, y, c)
+                    lambda z, w, y, c: (z + 1, w, y, c)
                     if z == step
-                    else ((z - 1, x, y, c) if z == self.Z - 1 - step else None),
+                    else ((z - 1, w, y, c) if z == self.Z - 1 - step else None),
                 )
             ]
             q = (q.astype(f32) + got[0].astype(f32)).astype(bf16)
@@ -214,9 +190,9 @@
         got = yield [
             self.move(
                 q,
-                lambda z, x, y, c: (z + 1, x, y, c)
+                lambda z, w, y, c: (z + 1, w, y, c)
                 if z == half - 1
-                else ((z - 1, x, y, c) if z == half else None),
+                else ((z - 1, w, y, c) if z == half else None),
             )
         ]
         q = (q.astype(f32) + got[0].astype(f32)).astype(bf16)
@@ -226,20 +202,37 @@
             got = yield [
                 self.move(
                     q,
-                    lambda z, x, y, c: (z - 1, x, y, c)
+                    lambda z, w, y, c: (z - 1, w, y, c)
                     if z == a
-                    else ((z + 1, x, y, c) if z == b else None),
+                    else ((z + 1, w, y, c) if z == b else None),
                 )
             ]
             q = jnp.where((self.z == a - 1) | (self.z == b + 1), got[0], q)
+        if over_group:
+            for d, e in reversed(halvings):
+                (q,) = yield [q]
+                if e:
+                    keep, send = self.by_core(self.cut(q, 1, 0, 2), self.cut(q, 1, 1, 2))
+                    (got,) = yield [self.flip(send, d, e)]
+                    q = keep
+                else:
+                    (got,) = yield [self.flip(q, d, e)]
+                low = self.bit(d, e) == 0
+                q = jnp.concatenate([jnp.where(low, q, got), jnp.where(low, got, q)], axis=0)
+            out["done"] = q
+            return
         keep, send = self.by_core(self.cut(q, axis, 0, 2), self.cut(q, axis, 1, 2))
-        keep, send = yield [keep, send]
-        moves = [(d, e) for d in range(self.X) for e in range(2) if d or e]
-        got = yield [
-            self.move((keep, send)[e], lambda z, x, y, c: (z, x + d, y, c ^ e)) for d, e in moves
-        ]
-        out["done"] = dict(zip(moves, got))
-        out["done"][0, 0] = keep
+        (send,) = yield [send]
+        got = yield [self.flip(send, 0, 1)]
+        pair = jnp.concatenate([keep, got[0]], axis=1 - axis)
+        (pair,) = yield [pair]
+        got = yield [self.flip(pair, order[0])]
+        quad = jnp.concatenate([pair, got[0]], axis=1 - axis)
+        (quad,) = yield [quad]
+        got = yield [self.flip(quad, order[1])]
+        out["done"] = [quad, got[0]]
+        a, b = order
+        out["from"] = [(0, 0), (0, 1), (a, 0), (a, 1), (b, 0), (b, 1), (a ^ b, 0), (a ^ b, 1)]
 
     def state_task(self, cur, cc, spread, direction, out):
         d = 1
@@ -255,57 +248,14 @@
         got = yield [self.shift_z(sent[0], direction)]
         out["state"] = got[0].astype(f32)
 
-    def small_task(self, v, over_tp, out):
-        def turn_z(a, d):
-            return self.move(a, lambda z, x, y, c: ((z + d) % self.Z, x, y, c))
-
-        def turn_group(a, d):
-            dx, dc = d // 2, d % 2
-            return self.move(a, lambda z, x, y, c: (z, x + dx, y, c ^ dc))
-
-        def from_group(d):
-            return ((self.x - d // 2) % self.X) * 2 + (self.c ^ (d % 2))
-
-        rounds = [
-            (self.Z, lambda d: (self.z - d) % self.Z, turn_z),
-            (self.Y, lambda d: (self.y - d) % self.Y, self.shift_y),
-            (self.TP, from_group, turn_group),
-        ]
-        for i, (n, source, shift) in enumerate(rounds):
-            sent = yield [v]
-            got = yield [shift(sent[0], d) for d in range(1, n)]
-            buf = jnp.zeros((n,) + v.shape, v.dtype)
-            for d, r in enumerate([v] + got):
-                buf = lax.dynamic_update_index_in_dim(buf, r, source(d), 0)
-            v = jnp.sum(buf, axis=0) if i < 2 else buf
-        out["sum"] = jnp.sum(v, axis=0) if over_tp else v
-
     def sum_tp_task(self, a, out):
-        moves = [(dx, dc) for dx in range(self.X) for dc in range(2) if dx or dc]
         sent = yield [a]
-        got = yield [
-            self.move(sent[0], lambda z, x, y, c: (z, x + dx, y, c ^ dc)) for dx, dc in moves
-        ]
-        total = a
+        got = yield [self.flip_core(sent[0])]
+        (a,) = yield [a + got[0]]
+        got = yield [self.flip(a, d) for d in range(1, self.W)]
         for r in got:
-            total = total + r
-        out["sum"] = total
-
-    def chunks_task(self, both, SW, out):
-        moves = [(dx, dc) for dx in range(self.X) for dc in range(2)]
-        parts = []
-        for dx, dc in moves:
-            jj = (self.x + dx) % self.X * 2 + (self.c ^ dc)
-            parts.append(lax.dynamic_slice_in_dim(both, SW * jj, SW, 2))
-        sent = yield parts[1:]
-        got = yield [
-            self.move(p, lambda z, x, y, c: (z, x + dx, y, c ^ dc))
-            for p, (dx, dc) in zip(sent, moves[1:])
-        ]
-        total = parts[0].astype(f32)
-        for r in got:
-            total = total + r.astype(f32)
-        out["sum"] = total
+            a = a + r
+        out["sum"] = a
 
     def one_task(self, arrays, send, out):
         sent = yield arrays
@@ -324,11 +274,11 @@
     def add(self, task, *args):
         out = {}
         gen = task(*args, out)
-        self.tasks.append([gen, next(gen), None])
+        self.tasks.append([gen, next(gen), None, out])
         return out
 
-    def settle(self, live):
-        flying = [t for t in self.tasks if t[2] is not None]
+    def settle(self, live, leave=()):
+        flying = [t for t in self.tasks if t[2] is not None and not any(t[3] is o for o in leave)]
         got, live = fence(([t[2] for t in flying], live))
         for t, r in zip(flying, got):
             t[2] = None
@@ -339,22 +289,15 @@
         return live
 
     def launch(self, live):
-        ready, live = fence(([t[1] for t in self.tasks], live))
-        for t, a in zip(self.tasks, ready):
+        waiting = [t for t in self.tasks if t[2] is None]
+        ready, live = fence(([t[1] for t in waiting], live))
+        for t, a in zip(waiting, ready):
             t[2] = t[0].send(a)
         return live
 
-    def tick(self, live):
-        return self.launch(self.settle(live))
-
 
 def low_dot(a, b, dims):
     return lax.dot_general(a.astype(bf16), b.astype(bf16), dims, preferred_element_type=f32)
-
-
-def silu_slope(v):
-    g = jax.nn.sigmoid(v)
-    return g * (1.0 + v * (1.0 - g))
 
 
 NT = (((1,), (1,)), ((), ()))
@@ -574,9 +517,13 @@
         gain_out[...] += part
 
 
-def input_grad_body(gg, xb, tb, wg, wx, wt, out):
+def input_grad_body(gg, xb, tb, wg, wx, wt, spill, rows, out, gain_out):
     total = bdot(gg[...], wg[...], NN) + bdot(xb[...], wx[...], NN) + bdot(tb[...], wt[...], NN)
-    out[...] = total.astype(bf16)
+    T = out.shape[1]
+    out[0, : T - HALO, :] = total[: T - HALO].astype(bf16)
+    out[0, T - HALO :, :] = (total[T - HALO : T] + spill[0].astype(f32)).astype(bf16)
+    part = jnp.sum(total * rows[...].astype(f32), axis=0, keepdims=True)
+    gain_out[0] = jnp.concatenate([part, jnp.zeros((7, part.shape[1]), f32)], axis=0)
 
 
 def intra_backward_body(
@@ -647,65 +594,69 @@
 
 
 def finish_body(
-    nb, pk, x, do, dxl, bc, leave, enter, cum, step, dec, dt, sel, hp, marks, kern, bias,
-    back_out, kg_out, sm_out, raw_out, dk_out, v_scr, m_scr,
+    nb, pk, x, do, dxl, bc, dbc, leave, enter, cum, step, dec, dt, sel, hp, marks, kern, bias,
+    back_out, dt_out, kg_out, sm_out, v_scr, m_scr, grad, dk,
 ):
     T = nb * BLOCK
     n = bc.shape[1] // 2
     g_id = pl.program_id(1)
+    last = pl.num_programs(1) - 1
+
+    @pl.when(g_id == 0)
+    def _():
+        dk[...] = jnp.zeros_like(dk)
+        dt_out[0] = jnp.zeros((T + HALO, 128), bf16)
+
+    @pl.when(g_id < last)
+    def _():
+        rate = hp[0, 1:2, :]
+        skip = wide(hp[0, 2:3, :])
+        strict = triangle(strict_lower=True)
+        sums = [0.0, 0.0, 0.0]
+        for b in range(nb):
+            rows = slice(b * BLOCK, (b + 1) * BLOCK)
+            c = cum[0, 0, rows, :]
+            st = step[0, 0, rows, :]
+            end = c[BLOCK - 1 :, :]
+            tail = wide(jnp.exp(end - c) * marks[0, rows, 3:4])
+            stw = wide(st)
+            lv = leave[0, b]
+            kl = bdot(bc[rows, :n], lv, NN) * tail
+            dxs = dxl[rows, :].astype(f32) + kl
+            dof = do[rows, :].astype(f32)
+            xf = x[rows, :].astype(f32)
+            xs = xf * stw
+            grad[rows, :] = skip * dof + stw * dxs
+            out4 = head_sum(xs * kl)
+            direct = head_sum(xf * dxs)
+            sums[2] = sums[2] + jnp.sum(head_sum(dof * xf), axis=0, keepdims=True)
+            dk[rows, :] += bdot(xs * tail, lv, NT)
+            both = jnp.sum(enter[0, b].astype(f32) * lv.astype(f32), axis=0, keepdims=True)
+            both = jnp.concatenate([both, jnp.zeros((15, LANES), f32)], axis=0)
+            through = head_sum(both)[:1] * jnp.exp(end) * marks[0, b * BLOCK : b * BLOCK + 1, 5:6]
+            decay = dec[0, 0, rows, :] + fdot(strict, out4, NN) + through
+            sums[1] = sums[1] - rate * jnp.sum(st * decay, axis=0, keepdims=True)
+            raw = bdot(dt[0, rows, :], sel[0], NN)[:, :GH] + hp[0, 0:1, :]
+            rg = (direct - rate * decay) * sigmoid(raw)
+            sums[0] = sums[0] + jnp.sum(rg, axis=0, keepdims=True)
+            padded = jnp.concatenate([rg, jnp.zeros((BLOCK, 128 - GH), f32)], axis=1)
+            spot = bdot(padded, sel[0], NT)
+            dt_out[0, rows, :] = (dt_out[0, rows, :].astype(f32) + spot).astype(bf16)
+        sm_out[0, 0] = jnp.concatenate(sums + [jnp.zeros((5, GH), f32)], axis=0)
+
+    @pl.when(g_id == last)
+    def _():
+        grad[...] = jnp.concatenate([dbc[:, :n] + dk[...], dbc[:, n:]], axis=1)
+
     v_scr[:HALO, :] = pk[0, T:, :].astype(f32)
     v_scr[HALO:, :] = pk[0, :T, :].astype(f32)
     pre = bias[...] + kern[0:1, :] * v_scr[HALO : HALO + T, :]
     for k in range(1, 4):
         pre = pre + kern[k : k + 1, :] * (v_scr[HALO - k : HALO - k + T, :] * marks[0, :, k - 1 : k])
     sg = sigmoid(pre)
-    slope = sg * (1.0 + pre * (1.0 - sg))
-    raw = bdot(dt[0, :T, :], sel[0], NN)[:, :GH] + hp[0, 0:1, :]
-    rate = hp[0, 1:2, :]
-    skip = wide(hp[0, 2:3, :])
-    strict = triangle(strict_lower=True)
-    sums = [0.0, 0.0, 0.0]
+    cg = grad[...] * (sg * (1.0 + pre * (1.0 - sg)))
     m_scr[:HALO, :] = jnp.zeros((HALO, LANES), f32)
     m_scr[HALO + T :, :] = jnp.zeros((HALO, LANES), f32)
-    grads = []
-    for b in range(nb):
-        rows = slice(b * BLOCK, (b + 1) * BLOCK)
-        c = cum[0, 0, rows, :]
-        st = step[0, 0, rows, :]
-        end = c[BLOCK - 1 :, :]
-        tail = wide(jnp.exp(end - c) * marks[0, rows, 3:4])
-        stw = wide(st)
-        keys = bc[rows, :n]
-        lv = leave[0, b]
-        kl = bdot(keys, lv, NN) * tail
-        dxs = dxl[rows, :].astype(f32) + kl
-        dof = do[rows, :].astype(f32)
-        xf = x[rows, :].astype(f32)
-        xs = xf * stw
-        grads.append(skip * dof + stw * dxs)
-        out4 = head_sum(xs * kl)
-        direct = head_sum(xf * dxs)
-        sums[2] = sums[2] + jnp.sum(head_sum(dof * xf), axis=0, keepdims=True)
-        dk = bdot(xs * tail, lv, NT)
-
-        @pl.when(g_id == 0)
-        def _(dk=dk, rows=rows):
-            dk_out[rows, :] = dk
-
-        @pl.when(g_id > 0)
-        def _(dk=dk, rows=rows):
-            dk_out[rows, :] += dk
-
-        both = jnp.sum(enter[0, b].astype(f32) * lv.astype(f32), axis=0, keepdims=True)
-        both = jnp.concatenate([both, jnp.zeros((15, LANES), f32)], axis=0)
-        through = head_sum(both)[:1] * jnp.exp(end) * marks[0, b * BLOCK : b * BLOCK + 1, 5:6]
-        decay = dec[0, 0, rows, :] + fdot(strict, out4, NN) + through
-        sums[1] = sums[1] - rate * jnp.sum(st * decay, axis=0, keepdims=True)
-        rg = (direct - rate * decay) * sigmoid(raw[rows])
-        sums[0] = sums[0] + jnp.sum(rg, axis=0, keepdims=True)
-        raw_out[0, 0, rows, :] = rg
-    cg = jnp.concatenate(grads, axis=0) * slope
-    sm_out[0, 0] = jnp.concatenate(sums + [jnp.zeros((5, GH), f32)], axis=0)
     kgs = []
     back = None
     for k in range(4):
@@ -770,7 +721,7 @@
     return pl.pallas_call(
         kernel,
         in_specs=[pl.BlockSpec(memory_space=pltpu.SMEM)]
-        + [pl.BlockSpec(memory_space=pl.ANY)] * len(arrays),
+        + [pl.BlockSpec(memory_space=pltpu.HBM)] * len(arrays),
         out_specs=pl.BlockSpec(memory_space=pl.ANY),
         out_shape=jax.ShapeDtypeStruct(shape, arrays[0].dtype),
         scratch_shapes=[pltpu.VMEM(p[2], p[0].dtype) for p in pieces]
@@ -848,31 +799,32 @@
     hd = inner // heads
     HL = heads // g.TP
     HW = HL * hd
-    SW = shared // g.TP
     CW = HW + shared
     own_len = tokens.shape[1]
     width = tokens.shape[2]
     own_d = in_weight.shape[0]
-    T = own_len * g.X
+    T = own_len * g.W
     TE = T + HALO
     nb = T // BLOCK
     NB = 2 * nb
     G = HW // LANES
     KW = HW + shared + 128
     j = g.j
-    other_j = g.x * 2 + 1 - g.c
+    other_j = g.w * 2 + 1 - g.c
 
     w_t = in_weight.T
+    n_rest = KW - HW
     rest = jnp.pad(w_t[2 * inner :], ((0, KW - CW - heads), (0, 0)))
-    far = g.swap_core(lax.dynamic_slice_in_dim(w_t, inner + HW * other_j, HW, 0))
-    far_rest = g.swap_core(rest)
-    n_rest = KW - HW
+
+    def with_rest(jj):
+        return jnp.concatenate([lax.dynamic_slice_in_dim(w_t, inner + HW * jj, HW, 0), rest], axis=0)
+
+    far = g.flip_core(with_rest(other_j))
     half_packed = assemble(
         [
             (w_t, (inner + HW * j, 0), (HW, own_d), (0, g.c * own_d)),
             (rest, None, (n_rest, own_d), (HW, g.c * own_d)),
-            (far, None, (HW, own_d), (0, (1 - g.c) * own_d)),
-            (far_rest, None, (n_rest, own_d), (HW, (1 - g.c) * own_d)),
+            (far, None, (KW, own_d), (0, (1 - g.c) * own_d)),
         ],
         (KW, 2 * own_d),
     )
@@ -883,28 +835,36 @@
 
     stages = Stages()
     at_n = stages.add(g.gather_task, normed, normed[own_len - HALO :])
-    at_packed = stages.add(g.fetch_task, half_packed, 1)
+    at_packed = stages.add(g.direct_task, half_packed, [9, 5], 1)
     in_weight, out_weight, cotangent = stages.launch([in_weight, out_weight, cotangent])
     w_t = in_weight.T
-    far_gate = g.swap_core(lax.dynamic_slice_in_dim(w_t, HW * other_j, HW, 0))
-    far_out = g.swap_core(lax.dynamic_slice_in_dim(out_weight, HW * other_j, HW, 1))
-    at_cot = stages.add(g.gather_task, g.own_first(cotangent[0]), None)
+    cot_own = g.own_first(cotangent[0])
+    near_gate = lax.dynamic_slice_in_dim(w_t, HW * j, HW, 0)
+    far_gate = lax.dynamic_slice_in_dim(w_t, HW * other_j, HW, 0)
+    near_out = lax.dynamic_slice_in_dim(out_weight, HW * j, HW, 1)
+    far_out = lax.dynamic_slice_in_dim(out_weight, HW * other_j, HW, 1)
+    at_seg = stages.add(g.one_task, [segments], g.flip_core)
+    at_far = stages.add(g.one_task, [far_gate, far_out], g.flip_core)
+    stages.settle([])
+    stages.launch([])
+    stages.settle([], leave=[at_n, at_packed])
+    far_gate, far_out = at_far["got"]
     half_gate = assemble(
         [
-            (w_t, (HW * j, 0), (HW, own_d), (0, g.c * own_d)),
+            (near_gate, None, (HW, own_d), (0, g.c * own_d)),
             (far_gate, None, (HW, own_d), (0, (1 - g.c) * own_d)),
         ],
         (HW, 2 * own_d),
     )
     half_out = assemble(
         [
-            (out_weight, (0, HW * j), (own_d, HW), (g.c * own_d, 0)),
+            (near_out, None, (own_d, HW), (g.c * own_d, 0)),
             (far_out, None, (own_d, HW), ((1 - g.c) * own_d, 0)),
         ],
         (2 * own_d, HW),
     )
 
-    s_lo, s_hi = g.by_core(segments, g.swap_core(segments))
+    s_lo, s_hi = g.by_core(segments, at_seg["got"][0])
     seg_all = jnp.concatenate([s_lo, s_hi], axis=0)
     seg_pad = jnp.concatenate([jnp.full((2, HALO), -1, jnp.int32), seg_all], axis=1)
     seg_ext = lax.dynamic_slice_in_dim(seg_pad, g.z * T, T + HALO, 1)
@@ -947,18 +907,17 @@
         [((2, T, 8), f32, (1, T, 8), lambda s: (s, 0, 0))],
         name="turn",
     )
-    held = stages.settle([half_gate, half_out, marks, flags, kernel_own, bias_own, hp, sel, gain_own])
-    half_gate, half_out, marks, flags, kernel_own, bias_own, hp, sel, gain_own = held
+    held = [half_gate, half_out, cot_own, marks, flags, kernel_own, bias_own, hp, sel, gain_own]
+    held = stages.settle(held)
+    half_gate, half_out, cot_own, marks, flags, kernel_own, bias_own, hp, sel, gain_own = held
+    at_gate = stages.add(g.direct_task, half_gate, [1], 1)
+    at_cot = stages.add(g.gather_task, cot_own, None)
     stages.launch([])
-    half_gate, half_out = stages.settle([half_gate, half_out])
+    stages.settle([], leave=[at_gate, at_cot])
     n_ext = at_n["all"].reshape(2 * TE, width)
     w_packed = at_packed["w"]
-    at_gate = stages.add(g.fetch_task, half_gate, 1)
-    n_ext, w_packed, half_out = stages.launch([n_ext, w_packed, half_out])
-
     packed = low_dot(n_ext, w_packed, NT).astype(bf16)
-    (packed,) = stages.settle([packed])
-    at_out = stages.add(g.direct_task, half_out, [4, 6, 6])
+    (packed,) = stages.settle([packed], leave=[at_gate])
     (packed,) = stages.launch([packed])
     packed = packed.reshape(2, TE, KW)
     marks_b = marks.reshape(NB, BLOCK, 8)
@@ -1010,6 +969,7 @@
     for b in range(1, nb):
         s_range = s_block[:, b] + carry_wide[:, b] * s_range
     s_range, x, bc, cum, row, step = stages.settle([s_range, x, bc, cum, row, step])
+    at_out = stages.add(g.direct_task, half_out, [1], 0)
     at_enter = stages.add(g.state_task, s_range, carry_range, spread, 1)
     x, bc, cum, row, step = stages.launch([x, bc, cum, row, step])
 
@@ -1053,12 +1013,10 @@
         flops=pair_flops * 8,
         name="intra_forward",
     )
-    (y_local,) = stages.settle([y_local])
     w_gate = at_gate["w"]
-    n_ext, w_gate = stages.launch([n_ext, w_gate])
     gate = low_dot(n_ext, w_gate, NT).astype(bf16)
-    (gate,) = stages.settle([gate])
-    while "state" not in at_enter or "w" not in at_out:
+    y_local, gate = stages.settle([y_local, gate])
+    while "state" not in at_enter or "w" not in at_out or "all" not in at_cot:
         stages.launch([])
         stages.settle([])
     enter = [at_enter["state"]]
@@ -1108,8 +1066,9 @@
         name="join",
     )
     at_sums = stages.add(g.sum_tp_task, sums)
-    stages.launch([])
-    stages.settle([])
+    while "sum" not in at_sums:
+        stages.launch([])
+        stages.settle([])
 
     def turn(spec):
         a, block, at = spec
@@ -1156,8 +1115,13 @@
     for b in range(nb - 2, -1, -1):
         d_range = de_block[:, b] + carry_wide[:, b] * d_range
     at_leave = stages.add(g.state_task, d_range, carry_range, spread, -1)
-    at_outy = stages.add(g.y_task, far_rows(out_part, g.Y), lambda: out_part(0))
+    at_outs = stages.add(
+        g.gradient_task, far_rows(out_part, g.Y), lambda: out_part(0), 0, (2, 1)
+    )
     x, d_out, normed_out, gate_grad = stages.launch([x, d_out, normed_out, gate_grad])
+    branch = low_dot(normed_out, w_out, NT).astype(bf16)
+    at_branch = stages.add(g.scatter_task, branch.reshape(2, g.W, own_len, width), (1, 2))
+    x, d_out = stages.launch([x, d_out])
     dxs, dec, dbc = call(
         intra_backward_body,
         (NB, G),
@@ -1186,14 +1150,10 @@
         name="intra_backward",
     )
     gate_far = far_rows(lambda i: in_part(gate_grad, i), g.Y)
-    dxs, gate_far, normed_out = stages.settle([dxs, gate_far, normed_out])
-    out_sum = g.sum_z(at_outy["q"])
-    at_gatey = stages.add(g.y_task, gate_far, lambda: in_part(gate_grad, 0))
-    dxs, normed_out, gate_grad = stages.launch([dxs, normed_out, gate_grad])
-    branch = low_dot(normed_out, w_out, NT).astype(bf16)
-    dxs, branch = stages.settle([dxs, branch])
-    gate_sum = g.sum_z(at_gatey["q"])
-    at_branch = stages.add(g.scatter_task, branch.reshape(2, g.X, own_len, width))
+    dxs, gate_far = stages.settle([dxs, gate_far])
+    at_gates = stages.add(
+        g.gradient_task, gate_far, lambda: in_part(gate_grad, 0), 1, (2, 1)
+    )
     while "state" not in at_leave:
         stages.launch([])
         stages.settle([])
@@ -1203,216 +1163,195 @@
     leave = jnp.stack(leave, axis=1).astype(bf16)
     leave, dxs = stages.launch([leave, dxs])
 
-    x_back, kg, sm, raw_grad, d_keys = call(
+    def held(s, k):
+        return s, jnp.minimum(k, G - 1)
+
+    def late_tile(a):
+        return (a, (T, LANES), lambda s, k: held(s, k))
+
+    def late_small(a):
+        return (a, (1, 1, T, GH), lambda s, k: (*held(s, k), 0, 0))
+
+    def late_state(a):
+        return (a, (1, nb, state, LANES), lambda s, k: (s, 0, 0, jnp.minimum(k, G - 1)))
+
+    x_back, dt_back, kg, sm = call(
         partial(finish_body, nb),
-        (2, G),
+        (2, G + 1),
         [
             (packed, (1, TE, LANES), lambda s, k: (s, 0, k)),
-            seq_tile(x),
-            seq_tile(d_out),
-            seq_tile(dxs),
+            late_tile(x),
+            late_tile(d_out),
+            late_tile(dxs),
             bc_seq,
-            seq_state(leave),
-            seq_state(enter),
-            seq_small(cum),
-            seq_small(step),
-            seq_small(dec),
+            (dbc, (T, shared), lambda s, k: (s, 0)),
+            late_state(leave),
+            late_state(enter),
+            late_small(cum),
+            late_small(step),
+            late_small(dec),
             (packed, (1, TE, 128), lambda s, k: (s, 0, dt_block)),
-            (sel, (1, 128, 128), lambda s, k: (k, 0, 0)),
-            (hp, (1, 8, GH), lambda s, k: (k, 0, 0)),
+            (sel, (1, 128, 128), lambda s, k: (jnp.minimum(k, G - 1), 0, 0)),
+            (hp, (1, 8, GH), lambda s, k: (jnp.minimum(k, G - 1), 0, 0)),
             seq_whole(marks),
             lane_tile(kernel_own),
             lane_tile(bias_own),
         ],
         [
-            ((2, TE, HW), bf16, (1, TE, LANES), lambda s, k: (s, 0, k)),
-            ((2, 8, HW), f32, (1, 8, LANES), lambda s, k: (s, 0, k)),
-            ((2, G, 8, GH), f32, (1, 1, 8, GH), lambda s, k: (s, k, 0, 0)),
-            ((2, G, T, GH), f32, (1, 1, T, GH), lambda s, k: (s, k, 0, 0)),
-            ((2 * T, state), f32, (T, state), lambda s, k: (s, 0)),
-        ],
-        [pltpu.VMEM((TE, LANES), f32), pltpu.VMEM((HALO + TE, LANES), f32)],
+            ((2, TE, CW), bf16, (1, TE, LANES), lambda s, k: (s, 0, k)),
+            ((2, TE, 128), bf16, (1, TE, 128), lambda s, k: (s, 0, 0)),
+            ((2, 8, CW), f32, (1, 8, LANES), lambda s, k: (s, 0, k)),
+            ((2, G, 8, GH), f32, (1, 1, 8, GH), lambda s, k: (*held(s, k), 0, 0)),
+        ],
+        [
+            pltpu.VMEM((TE, LANES), f32),
+            pltpu.VMEM((HALO + TE, LANES), f32),
+            pltpu.VMEM((T, LANES), f32),
+            pltpu.VMEM((T, state), f32),
+        ],
         flops=pair_flops * 16,
         name="finish",
     )
-    x_back = x_back.reshape(2 * TE, HW)
-    cols = min(HW, 512)
-    NC = HW // cols
-
-    def x_cut(k):
-        return lax.slice_in_dim(x_back, k * cols, (k + 1) * cols, axis=1)
-
-    def x_task(k):
-        return (
-            g.gradient_task,
-            far_rows(lambda i: in_part(x_cut(k), i), g.Y),
-            lambda: in_part(x_cut(k), 0),
-            1,
-        )
-
-    kg = jnp.sum(kg, axis=0)
-    x_kg, x_bg = kg[:taps], kg[taps]
-    sm = jnp.sum(sm, axis=0)[:, :3].transpose(1, 0, 2).reshape(3, HL)
-
-    both = jnp.concatenate([dbc[:, :state] + d_keys, dbc[:, state:]], axis=-1)
-    both = both.astype(bf16).reshape(2, T, shared)
-    task = x_task(0)
-    task, both, x_back = stages.settle([task[1], both, x_back])
-    task = (g.gradient_task, task, lambda: in_part(x_cut(0), 0), 1)
-    at_xs = [stages.add(*task)]
-    at_both = stages.add(g.chunks_task, both, SW)
-    x_back, raw_grad = stages.launch([x_back, raw_grad])
-    later = [x_task(k) for k in range(1, NC)]
-    later_far, raw_grad = stages.settle([[t[1] for t in later], raw_grad])
-    for k in range(1, NC):
-        at_xs.append(
-            stages.add(g.gradient_task, later_far[k - 1], lambda k=k: in_part(x_cut(k), 0), 1)
-        )
-    (raw_grad,) = stages.launch([raw_grad])
-    both_sum = at_both["sum"]
-
-    def own_shared(a):
-        return lax.dynamic_slice_in_dim(a, HW + SW * j, SW, a.ndim - 1)
-
-    sh_in = own_shared(packed).astype(f32)
-    sh_in = jnp.concatenate([sh_in[:, T:], sh_in[:, :T]], axis=1)
-    sh_kernel = own_shared(kernel_own)
-    sh_pre = own_shared(bias_own)[None]
-    same = [None] + [marks[:, :, k - 1 : k] for k in range(1, taps)]
-    moved = [sh_in[:, HALO - k : HALO - k + T] for k in range(taps)]
-    for k in range(taps):
-        moved[k] = moved[k] if k == 0 else moved[k] * same[k]
-        sh_pre = sh_pre + sh_kernel[k] * moved[k]
-    cg = both_sum * silu_slope(sh_pre)
-    s_back = 0.0
-    s_kg = []
-    for k in range(taps):
-        m = cg if k == 0 else cg * same[k]
-        s_kg.append(jnp.sum(cg * moved[k], axis=(0, 1)))
-        s_back = s_back + jnp.pad(sh_kernel[k] * m, ((0, 0), (HALO - k, k), (0, 0)))
-    s_kg, s_bg = jnp.stack(s_kg), jnp.sum(cg, axis=(0, 1))
-    s_back = jnp.concatenate([s_back[:, HALO:], s_back[:, :HALO]], axis=1)
-    raw_low = raw_grad.transpose(0, 2, 1, 3).reshape(2, T, HL)
-    raw_low = jnp.pad(raw_low, ((0, 0), (0, HALO), (0, 0)))
-    tail_w = SW + HL
-    pad_w = 128 - tail_w
-    tail_back = jnp.concatenate([s_back, raw_low, jnp.zeros((2, TE, pad_w), f32)], axis=-1)
-    tail_back = tail_back.astype(bf16).reshape(2 * TE, 128)
-    tail_cut = tail_back[:, :tail_w]
-    w_tail = jnp.concatenate(
-        [
-            lax.dynamic_slice_in_dim(w_packed, HW + SW * j, SW, 0),
-            lax.dynamic_slice_in_dim(w_packed, CW + HL * j, HL, 0),
-            jnp.zeros((pad_w, width), bf16),
-        ],
-        axis=0,
-    )
-    k_all = jnp.concatenate([x_kg, s_kg], axis=1)
-    b_all = jnp.concatenate([x_bg, s_bg])
-    small = jnp.concatenate([gain_grad.reshape(-1), k_all.reshape(-1), b_all, sm.reshape(-1)])
-    n_small = small.shape[0]
-    small = jnp.pad(small, (0, -n_small % 1024)).reshape(-1, 128)
-    tail_far = far_rows(lambda i: in_part(tail_cut, i), g.Y)
-    tail_far, small = stages.settle([tail_far, small])
-    at_tail = stages.add(g.gradient_task, tail_far, lambda: in_part(tail_cut, 0), 1)
-    at_small = stages.add(g.small_task, small, False)
-    x_back, tail_back, gate_grad = stages.launch([x_back, tail_back, gate_grad])
+    edge = jnp.concatenate([x_back[:, T:], dt_back[:, T:]], axis=-1).reshape(2 * HALO, KW)
+    spill = low_dot(edge, w_packed, NN).astype(bf16).reshape(2, HALO, width)
+    x_flat = x_back.reshape(2 * TE, CW)
+    dt_flat = dt_back.reshape(2 * TE, 128)
+
+    def x_part(i):
+        return in_part(x_flat[:, :HW], i)
+
+    x_far = far_rows(x_part, g.Y)
+    x_far, spill, x_flat, dt_flat, kg, sm = stages.settle([x_far, spill, x_flat, dt_flat, kg, sm])
+    at_x = stages.add(g.gradient_task, x_far, lambda: x_part(0), 1, (2, 1))
+    at_spill = stages.add(g.one_task, [spill], lambda a: g.shift_z(a, -1))
+    x_flat, dt_flat = stages.launch([x_flat, dt_flat])
+    rest_back = jnp.concatenate([x_flat[:, HW:], dt_flat[:, :heads]], axis=1)
+    rest = [in_part(rest_back, i) for i in range(g.Y)]
+    (rest,) = stages.settle([rest], leave=[at_gates, at_x, at_branch])
+    spill = at_spill["got"][0]
+    spill, gate_grad, x_flat, dt_flat = stages.launch([spill, gate_grad, x_flat, dt_flat])
 
     NW = 512
-    (n_grad,) = call(
+    n_grad, pre_grad = call(
         input_grad_body,
-        (width // NW,),
-        [
-            (gate_grad, (2 * TE, HW), lambda n: (0, 0)),
-            (x_back, (2 * TE, HW), lambda n: (0, 0)),
-            (tail_back, (2 * TE, 128), lambda n: (0, 0)),
-            (w_gate, (HW, NW), lambda n: (0, n)),
-            (w_packed, (HW, NW), lambda n: (0, n)),
-            (w_tail, (128, NW), lambda n: (0, n)),
-        ],
-        [((2 * TE, width), bf16, (2 * TE, NW), lambda n: (0, n))],
+        (2, width // NW),
+        [
+            (gate_grad, (TE, HW), lambda s, n: (s, 0)),
+            (x_flat, (TE, CW), lambda s, n: (s, 0)),
+            (dt_flat, (TE, 128), lambda s, n: (s, 0)),
+            (w_gate, (HW, NW), lambda s, n: (0, n)),
+            (w_packed, (CW, NW), lambda s, n: (0, n)),
+            (w_packed, (128, NW), lambda s, n: (CW // 128, n)),
+            (spill, (1, HALO, NW), lambda s, n: (s, 0, n)),
+            (n_ext, (TE, NW), lambda s, n: (s, n)),
+        ],
+        [
+            ((2, T, width), bf16, (1, T, NW), lambda s, n: (s, 0, n)),
+            ((2, 8, width), f32, (1, 8, NW), lambda s, n: (s, 0, n)),
+        ],
         flops=2 * 2 * TE * width * (2 * HW + 128),
         name="input_grad",
     )
-    n_grad = n_grad.reshape(2, TE, width)
-    (n_grad,) = stages.settle([n_grad])
-    at_spill = stages.add(g.one_task, [n_grad[:, T:]], lambda a: g.shift_z(a, -1))
-    at_gates = stages.add(g.spread_task, gate_sum, 1)
-    (n_grad,) = stages.launch([n_grad])
-    (n_grad,) = stages.settle([n_grad])
-    last = n_grad[:, T - HALO : T].astype(f32) + at_spill["got"][0].astype(f32)
-    n_grad = jnp.concatenate([n_grad[:, : T - HALO], last.astype(bf16)], axis=1)
-    at_ngrad = stages.add(g.scatter_task, n_grad.reshape(2, g.X, own_len, width))
-    at_outs = stages.add(g.spread_task, out_sum, 0)
+
+    def lay(a, lines):
+        flat = a.reshape(-1)
+        return jnp.pad(flat, (0, lines * own_d - flat.shape[0])).reshape(lines, own_d)
+
+    per = HW // own_d
+    lines = inner // own_d
+    pre_part = g.own_first_back(jnp.sum(pre_grad, axis=(0, 1))) / pre_gain
+    kg = jnp.sum(kg, axis=0)[:5]
+    sm = jnp.sum(sm, axis=0)[:, :3].transpose(1, 0, 2).reshape(3, HL)
+    heads_all = lax.dynamic_update_slice(jnp.zeros((3, heads), f32), sm, (0, HL * j))
+    wide_rows = jnp.concatenate([gain_grad, kg[:, :HW]], axis=0).reshape(6, per, own_d)
+    wide_rows = lax.dynamic_update_slice(
+        jnp.zeros((6, lines, own_d), f32), wide_rows, (0, per * j, 0)
+    )
+    shared_lines = -(-5 * shared // own_d)
+    pre_lines = width // own_d
+    small = jnp.concatenate(
+        [
+            wide_rows.reshape(6 * lines, own_d),
+            lay(kg[:, HW:], shared_lines),
+            lay(heads_all, 1),
+            pre_part.reshape(pre_lines, own_d),
+        ],
+        axis=0,
+    )
+    n_rest = shared + heads
+    small = jnp.pad(small, ((0, -(n_rest + small.shape[0]) % 128), (0, 0)))
+    copies = jnp.concatenate([small] * 2, axis=1)
+    rest = [jnp.concatenate([p, copies], axis=0) for p in rest]
+    rest_far = [p.astype(bf16) for p in rest[1:]]
+    n_grad, rest_far = stages.settle([n_grad, rest_far], leave=[at_gates, at_outs])
+    at_rest = stages.add(g.gradient_task, rest_far, lambda: rest[0], 1, None)
+    at_ngrad = stages.add(g.scatter_task, n_grad.reshape(2, g.W, own_len, width), (1, 2))
     stages.launch([])
 
     in_shape = (2 * inner + shared + heads, own_d)
-    out_shape = (own_d, inner)
-    dest = {(d, e): (g.x - d) % g.X * 2 + (g.c ^ e) for d in range(g.X) for e in range(2)}
-
-    def place_rows(done, first, buf):
-        keys = list(done)
-        moves = [
-            (i, (0, 0), done[k].shape, (first + HW * dest[k], 0)) for i, k in enumerate(keys)
+
+    def moves_of(a, first, axis):
+        n = a["done"][0].shape[axis] // 4
+        moves = []
+        for i, (d, e) in enumerate(a["from"]):
+            source, target, sizes = [0, 0], [0, 0], [own_d, own_d]
+            source[axis], sizes[axis] = i % 4 * n, n
+            target[axis] = first + HW * ((g.w ^ d) * 2 + (g.c ^ e))
+            moves.append((i // 4, tuple(source), tuple(sizes), tuple(target)))
+        return moves
+
+    in_buf, out_weight_gradient = None, None
+    todo = [(at_gates, 0), (at_x, inner)]
+    plan = iter(
+        [
+            ([at_x, at_outs, at_gates], []),
+            ([at_x], [at_rest]),
+            ([at_x, at_outs, at_ngrad], [at_rest]),
+            ([at_x, at_outs, at_ngrad, at_gates], []),
         ]
-        return place([done[k] for k in keys], moves, in_shape, buf)
-
-    in_buf = place_rows(at_gates["done"], 0, None)
-    (in_buf,) = stages.settle([in_buf])
-    stages.launch([])
-    keys = list(at_outs["done"])
-    moves = [(i, (0, 0), (own_d, HW), (0, HW * dest[k])) for i, k in enumerate(keys)]
-    out_weight_gradient = place([at_outs["done"][k] for k in keys], moves, out_shape, None)
-    (out_weight_gradient,) = stages.settle([out_weight_gradient])
-    while "sum" not in at_ngrad:
+    )
+    while stages.tasks:
+        leave_now, _ = next(plan, ([], []))
+        stages.settle([], leave=leave_now)
+        if not stages.tasks:
+            break
         stages.launch([])
-        stages.settle([])
-    stages.launch([])
-    n_grad = g.own_first_back(at_ngrad["sum"])
-    pre_grad = jnp.sum(n_grad * series * scale, axis=0)
-    lifted_n = n_grad * pre_gain[None, :]
+        if out_weight_gradient is None and "done" in at_outs:
+            out_weight_gradient = place(
+                at_outs["done"], moves_of(at_outs, 0, 1), (own_d, inner), None
+            )
+        for a, first in list(todo):
+            if "done" in a:
+                in_buf = place(a["done"], moves_of(a, first, 0), in_shape, in_buf)
+                todo.remove((a, first))
+    for a, first in todo:
+        in_buf = place(a["done"], moves_of(a, first, 0), in_shape, in_buf)
+    if out_weight_gradient is None:
+        out_weight_gradient = place(at_outs["done"], moves_of(at_outs, 0, 1), (own_d, inner), None)
+    rest_done = at_rest["done"]
+    in_buf = place(
+        [rest_done], [(0, (0, 0), (n_rest, own_d), (2 * inner, 0))], in_shape, in_buf
+    )
+    n_own = g.own_first_back(at_ngrad["sum"])
+    lifted_n = n_own * pre_gain[None, :]
     token_gradient = (
         cotangent[0].astype(f32)
         + scale * lifted_n
         - series * scale**3 * jnp.mean(series * lifted_n, axis=-1, keepdims=True)
     )[None]
     block_output = (series + g.own_first_back(at_branch["sum"])).astype(bf16)[None]
-    at_pre = stages.add(g.small_task, pre_grad.reshape(-1, 128), True)
-    flying = {"x": list(enumerate(at_xs)), "tail": True}
-    while stages.tasks or flying["x"] or flying["tail"]:
-        if stages.tasks:
-            (in_buf,) = stages.settle([in_buf])
-            if stages.tasks:
-                stages.launch([])
-        for k, a in list(flying["x"]):
-            if "done" in a:
-                in_buf = place_rows(a["done"], inner + k * cols, in_buf)
-                flying["x"].remove((k, a))
-        if flying["tail"] and "done" in at_tail:
-            keys = list(at_tail["done"])
-            moves = []
-            for i, k in enumerate(keys):
-                moves.append((i, (0, 0), (SW, own_d), (2 * inner + SW * dest[k], 0)))
-                moves.append((i, (SW, 0), (HL, own_d), (2 * inner + shared + HL * dest[k], 0)))
-            in_buf = place([at_tail["done"][k] for k in keys], moves, in_shape, in_buf)
-            flying["tail"] = False
     in_weight_gradient = in_buf.T
 
-    small = at_small["sum"].reshape(g.TP, -1)[:, :n_small]
-    pre_total = at_pre["sum"].reshape(-1)
-    gain_total = small[:, :HW].reshape(-1)
-    at = HW
-    kt = small[:, at : at + taps * (HW + SW)].reshape(g.TP, taps, HW + SW).transpose(1, 0, 2)
-    at += taps * (HW + SW)
-    kernel_total = jnp.concatenate(
-        [kt[:, :, :HW].reshape(taps, -1), kt[:, :, HW:].reshape(taps, -1)], axis=1
-    )
-    bt = small[:, at : at + HW + SW]
-    at += HW + SW
-    bias_total = jnp.concatenate([bt[:, :HW].reshape(-1), bt[:, HW:].reshape(-1)])
-    step_total = small[:, at : at + HL].reshape(-1)
-    decay_total = small[:, at + HL : at + 2 * HL].reshape(-1)
-    skip_total = small[:, at + 2 * HL : at + 3 * HL].reshape(-1)
+    small = rest_done[n_rest:].astype(f32)
+    gain_total = small[:lines].reshape(-1)
+    kb = small[lines : 6 * lines].reshape(5, inner)
+    at = 6 * lines
+    shared_kb = small[at : at + shared_lines].reshape(-1)[: 5 * shared].reshape(5, shared)
+    kb = jnp.concatenate([kb, shared_kb], axis=1)
+    kernel_total, bias_total = kb[:taps], kb[taps]
+    at += shared_lines
+    step_total, decay_total, skip_total = small[at, : 3 * heads].reshape(3, heads)
+    pre_total = small[at + 1 : at + 1 + pre_lines].reshape(-1)
     return (
         block_output,
         token_gradient,

time: 849 us -> 739 us (0.87)
  waiting for transfers between devices: 338 us -> 251 us
  starting transfers between devices: 99.8 us -> 67.7 us
  between operations: 16.6 us -> 2.73 us
  matrix products: 62.7 us -> 75.6 us
  Pallas kernels: 167 us -> 178 us
    psum x1 -> x0, waiting for transfers between devices: 101 us -> none  [sum_z(): return lax.psum(q, 'seq', axis_index_groups=groups)]
    ppermute x81 -> x58, starting transfers between devices: 99.8 us -> 67.7 us  [move(): return lax.ppermute(a, AXES, pairs)]
    ppermute x81 -> x58, waiting for transfers between devices: 236 us -> 251 us  [move(): return lax.ppermute(a, AXES, pairs)]
    unnamed x279 -> x206, local copies, waits for them, and re-layouts: 38 us -> 52.2 us
    concatenate x7 -> x18, other arithmetic: 3.18 us -> 16.3 us  [the longest x3 5.42 us: gradient_task(): quad = jnp.concatenate([pair, got[0]], axis=1 - axis)]
    dot_general x14 -> x13, matrix products: 62.7 us -> 75.6 us  [low_dot(): lax.dot_general(a.astype(bf16), b.astype(bf16), dims, preferred_element_t...]
    pallas_call x8, Pallas kernels: 129 us -> 142 us  [call(): pl.pallas_call(kernel, grid=grid, in_specs=[pl.BlockSpec(b, m) for _, b,...]
    pallas_call x5 -> x4, Pallas kernels: 18.7 us -> 16.2 us  [place(): pl.pallas_call(kernel, in_specs=[pl.BlockSpec(memory_space=pltpu.SMEM)] +...]
  transfers between devices with their start and end apart: 82 -> 58, of which waited for: 30 -> 25; matrix products, arithmetic and copies ran while one was open for 15% -> 11% of each run, Pallas kernels for 16% -> 20%
where the time goes in v3:
time: 739 us; the launch traced here: 727 us
  waiting for transfers between devices  251 us (34%)
  Pallas kernels  178 us (24%)
  local copies, waits for them, and re-layouts  78.2 us (11%)
  matrix products  75.6 us (10%)
  other arithmetic  73.8 us (10%)
  starting transfers between devices  67.7 us (9%)
    ppermute x58, waiting for transfers between devices, move(): return lax.ppermute(a, AXES, pairs)  251 us
    pallas_call x8, Pallas kernels, call(): pl.pallas_call(kernel, grid=grid, in_specs=[pl.BlockSpec(b, m) for _, b,...  142 us
    dot_general x13, matrix products, low_dot(): lax.dot_general(a.astype(bf16), b.astype(bf16), dims, preferred_element_t...  75.6 us
    ppermute x58, starting transfers between devices, move(): return lax.ppermute(a, AXES, pairs)  67.7 us
    unnamed x206, local copies, waits for them, and re-layouts  52.2 us
    pallas_call x8, Pallas kernels, assemble(): pl.pallas_call(kernel, in_specs=[pl.BlockSpec(memory_space=pltpu.SMEM)] +...  19.8 us
    pallas_call x4, Pallas kernels, place(): pl.pallas_call(kernel, in_specs=[pl.BlockSpec(memory_space=pltpu.SMEM)] +...  16.2 us
  transfers between devices with their start and end apart: 58, of which 25 were waited for; matrix products, arithmetic and copies ran while one was open for 11% of the time, Pallas kernels for 20%

profile of v3, /device:TPU:1, one launch (start us, length us, event | category | flops | bytes accessed | tf_op | source)
XLA Modules:
  0.0 726.6 jit_solution(5473829339842964147)
XLA Ops:
  28.9 15.5 %collective-permute-done.1 = bf16[256,2048]{1,0:T(8,128)(2,1)} collective-permute-done((bf16[256,2048]{1,0:T(8,128)(2,1)}, bf16[256,2048]{1,0:T(8,128)(2,1)}, u32[]{:S(2)}, u32[]{:S(2)}) %collective-permute-start.1) | collective-permute-done | bytes 1048608 | tf_op jit(solution)/shard_map/ppermute | solution.py:48
  88.6 6.7 assemble.11
  95.3 12.7 %convolution_convert_fusion.1 = bf16[2080,896]{1,0:T(8,128)(2,1)} fusion(bf16[2080,2048]{1,0:T(8,128)(2,1)} %bitcast.287, bf16[896,2048]{1,0:T(8,128)(2,1)S(1)} %assemble.12.wx.wt), kind=kOutput, calls=%fused_computation.5 | convolution fusion | flops 7635496960 | bytes 15917056 | tf_op jit(solution)/shard_map/dot_general | solution.py:300
  118.2 22.2 %convolve.1 = (bf16[2048,512]{1,0:T(8,128)(2,1)S(1)}, bf16[2048,256]{1,0:T(8,128)(2,1)S(1)}, f32[2,4,128,512]{3,2,1,0:T(8,128)S(1)}, f32[2,2,1024,4]{3,2,1,0:T(8...) custom-call(bf16[2,1040,896]{2,1,0:T(8,128)(2,1)S(1)} %bitcast.280, ...), custom_call_target="tpu_custom_call" | custom-call | flops 2684354560 | bytes 13040896 | tf_op jit(solution)/shard_map/convolve/pallas_call | solution.py:367
  150.9 9.7 %collective-permute-done.17 = bf16[128,2048]{1,0:T(8,128)(2,1)} collective-permute-done((bf16[128,2048]{1,0:T(8,128)(2,1)}, bf16[128,2048]{1,0:T(8,128)(2,1)}, u32[]{:S(2)}, u32[]{:S(2)}) %collective-permute-start.17) | collective-permute-done | bytes 524320 | tf_op jit(solution)/shard_map/ppermute | solution.py:48
  170.6 9.1 %convolution_convert_fusion.2 = bf16[2080,512]{1,0:T(8,128)(2,1)S(1)} fusion(bf16[2080,2048]{1,0:T(8,128)(2,1)} %bitcast.288, bf16[512,2048]{1,0:T(8,128)(2,1)S(1)} %assemble.13.wg), kind=kOutput, calls=%fused_computation.6 | convolution fusion | flops 4363141120 | bytes 12746752 | tf_op jit(solution)/shard_map/dot_general | solution.py:300
  179.8 10.9 %intra_forward.1.y = bf16[2048,512]{1,0:T(8,128)(2,1)S(1)} custom-call(bf16[2048,512]{1,0:T(8,128)(2,1)S(1)} %copy-done.58, bf16[2048,256]{1,0:T(8,128)(2,1)S(1)} %copy-done.26, f32[2,2,1024,4]{3,2,1,0:T(8,128)S(1)} %copy-done.16, f32[2,2,4,4,256]{4,3,2,1,0:T(4,128)S(1)} %get-tuple-element.253.row, f32[2,2,1024,4]{3,2,1,0:T(8,128)S(1)} %copy-done.62, ...), custom_call_target="tpu_custom_call" | custom-call | flops 4294967296 | bytes 5570816 | tf_op jit(solution)/shard_map/intra_forward/pallas_call | solution.py:367
  197.9 8.1 %convolution_convert_fusion.3.og = bf16[2048,512]{1,0:T(8,128)(2,1)S(1)} fusion(bf16[2048,2048]{1,0:T(8,128)(2,1)} %bitcast.298, bf16[2048,512]{1,0:T(8,128)(2,1)S(1)} %assemble.15), kind=kOutput, calls=%fused_computation.35 | convolution fusion | flops 4296015872 | bytes 12582912 | tf_op jit(solution)/shard_map/dot_general | solution.py:300
  206.2 8.3 %join.1 = (bf16[2048,512]{1,0:T(8,128)(2,1)S(1)}, f32[2,8,1024]{2,1,0:T(8,128)S(1)}) custom-call(bf16[2048,512]{1,0:T(8,128)(2,1)S(1)} %intra_forward.1.y, bf16[2048,256]{1,0:T(8,128)(2,1)S(1)} %copy-done.26, bf16[2,4,128,512]{3,2,1,0:T(8,128)(2,1)S(1)} %maximum_convert_fusion.enter, f32[2,2,1024,4]{3,2,1,0:T(8,128)S(1)} %copy-done.16, ...), custom_call_target="tpu_custom_call" | custom-call | flops 536870912 | bytes 10717184 | tf_op jit(solution)/shard_map/join/pallas_call | solution.py:367
  222.0 12.3 %gates.1 = (bf16[2048,512]{1,0:T(8,128)(2,1)S(1)}, bf16[2,1040,512]{2,1,0:T(8,128)(2,1)}, bf16[2048,512]{1,0:T(8,128)(2,1)S(1)}, f32[1,512]{1,0:T(1,128)S(1)}, f32[2,4,128,512]{3,2,1,0:T(8,128)S(1)}) custom-call(bf16[2048,512]{1,0:T(8,128)(2,1)S(1)} %get-tuple-element.264.mixed, bf16[2,1040,512]{2,1,0:T(8,128)(2,1)} %bitcast.258, ...), custom_call_target="tpu_custom_call" | custom-call | flops 536870912 | bytes 15994880 | tf_op jit(solution)/shard_map/gates/pallas_call | solution.py:367
  238.9 4.8 convolution_convert_fusion
  257.0 37.4 %intra_backward.1 = (bf16[2048,512]{1,0:T(8,128)(2,1)S(1)}, f32[2,2,1024,4]{3,2,1,0:T(8,128)S(1)}, f32[2048,256]{1,0:T(8,128)S(1)}) custom-call(bf16[2048,512]{1,0:T(8,128)(2,1)S(1)} %copy-done.59, bf16[2048,256]{1,0:T(8,128)(2,1)S(1)} %copy-done.27, bf16[2048,512]{1,0:T(8,128)(2,1)S(1)} %copy-done.52, f32[2,2,1024,4]{3,2,1,0:T(8,128)} %copy-done.15, ...), custom_call_target="tpu_custom_call" | custom-call | flops 8589934592 | bytes 10878976 | tf_op jit(solution)/shard_map/intra_backward/pallas_call | solution.py:367
  294.5 8.0 %fusion.39 = bf16[512,1024]{1,0:T(8,128)(2,1)} fusion(bf16[2080,512]{1,0:T(8,128)(2,1)S(1)} %bitcast.275, bf16[2080,2048]{1,0:T(8,128)(2,1)} %bitcast.289), kind=kOutput, calls=%fused_computation.69 | convolution fusion | flops 2181562368 | bytes 7438336 | tf_op jit(solution)/shard_map/dot_general | solution.py:300
  302.5 4.6 fusion.2
  328.4 31.8 %finish.1 = (bf16[2,1040,768]{2,1,0:T(8,128)(2,1)}, bf16[2,1040,128]{2,1,0:T(8,128)(2,1)S(1)}, f32[2,8,768]{2,1,0:T(8,128)S(1)}, f32[2,2,8,4]{3,2,1,0:T(8,128)S(1)}) custom-call(bf16[2,1040,896]{2,1,0:T(8,128)(2,1)} %bitcast.278, bf16[2048,512]{1,0:T(8,128)(2,1)S(1)} %copy-done.60, bf16[2048,512]{1,0:T(8,128)(2,1)S(1)} %copy-done.53, ...), custom_call_target="tpu_custom_call" | custom-call | flops 8589934592 | bytes 23109376 | tf_op jit(solution)/shard_map/finish/pallas_call | solution.py:367
  362.4 5.9 fusion.42
  371.5 6.1 add_convert_fusion.4
  391.9 6.3 collective-permute-done.36.spill
  407.1 17.9 %input_grad.1 = (bf16[2,1024,2048]{2,1,0:T(8,128)(2,1)}, f32[2,8,2048]{2,1,0:T(8,128)S(1)}) custom-call(bf16[2080,512]{1,0:T(8,128)(2,1)S(1)} %bitcast.277, bf16[2080,768]{1,0:T(8,128)(2,1)S(1)} %bitcast.269, bf16[2080,128]{1,0:T(8,128)(2,1)S(1)} %bitcast.274, bf16[512,2048]{1,0:T(8,128)(2,1)S(1)} %copy-done.37, bf16[896,2048]{1,0:T(8,128)(2,1)S(1)} %copy-done.4, ...), custom_call_target="tpu_custom_call" | custom-call | flops 9814671360 | bytes 32464896 | tf_op jit(solution)/shard_map/input_grad/pallas_call | solution.py:367
  425.3 6.9 add_convert_fusion.3
  438.2 17.9 %collective-permute-done.37 = bf16[384,1024]{1,0:T(8,128)(2,1)S(1)} collective-permute-done((bf16[384,1024]{1,0:T(8,128)(2,1)S(1)}, bf16[384,1024]{1,0:T(8,128)(2,1)S(1)}, u32[]{:S(2)}, u32[]{:S(2)}) %collective-permute-start.37) | collective-permute-done | bytes 786464 | tf_op jit(solution)/shard_map/ppermute | solution.py:48
  456.1 5.4 fusion
  467.5 45.4 %collective-permute-done.40 = bf16[512,1024]{1,0:T(8,128)(2,1)} collective-permute-done((bf16[512,1024]{1,0:T(8,128)(2,1)}, bf16[512,1024]{1,0:T(8,128)(2,1)}, u32[]{:S(2)}, u32[]{:S(2)}) %collective-permute-start.40) | collective-permute-done | bytes 1048608 | tf_op jit(solution)/shard_map/ppermute | solution.py:48
  523.9 46.4 %collective-permute-done.45 = bf16[96,1024]{1,0:T(8,128)(2,1)S(1)} collective-permute-done((bf16[96,1024]{1,0:T(8,128)(2,1)S(1)}, bf16[96,1024]{1,0:T(8,128)(2,1)S(1)}, u32[]{:S(2)}, u32[]{:S(2)}) %collective-permute-start.45) | collective-permute-done | bytes 196640 | tf_op jit(solution)/shard_map/ppermute | solution.py:48
  573.1 23.1 %collective-permute-done.48 = bf16[48,1024]{1,0:T(8,128)(2,1)S(1)} collective-permute-done((bf16[48,1024]{1,0:T(8,128)(2,1)S(1)}, bf16[48,1024]{1,0:T(8,128)(2,1)S(1)}, u32[]{:S(2)}, u32[]{:S(2)}) %collective-permute-start.48) | collective-permute-done | bytes 98336 | tf_op jit(solution)/shard_map/ppermute | solution.py:48
  596.3 5.0 collective-permute-done.49
  617.3 33.1 %collective-permute-done.51.refs_1_ = bf16[2048,512]{1,0:T(8,128)(2,1)} collective-permute-done((bf16[2048,512]{1,0:T(8,128)(2,1)}, bf16[2048,512]{1,0:T(8,128)(2,1)}, u32[]{:S(2)}, u32[]{:S(2)}) %collective-permute-start.51) | collective-permute-done | bytes 2097184 | tf_op jit(solution)/shard_map/ppermute | solution.py:48
  656.8 14.5 %collective-permute-done.54 = bf16[1024,512]{1,0:T(8,128)(2,1)} collective-permute-done((bf16[1024,512]{1,0:T(8,128)(2,1)S(1)}, bf16[1024,512]{1,0:T(8,128)(2,1)}, u32[]{:S(2)}, u32[]{:S(2)}) %collective-permute-start.54) | collective-permute-done | bytes 1048608 | tf_op jit(solution)/shard_map/ppermute | solution.py:48
  680.8 6.2 collective-permute-start.57
  689.5 5.2 place.7
  694.7 5.9 place.4.refs_2_
  700.6 14.4 %collective-permute-done.56.refs_1_ = bf16[2048,512]{1,0:T(8,128)(2,1)S(1)} collective-permute-done((bf16[2048,512]{1,0:T(8,128)(2,1)S(1)}, bf16[2048,512]{1,0:T(8,128)(2,1)S(1)}, u32[]{:S(2)}, u32[]{:S(2)}) %collective-permute-start.56) | collective-permute-done | bytes 2097184 | tf_op jit(solution)/shard_map/ppermute | solution.py:48
  (505 shorter events, 256.1 us)
Async XLA Ops:
  16.9 29.3 %collective-permute-start.5 = (bf16[576,1024]{1,0:T(8,128)(2,1)}, bf16[576,1024]{1,0:T(8,128)(2,1)}, u32[]{:S(2)}, u32[]{:S(2)}) collective-permute-start(bf16[576,1024]{1,0:T(8,128)(2,1)} %slice.330), channel_id=1, source_target_pairs={{0,2},{1,3},{2,0},{3,1},{4,6},{5,7},{6,4},{7,5},{8,10},{9,11},{10,... | collective-permute-start | bytes 3538952 | tf_op jit(solution)/shard_map/ppermute | solution.py:48
  19.6 24.8 %collective-permute-start.1 = (bf16[256,2048]{1,0:T(8,128)(2,1)}, bf16[256,2048]{1,0:T(8,128)(2,1)}, u32[]{:S(2)}, u32[]{:S(2)}) collective-permute-start(bf16[256,2048]{1,0:T(8,128)(2,1)} %get-tuple-element.190), channel_id=1, source_target_pairs={{0,4},{1,5},{2,6},{3,7},{4,0},{5,1},{6,2},{7,3},{8,12},{9,13},{10,... | collective-permute-start | bytes 3145736 | tf_op jit(solution)/shard_map/ppermute | solution.py:48
  20.8 24.5 %collective-permute-start.2 = (bf16[256,2048]{1,0:T(8,128)(2,1)}, bf16[256,2048]{1,0:T(8,128)(2,1)}, u32[]{:S(2)}, u32[]{:S(2)}) collective-permute-start(bf16[256,2048]{1,0:T(8,128)(2,1)} %get-tuple-element.190), channel_id=1, source_target_pairs={{0,8},{1,9},{2,10},{3,11},{4,12},{5,13},{6,14},{7,15},{8,0},{9,1},... | collective-permute-start | bytes 3145736 | tf_op jit(solution)/shard_map/ppermute | solution.py:48
  53.8 23.6 %collective-permute-start.8 = (bf16[3,256,2048]{2,1,0:T(8,128)(2,1)}, bf16[3,256,2048]{2,1,0:T(8,128)(2,1)S(1)}, u32[]{:S(2)}, u32[]{:S(2)}) collective-permute-start(bf16[3,256,2048]{2,1,0:T(8,128)(2,1)} %pad_maximum_fusion), channel_id=1, source_target_pairs={{0,1},{1,0},{2,3},{3,2},{4,5},{5,4},{6,7},{7,6},{8,9},{9,8},{10,11... | collective-permute-start | bytes 9437192 | tf_op jit(solution)/shard_map/ppermute | solution.py:48
  83.5 25.1 %collective-permute-start.14 = (bf16[256,2048]{1,0:T(8,128)(2,1)}, bf16[256,2048]{1,0:T(8,128)(2,1)S(1)}, u32[]{:S(2)}, u32[]{:S(2)}) collective-permute-start(bf16[256,2048]{1,0:T(8,128)(2,1)} %pad_maximum_fusion.10), channel_id=1, source_target_pairs={{0,4},{1,5},{2,6},{3,7},{4,0},{5,1},{6,2},{7,3},{8,12},{9,13},{10,... | collective-permute-start | bytes 3145736 | tf_op jit(solution)/shard_map/ppermute | solution.py:48
  83.9 24.7 %collective-permute-start.15 = (bf16[256,2048]{1,0:T(8,128)(2,1)}, bf16[256,2048]{1,0:T(8,128)(2,1)S(1)}, u32[]{:S(2)}, u32[]{:S(2)}) collective-permute-start(bf16[256,2048]{1,0:T(8,128)(2,1)} %pad_maximum_fusion.10), channel_id=1, source_target_pairs={{0,8},{1,9},{2,10},{3,11},{4,12},{5,13},{6,14},{7,15},{8,0},{9,1},... | collective-permute-start | bytes 3145736 | tf_op jit(solution)/shard_map/ppermute | solution.py:48
  112.5 49.1 %collective-permute-start.19 = (bf16[3,256,2048]{2,1,0:T(8,128)(2,1)}, bf16[3,256,2048]{2,1,0:T(8,128)(2,1)S(1)}, u32[]{:S(2)}, u32[]{:S(2)}) collective-permute-start(bf16[3,256,2048]{2,1,0:T(8,128)(2,1)} %pad_maximum_fusion.1), channel_id=1, source_target_pairs={{0,1},{1,0},{2,3},{3,2},{4,5},{5,4},{6,7},{7,6},{8,9},{9,8},{10,11... | collective-permute-start | bytes 9437192 | tf_op jit(solution)/shard_map/ppermute | solution.py:48
  113.7 37.2 %collective-permute-start.13 = (bf16[512,1024]{1,0:T(8,128)(2,1)}, bf16[512,1024]{1,0:T(8,128)(2,1)}, u32[]{:S(2)}, u32[]{:S(2)}) collective-permute-start(bf16[512,1024]{1,0:T(8,128)(2,1)} %copy-done.31), channel_id=1, source_target_pairs={{0,2},{1,3},{2,0},{3,1},{4,6},{5,7},{6,4},{7,5},{8,10},{9,11},{10,... | collective-permute-start | bytes 3145736 | tf_op jit(solution)/shard_map/ppermute | solution.py:48
  162.8 27.9 %collective-permute-start.20 = (bf16[256,2048]{1,0:T(8,128)(2,1)S(1)}, bf16[256,2048]{1,0:T(8,128)(2,1)S(1)}, u32[]{:S(2)}, u32[]{:S(2)}) collective-permute-start(bf16[256,2048]{1,0:T(8,128)(2,1)S(1)} %pad_maximum_fusion.11), channel_id=1, source_target_pairs={{0,1},{1,0},{2,3},{3,2},{4,5},{5,4},{6,7},{7,6},{8,9},{9,8},{10,11... | collective-permute-start | bytes 3145736 | tf_op jit(solution)/shard_map/ppermute | solution.py:48
  164.3 26.4 %collective-permute-start.21 = (bf16[1024,512]{1,0:T(8,128)(2,1)S(1)}, bf16[1024,512]{1,0:T(8,128)(2,1)S(1)}, u32[]{:S(2)}, u32[]{:S(2)}) collective-permute-start(bf16[1024,512]{1,0:T(8,128)(2,1)S(1)} %copy-done.30), channel_id=1, source_target_pairs={{0,2},{1,3},{2,0},{3,1},{4,6},{5,7},{6,4},{7,5},{8,10},{9,11},{10,... | collective-permute-start | bytes 3145736 | tf_op jit(solution)/shard_map/ppermute | solution.py:48
  164.6 26.2 %collective-permute-start.22 = (bf16[2,128,512]{2,1,0:T(8,128)(2,1)S(1)}, bf16[2,128,512]{2,1,0:T(8,128)(2,1)S(1)}, u32[]{:S(2)}, u32[]{:S(2)}) collective-permute-start(bf16[2,128,512]{2,1,0:T(8,128)(2,1)S(1)} %fusion.55), channel_id=1, source_target_pairs={{0,16},{1,17},{2,18},{3,19},{4,20},{5,21},{6,22},{7,23},{8,24},{9,... | collective-permute-start | bytes 786440 | tf_op jit(solution)/shard_map/ppermute | solution.py:48
  247.2 59.9 %collective-permute-start.29 = (bf16[4,256,2048]{2,1,0:T(8,128)(2,1)}, bf16[4,256,2048]{2,1,0:T(8,128)(2,1)}, u32[]{:S(2)}, u32[]{:S(2)}) collective-permute-start(bf16[4,256,2048]{2,1,0:T(8,128)(2,1)} %bitcast.63), channel_id=1, source_target_pairs={{0,1},{1,0},{2,3},{3,2},{4,5},{5,4},{6,7},{7,6},{8,9},{9,8},{10,11... | collective-permute-start | bytes 12582920 | tf_op jit(solution)/shard_map/ppermute | solution.py:48
  248.8 58.3 %collective-permute-start.27 = (bf16[2,128,512]{2,1,0:T(8,128)(2,1)}, bf16[2,128,512]{2,1,0:T(8,128)(2,1)S(1)}, u32[]{:S(2)}, u32[]{:S(2)}) collective-permute-start(bf16[2,128,512]{2,1,0:T(8,128)(2,1)} %fusion.54), channel_id=1, source_target_pairs={{16,0},{17,1},{18,2},{19,3},{20,4},{21,5},{22,6},{23,7},{24,8},{25... | collective-permute-start | bytes 786440 | tf_op jit(solution)/shard_map/ppermute | solution.py:48
  250.1 57.0 %collective-permute-start.28 = (bf16[1024,512]{1,0:T(8,128)(2,1)}, bf16[1024,512]{1,0:T(8,128)(2,1)S(1)}, u32[]{:S(2)}, u32[]{:S(2)}) collective-permute-start(bf16[1024,512]{1,0:T(8,128)(2,1)} %fusion.47), channel_id=1, source_target_pairs={{0,2},{1,3},{2,0},{3,1},{4,6},{5,7},{6,4},{7,5},{8,10},{9,11},{10,... | collective-permute-start | bytes 3145736 | tf_op jit(solution)/shard_map/ppermute | solution.py:48
  318.6 49.6 %collective-permute-start.31 = (bf16[2,256,2048]{2,1,0:T(8,128)(2,1)}, bf16[2,256,2048]{2,1,0:T(8,128)(2,1)}, u32[]{:S(2)}, u32[]{:S(2)}) collective-permute-start(bf16[2,256,2048]{2,1,0:T(8,128)(2,1)} %pad_maximum_fusion.2), channel_id=1, source_target_pairs={{0,4},{1,5},{2,6},{3,7},{4,0},{5,1},{6,2},{7,3},{8,12},{9,13},{10,... | collective-permute-start | bytes 6291464 | tf_op jit(solution)/shard_map/ppermute | solution.py:48
  319.0 49.2 %collective-permute-start.30 = (bf16[1024,512]{1,0:T(8,128)(2,1)}, bf16[1024,512]{1,0:T(8,128)(2,1)S(1)}, u32[]{:S(2)}, u32[]{:S(2)}) collective-permute-start(bf16[1024,512]{1,0:T(8,128)(2,1)} %add_convert_fusion.7), channel_id=1, source_target_pairs={{0,16},{1,17},{2,18},{3,19},{4,20},{5,21},{6,22},{7,23},{8,24},{9,... | collective-permute-start | bytes 3145736 | tf_op jit(solution)/shard_map/ppermute | solution.py:48
  322.0 46.2 %collective-permute-start.32 = (bf16[512,1024]{1,0:T(8,128)(2,1)}, bf16[512,1024]{1,0:T(8,128)(2,1)S(1)}, u32[]{:S(2)}, u32[]{:S(2)}) collective-permute-start(bf16[512,1024]{1,0:T(8,128)(2,1)} %fusion.39), channel_id=1, source_target_pairs={{0,2},{1,3},{2,0},{3,1},{4,6},{5,7},{6,4},{7,5},{8,10},{9,11},{10,... | collective-permute-start | bytes 3145736 | tf_op jit(solution)/shard_map/ppermute | solution.py:48
  389.3 36.0 %collective-permute-start.33 = (bf16[256,2048]{1,0:T(8,128)(2,1)}, bf16[256,2048]{1,0:T(8,128)(2,1)}, u32[]{:S(2)}, u32[]{:S(2)}) collective-permute-start(bf16[256,2048]{1,0:T(8,128)(2,1)} %fusion.50), channel_id=1, source_target_pairs={{0,8},{1,9},{2,10},{3,11},{4,12},{5,13},{6,14},{7,15},{8,0},{9,1},... | collective-permute-start | bytes 3145736 | tf_op jit(solution)/shard_map/ppermute | solution.py:48
  390.6 34.7 %collective-permute-start.34 = (bf16[512,1024]{1,0:T(8,128)(2,1)}, bf16[512,1024]{1,0:T(8,128)(2,1)}, u32[]{:S(2)}, u32[]{:S(2)}) collective-permute-start(bf16[512,1024]{1,0:T(8,128)(2,1)} %fusion.42), channel_id=1, source_target_pairs={{0,2},{1,3},{2,0},{3,1},{4,6},{5,7},{6,4},{7,5},{8,10},{9,11},{10,... | collective-permute-start | bytes 3145736 | tf_op jit(solution)/shard_map/ppermute | solution.py:48
  465.1 47.8 %collective-permute-start.42 = (bf16[2,256,2048]{2,1,0:T(8,128)(2,1)S(1)}, bf16[2,256,2048]{2,1,0:T(8,128)(2,1)}, u32[]{:S(2)}, u32[]{:S(2)}) collective-permute-start(bf16[2,256,2048]{2,1,0:T(8,128)(2,1)S(1)} %pad_maximum_fusion.3), channel_id=1, source_target_pairs={{0,4},{1,5},{2,6},{3,7},{4,0},{5,1},{6,2},{7,3},{8,12},{9,13},{10,... | collective-permute-start | bytes 6291464 | tf_op jit(solution)/shard_map/ppermute | solution.py:48
  466.3 46.6 %collective-permute-start.40 = (bf16[512,1024]{1,0:T(8,128)(2,1)}, bf16[512,1024]{1,0:T(8,128)(2,1)}, u32[]{:S(2)}, u32[]{:S(2)}) collective-permute-start(bf16[512,1024]{1,0:T(8,128)(2,1)} %add_convert_fusion.4), channel_id=1, source_target_pairs={{0,16},{1,17},{2,18},{3,19},{4,20},{5,21},{6,22},{7,23},{8,24},{9,... | collective-permute-start | bytes 3145736 | tf_op jit(solution)/shard_map/ppermute | solution.py:48
  466.3 46.6 %collective-permute-start.39 = (bf16[512,1024]{1,0:T(8,128)(2,1)S(1)}, bf16[512,1024]{1,0:T(8,128)(2,1)}, u32[]{:S(2)}, u32[]{:S(2)}) collective-permute-start(bf16[512,1024]{1,0:T(8,128)(2,1)S(1)} %copy-done.75), channel_id=1, source_target_pairs={{0,8},{1,9},{2,10},{3,11},{4,12},{5,13},{6,14},{7,15},{8,0},{9,1},... | collective-permute-start | bytes 3145736 | tf_op jit(solution)/shard_map/ppermute | solution.py:48
  466.3 46.6 %collective-permute-start.41 = (bf16[192,1024]{1,0:T(8,128)(2,1)}, bf16[192,1024]{1,0:T(8,128)(2,1)S(1)}, u32[]{:S(2)}, u32[]{:S(2)}) collective-permute-start(bf16[192,1024]{1,0:T(8,128)(2,1)} %constant_dynamic-slice_fusion.14), channel_id=1, source_target_pairs={{0,1},{1,0},{2,3},{3,2},{4,5},{5,4},{6,7},{7,6},{8,9},{9,8},{10,11... | collective-permute-start | bytes 1179656 | tf_op jit(solution)/shard_map/ppermute | solution.py:48
  520.3 81.1 %collective-permute-start.43 = (bf16[512,2048]{1,0:T(8,128)(2,1)S(1)}, bf16[512,2048]{1,0:T(8,128)(2,1)}, u32[]{:S(2)}, u32[]{:S(2)}) collective-permute-start(bf16[512,2048]{1,0:T(8,128)(2,1)S(1)} %pad_maximum_fusion.4.refs_0_), channel_id=1, source_target_pairs={{0,4},{1,5},{2,6},{3,7},{4,0},{5,1},{6,2},{7,3},{8,12},{9,13},{10,... | collective-permute-start | bytes 6291464 | tf_op jit(solution)/shard_map/ppermute | solution.py:48
  521.4 48.9 %collective-permute-start.44 = (bf16[512,512]{1,0:T(8,128)(2,1)S(1)}, bf16[512,512]{1,0:T(8,128)(2,1)}, u32[]{:S(2)}, u32[]{:S(2)}) collective-permute-start(bf16[512,512]{1,0:T(8,128)(2,1)S(1)} %get-tuple-element.342), channel_id=1, source_target_pairs={{0,1},{1,0},{2,3},{3,2},{4,5},{5,4},{6,7},{7,6},{8,9},{9,8},{10,11... | collective-permute-start | bytes 1572872 | tf_op jit(solution)/shard_map/ppermute | solution.py:48
  523.1 47.2 %collective-permute-start.45 = (bf16[96,1024]{1,0:T(8,128)(2,1)S(1)}, bf16[96,1024]{1,0:T(8,128)(2,1)S(1)}, u32[]{:S(2)}, u32[]{:S(2)}) collective-permute-start(bf16[96,1024]{1,0:T(8,128)(2,1)S(1)} %constant_dynamic-slice_fusion.11), channel_id=1, source_target_pairs={{0,4},{1,5},{2,6},{3,7},{4,0},{5,1},{6,2},{7,3},{8,12},{9,13},{10,... | collective-permute-start | bytes 589832 | tf_op jit(solution)/shard_map/ppermute | solution.py:48
  523.6 72.7 %collective-permute-start.47 = (bf16[512,1024]{1,0:T(8,128)(2,1)}, bf16[512,1024]{1,0:T(8,128)(2,1)}, u32[]{:S(2)}, u32[]{:S(2)}) collective-permute-start(bf16[512,1024]{1,0:T(8,128)(2,1)} %add_convert_fusion.3), channel_id=1, source_target_pairs={{0,16},{1,17},{2,18},{3,19},{4,20},{5,21},{6,22},{7,23},{8,24},{9,... | collective-permute-start | bytes 3145736 | tf_op jit(solution)/shard_map/ppermute | solution.py:48
  523.6 77.8 %collective-permute-start.50 = (bf16[256,2048]{1,0:T(8,128)(2,1)}, bf16[256,2048]{1,0:T(8,128)(2,1)}, u32[]{:S(2)}, u32[]{:S(2)}) collective-permute-start(bf16[256,2048]{1,0:T(8,128)(2,1)} %fusion.51), channel_id=1, source_target_pairs={{0,8},{1,9},{2,10},{3,11},{4,12},{5,13},{6,14},{7,15},{8,0},{9,1},... | collective-permute-start | bytes 3145736 | tf_op jit(solution)/shard_map/ppermute | solution.py:48
  571.6 29.8 %collective-permute-start.46 = (bf16[1024,512]{1,0:T(8,128)(2,1)S(1)}, bf16[1024,512]{1,0:T(8,128)(2,1)}, u32[]{:S(2)}, u32[]{:S(2)}) collective-permute-start(bf16[1024,512]{1,0:T(8,128)(2,1)S(1)} %pad_maximum_fusion.14), channel_id=1, source_target_pairs={{0,8},{1,9},{2,10},{3,11},{4,12},{5,13},{6,14},{7,15},{8,0},{9,1},... | collective-permute-start | bytes 3145736 | tf_op jit(solution)/shard_map/ppermute | solution.py:48
  571.7 24.5 %collective-permute-start.48 = (bf16[48,1024]{1,0:T(8,128)(2,1)S(1)}, bf16[48,1024]{1,0:T(8,128)(2,1)S(1)}, u32[]{:S(2)}, u32[]{:S(2)}) collective-permute-start(bf16[48,1024]{1,0:T(8,128)(2,1)S(1)} %constant_dynamic-slice_fusion.10), channel_id=1, source_target_pairs={{0,8},{1,9},{2,10},{3,11},{4,12},{5,13},{6,14},{7,15},{8,0},{9,1},... | collective-permute-start | bytes 294920 | tf_op jit(solution)/shard_map/ppermute | solution.py:48
  606.9 43.5 %collective-permute-start.51 = (bf16[2048,512]{1,0:T(8,128)(2,1)}, bf16[2048,512]{1,0:T(8,128)(2,1)}, u32[]{:S(2)}, u32[]{:S(2)}) collective-permute-start(bf16[2048,512]{1,0:T(8,128)(2,1)} %pad_maximum_fusion.5.refs_0_), channel_id=1, source_target_pairs={{0,4},{1,5},{2,6},{3,7},{4,0},{5,1},{6,2},{7,3},{8,12},{9,13},{10,... | collective-permute-start | bytes 6291464 | tf_op jit(solution)/shard_map/ppermute | solution.py:48
  672.8 42.2 %collective-permute-start.56 = (bf16[2048,512]{1,0:T(8,128)(2,1)S(1)}, bf16[2048,512]{1,0:T(8,128)(2,1)S(1)}, u32[]{:S(2)}, u32[]{:S(2)}) collective-permute-start(bf16[2048,512]{1,0:T(8,128)(2,1)S(1)} %pad_maximum_fusion.6.refs_0_), channel_id=1, source_target_pairs={{0,4},{1,5},{2,6},{3,7},{4,0},{5,1},{6,2},{7,3},{8,12},{9,13},{10,... | collective-permute-start | bytes 6291464 | tf_op jit(solution)/shard_map/ppermute | solution.py:48
  (129 other events, 962.7 us)

commit v4 on v3

--- a/solution.py
+++ b/solution.py
@@ -160,7 +160,7 @@
     def gradient_task(self, send, own_part, axis, order, out):
         half = self.Z // 2
         over_group = order is None
-        halvings = [(0, 1), (1, 0), (2, 0)]
+        halvings = [(0, 1), (2, 0), (1, 0)]
         sent = yield send
         got = yield [self.shift_y(p, -i - 1) for i, p in enumerate(sent)]
         acc = own_part()
@@ -288,8 +288,8 @@
                 self.tasks.remove(t)
         return live
 
-    def launch(self, live):
-        waiting = [t for t in self.tasks if t[2] is None]
+    def launch(self, live, hold=()):
+        waiting = [t for t in self.tasks if t[2] is None and not any(t[3] is o for o in hold)]
         ready, live = fence(([t[1] for t in waiting], live))
         for t, a in zip(waiting, ready):
             t[2] = t[0].send(a)
@@ -372,7 +372,7 @@
         out_shape=[jax.ShapeDtypeStruct(s, d) for s, d, _, _ in outs],
         scratch_shapes=list(scratch),
         compiler_params=pltpu.CompilerParams(vmem_limit_bytes=VMEM_LIMIT),
-        cost_estimate=pl.CostEstimate(flops=flops, bytes_accessed=total, transcendentals=0),
+        cost_estimate=pl.CostEstimate(flops=0, bytes_accessed=1024, transcendentals=0),
         name=name,
     )(*arrays)
 
@@ -517,13 +517,11 @@
         gain_out[...] += part
 
 
-def input_grad_body(gg, xb, tb, wg, wx, wt, spill, rows, out, gain_out):
+def input_grad_body(gg, xb, tb, wg, wx, wt, spill, out):
     total = bdot(gg[...], wg[...], NN) + bdot(xb[...], wx[...], NN) + bdot(tb[...], wt[...], NN)
     T = out.shape[1]
     out[0, : T - HALO, :] = total[: T - HALO].astype(bf16)
     out[0, T - HALO :, :] = (total[T - HALO : T] + spill[0].astype(f32)).astype(bf16)
-    part = jnp.sum(total * rows[...].astype(f32), axis=0, keepdims=True)
-    gain_out[0] = jnp.concatenate([part, jnp.zeros((7, part.shape[1]), f32)], axis=0)
 
 
 def intra_backward_body(
@@ -968,7 +966,9 @@
     s_range = s_block[:, 0]
     for b in range(1, nb):
         s_range = s_block[:, b] + carry_wide[:, b] * s_range
-    s_range, x, bc, cum, row, step = stages.settle([s_range, x, bc, cum, row, step])
+    s_range, x, bc, cum, row, step = stages.settle(
+        [s_range, x, bc, cum, row, step], leave=[at_cot]
+    )
     at_out = stages.add(g.direct_task, half_out, [1], 0)
     at_enter = stages.add(g.state_task, s_range, carry_range, spread, 1)
     x, bc, cum, row, step = stages.launch([x, bc, cum, row, step])
@@ -1151,9 +1151,20 @@
     )
     gate_far = far_rows(lambda i: in_part(gate_grad, i), g.Y)
     dxs, gate_far = stages.settle([dxs, gate_far])
-    at_gates = stages.add(
-        g.gradient_task, gate_far, lambda: in_part(gate_grad, 0), 1, (2, 1)
-    )
+    kept = {}
+
+    def gate_first():
+        kept["gate"] = in_part(gate_grad, 0)
+        return kept["gate"]
+
+    at_gates = stages.add(g.gradient_task, gate_far, gate_first, 1, (2, 1))
+
+    def gain_part(own, far, w):
+        parts = []
+        for i, p in enumerate([own] + far):
+            parts.append(jnp.sum(p.astype(f32) * g.cut(w, 1, i, g.Y).astype(f32), axis=0))
+        return jnp.concatenate(parts)
+
     while "state" not in at_leave:
         stages.launch([])
         stages.settle([])
@@ -1222,17 +1233,57 @@
 
     x_far = far_rows(x_part, g.Y)
     x_far, spill, x_flat, dt_flat, kg, sm = stages.settle([x_far, spill, x_flat, dt_flat, kg, sm])
-    at_x = stages.add(g.gradient_task, x_far, lambda: x_part(0), 1, (2, 1))
+    at_x = stages.add(g.gradient_task, x_far, lambda: x_own, 1, (2, 1))
     at_spill = stages.add(g.one_task, [spill], lambda a: g.shift_z(a, -1))
-    x_flat, dt_flat = stages.launch([x_flat, dt_flat])
+    x_flat, dt_flat, kg, sm = stages.launch([x_flat, dt_flat, kg, sm])
+    x_own = x_part(0)
     rest_back = jnp.concatenate([x_flat[:, HW:], dt_flat[:, :heads]], axis=1)
     rest = [in_part(rest_back, i) for i in range(g.Y)]
-    (rest,) = stages.settle([rest], leave=[at_gates, at_x, at_branch])
+    gate_own = kept["gate"]
+
+    def lay(a, lines):
+        flat = a.reshape(-1)
+        return jnp.pad(flat, (0, lines * own_d - flat.shape[0])).reshape(lines, own_d)
+
+    per = HW // own_d
+    lines = inner // own_d
+    pre_part = (
+        gain_part(gate_own, gate_far, w_gate)
+        + gain_part(x_own, x_far, w_packed[:HW])
+        + gain_part(rest[0], rest[1:], w_packed[HW : HW + shared + heads])
+    )
+    pre_part = g.own_first_back(pre_part) / pre_gain
+    kg = jnp.sum(kg, axis=0)[:5]
+    sm = jnp.sum(sm, axis=0)[:, :3].transpose(1, 0, 2).reshape(3, HL)
+    heads_all = lax.dynamic_update_slice(jnp.zeros((3, heads), f32), sm, (0, HL * j))
+    wide_rows = jnp.concatenate([gain_grad, kg[:, :HW]], axis=0).reshape(6, per, own_d)
+    wide_rows = lax.dynamic_update_slice(
+        jnp.zeros((6, lines, own_d), f32), wide_rows, (0, per * j, 0)
+    )
+    shared_lines = -(-5 * shared // own_d)
+    pre_lines = width // own_d
+    small = jnp.concatenate(
+        [
+            wide_rows.reshape(6 * lines, own_d),
+            lay(kg[:, HW:], shared_lines),
+            lay(heads_all, 1),
+            pre_part.reshape(pre_lines, own_d),
+        ],
+        axis=0,
+    )
+    n_rest = shared + heads
+    small = jnp.pad(small, ((0, -(n_rest + small.shape[0]) % 128), (0, 0)))
+    copies = jnp.concatenate([small] * 2, axis=1)
+    rest = [jnp.concatenate([p, copies], axis=0) for p in rest]
+    rest_far = [p.astype(bf16) for p in rest[1:]]
+    held = stages.settle([x_own, x_flat, dt_flat, rest_far, rest[0]], leave=[at_gates])
+    x_own, x_flat, dt_flat, rest_far, rest_own = held
+    at_rest = stages.add(g.gradient_task, rest_far, lambda: rest_own, 1, None)
     spill = at_spill["got"][0]
     spill, gate_grad, x_flat, dt_flat = stages.launch([spill, gate_grad, x_flat, dt_flat])
 
     NW = 512
-    n_grad, pre_grad = call(
+    (n_grad,) = call(
         input_grad_body,
         (2, width // NW),
         [
@@ -1243,50 +1294,13 @@
             (w_packed, (CW, NW), lambda s, n: (0, n)),
             (w_packed, (128, NW), lambda s, n: (CW // 128, n)),
             (spill, (1, HALO, NW), lambda s, n: (s, 0, n)),
-            (n_ext, (TE, NW), lambda s, n: (s, n)),
         ],
         [
             ((2, T, width), bf16, (1, T, NW), lambda s, n: (s, 0, n)),
-            ((2, 8, width), f32, (1, 8, NW), lambda s, n: (s, 0, n)),
         ],
         flops=2 * 2 * TE * width * (2 * HW + 128),
         name="input_grad",
     )
-
-    def lay(a, lines):
-        flat = a.reshape(-1)
-        return jnp.pad(flat, (0, lines * own_d - flat.shape[0])).reshape(lines, own_d)
-
-    per = HW // own_d
-    lines = inner // own_d
-    pre_part = g.own_first_back(jnp.sum(pre_grad, axis=(0, 1))) / pre_gain
-    kg = jnp.sum(kg, axis=0)[:5]
-    sm = jnp.sum(sm, axis=0)[:, :3].transpose(1, 0, 2).reshape(3, HL)
-    heads_all = lax.dynamic_update_slice(jnp.zeros((3, heads), f32), sm, (0, HL * j))
-    wide_rows = jnp.concatenate([gain_grad, kg[:, :HW]], axis=0).reshape(6, per, own_d)
-    wide_rows = lax.dynamic_update_slice(
-        jnp.zeros((6, lines, own_d), f32), wide_rows, (0, per * j, 0)
-    )
-    shared_lines = -(-5 * shared // own_d)
-    pre_lines = width // own_d
-    small = jnp.concatenate(
-        [
-            wide_rows.reshape(6 * lines, own_d),
-            lay(kg[:, HW:], shared_lines),
-            lay(heads_all, 1),
-            pre_part.reshape(pre_lines, own_d),
-        ],
-        axis=0,
-    )
-    n_rest = shared + heads
-    small = jnp.pad(small, ((0, -(n_rest + small.shape[0]) % 128), (0, 0)))
-    copies = jnp.concatenate([small] * 2, axis=1)
-    rest = [jnp.concatenate([p, copies], axis=0) for p in rest]
-    rest_far = [p.astype(bf16) for p in rest[1:]]
-    n_grad, rest_far = stages.settle([n_grad, rest_far], leave=[at_gates, at_outs])
-    at_rest = stages.add(g.gradient_task, rest_far, lambda: rest[0], 1, None)
-    at_ngrad = stages.add(g.scatter_task, n_grad.reshape(2, g.W, own_len, width), (1, 2))
-    stages.launch([])
 
     in_shape = (2 * inner + shared + heads, own_d)
 
@@ -1300,38 +1314,34 @@
             moves.append((i // 4, tuple(source), tuple(sizes), tuple(target)))
         return moves
 
-    in_buf, out_weight_gradient = None, None
-    todo = [(at_gates, 0), (at_x, inner)]
-    plan = iter(
-        [
-            ([at_x, at_outs, at_gates], []),
-            ([at_x], [at_rest]),
-            ([at_x, at_outs, at_ngrad], [at_rest]),
-            ([at_x, at_outs, at_ngrad, at_gates], []),
-        ]
-    )
-    while stages.tasks:
-        leave_now, _ = next(plan, ([], []))
-        stages.settle([], leave=leave_now)
-        if not stages.tasks:
-            break
+    (n_grad,) = stages.settle([n_grad], leave=[at_x])
+    at_ngrad = stages.add(g.scatter_task, n_grad.reshape(2, g.W, own_len, width), (2, 1))
+    if g.Z == 2:
         stages.launch([])
-        if out_weight_gradient is None and "done" in at_outs:
-            out_weight_gradient = place(
-                at_outs["done"], moves_of(at_outs, 0, 1), (own_d, inner), None
-            )
-        for a, first in list(todo):
-            if "done" in a:
-                in_buf = place(a["done"], moves_of(a, first, 0), in_shape, in_buf)
-                todo.remove((a, first))
-    for a, first in todo:
-        in_buf = place(a["done"], moves_of(a, first, 0), in_shape, in_buf)
-    if out_weight_gradient is None:
-        out_weight_gradient = place(at_outs["done"], moves_of(at_outs, 0, 1), (own_d, inner), None)
-    rest_done = at_rest["done"]
-    in_buf = place(
-        [rest_done], [(0, (0, 0), (n_rest, own_d), (2 * inner, 0))], in_shape, in_buf
-    )
+        stages.settle([], leave=[at_x, at_outs])
+        stages.launch([], hold=[at_gates, at_ngrad])
+        stages.settle([], leave=[at_x, at_outs])
+        stages.launch([], hold=[at_ngrad])
+    else:
+        stages.launch([])
+    stages.settle([])
+    while "done" not in at_outs:
+        stages.launch([])
+        stages.settle([])
+    stages.launch([])
+    out_weight_gradient = place(at_outs["done"], moves_of(at_outs, 0, 1), (own_d, inner), None)
+    block_output = (series + g.own_first_back(at_branch["sum"])).astype(bf16)[None]
+    out_weight_gradient, block_output = stages.settle([out_weight_gradient, block_output])
+    while "done" not in at_gates:
+        stages.launch([])
+        stages.settle([])
+    stages.launch([])
+    in_buf = place(at_gates["done"], moves_of(at_gates, 0, 0), in_shape, None)
+    (in_buf,) = stages.settle([in_buf])
+    while "sum" not in at_ngrad:
+        stages.launch([])
+        stages.settle([])
+    stages.launch([])
     n_own = g.own_first_back(at_ngrad["sum"])
     lifted_n = n_own * pre_gain[None, :]
     token_gradient = (
@@ -1339,7 +1349,21 @@
         + scale * lifted_n
         - series * scale**3 * jnp.mean(series * lifted_n, axis=-1, keepdims=True)
     )[None]
-    block_output = (series + g.own_first_back(at_branch["sum"])).astype(bf16)[None]
+    token_gradient, in_buf = stages.settle([token_gradient, in_buf])
+    while "done" not in at_x:
+        stages.launch([])
+        (in_buf,) = stages.settle([in_buf])
+    if stages.tasks:
+        stages.launch([])
+    in_buf = place(at_x["done"], moves_of(at_x, inner, 0), in_shape, in_buf)
+    while stages.tasks:
+        (in_buf,) = stages.settle([in_buf])
+        if stages.tasks:
+            stages.launch([])
+    rest_done = at_rest["done"]
+    in_buf = place(
+        [rest_done], [(0, (0, 0), (shared + heads, own_d), (2 * inner, 0))], in_shape, in_buf
+    )
     in_weight_gradient = in_buf.T
 
     small = rest_done[n_rest:].astype(f32)

time: 739 us -> 682 us (0.923)
  waiting for transfers between devices: 251 us -> 203 us
  starting transfers between devices: 67.7 us -> 59.3 us
  other arithmetic: 73.8 us -> 82.1 us
    ppermute x58, waiting for transfers between devices: 251 us -> 203 us  [move(): return lax.ppermute(a, AXES, pairs)]
    unnamed x206 -> x220, local copies, waits for them, and re-layouts: 52.2 us -> 43.3 us
    ppermute x58, starting transfers between devices: 67.7 us -> 59.3 us  [move(): return lax.ppermute(a, AXES, pairs)]
  transfers between devices with their start and end apart: 58 -> 58, of which waited for: 25 -> 22; matrix products, arithmetic and copies ran while one was open for 11% -> 14% of each run, Pallas kernels for 20% -> 22%
where the time goes in v4:
time: 682 us; the launch traced here: 676 us
  waiting for transfers between devices  203 us (30%)
  Pallas kernels  178 us (26%)
  other arithmetic  82.1 us (12%)
  matrix products  80 us (12%)
  local copies, waits for them, and re-layouts  71.2 us (10%)
  starting transfers between devices  59.3 us (9%)
    ppermute x58, waiting for transfers between devices, move(): return lax.ppermute(a, AXES, pairs)  203 us
    pallas_call x8, Pallas kernels, call(): pl.pallas_call(kernel, grid=grid, in_specs=[pl.BlockSpec(b, m) for _, b,...  141 us
    dot_general x13, matrix products, low_dot(): lax.dot_general(a.astype(bf16), b.astype(bf16), dims, preferred_element_t...  80 us
    ppermute x58, starting transfers between devices, move(): return lax.ppermute(a, AXES, pairs)  59.3 us
    unnamed x220, local copies, waits for them, and re-layouts  43.3 us
    pallas_call x8, Pallas kernels, assemble(): pl.pallas_call(kernel, in_specs=[pl.BlockSpec(memory_space=pltpu.SMEM)] +...  20.2 us
    pallas_call x4, Pallas kernels, place(): pl.pallas_call(kernel, in_specs=[pl.BlockSpec(memory_space=pltpu.SMEM)] +...  17.2 us
  transfers between devices with their start and end apart: 58, of which 22 were waited for; matrix products, arithmetic and copies ran while one was open for 14% of the time, Pallas kernels for 22%

profile of v4, /device:TPU:1, one launch (start us, length us, event | category | flops | bytes accessed | tf_op | source)
XLA Modules:
  0.0 676.3 jit_solution(10189480968954357653)
XLA Ops:
  28.6 15.6 %collective-permute-done.1 = bf16[256,2048]{1,0:T(8,128)(2,1)} collective-permute-done((bf16[256,2048]{1,0:T(8,128)(2,1)}, bf16[256,2048]{1,0:T(8,128)(2,1)}, u32[]{:S(2)}, u32[]{:S(2)}) %collective-permute-start.1) | collective-permute-done | bytes 1048608 | tf_op jit(solution)/shard_map/ppermute | solution.py:48
  89.2 7.1 %assemble.11 = bf16[2,1040,2048]{2,1,0:T(8,128)(2,1)} custom-call(s32[18]{0:T(128)S(1)} %stack.286.index, bf16[1,256,2048]{2,1,0:T(8,128)(2,1)S(1)} %copy-done.19, bf16[3,256,2048]{2,1,0:T(8,128)(2,1)} %collective-permute-done.8.refs_1_.refs_3_.refs_5_, bf16[1,256,2048]{2,1,0:T(8,128)(2,1)} %bitcast.13.refs_2_, ...), custom_call_target="tpu_custom_call" | custom-call | bytes 17039360 | tf_op jit(solution)/shard_map/assemble/pallas_call | solution.py:719
  96.3 11.5 %convolution_convert_fusion.1 = bf16[2080,896]{1,0:T(8,128)(2,1)S(1)} fusion(bf16[2080,2048]{1,0:T(8,128)(2,1)} %bitcast.285, bf16[896,2048]{1,0:T(8,128)(2,1)S(1)} %assemble.12.wx.wt), kind=kOutput, calls=%fused_computation.5 | convolution fusion | flops 7635496960 | bytes 15917056 | tf_op jit(solution)/shard_map/dot_general | solution.py:300
  117.9 22.1 %convolve.1 = (bf16[2048,512]{1,0:T(8,128)(2,1)S(1)}, bf16[2048,256]{1,0:T(8,128)(2,1)S(1)}, f32[2,4,128,512]{3,2,1,0:T(8,128)S(1)}, f32[2,2,1024,4]{3,2,1,0:T(8...) custom-call(bf16[2,1040,896]{2,1,0:T(8,128)(2,1)S(1)} %bitcast.251, ...), custom_call_target="tpu_custom_call" | custom-call | bytes 1024 | tf_op jit(solution)/shard_map/convolve/pallas_call | solution.py:367
  155.1 10.1 %convolution_convert_fusion.2 = bf16[2080,512]{1,0:T(8,128)(2,1)} fusion(bf16[2080,2048]{1,0:T(8,128)(2,1)} %bitcast.286, bf16[512,2048]{1,0:T(8,128)(2,1)S(1)} %assemble.13.wg), kind=kOutput, calls=%fused_computation.6 | convolution fusion | flops 4363141120 | bytes 12746752 | tf_op jit(solution)/shard_map/dot_general | solution.py:300
  165.3 10.9 %intra_forward.1.y = bf16[2048,512]{1,0:T(8,128)(2,1)S(1)} custom-call(bf16[2048,512]{1,0:T(8,128)(2,1)S(1)} %copy-done.10, bf16[2048,256]{1,0:T(8,128)(2,1)S(1)} %copy-done.6, f32[2,2,1024,4]{3,2,1,0:T(8,128)S(1)} %get-tuple-element.253.cum, f32[2,2,4,4,256]{4,3,2,1,0:T(4,128)S(1)} %get-tuple-element.254.row, f32[2,2,1024,4]{3,2,1,0:T(8,128)S(1)} %copy-done.14, ...), custom_call_target="tpu_custom_call" | custom-call | bytes 1024 | tf_op jit(solution)/shard_map/intra_forward/pallas_call | solution.py:367
  187.5 5.5 assemble.14
  193.1 8.3 %convolution_convert_fusion.3.og = bf16[2048,512]{1,0:T(8,128)(2,1)S(1)} fusion(bf16[2048,2048]{1,0:T(8,128)(2,1)} %bitcast.295, bf16[2048,512]{1,0:T(8,128)(2,1)S(1)} %assemble.15), kind=kOutput, calls=%fused_computation.35 | convolution fusion | flops 4296015872 | bytes 12582912 | tf_op jit(solution)/shard_map/dot_general | solution.py:300
  201.4 8.3 %join.1 = (bf16[2048,512]{1,0:T(8,128)(2,1)S(1)}, f32[2,8,1024]{2,1,0:T(8,128)S(1)}) custom-call(bf16[2048,512]{1,0:T(8,128)(2,1)S(1)} %copy-done.29, bf16[2048,256]{1,0:T(8,128)(2,1)S(1)} %copy-done.7, bf16[2,4,128,512]{3,2,1,0:T(8,128)(2,1)S(1)} %maximum_convert_fusion.enter, f32[2,2,1024,4]{3,2,1,0:T(8,128)S(1)} %get-tuple-element.253.cum, ...), custom_call_target="tpu_custom_call" | custom-call | bytes 1024 | tf_op jit(solution)/shard_map/join/pallas_call | solution.py:367
  217.0 12.0 %gates.1 = (bf16[2048,512]{1,0:T(8,128)(2,1)S(1)}, bf16[2,1040,512]{2,1,0:T(8,128)(2,1)}, bf16[2048,512]{1,0:T(8,128)(2,1)S(1)}, f32[1,512]{1,0:T(1,128)S(1)}, f32[2,4,128,512]{3,2,1,0:T(8,128)S(1)}) custom-call(bf16[2048,512]{1,0:T(8,128)(2,1)S(1)} %get-tuple-element.266.mixed, bf16[2,1040,512]{2,1,0:T(8,128)(2,1)} %bitcast.262, ...), custom_call_target="tpu_custom_call" | custom-call | bytes 1024 | tf_op jit(solution)/shard_map/gates/pallas_call | solution.py:367
  230.3 6.5 fusion.42
  249.6 6.7 fusion.34
  256.4 37.9 %intra_backward.1 = (bf16[2048,512]{1,0:T(8,128)(2,1)S(1)}, f32[2,2,1024,4]{3,2,1,0:T(8,128)S(1)}, f32[2048,256]{1,0:T(8,128)S(1)}) custom-call(bf16[2048,512]{1,0:T(8,128)(2,1)S(1)} %copy-done.11, bf16[2048,256]{1,0:T(8,128)(2,1)S(1)} %copy-done.8, bf16[2048,512]{1,0:T(8,128)(2,1)S(1)} %copy-done.26, f32[2,2,1024,4]{3,2,1,0:T(8,128)} %copy-done.4, ...), custom_call_target="tpu_custom_call" | custom-call | bytes 1024 | tf_op jit(solution)/shard_map/intra_backward/pallas_call | solution.py:367
  294.3 8.1 %add_convert_fusion.7 = bf16[1024,512]{1,0:T(8,128)(2,1)} fusion(bf16[1024,512]{1,0:T(8,128)(2,1)} %collective-permute-done.28, bf16[2048,512]{1,0:T(8,128)(2,1)S(1)} %copy-done.64, bf16[2048,2048]{1,0:T(8,128)(2,1)} %bitcast.297), kind=kOutput, calls=%fused_computation.69 | convolution fusion | flops 2149056512 | bytes 8388608 | tf_op jit(solution)/shard_map/dot_general | solution.py:300
  321.9 31.8 %finish.1 = (bf16[2,1040,768]{2,1,0:T(8,128)(2,1)}, bf16[2,1040,128]{2,1,0:T(8,128)(2,1)S(1)}, f32[2,8,768]{2,1,0:T(8,128)S(1)}, f32[2,2,8,4]{3,2,1,0:T(8,128)S(1)}) custom-call(bf16[2,1040,896]{2,1,0:T(8,128)(2,1)} %bitcast.253, bf16[2048,512]{1,0:T(8,128)(2,1)S(1)} %copy-done.12, bf16[2048,512]{1,0:T(8,128)(2,1)S(1)} %copy-done.27, ...), custom_call_target="tpu_custom_call" | custom-call | bytes 1024 | tf_op jit(solution)/shard_map/finish/pallas_call | solution.py:367
  356.2 5.9 fusion.37
  364.7 6.5 multiply_reduce_fusion.3
  374.2 5.4 multiply_reduce_fusion.1
  395.4 26.2 %collective-permute-done.34 = bf16[256,2048]{1,0:T(8,128)(2,1)} collective-permute-done((bf16[256,2048]{1,0:T(8,128)(2,1)}, bf16[256,2048]{1,0:T(8,128)(2,1)}, u32[]{:S(2)}, u32[]{:S(2)}) %collective-permute-start.34) | collective-permute-done | bytes 1048608 | tf_op jit(solution)/shard_map/ppermute | solution.py:48
  433.9 16.9 %input_grad.1 = bf16[2,1024,2048]{2,1,0:T(8,128)(2,1)} custom-call(bf16[2080,512]{1,0:T(8,128)(2,1)S(1)} %bitcast.274, bf16[2080,768]{1,0:T(8,128)(2,1)S(1)} %bitcast.271, bf16[2080,128]{1,0:T(8,128)(2,1)S(1)} %bitcast.277, bf16[512,2048]{1,0:T(8,128)(2,1)S(1)} %copy-done.24, bf16[896,2048]{1,0:T(8,128)(2,1)S(1)} %copy-done.3, ...), custom_call_target="tpu_custom_call" | custom-call | bytes 1024 | tf_op jit(solution)/shard_map/input_grad/pallas_call | solution.py:367
  450.8 9.7 %collective-permute-done.37 = bf16[512,1024]{1,0:T(8,128)(2,1)} collective-permute-done((bf16[512,1024]{1,0:T(8,128)(2,1)}, bf16[512,1024]{1,0:T(8,128)(2,1)}, u32[]{:S(2)}, u32[]{:S(2)}) %collective-permute-start.37) | collective-permute-done | bytes 1048608 | tf_op jit(solution)/shard_map/ppermute | solution.py:48
  474.8 6.4 collective-permute-done.41
  485.6 6.4 collective-permute-done.43
  493.1 5.4 fusion
  502.4 29.7 %collective-permute-done.46 = bf16[512,1024]{1,0:T(8,128)(2,1)S(1)} collective-permute-done((bf16[512,1024]{1,0:T(8,128)(2,1)S(1)}, bf16[512,1024]{1,0:T(8,128)(2,1)S(1)}, u32[]{:S(2)}, u32[]{:S(2)}) %collective-permute-start.46) | collective-permute-done | bytes 1048608 | tf_op jit(solution)/shard_map/ppermute | solution.py:48
  532.1 5.7 collective-permute-done.45
  547.8 5.2 place.4
  553.1 33.3 %collective-permute-done.50 = bf16[48,1024]{1,0:T(8,128)(2,1)S(1)} collective-permute-done((bf16[48,1024]{1,0:T(8,128)(2,1)S(1)}, bf16[48,1024]{1,0:T(8,128)(2,1)S(1)}, u32[]{:S(2)}, u32[]{:S(2)}) %collective-permute-start.50) | collective-permute-done | bytes 98336 | tf_op jit(solution)/shard_map/ppermute | solution.py:48
  593.0 5.9 place.5.refs_2_
  598.9 16.4 %collective-permute-done.53 = bf16[48,1024]{1,0:T(8,128)(2,1)S(1)} collective-permute-done((bf16[48,1024]{1,0:T(8,128)(2,1)S(1)}, bf16[48,1024]{1,0:T(8,128)(2,1)S(1)}, u32[]{:S(2)}, u32[]{:S(2)}) %collective-permute-start.53) | collective-permute-done | bytes 98336 | tf_op jit(solution)/shard_map/ppermute | solution.py:48
  626.1 35.1 %collective-permute-done.55.refs_1_ = bf16[2048,512]{1,0:T(8,128)(2,1)} collective-permute-done((bf16[2048,512]{1,0:T(8,128)(2,1)S(1)}, bf16[2048,512]{1,0:T(8,128)(2,1)}, u32[]{:S(2)}, u32[]{:S(2)}) %collective-permute-start.55) | collective-permute-done | bytes 2097184 | tf_op jit(solution)/shard_map/ppermute | solution.py:48
  666.5 5.2 place.6.refs_1_
  (519 shorter events, 245.7 us)
Async XLA Ops:
  16.7 29.3 %collective-permute-start.5 = (bf16[576,1024]{1,0:T(8,128)(2,1)}, bf16[576,1024]{1,0:T(8,128)(2,1)}, u32[]{:S(2)}, u32[]{:S(2)}) collective-permute-start(bf16[576,1024]{1,0:T(8,128)(2,1)} %slice.360), channel_id=1, source_target_pairs={{0,2},{1,3},{2,0},{3,1},{4,6},{5,7},{6,4},{7,5},{8,10},{9,11},{10,... | collective-permute-start | bytes 3538952 | tf_op jit(solution)/shard_map/ppermute | solution.py:48
  19.4 24.8 %collective-permute-start.1 = (bf16[256,2048]{1,0:T(8,128)(2,1)}, bf16[256,2048]{1,0:T(8,128)(2,1)}, u32[]{:S(2)}, u32[]{:S(2)}) collective-permute-start(bf16[256,2048]{1,0:T(8,128)(2,1)} %get-tuple-element.194), channel_id=1, source_target_pairs={{0,4},{1,5},{2,6},{3,7},{4,0},{5,1},{6,2},{7,3},{8,12},{9,13},{10,... | collective-permute-start | bytes 3145736 | tf_op jit(solution)/shard_map/ppermute | solution.py:48
  20.6 24.5 %collective-permute-start.2 = (bf16[256,2048]{1,0:T(8,128)(2,1)}, bf16[256,2048]{1,0:T(8,128)(2,1)}, u32[]{:S(2)}, u32[]{:S(2)}) collective-permute-start(bf16[256,2048]{1,0:T(8,128)(2,1)} %get-tuple-element.194), channel_id=1, source_target_pairs={{0,8},{1,9},{2,10},{3,11},{4,12},{5,13},{6,14},{7,15},{8,0},{9,1},... | collective-permute-start | bytes 3145736 | tf_op jit(solution)/shard_map/ppermute | solution.py:48
  53.6 26.9 %collective-permute-start.8 = (bf16[3,256,2048]{2,1,0:T(8,128)(2,1)}, bf16[3,256,2048]{2,1,0:T(8,128)(2,1)}, u32[]{:S(2)}, u32[]{:S(2)}) collective-permute-start(bf16[3,256,2048]{2,1,0:T(8,128)(2,1)} %pad_maximum_fusion), channel_id=1, source_target_pairs={{0,1},{1,0},{2,3},{3,2},{4,5},{5,4},{6,7},{7,6},{8,9},{9,8},{10,11... | collective-permute-start | bytes 9437192 | tf_op jit(solution)/shard_map/ppermute | solution.py:48
  86.6 25.1 %collective-permute-start.13 = (bf16[256,2048]{1,0:T(8,128)(2,1)}, bf16[256,2048]{1,0:T(8,128)(2,1)S(1)}, u32[]{:S(2)}, u32[]{:S(2)}) collective-permute-start(bf16[256,2048]{1,0:T(8,128)(2,1)} %pad_maximum_fusion.10), channel_id=1, source_target_pairs={{0,4},{1,5},{2,6},{3,7},{4,0},{5,1},{6,2},{7,3},{8,12},{9,13},{10,... | collective-permute-start | bytes 3145736 | tf_op jit(solution)/shard_map/ppermute | solution.py:48
  86.9 24.8 %collective-permute-start.14 = (bf16[256,2048]{1,0:T(8,128)(2,1)}, bf16[256,2048]{1,0:T(8,128)(2,1)S(1)}, u32[]{:S(2)}, u32[]{:S(2)}) collective-permute-start(bf16[256,2048]{1,0:T(8,128)(2,1)} %pad_maximum_fusion.10), channel_id=1, source_target_pairs={{0,8},{1,9},{2,10},{3,11},{4,12},{5,13},{6,14},{7,15},{8,0},{9,1},... | collective-permute-start | bytes 3145736 | tf_op jit(solution)/shard_map/ppermute | solution.py:48
  115.4 63.2 %collective-permute-start.18 = (bf16[3,256,2048]{2,1,0:T(8,128)(2,1)}, bf16[3,256,2048]{2,1,0:T(8,128)(2,1)}, u32[]{:S(2)}, u32[]{:S(2)}) collective-permute-start(bf16[3,256,2048]{2,1,0:T(8,128)(2,1)} %pad_maximum_fusion.1), channel_id=1, source_target_pairs={{0,1},{1,0},{2,3},{3,2},{4,5},{5,4},{6,7},{7,6},{8,9},{9,8},{10,11... | collective-permute-start | bytes 9437192 | tf_op jit(solution)/shard_map/ppermute | solution.py:48
  116.6 32.1 %collective-permute-start.19 = (bf16[512,1024]{1,0:T(8,128)(2,1)}, bf16[512,1024]{1,0:T(8,128)(2,1)}, u32[]{:S(2)}, u32[]{:S(2)}) collective-permute-start(bf16[512,1024]{1,0:T(8,128)(2,1)} %assemble.9.refs_0_), channel_id=1, source_target_pairs={{0,2},{1,3},{2,0},{3,1},{4,6},{5,7},{6,4},{7,5},{8,10},{9,11},{10,... | collective-permute-start | bytes 3145736 | tf_op jit(solution)/shard_map/ppermute | solution.py:48
  145.6 31.9 %collective-permute-start.16 = (bf16[128,2048]{1,0:T(8,128)(2,1)}, bf16[128,2048]{1,0:T(8,128)(2,1)S(1)}, u32[]{:S(2)}, u32[]{:S(2)}) collective-permute-start(bf16[128,2048]{1,0:T(8,128)(2,1)} %slice.298), channel_id=1, source_target_pairs={{0,8},{1,9},{2,10},{3,11},{4,12},{5,13},{6,14},{7,15},{8,0},{9,1},... | collective-permute-start | bytes 1572872 | tf_op jit(solution)/shard_map/ppermute | solution.py:48
  145.9 31.7 %collective-permute-start.17 = (bf16[128,2048]{1,0:T(8,128)(2,1)}, bf16[128,2048]{1,0:T(8,128)(2,1)S(1)}, u32[]{:S(2)}, u32[]{:S(2)}) collective-permute-start(bf16[128,2048]{1,0:T(8,128)(2,1)} %slice.299), channel_id=1, source_target_pairs={{0,4},{1,5},{2,6},{3,7},{4,0},{5,1},{6,2},{7,3},{8,12},{9,13},{10,... | collective-permute-start | bytes 1572872 | tf_op jit(solution)/shard_map/ppermute | solution.py:48
  148.7 28.8 %collective-permute-start.20 = (bf16[1024,512]{1,0:T(8,128)(2,1)S(1)}, bf16[1024,512]{1,0:T(8,128)(2,1)S(1)}, u32[]{:S(2)}, u32[]{:S(2)}) collective-permute-start(bf16[1024,512]{1,0:T(8,128)(2,1)S(1)} %copy-done.41), channel_id=1, source_target_pairs={{0,2},{1,3},{2,0},{3,1},{4,6},{5,7},{6,4},{7,5},{8,10},{9,11},{10,... | collective-permute-start | bytes 3145736 | tf_op jit(solution)/shard_map/ppermute | solution.py:48
  149.0 28.5 %collective-permute-start.21 = (bf16[2,128,512]{2,1,0:T(8,128)(2,1)S(1)}, bf16[2,128,512]{2,1,0:T(8,128)(2,1)S(1)}, u32[]{:S(2)}, u32[]{:S(2)}) collective-permute-start(bf16[2,128,512]{2,1,0:T(8,128)(2,1)S(1)} %fusion.50), channel_id=1, source_target_pairs={{0,16},{1,17},{2,18},{3,19},{4,20},{5,21},{6,22},{7,23},{8,24},{9,... | collective-permute-start | bytes 786440 | tf_op jit(solution)/shard_map/ppermute | solution.py:48
  245.1 49.2 %collective-permute-start.29 = (bf16[4,256,2048]{2,1,0:T(8,128)(2,1)}, bf16[4,256,2048]{2,1,0:T(8,128)(2,1)}, u32[]{:S(2)}, u32[]{:S(2)}) collective-permute-start(bf16[4,256,2048]{2,1,0:T(8,128)(2,1)} %bitcast.62), channel_id=1, source_target_pairs={{0,1},{1,0},{2,3},{3,2},{4,5},{5,4},{6,7},{7,6},{8,9},{9,8},{10,11... | collective-permute-start | bytes 12582920 | tf_op jit(solution)/shard_map/ppermute | solution.py:48
  246.8 47.5 %collective-permute-start.28 = (bf16[1024,512]{1,0:T(8,128)(2,1)}, bf16[1024,512]{1,0:T(8,128)(2,1)}, u32[]{:S(2)}, u32[]{:S(2)}) collective-permute-start(bf16[1024,512]{1,0:T(8,128)(2,1)} %fusion.42), channel_id=1, source_target_pairs={{0,2},{1,3},{2,0},{3,1},{4,6},{5,7},{6,4},{7,5},{8,10},{9,11},{10,... | collective-permute-start | bytes 3145736 | tf_op jit(solution)/shard_map/ppermute | solution.py:48
  248.0 46.2 %collective-permute-start.27 = (bf16[2,128,512]{2,1,0:T(8,128)(2,1)}, bf16[2,128,512]{2,1,0:T(8,128)(2,1)S(1)}, u32[]{:S(2)}, u32[]{:S(2)}) collective-permute-start(bf16[2,128,512]{2,1,0:T(8,128)(2,1)} %fusion.49), channel_id=1, source_target_pairs={{16,0},{17,1},{18,2},{19,3},{20,4},{21,5},{22,6},{23,7},{24,8},{25... | collective-permute-start | bytes 786440 | tf_op jit(solution)/shard_map/ppermute | solution.py:48
  311.8 50.3 %collective-permute-start.31 = (bf16[2,256,2048]{2,1,0:T(8,128)(2,1)}, bf16[2,256,2048]{2,1,0:T(8,128)(2,1)}, u32[]{:S(2)}, u32[]{:S(2)}) collective-permute-start(bf16[2,256,2048]{2,1,0:T(8,128)(2,1)} %pad_maximum_fusion.2), channel_id=1, source_target_pairs={{0,4},{1,5},{2,6},{3,7},{4,0},{5,1},{6,2},{7,3},{8,12},{9,13},{10,... | collective-permute-start | bytes 6291464 | tf_op jit(solution)/shard_map/ppermute | solution.py:48
  312.9 49.3 %collective-permute-start.30 = (bf16[1024,512]{1,0:T(8,128)(2,1)}, bf16[1024,512]{1,0:T(8,128)(2,1)S(1)}, u32[]{:S(2)}, u32[]{:S(2)}) collective-permute-start(bf16[1024,512]{1,0:T(8,128)(2,1)} %add_convert_fusion.7), channel_id=1, source_target_pairs={{0,16},{1,17},{2,18},{3,19},{4,20},{5,21},{6,22},{7,23},{8,24},{9,... | collective-permute-start | bytes 3145736 | tf_op jit(solution)/shard_map/ppermute | solution.py:48
  315.6 46.5 %collective-permute-start.32 = (bf16[512,1024]{1,0:T(8,128)(2,1)}, bf16[512,1024]{1,0:T(8,128)(2,1)S(1)}, u32[]{:S(2)}, u32[]{:S(2)}) collective-permute-start(bf16[512,1024]{1,0:T(8,128)(2,1)} %fusion.34), channel_id=1, source_target_pairs={{0,2},{1,3},{2,0},{3,1},{4,6},{5,7},{6,4},{7,5},{8,10},{9,11},{10,... | collective-permute-start | bytes 3145736 | tf_op jit(solution)/shard_map/ppermute | solution.py:48
  381.1 40.4 %collective-permute-start.34 = (bf16[256,2048]{1,0:T(8,128)(2,1)}, bf16[256,2048]{1,0:T(8,128)(2,1)}, u32[]{:S(2)}, u32[]{:S(2)}) collective-permute-start(bf16[256,2048]{1,0:T(8,128)(2,1)} %fusion.45), channel_id=1, source_target_pairs={{0,8},{1,9},{2,10},{3,11},{4,12},{5,13},{6,14},{7,15},{8,0},{9,1},... | collective-permute-start | bytes 3145736 | tf_op jit(solution)/shard_map/ppermute | solution.py:48
  381.5 40.1 %collective-permute-start.35 = (bf16[512,1024]{1,0:T(8,128)(2,1)}, bf16[512,1024]{1,0:T(8,128)(2,1)}, u32[]{:S(2)}, u32[]{:S(2)}) collective-permute-start(bf16[512,1024]{1,0:T(8,128)(2,1)} %fusion.37), channel_id=1, source_target_pairs={{0,2},{1,3},{2,0},{3,1},{4,6},{5,7},{6,4},{7,5},{8,10},{9,11},{10,... | collective-permute-start | bytes 3145736 | tf_op jit(solution)/shard_map/ppermute | solution.py:48
  389.3 61.5 %collective-permute-start.38 = (bf16[512,1024]{1,0:T(8,128)(2,1)}, bf16[512,1024]{1,0:T(8,128)(2,1)}, u32[]{:S(2)}, u32[]{:S(2)}) collective-permute-start(bf16[512,1024]{1,0:T(8,128)(2,1)} %get-tuple-element.310), channel_id=1, source_target_pairs={{0,16},{1,17},{2,18},{3,19},{4,20},{5,21},{6,22},{7,23},{8,24},{9,... | collective-permute-start | bytes 3145736 | tf_op jit(solution)/shard_map/ppermute | solution.py:48
  426.4 34.0 %collective-permute-start.37 = (bf16[512,1024]{1,0:T(8,128)(2,1)}, bf16[512,1024]{1,0:T(8,128)(2,1)}, u32[]{:S(2)}, u32[]{:S(2)}) collective-permute-start(bf16[512,1024]{1,0:T(8,128)(2,1)} %pad_maximum_fusion.13), channel_id=1, source_target_pairs={{0,8},{1,9},{2,10},{3,11},{4,12},{5,13},{6,14},{7,15},{8,0},{9,1},... | collective-permute-start | bytes 3145736 | tf_op jit(solution)/shard_map/ppermute | solution.py:48
  474.4 57.7 %collective-permute-start.44 = (bf16[512,2048]{1,0:T(8,128)(2,1)S(1)}, bf16[512,2048]{1,0:T(8,128)(2,1)}, u32[]{:S(2)}, u32[]{:S(2)}) collective-permute-start(bf16[512,2048]{1,0:T(8,128)(2,1)S(1)} %pad_maximum_fusion.3.refs_0_), channel_id=1, source_target_pairs={{0,4},{1,5},{2,6},{3,7},{4,0},{5,1},{6,2},{7,3},{8,12},{9,13},{10,... | collective-permute-start | bytes 6291464 | tf_op jit(solution)/shard_map/ppermute | solution.py:48
  484.3 47.8 %collective-permute-start.46 = (bf16[512,1024]{1,0:T(8,128)(2,1)S(1)}, bf16[512,1024]{1,0:T(8,128)(2,1)S(1)}, u32[]{:S(2)}, u32[]{:S(2)}) collective-permute-start(bf16[512,1024]{1,0:T(8,128)(2,1)S(1)} %copy-done.73), channel_id=1, source_target_pairs={{0,16},{1,17},{2,18},{3,19},{4,20},{5,21},{6,22},{7,23},{8,24},{9,... | collective-permute-start | bytes 3145736 | tf_op jit(solution)/shard_map/ppermute | solution.py:48
  493.0 44.8 %collective-permute-start.45 = (bf16[1024,512]{1,0:T(8,128)(2,1)S(1)}, bf16[1024,512]{1,0:T(8,128)(2,1)S(1)}, u32[]{:S(2)}, u32[]{:S(2)}) collective-permute-start(bf16[1024,512]{1,0:T(8,128)(2,1)S(1)} %pad_maximum_fusion.14), channel_id=1, source_target_pairs={{0,8},{1,9},{2,10},{3,11},{4,12},{5,13},{6,14},{7,15},{8,0},{9,1},... | collective-permute-start | bytes 3145736 | tf_op jit(solution)/shard_map/ppermute | solution.py:48
  500.6 31.6 %collective-permute-start.47 = (bf16[48,1024]{1,0:T(8,128)(2,1)S(1)}, bf16[48,1024]{1,0:T(8,128)(2,1)S(1)}, u32[]{:S(2)}, u32[]{:S(2)}) collective-permute-start(bf16[48,1024]{1,0:T(8,128)(2,1)S(1)} %constant_dynamic-slice_fusion.12), channel_id=1, source_target_pairs={{0,4},{1,5},{2,6},{3,7},{4,0},{5,1},{6,2},{7,3},{8,12},{9,13},{10,... | collective-permute-start | bytes 294920 | tf_op jit(solution)/shard_map/ppermute | solution.py:48
  540.7 45.6 %collective-permute-start.48 = (bf16[2048,512]{1,0:T(8,128)(2,1)}, bf16[2048,512]{1,0:T(8,128)(2,1)}, u32[]{:S(2)}, u32[]{:S(2)}) collective-permute-start(bf16[2048,512]{1,0:T(8,128)(2,1)} %pad_maximum_fusion.4.refs_0_), channel_id=1, source_target_pairs={{0,4},{1,5},{2,6},{3,7},{4,0},{5,1},{6,2},{7,3},{8,12},{9,13},{10,... | collective-permute-start | bytes 6291464 | tf_op jit(solution)/shard_map/ppermute | solution.py:48
  541.2 47.2 %collective-permute-start.51 = (bf16[2,256,2048]{2,1,0:T(8,128)(2,1)}, bf16[2,256,2048]{2,1,0:T(8,128)(2,1)}, u32[]{:S(2)}, u32[]{:S(2)}) collective-permute-start(bf16[2,256,2048]{2,1,0:T(8,128)(2,1)} %pad_maximum_fusion.5), channel_id=1, source_target_pairs={{0,8},{1,9},{2,10},{3,11},{4,12},{5,13},{6,14},{7,15},{8,0},{9,1},... | collective-permute-start | bytes 6291464 | tf_op jit(solution)/shard_map/ppermute | solution.py:48
  543.7 42.6 %collective-permute-start.49 = (bf16[512,512]{1,0:T(8,128)(2,1)S(1)}, bf16[512,512]{1,0:T(8,128)(2,1)S(1)}, u32[]{:S(2)}, u32[]{:S(2)}) collective-permute-start(bf16[512,512]{1,0:T(8,128)(2,1)S(1)} %copy-done.87), channel_id=1, source_target_pairs={{0,1},{1,0},{2,3},{3,2},{4,5},{5,4},{6,7},{7,6},{8,9},{9,8},{10,11... | collective-permute-start | bytes 1572872 | tf_op jit(solution)/shard_map/ppermute | solution.py:48
  546.4 39.9 %collective-permute-start.50 = (bf16[48,1024]{1,0:T(8,128)(2,1)S(1)}, bf16[48,1024]{1,0:T(8,128)(2,1)S(1)}, u32[]{:S(2)}, u32[]{:S(2)}) collective-permute-start(bf16[48,1024]{1,0:T(8,128)(2,1)S(1)} %add_convert_fusion.13), channel_id=1, source_target_pairs={{0,16},{1,17},{2,18},{3,19},{4,20},{5,21},{6,22},{7,23},{8,24},{9,... | collective-permute-start | bytes 294920 | tf_op jit(solution)/shard_map/ppermute | solution.py:48
  591.5 24.9 %collective-permute-start.54 = (bf16[256,2048]{1,0:T(8,128)(2,1)}, bf16[256,2048]{1,0:T(8,128)(2,1)}, u32[]{:S(2)}, u32[]{:S(2)}) collective-permute-start(bf16[256,2048]{1,0:T(8,128)(2,1)} %fusion.46), channel_id=1, source_target_pairs={{0,4},{1,5},{2,6},{3,7},{4,0},{5,1},{6,2},{7,3},{8,12},{9,13},{10,... | collective-permute-start | bytes 3145736 | tf_op jit(solution)/shard_map/ppermute | solution.py:48
  618.0 43.2 %collective-permute-start.55 = (bf16[2048,512]{1,0:T(8,128)(2,1)S(1)}, bf16[2048,512]{1,0:T(8,128)(2,1)}, u32[]{:S(2)}, u32[]{:S(2)}) collective-permute-start(bf16[2048,512]{1,0:T(8,128)(2,1)S(1)} %pad_maximum_fusion.6.refs_0_), channel_id=1, source_target_pairs={{0,4},{1,5},{2,6},{3,7},{4,0},{5,1},{6,2},{7,3},{8,12},{9,13},{10,... | collective-permute-start | bytes 6291464 | tf_op jit(solution)/shard_map/ppermute | solution.py:48
  (135 other events, 983.6 us)

commit v5 on v4

--- a/solution.py
+++ b/solution.py
@@ -367,7 +367,10 @@
     return pl.pallas_call(
         kernel,
         grid=grid,
-        in_specs=[pl.BlockSpec(b, m) for _, b, m in ins],
+        in_specs=[
+            pl.BlockSpec(memory_space=pltpu.SMEM) if b is None else pl.BlockSpec(b, m)
+            for _, b, m in ins
+        ],
         out_specs=[pl.BlockSpec(b, m) for _, _, b, m in outs],
         out_shape=[jax.ShapeDtypeStruct(s, d) for s, d, _, _ in outs],
         scratch_shapes=list(scratch),
@@ -515,6 +518,43 @@
     @pl.when(pl.program_id(1) > 0)
     def _():
         gain_out[...] += part
+
+
+def small_body(Y, HW, HL, heads, place_ref, *refs):
+    pairs, (gain, kg, sm, pre_gain), out = refs[: 5 * Y], refs[5 * Y : -1], refs[-1]
+    j, y = place_ref[0], place_ref[1]
+    own_d = out.shape[1]
+    per = HW // own_d
+    lines = per * (heads // HL)
+    shared = kg.shape[2] - HW
+    out[...] = jnp.zeros_like(out)
+    both = kg[0] + kg[1]
+    for q in range(per):
+        lanes = slice(q * own_d, (q + 1) * own_d)
+        out[pl.ds(per * j + q, 1), :] = gain[:, lanes]
+        for k in range(5):
+            out[pl.ds((k + 1) * lines + per * j + q, 1), :] = both[k : k + 1, lanes]
+    at = 6 * lines
+    out[at : at + 5, :shared] = both[:5, HW:]
+    lane = lax.broadcasted_iota(jnp.int32, (1, own_d), 1)
+    row = jnp.zeros((1, own_d), f32)
+    for k in range(3):
+        for h in range(HL):
+            value = sm[0, h // GH, k : k + 1, h % GH : h % GH + 1]
+            value = value + sm[1, h // GH, k : k + 1, h % GH : h % GH + 1]
+            row = jnp.where(lane == k * heads + HL * j + h, value, row)
+    out[at + 5 : at + 6, :] = row
+    for i in range(Y):
+        wg, pg, wp, px, pr = pairs[5 * i : 5 * i + 5]
+        n = pr.shape[0]
+        total = jnp.sum(wg[...].astype(f32) * pg[...].astype(f32), axis=0, keepdims=True)
+        total += jnp.sum(wp[:HW, :].astype(f32) * px[...].astype(f32), axis=0, keepdims=True)
+        total += jnp.sum(wp[HW : HW + n, :].astype(f32) * pr[...].astype(f32), axis=0, keepdims=True)
+        rows = total.shape[1] // own_d
+        first = lax.rem(y - i + Y, Y) * rows
+        for q in range(rows):
+            part = total[:, q * own_d : (q + 1) * own_d]
+            out[pl.ds(at + 6 + first + q, 1), :] = part / pre_gain[pl.ds(first + q, 1), :]
 
 
 def input_grad_body(gg, xb, tb, wg, wx, wt, spill, out):
@@ -1159,12 +1199,6 @@
 
     at_gates = stages.add(g.gradient_task, gate_far, gate_first, 1, (2, 1))
 
-    def gain_part(own, far, w):
-        parts = []
-        for i, p in enumerate([own] + far):
-            parts.append(jnp.sum(p.astype(f32) * g.cut(w, 1, i, g.Y).astype(f32), axis=0))
-        return jnp.concatenate(parts)
-
     while "state" not in at_leave:
         stages.launch([])
         stages.settle([])
@@ -1241,38 +1275,31 @@
     rest = [in_part(rest_back, i) for i in range(g.Y)]
     gate_own = kept["gate"]
 
-    def lay(a, lines):
-        flat = a.reshape(-1)
-        return jnp.pad(flat, (0, lines * own_d - flat.shape[0])).reshape(lines, own_d)
-
-    per = HW // own_d
+    n_rest = shared + heads
     lines = inner // own_d
-    pre_part = (
-        gain_part(gate_own, gate_far, w_gate)
-        + gain_part(x_own, x_far, w_packed[:HW])
-        + gain_part(rest[0], rest[1:], w_packed[HW : HW + shared + heads])
-    )
-    pre_part = g.own_first_back(pre_part) / pre_gain
-    kg = jnp.sum(kg, axis=0)[:5]
-    sm = jnp.sum(sm, axis=0)[:, :3].transpose(1, 0, 2).reshape(3, HL)
-    heads_all = lax.dynamic_update_slice(jnp.zeros((3, heads), f32), sm, (0, HL * j))
-    wide_rows = jnp.concatenate([gain_grad, kg[:, :HW]], axis=0).reshape(6, per, own_d)
-    wide_rows = lax.dynamic_update_slice(
-        jnp.zeros((6, lines, own_d), f32), wide_rows, (0, per * j, 0)
-    )
-    shared_lines = -(-5 * shared // own_d)
     pre_lines = width // own_d
-    small = jnp.concatenate(
-        [
-            wide_rows.reshape(6 * lines, own_d),
-            lay(kg[:, HW:], shared_lines),
-            lay(heads_all, 1),
-            pre_part.reshape(pre_lines, own_d),
-        ],
-        axis=0,
-    )
-    n_rest = shared + heads
-    small = jnp.pad(small, ((0, -(n_rest + small.shape[0]) % 128), (0, 0)))
+    lanes = width // g.Y
+    n_small = 6 * lines + 6 + pre_lines
+    n_small += -(n_rest + n_small) % 128
+    ins = [(jnp.stack([j, g.y]).astype(jnp.int32), None, None)]
+    for i in range(g.Y):
+        for a, rows, col in (
+            (w_gate, HW, i),
+            (([gate_own] + gate_far)[i], HW, 0),
+            (w_packed, KW, i),
+            (([x_own] + x_far)[i], HW, 0),
+            (rest[i], n_rest, 0),
+        ):
+            ins.append((a, (rows, lanes), lambda n, col=col: (0, col)))
+    for a in (gain_grad, kg, sm, pre_gain.reshape(pre_lines, own_d)):
+        ins.append((a, a.shape, lambda n, d=a.ndim: (0,) * d))
+    (small,) = call(
+        partial(small_body, g.Y, HW, HL, heads),
+        (1,),
+        ins,
+        [((n_small, own_d), f32, (n_small, own_d), lambda n: (0, 0))],
+        name="small",
+    )
     copies = jnp.concatenate([small] * 2, axis=1)
     rest = [jnp.concatenate([p, copies], axis=0) for p in rest]
     rest_far = [p.astype(bf16) for p in rest[1:]]
@@ -1370,12 +1397,10 @@
     gain_total = small[:lines].reshape(-1)
     kb = small[lines : 6 * lines].reshape(5, inner)
     at = 6 * lines
-    shared_kb = small[at : at + shared_lines].reshape(-1)[: 5 * shared].reshape(5, shared)
-    kb = jnp.concatenate([kb, shared_kb], axis=1)
+    kb = jnp.concatenate([kb, small[at : at + 5, :shared]], axis=1)
     kernel_total, bias_total = kb[:taps], kb[taps]
-    at += shared_lines
-    step_total, decay_total, skip_total = small[at, : 3 * heads].reshape(3, heads)
-    pre_total = small[at + 1 : at + 1 + pre_lines].reshape(-1)
+    step_total, decay_total, skip_total = small[at + 5, : 3 * heads].reshape(3, heads)
+    pre_total = small[at + 6 : at + 6 + pre_lines].reshape(-1)
     return (
         block_output,
         token_gradient,

time: 682 us -> 672 us (0.985)
  waiting for transfers between devices: 203 us -> 213 us
  local copies, waits for them, and re-layouts: 71.2 us -> 63.7 us
  matrix products: 80 us -> 73 us
    ppermute x58, waiting for transfers between devices: 203 us -> 213 us  [move(): return lax.ppermute(a, AXES, pairs)]
    dot_general x13, matrix products: 80 us -> 73 us  [low_dot(): lax.dot_general(a.astype(bf16), b.astype(bf16), dims, preferred_element_t...]
    unnamed x220 -> x218, local copies, waits for them, and re-layouts: 43.3 us -> 37.4 us
    pallas_call x8 -> x9, Pallas kernels: 141 us -> 144 us  [call(): pl.pallas_call(kernel, grid=grid, in_specs=[pl.BlockSpec(memory_space=plt...]
  transfers between devices with their start and end apart: 58 -> 58, of which waited for: 22 -> 24; matrix products, arithmetic and copies ran while one was open for 14% -> 13% of each run, Pallas kernels for 22% -> 23%
where the time goes in v5:
time: 672 us; the launch traced here: 667 us
  waiting for transfers between devices  213 us (32%)
  Pallas kernels  181 us (27%)
  other arithmetic  77.7 us (12%)
  matrix products  73 us (11%)
  local copies, waits for them, and re-layouts  63.7 us (9%)
  starting transfers between devices  56.3 us (8%)
    ppermute x58, waiting for transfers between devices, move(): return lax.ppermute(a, AXES, pairs)  213 us
    pallas_call x9, Pallas kernels, call(): pl.pallas_call(kernel, grid=grid, in_specs=[pl.BlockSpec(memory_space=plt...  144 us
    dot_general x13, matrix products, low_dot(): lax.dot_general(a.astype(bf16), b.astype(bf16), dims, preferred_element_t...  73 us
    ppermute x58, starting transfers between devices, move(): return lax.ppermute(a, AXES, pairs)  56.3 us
    unnamed x218, local copies, waits for them, and re-layouts  37.4 us
    pallas_call x8, Pallas kernels, assemble(): pl.pallas_call(kernel, in_specs=[pl.BlockSpec(memory_space=pltpu.SMEM)] +...  20.2 us
    pallas_call x4, Pallas kernels, place(): pl.pallas_call(kernel, in_specs=[pl.BlockSpec(memory_space=pltpu.SMEM)] +...  17.2 us
  transfers between devices with their start and end apart: 58, of which 24 were waited for; matrix products, arithmetic and copies ran while one was open for 13% of the time, Pallas kernels for 23%

profile of v5, /device:TPU:1, one launch (start us, length us, event | category | flops | bytes accessed | tf_op | source)
XLA Modules:
  0.0 667.1 jit_solution(11120595940498374727)
XLA Ops:
  28.6 15.7 %collective-permute-done.1 = bf16[256,2048]{1,0:T(8,128)(2,1)} collective-permute-done((bf16[256,2048]{1,0:T(8,128)(2,1)}, bf16[256,2048]{1,0:T(8,128)(2,1)}, u32[]{:S(2)}, u32[]{:S(2)}) %collective-permute-start.1) | collective-permute-done | bytes 1048608 | tf_op jit(solution)/shard_map/ppermute | solution.py:48
  89.1 7.2 %assemble.11 = bf16[2,1040,2048]{2,1,0:T(8,128)(2,1)} custom-call(s32[18]{0:T(128)S(1)} %stack.295.index, bf16[1,256,2048]{2,1,0:T(8,128)(2,1)S(1)} %copy-done.21, bf16[3,256,2048]{2,1,0:T(8,128)(2,1)} %collective-permute-done.8.refs_1_.refs_3_.refs_5_, bf16[1,256,2048]{2,1,0:T(8,128)(2,1)} %bitcast.13.refs_2_, ...), custom_call_target="tpu_custom_call" | custom-call | bytes 17039360 | tf_op jit(solution)/shard_map/assemble/pallas_call | solution.py:759
  96.2 11.5 %convolution_convert_fusion.1 = bf16[2080,896]{1,0:T(8,128)(2,1)S(1)} fusion(bf16[2080,2048]{1,0:T(8,128)(2,1)} %bitcast.282, bf16[896,2048]{1,0:T(8,128)(2,1)S(1)} %assemble.12.refs_2_.refs_7_.wx.wt), kind=kOutput, calls=%fused_computation.5 | convolution fusion | flops 7635496960 | bytes 15917056 | tf_op jit(solution)/shard_map/dot_general | solution.py:300
  117.8 22.1 %convolve.1 = (bf16[2048,512]{1,0:T(8,128)(2,1)S(1)}, bf16[2048,256]{1,0:T(8,128)(2,1)S(1)}, f32[2,4,128,512]{3,2,1,0:T(8,128)S(1)}, f32[2,2,1024,4]{3,2,1,0:T(8...) custom-call(bf16[2,1040,896]{2,1,0:T(8,128)(2,1)S(1)} %bitcast.248, ...), custom_call_target="tpu_custom_call" | custom-call | bytes 1024 | tf_op jit(solution)/shard_map/convolve/pallas_call | solution.py:367
  155.0 10.1 %convolution_convert_fusion.2 = bf16[2080,512]{1,0:T(8,128)(2,1)} fusion(bf16[2080,2048]{1,0:T(8,128)(2,1)} %bitcast.283, bf16[512,2048]{1,0:T(8,128)(2,1)S(1)} %assemble.13.refs_0_.refs_5_.wg), kind=kOutput, calls=%fused_computation.6 | convolution fusion | flops 4363141120 | bytes 12746752 | tf_op jit(solution)/shard_map/dot_general | solution.py:300
  165.2 10.9 %intra_forward.1.y = bf16[2048,512]{1,0:T(8,128)(2,1)S(1)} custom-call(bf16[2048,512]{1,0:T(8,128)(2,1)S(1)} %copy-done.12, bf16[2048,256]{1,0:T(8,128)(2,1)S(1)} %copy-done.8, f32[2,2,1024,4]{3,2,1,0:T(8,128)S(1)} %get-tuple-element.253.cum, f32[2,2,4,4,256]{4,3,2,1,0:T(4,128)S(1)} %get-tuple-element.254.row, f32[2,2,1024,4]{3,2,1,0:T(8,128)S(1)} %copy-done.16, ...), custom_call_target="tpu_custom_call" | custom-call | bytes 1024 | tf_op jit(solution)/shard_map/intra_forward/pallas_call | solution.py:367
  187.4 5.5 assemble.14
  192.9 8.3 %convolution_convert_fusion.3.og = bf16[2048,512]{1,0:T(8,128)(2,1)S(1)} fusion(bf16[2048,2048]{1,0:T(8,128)(2,1)} %bitcast.292, bf16[2048,512]{1,0:T(8,128)(2,1)S(1)} %assemble.15), kind=kOutput, calls=%fused_computation.35 | convolution fusion | flops 4296015872 | bytes 12582912 | tf_op jit(solution)/shard_map/dot_general | solution.py:300
  201.3 8.3 %join.1 = (bf16[2048,512]{1,0:T(8,128)(2,1)S(1)}, f32[2,8,1024]{2,1,0:T(8,128)S(1)}) custom-call(bf16[2048,512]{1,0:T(8,128)(2,1)S(1)} %copy-done.29, bf16[2048,256]{1,0:T(8,128)(2,1)S(1)} %copy-done.9, bf16[2,4,128,512]{3,2,1,0:T(8,128)(2,1)S(1)} %maximum_convert_fusion.enter, f32[2,2,1024,4]{3,2,1,0:T(8,128)S(1)} %get-tuple-element.253.cum, ...), custom_call_target="tpu_custom_call" | custom-call | bytes 1024 | tf_op jit(solution)/shard_map/join/pallas_call | solution.py:367
  216.9 12.0 %gates.1 = (bf16[2048,512]{1,0:T(8,128)(2,1)S(1)}, bf16[2,1040,512]{2,1,0:T(8,128)(2,1)}, bf16[2048,512]{1,0:T(8,128)(2,1)S(1)}, f32[1,512]{1,0:T(1,128)S(1)}, f32[2,4,128,512]{3,2,1,0:T(8,128)S(1)}) custom-call(bf16[2048,512]{1,0:T(8,128)(2,1)S(1)} %get-tuple-element.266.mixed, bf16[2,1040,512]{2,1,0:T(8,128)(2,1)} %bitcast.259, ...), custom_call_target="tpu_custom_call" | custom-call | bytes 1024 | tf_op jit(solution)/shard_map/gates/pallas_call | solution.py:367
  230.1 6.5 fusion.42
  249.5 6.7 %fusion.34.refs_6_ = bf16[512,1024]{1,0:T(8,128)(2,1)} fusion(bf16[2080,512]{1,0:T(8,128)(2,1)} %bitcast.269, bf16[2080,2048]{1,0:T(8,128)(2,1)} %bitcast.284), kind=kOutput, calls=%fused_computation.69 | convolution fusion | flops 2181562368 | bytes 7438336 | tf_op jit(solution)/shard_map/dot_general | solution.py:300
  256.3 37.9 %intra_backward.1 = (bf16[2048,512]{1,0:T(8,128)(2,1)S(1)}, f32[2,2,1024,4]{3,2,1,0:T(8,128)S(1)}, f32[2048,256]{1,0:T(8,128)S(1)}) custom-call(bf16[2048,512]{1,0:T(8,128)(2,1)S(1)} %copy-done.13, bf16[2048,256]{1,0:T(8,128)(2,1)S(1)} %copy-done.10, bf16[2048,512]{1,0:T(8,128)(2,1)S(1)} %copy-done.26, f32[2,2,1024,4]{3,2,1,0:T(8,128)} %copy-done.4, ...), custom_call_target="tpu_custom_call" | custom-call | bytes 1024 | tf_op jit(solution)/shard_map/intra_backward/pallas_call | solution.py:367
  294.3 8.0 %add_convert_fusion.7 = bf16[1024,512]{1,0:T(8,128)(2,1)} fusion(bf16[1024,512]{1,0:T(8,128)(2,1)} %collective-permute-done.28, bf16[2048,512]{1,0:T(8,128)(2,1)S(1)} %copy-done.64, bf16[2048,2048]{1,0:T(8,128)(2,1)} %bitcast.294), kind=kOutput, calls=%fused_computation.65 | convolution fusion | flops 2149056512 | bytes 8388608 | tf_op jit(solution)/shard_map/dot_general | solution.py:300
  312.9 5.3 fusion.10.refs_1_
  321.3 31.8 %finish.1 = (bf16[2,1040,768]{2,1,0:T(8,128)(2,1)}, bf16[2,1040,128]{2,1,0:T(8,128)(2,1)S(1)}, f32[2,8,768]{2,1,0:T(8,128)S(1)}, f32[2,2,8,4]{3,2,1,0:T(8,128)S(1)}) custom-call(bf16[2,1040,896]{2,1,0:T(8,128)(2,1)} %bitcast.250, bf16[2048,512]{1,0:T(8,128)(2,1)S(1)} %copy-done.14, bf16[2048,512]{1,0:T(8,128)(2,1)S(1)} %copy-done.27, ...), custom_call_target="tpu_custom_call" | custom-call | bytes 1024 | tf_op jit(solution)/shard_map/finish/pallas_call | solution.py:367
  360.3 6.7 %collective-permute-done.30 = bf16[1024,512]{1,0:T(8,128)(2,1)S(1)} collective-permute-done((bf16[1024,512]{1,0:T(8,128)(2,1)S(1)}, bf16[1024,512]{1,0:T(8,128)(2,1)S(1)}, u32[]{:S(2)}, u32[]{:S(2)}) %collective-permute-start.30) | collective-permute-done | bytes 1048608 | tf_op jit(solution)/shard_map/ppermute | solution.py:48
  386.8 29.0 %collective-permute-done.34 = bf16[256,2048]{1,0:T(8,128)(2,1)S(1)} collective-permute-done((bf16[256,2048]{1,0:T(8,128)(2,1)S(1)}, bf16[256,2048]{1,0:T(8,128)(2,1)S(1)}, u32[]{:S(2)}, u32[]{:S(2)}) %collective-permute-start.34) | collective-permute-done | bytes 1048608 | tf_op jit(solution)/shard_map/ppermute | solution.py:48
  423.9 16.6 %input_grad.1 = bf16[2,1024,2048]{2,1,0:T(8,128)(2,1)} custom-call(bf16[2080,512]{1,0:T(8,128)(2,1)S(1)} %bitcast.271, bf16[2080,768]{1,0:T(8,128)(2,1)S(1)} %bitcast.268, bf16[2080,128]{1,0:T(8,128)(2,1)S(1)} %bitcast.274, bf16[512,2048]{1,0:T(8,128)(2,1)S(1)} %copy-done.6, bf16[896,2048]{1,0:T(8,128)(2,1)S(1)} %copy-done.2, ...), custom_call_target="tpu_custom_call" | custom-call | bytes 1024 | tf_op jit(solution)/shard_map/input_grad/pallas_call | solution.py:367
  440.5 10.3 %collective-permute-done.37 = bf16[512,1024]{1,0:T(8,128)(2,1)} collective-permute-done((bf16[512,1024]{1,0:T(8,128)(2,1)}, bf16[512,1024]{1,0:T(8,128)(2,1)}, u32[]{:S(2)}, u32[]{:S(2)}) %collective-permute-start.37) | collective-permute-done | bytes 1048608 | tf_op jit(solution)/shard_map/ppermute | solution.py:48
  465.6 6.3 collective-permute-done.41
  476.4 6.9 %collective-permute-done.43 = bf16[96,1024]{1,0:T(8,128)(2,1)} collective-permute-done((bf16[96,1024]{1,0:T(8,128)(2,1)}, bf16[96,1024]{1,0:T(8,128)(2,1)}, u32[]{:S(2)}, u32[]{:S(2)}) %collective-permute-start.43) | collective-permute-done | bytes 196640 | tf_op jit(solution)/shard_map/ppermute | solution.py:48
  484.4 5.4 fusion
  494.2 28.7 %collective-permute-done.46 = bf16[512,1024]{1,0:T(8,128)(2,1)S(1)} collective-permute-done((bf16[512,1024]{1,0:T(8,128)(2,1)S(1)}, bf16[512,1024]{1,0:T(8,128)(2,1)S(1)}, u32[]{:S(2)}, u32[]{:S(2)}) %collective-permute-start.46) | collective-permute-done | bytes 1048608 | tf_op jit(solution)/shard_map/ppermute | solution.py:48
  522.9 5.7 collective-permute-done.45
  538.9 5.2 place.4
  544.2 33.0 %collective-permute-done.50 = bf16[48,1024]{1,0:T(8,128)(2,1)S(1)} collective-permute-done((bf16[48,1024]{1,0:T(8,128)(2,1)S(1)}, bf16[48,1024]{1,0:T(8,128)(2,1)S(1)}, u32[]{:S(2)}, u32[]{:S(2)}) %collective-permute-start.50) | collective-permute-done | bytes 98336 | tf_op jit(solution)/shard_map/ppermute | solution.py:48
  583.8 5.9 place.5.refs_2_
  589.7 16.4 %collective-permute-done.53 = bf16[48,1024]{1,0:T(8,128)(2,1)S(1)} collective-permute-done((bf16[48,1024]{1,0:T(8,128)(2,1)S(1)}, bf16[48,1024]{1,0:T(8,128)(2,1)S(1)}, u32[]{:S(2)}, u32[]{:S(2)}) %collective-permute-start.53) | collective-permute-done | bytes 98336 | tf_op jit(solution)/shard_map/ppermute | solution.py:48
  616.9 35.2 %collective-permute-done.55.refs_1_ = bf16[2048,512]{1,0:T(8,128)(2,1)} collective-permute-done((bf16[2048,512]{1,0:T(8,128)(2,1)S(1)}, bf16[2048,512]{1,0:T(8,128)(2,1)}, u32[]{:S(2)}, u32[]{:S(2)}) %collective-permute-start.55) | collective-permute-done | bytes 2097184 | tf_op jit(solution)/shard_map/ppermute | solution.py:48
  652.2 5.1 collective-permute-start.57
  657.3 5.2 place.6.refs_1_
  (497 shorter events, 234.8 us)
Async XLA Ops:
  16.7 29.3 %collective-permute-start.5 = (bf16[576,1024]{1,0:T(8,128)(2,1)}, bf16[576,1024]{1,0:T(8,128)(2,1)}, u32[]{:S(2)}, u32[]{:S(2)}) collective-permute-start(bf16[576,1024]{1,0:T(8,128)(2,1)} %slice.307), channel_id=1, source_target_pairs={{0,2},{1,3},{2,0},{3,1},{4,6},{5,7},{6,4},{7,5},{8,10},{9,11},{10,... | collective-permute-start | bytes 3538952 | tf_op jit(solution)/shard_map/ppermute | solution.py:48
  19.4 24.8 %collective-permute-start.1 = (bf16[256,2048]{1,0:T(8,128)(2,1)}, bf16[256,2048]{1,0:T(8,128)(2,1)}, u32[]{:S(2)}, u32[]{:S(2)}) collective-permute-start(bf16[256,2048]{1,0:T(8,128)(2,1)} %get-tuple-element.194), channel_id=1, source_target_pairs={{0,4},{1,5},{2,6},{3,7},{4,0},{5,1},{6,2},{7,3},{8,12},{9,13},{10,... | collective-permute-start | bytes 3145736 | tf_op jit(solution)/shard_map/ppermute | solution.py:48
  20.6 24.5 %collective-permute-start.2 = (bf16[256,2048]{1,0:T(8,128)(2,1)}, bf16[256,2048]{1,0:T(8,128)(2,1)}, u32[]{:S(2)}, u32[]{:S(2)}) collective-permute-start(bf16[256,2048]{1,0:T(8,128)(2,1)} %get-tuple-element.194), channel_id=1, source_target_pairs={{0,8},{1,9},{2,10},{3,11},{4,12},{5,13},{6,14},{7,15},{8,0},{9,1},... | collective-permute-start | bytes 3145736 | tf_op jit(solution)/shard_map/ppermute | solution.py:48
  53.6 26.8 %collective-permute-start.8 = (bf16[3,256,2048]{2,1,0:T(8,128)(2,1)}, bf16[3,256,2048]{2,1,0:T(8,128)(2,1)}, u32[]{:S(2)}, u32[]{:S(2)}) collective-permute-start(bf16[3,256,2048]{2,1,0:T(8,128)(2,1)} %pad_maximum_fusion), channel_id=1, source_target_pairs={{0,1},{1,0},{2,3},{3,2},{4,5},{5,4},{6,7},{7,6},{8,9},{9,8},{10,11... | collective-permute-start | bytes 9437192 | tf_op jit(solution)/shard_map/ppermute | solution.py:48
  86.5 25.1 %collective-permute-start.13 = (bf16[256,2048]{1,0:T(8,128)(2,1)}, bf16[256,2048]{1,0:T(8,128)(2,1)S(1)}, u32[]{:S(2)}, u32[]{:S(2)}) collective-permute-start(bf16[256,2048]{1,0:T(8,128)(2,1)} %pad_maximum_fusion.10), channel_id=1, source_target_pairs={{0,4},{1,5},{2,6},{3,7},{4,0},{5,1},{6,2},{7,3},{8,12},{9,13},{10,... | collective-permute-start | bytes 3145736 | tf_op jit(solution)/shard_map/ppermute | solution.py:48
  86.8 24.8 %collective-permute-start.14 = (bf16[256,2048]{1,0:T(8,128)(2,1)}, bf16[256,2048]{1,0:T(8,128)(2,1)S(1)}, u32[]{:S(2)}, u32[]{:S(2)}) collective-permute-start(bf16[256,2048]{1,0:T(8,128)(2,1)} %pad_maximum_fusion.10), channel_id=1, source_target_pairs={{0,8},{1,9},{2,10},{3,11},{4,12},{5,13},{6,14},{7,15},{8,0},{9,1},... | collective-permute-start | bytes 3145736 | tf_op jit(solution)/shard_map/ppermute | solution.py:48
  115.3 63.2 %collective-permute-start.18 = (bf16[3,256,2048]{2,1,0:T(8,128)(2,1)}, bf16[3,256,2048]{2,1,0:T(8,128)(2,1)}, u32[]{:S(2)}, u32[]{:S(2)}) collective-permute-start(bf16[3,256,2048]{2,1,0:T(8,128)(2,1)} %pad_maximum_fusion.1), channel_id=1, source_target_pairs={{0,1},{1,0},{2,3},{3,2},{4,5},{5,4},{6,7},{7,6},{8,9},{9,8},{10,11... | collective-permute-start | bytes 9437192 | tf_op jit(solution)/shard_map/ppermute | solution.py:48
  116.5 32.1 %collective-permute-start.19 = (bf16[512,1024]{1,0:T(8,128)(2,1)}, bf16[512,1024]{1,0:T(8,128)(2,1)}, u32[]{:S(2)}, u32[]{:S(2)}) collective-permute-start(bf16[512,1024]{1,0:T(8,128)(2,1)} %assemble.9.refs_0_), channel_id=1, source_target_pairs={{0,2},{1,3},{2,0},{3,1},{4,6},{5,7},{6,4},{7,5},{8,10},{9,11},{10,... | collective-permute-start | bytes 3145736 | tf_op jit(solution)/shard_map/ppermute | solution.py:48
  145.5 31.9 %collective-permute-start.16 = (bf16[128,2048]{1,0:T(8,128)(2,1)}, bf16[128,2048]{1,0:T(8,128)(2,1)S(1)}, u32[]{:S(2)}, u32[]{:S(2)}) collective-permute-start(bf16[128,2048]{1,0:T(8,128)(2,1)} %slice.256), channel_id=1, source_target_pairs={{0,8},{1,9},{2,10},{3,11},{4,12},{5,13},{6,14},{7,15},{8,0},{9,1},... | collective-permute-start | bytes 1572872 | tf_op jit(solution)/shard_map/ppermute | solution.py:48
  145.7 31.7 %collective-permute-start.17 = (bf16[128,2048]{1,0:T(8,128)(2,1)}, bf16[128,2048]{1,0:T(8,128)(2,1)S(1)}, u32[]{:S(2)}, u32[]{:S(2)}) collective-permute-start(bf16[128,2048]{1,0:T(8,128)(2,1)} %slice.257), channel_id=1, source_target_pairs={{0,4},{1,5},{2,6},{3,7},{4,0},{5,1},{6,2},{7,3},{8,12},{9,13},{10,... | collective-permute-start | bytes 1572872 | tf_op jit(solution)/shard_map/ppermute | solution.py:48
  148.6 28.8 %collective-permute-start.20 = (bf16[1024,512]{1,0:T(8,128)(2,1)S(1)}, bf16[1024,512]{1,0:T(8,128)(2,1)S(1)}, u32[]{:S(2)}, u32[]{:S(2)}) collective-permute-start(bf16[1024,512]{1,0:T(8,128)(2,1)S(1)} %copy-done.41), channel_id=1, source_target_pairs={{0,2},{1,3},{2,0},{3,1},{4,6},{5,7},{6,4},{7,5},{8,10},{9,11},{10,... | collective-permute-start | bytes 3145736 | tf_op jit(solution)/shard_map/ppermute | solution.py:48
  148.9 28.5 %collective-permute-start.21 = (bf16[2,128,512]{2,1,0:T(8,128)(2,1)S(1)}, bf16[2,128,512]{2,1,0:T(8,128)(2,1)S(1)}, u32[]{:S(2)}, u32[]{:S(2)}) collective-permute-start(bf16[2,128,512]{2,1,0:T(8,128)(2,1)S(1)} %fusion.50), channel_id=1, source_target_pairs={{0,16},{1,17},{2,18},{3,19},{4,20},{5,21},{6,22},{7,23},{8,24},{9,... | collective-permute-start | bytes 786440 | tf_op jit(solution)/shard_map/ppermute | solution.py:48
  245.1 49.2 %collective-permute-start.29 = (bf16[4,256,2048]{2,1,0:T(8,128)(2,1)}, bf16[4,256,2048]{2,1,0:T(8,128)(2,1)}, u32[]{:S(2)}, u32[]{:S(2)}) collective-permute-start(bf16[4,256,2048]{2,1,0:T(8,128)(2,1)} %bitcast.62), channel_id=1, source_target_pairs={{0,1},{1,0},{2,3},{3,2},{4,5},{5,4},{6,7},{7,6},{8,9},{9,8},{10,11... | collective-permute-start | bytes 12582920 | tf_op jit(solution)/shard_map/ppermute | solution.py:48
  246.7 47.5 %collective-permute-start.28 = (bf16[1024,512]{1,0:T(8,128)(2,1)}, bf16[1024,512]{1,0:T(8,128)(2,1)}, u32[]{:S(2)}, u32[]{:S(2)}) collective-permute-start(bf16[1024,512]{1,0:T(8,128)(2,1)} %fusion.42), channel_id=1, source_target_pairs={{0,2},{1,3},{2,0},{3,1},{4,6},{5,7},{6,4},{7,5},{8,10},{9,11},{10,... | collective-permute-start | bytes 3145736 | tf_op jit(solution)/shard_map/ppermute | solution.py:48
  248.0 46.2 %collective-permute-start.27 = (bf16[2,128,512]{2,1,0:T(8,128)(2,1)}, bf16[2,128,512]{2,1,0:T(8,128)(2,1)S(1)}, u32[]{:S(2)}, u32[]{:S(2)}) collective-permute-start(bf16[2,128,512]{2,1,0:T(8,128)(2,1)} %fusion.49), channel_id=1, source_target_pairs={{16,0},{17,1},{18,2},{19,3},{20,4},{21,5},{22,6},{23,7},{24,8},{25... | collective-permute-start | bytes 786440 | tf_op jit(solution)/shard_map/ppermute | solution.py:48
  311.7 55.3 %collective-permute-start.31 = (bf16[2,256,2048]{2,1,0:T(8,128)(2,1)}, bf16[2,256,2048]{2,1,0:T(8,128)(2,1)}, u32[]{:S(2)}, u32[]{:S(2)}) collective-permute-start(bf16[2,256,2048]{2,1,0:T(8,128)(2,1)} %pad_maximum_fusion.2), channel_id=1, source_target_pairs={{0,4},{1,5},{2,6},{3,7},{4,0},{5,1},{6,2},{7,3},{8,12},{9,13},{10,... | collective-permute-start | bytes 6291464 | tf_op jit(solution)/shard_map/ppermute | solution.py:48
  318.2 48.8 %collective-permute-start.30 = (bf16[1024,512]{1,0:T(8,128)(2,1)S(1)}, bf16[1024,512]{1,0:T(8,128)(2,1)S(1)}, u32[]{:S(2)}, u32[]{:S(2)}) collective-permute-start(bf16[1024,512]{1,0:T(8,128)(2,1)S(1)} %copy-done.78), channel_id=1, source_target_pairs={{0,16},{1,17},{2,18},{3,19},{4,20},{5,21},{6,22},{7,23},{8,24},{9,... | collective-permute-start | bytes 3145736 | tf_op jit(solution)/shard_map/ppermute | solution.py:48
  321.0 46.0 %collective-permute-start.32 = (bf16[512,1024]{1,0:T(8,128)(2,1)S(1)}, bf16[512,1024]{1,0:T(8,128)(2,1)S(1)}, u32[]{:S(2)}, u32[]{:S(2)}) collective-permute-start(bf16[512,1024]{1,0:T(8,128)(2,1)S(1)} %copy-done.50), channel_id=1, source_target_pairs={{0,2},{1,3},{2,0},{3,1},{4,6},{5,7},{6,4},{7,5},{8,10},{9,11},{10,... | collective-permute-start | bytes 3145736 | tf_op jit(solution)/shard_map/ppermute | solution.py:48
  374.0 41.8 %collective-permute-start.34 = (bf16[256,2048]{1,0:T(8,128)(2,1)S(1)}, bf16[256,2048]{1,0:T(8,128)(2,1)S(1)}, u32[]{:S(2)}, u32[]{:S(2)}) collective-permute-start(bf16[256,2048]{1,0:T(8,128)(2,1)S(1)} %fusion.45), channel_id=1, source_target_pairs={{0,8},{1,9},{2,10},{3,11},{4,12},{5,13},{6,14},{7,15},{8,0},{9,1},... | collective-permute-start | bytes 3145736 | tf_op jit(solution)/shard_map/ppermute | solution.py:48
  374.0 41.8 %collective-permute-start.35 = (bf16[512,1024]{1,0:T(8,128)(2,1)S(1)}, bf16[512,1024]{1,0:T(8,128)(2,1)S(1)}, u32[]{:S(2)}, u32[]{:S(2)}) collective-permute-start(bf16[512,1024]{1,0:T(8,128)(2,1)S(1)} %fusion.37.refs_8_), channel_id=1, source_target_pairs={{0,2},{1,3},{2,0},{3,1},{4,6},{5,7},{6,4},{7,5},{8,10},{9,11},{10,... | collective-permute-start | bytes 3145736 | tf_op jit(solution)/shard_map/ppermute | solution.py:48
  379.0 61.5 %collective-permute-start.38 = (bf16[512,1024]{1,0:T(8,128)(2,1)}, bf16[512,1024]{1,0:T(8,128)(2,1)}, u32[]{:S(2)}, u32[]{:S(2)}) collective-permute-start(bf16[512,1024]{1,0:T(8,128)(2,1)} %add_convert_fusion.4), channel_id=1, source_target_pairs={{0,16},{1,17},{2,18},{3,19},{4,20},{5,21},{6,22},{7,23},{8,24},{9,... | collective-permute-start | bytes 3145736 | tf_op jit(solution)/shard_map/ppermute | solution.py:48
  418.3 32.5 %collective-permute-start.37 = (bf16[512,1024]{1,0:T(8,128)(2,1)}, bf16[512,1024]{1,0:T(8,128)(2,1)}, u32[]{:S(2)}, u32[]{:S(2)}) collective-permute-start(bf16[512,1024]{1,0:T(8,128)(2,1)} %pad_maximum_fusion.13), channel_id=1, source_target_pairs={{0,8},{1,9},{2,10},{3,11},{4,12},{5,13},{6,14},{7,15},{8,0},{9,1},... | collective-permute-start | bytes 3145736 | tf_op jit(solution)/shard_map/ppermute | solution.py:48
  465.2 57.7 %collective-permute-start.44 = (bf16[512,2048]{1,0:T(8,128)(2,1)S(1)}, bf16[512,2048]{1,0:T(8,128)(2,1)}, u32[]{:S(2)}, u32[]{:S(2)}) collective-permute-start(bf16[512,2048]{1,0:T(8,128)(2,1)S(1)} %pad_maximum_fusion.3.refs_0_), channel_id=1, source_target_pairs={{0,4},{1,5},{2,6},{3,7},{4,0},{5,1},{6,2},{7,3},{8,12},{9,13},{10,... | collective-permute-start | bytes 6291464 | tf_op jit(solution)/shard_map/ppermute | solution.py:48
  475.1 47.8 %collective-permute-start.46 = (bf16[512,1024]{1,0:T(8,128)(2,1)S(1)}, bf16[512,1024]{1,0:T(8,128)(2,1)S(1)}, u32[]{:S(2)}, u32[]{:S(2)}) collective-permute-start(bf16[512,1024]{1,0:T(8,128)(2,1)S(1)} %copy-done.73), channel_id=1, source_target_pairs={{0,16},{1,17},{2,18},{3,19},{4,20},{5,21},{6,22},{7,23},{8,24},{9,... | collective-permute-start | bytes 3145736 | tf_op jit(solution)/shard_map/ppermute | solution.py:48
  484.3 44.3 %collective-permute-start.45 = (bf16[1024,512]{1,0:T(8,128)(2,1)S(1)}, bf16[1024,512]{1,0:T(8,128)(2,1)S(1)}, u32[]{:S(2)}, u32[]{:S(2)}) collective-permute-start(bf16[1024,512]{1,0:T(8,128)(2,1)S(1)} %pad_maximum_fusion.14), channel_id=1, source_target_pairs={{0,8},{1,9},{2,10},{3,11},{4,12},{5,13},{6,14},{7,15},{8,0},{9,1},... | collective-permute-start | bytes 3145736 | tf_op jit(solution)/shard_map/ppermute | solution.py:48
  491.8 31.1 %collective-permute-start.47 = (bf16[48,1024]{1,0:T(8,128)(2,1)S(1)}, bf16[48,1024]{1,0:T(8,128)(2,1)S(1)}, u32[]{:S(2)}, u32[]{:S(2)}) collective-permute-start(bf16[48,1024]{1,0:T(8,128)(2,1)S(1)} %constant_dynamic-slice_fusion.12), channel_id=1, source_target_pairs={{0,4},{1,5},{2,6},{3,7},{4,0},{5,1},{6,2},{7,3},{8,12},{9,13},{10,... | collective-permute-start | bytes 294920 | tf_op jit(solution)/shard_map/ppermute | solution.py:48
  531.6 45.6 %collective-permute-start.48 = (bf16[2048,512]{1,0:T(8,128)(2,1)}, bf16[2048,512]{1,0:T(8,128)(2,1)}, u32[]{:S(2)}, u32[]{:S(2)}) collective-permute-start(bf16[2048,512]{1,0:T(8,128)(2,1)} %pad_maximum_fusion.4.refs_0_), channel_id=1, source_target_pairs={{0,4},{1,5},{2,6},{3,7},{4,0},{5,1},{6,2},{7,3},{8,12},{9,13},{10,... | collective-permute-start | bytes 6291464 | tf_op jit(solution)/shard_map/ppermute | solution.py:48
  532.0 47.2 %collective-permute-start.51 = (bf16[2,256,2048]{2,1,0:T(8,128)(2,1)}, bf16[2,256,2048]{2,1,0:T(8,128)(2,1)}, u32[]{:S(2)}, u32[]{:S(2)}) collective-permute-start(bf16[2,256,2048]{2,1,0:T(8,128)(2,1)} %pad_maximum_fusion.5), channel_id=1, source_target_pairs={{0,8},{1,9},{2,10},{3,11},{4,12},{5,13},{6,14},{7,15},{8,0},{9,1},... | collective-permute-start | bytes 6291464 | tf_op jit(solution)/shard_map/ppermute | solution.py:48
  534.3 42.9 %collective-permute-start.49 = (bf16[512,512]{1,0:T(8,128)(2,1)S(1)}, bf16[512,512]{1,0:T(8,128)(2,1)S(1)}, u32[]{:S(2)}, u32[]{:S(2)}) collective-permute-start(bf16[512,512]{1,0:T(8,128)(2,1)S(1)} %copy-done.86), channel_id=1, source_target_pairs={{0,1},{1,0},{2,3},{3,2},{4,5},{5,4},{6,7},{7,6},{8,9},{9,8},{10,11... | collective-permute-start | bytes 1572872 | tf_op jit(solution)/shard_map/ppermute | solution.py:48
  536.9 40.2 %collective-permute-start.50 = (bf16[48,1024]{1,0:T(8,128)(2,1)S(1)}, bf16[48,1024]{1,0:T(8,128)(2,1)S(1)}, u32[]{:S(2)}, u32[]{:S(2)}) collective-permute-start(bf16[48,1024]{1,0:T(8,128)(2,1)S(1)} %add_convert_fusion.13), channel_id=1, source_target_pairs={{0,16},{1,17},{2,18},{3,19},{4,20},{5,21},{6,22},{7,23},{8,24},{9,... | collective-permute-start | bytes 294920 | tf_op jit(solution)/shard_map/ppermute | solution.py:48
  582.3 24.8 %collective-permute-start.54 = (bf16[256,2048]{1,0:T(8,128)(2,1)}, bf16[256,2048]{1,0:T(8,128)(2,1)}, u32[]{:S(2)}, u32[]{:S(2)}) collective-permute-start(bf16[256,2048]{1,0:T(8,128)(2,1)} %fusion.46), channel_id=1, source_target_pairs={{0,4},{1,5},{2,6},{3,7},{4,0},{5,1},{6,2},{7,3},{8,12},{9,13},{10,... | collective-permute-start | bytes 3145736 | tf_op jit(solution)/shard_map/ppermute | solution.py:48
  608.9 43.2 %collective-permute-start.55 = (bf16[2048,512]{1,0:T(8,128)(2,1)S(1)}, bf16[2048,512]{1,0:T(8,128)(2,1)}, u32[]{:S(2)}, u32[]{:S(2)}) collective-permute-start(bf16[2048,512]{1,0:T(8,128)(2,1)S(1)} %pad_maximum_fusion.6.refs_0_), channel_id=1, source_target_pairs={{0,4},{1,5},{2,6},{3,7},{4,0},{5,1},{6,2},{7,3},{8,12},{9,13},{10,... | collective-permute-start | bytes 6291464 | tf_op jit(solution)/shard_map/ppermute | solution.py:48
  (134 other events, 952.9 us)

commit v6 on v5

--- a/solution.py
+++ b/solution.py
@@ -858,9 +858,10 @@
         return jnp.concatenate([lax.dynamic_slice_in_dim(w_t, inner + HW * jj, HW, 0), rest], axis=0)
 
     far = g.flip_core(with_rest(other_j))
+    near = lax.dynamic_slice_in_dim(w_t, inner + HW * j, HW, 0)
     half_packed = assemble(
         [
-            (w_t, (inner + HW * j, 0), (HW, own_d), (0, g.c * own_d)),
+            (near, None, (HW, own_d), (0, g.c * own_d)),
             (rest, None, (n_rest, own_d), (HW, g.c * own_d)),
             (far, None, (KW, own_d), (0, (1 - g.c) * own_d)),
         ],

time: 672 us -> 668 us (level)
  no operation moved by 1% of the time
where the time goes in v6:
time: 668 us; the launch traced here: 663 us
  waiting for transfers between devices  213 us (32%)
  Pallas kernels  181 us (27%)
  other arithmetic  76.8 us (11%)
  matrix products  73 us (11%)
  local copies, waits for them, and re-layouts  60.2 us (9%)
  starting transfers between devices  56.3 us (8%)
    ppermute x58, waiting for transfers between devices, move(): return lax.ppermute(a, AXES, pairs)  213 us
    pallas_call x9, Pallas kernels, call(): pl.pallas_call(kernel, grid=grid, in_specs=[pl.BlockSpec(memory_space=plt...  144 us
    dot_general x13, matrix products, low_dot(): lax.dot_general(a.astype(bf16), b.astype(bf16), dims, preferred_element_t...  73 us
    ppermute x58, starting transfers between devices, move(): return lax.ppermute(a, AXES, pairs)  56.3 us
    unnamed x218, local copies, waits for them, and re-layouts  34.1 us
    pallas_call x8, Pallas kernels, assemble(): pl.pallas_call(kernel, in_specs=[pl.BlockSpec(memory_space=pltpu.SMEM)] +...  20.2 us
    pallas_call x4, Pallas kernels, place(): pl.pallas_call(kernel, in_specs=[pl.BlockSpec(memory_space=pltpu.SMEM)] +...  17.2 us
  transfers between devices with their start and end apart: 58, of which 24 were waited for; matrix products, arithmetic and copies ran while one was open for 13% of the time, Pallas kernels for 23%

profile of v6, /device:TPU:1, one launch (start us, length us, event | category | flops | bytes accessed | tf_op | source)
XLA Modules:
  0.0 662.7 jit_solution(10748955022611195708)
XLA Ops:
  24.1 15.7 %collective-permute-done.1 = bf16[256,2048]{1,0:T(8,128)(2,1)} collective-permute-done((bf16[256,2048]{1,0:T(8,128)(2,1)}, bf16[256,2048]{1,0:T(8,128)(2,1)}, u32[]{:S(2)}, u32[]{:S(2)}) %collective-permute-start.1) | collective-permute-done | bytes 1048608 | tf_op jit(solution)/shard_map/ppermute | solution.py:48
  84.7 7.2 %assemble.11 = bf16[2,1040,2048]{2,1,0:T(8,128)(2,1)} custom-call(s32[18]{0:T(128)S(1)} %stack.293.index, bf16[1,256,2048]{2,1,0:T(8,128)(2,1)S(1)} %copy-done.20, bf16[3,256,2048]{2,1,0:T(8,128)(2,1)} %collective-permute-done.8.refs_1_.refs_3_.refs_5_, bf16[1,256,2048]{2,1,0:T(8,128)(2,1)} %bitcast.13.refs_2_, ...), custom_call_target="tpu_custom_call" | custom-call | bytes 17039360 | tf_op jit(solution)/shard_map/assemble/pallas_call | solution.py:759
  91.8 11.5 %convolution_convert_fusion.1 = bf16[2080,896]{1,0:T(8,128)(2,1)S(1)} fusion(bf16[2080,2048]{1,0:T(8,128)(2,1)} %bitcast.282, bf16[896,2048]{1,0:T(8,128)(2,1)S(1)} %assemble.12.refs_2_.refs_7_.wx.wt), kind=kOutput, calls=%fused_computation.5 | convolution fusion | flops 7635496960 | bytes 15917056 | tf_op jit(solution)/shard_map/dot_general | solution.py:300
  113.4 22.1 %convolve.1 = (bf16[2048,512]{1,0:T(8,128)(2,1)S(1)}, bf16[2048,256]{1,0:T(8,128)(2,1)S(1)}, f32[2,4,128,512]{3,2,1,0:T(8,128)S(1)}, f32[2,2,1024,4]{3,2,1,0:T(8...) custom-call(bf16[2,1040,896]{2,1,0:T(8,128)(2,1)S(1)} %bitcast.250, ...), custom_call_target="tpu_custom_call" | custom-call | bytes 1024 | tf_op jit(solution)/shard_map/convolve/pallas_call | solution.py:367
  150.6 10.1 %convolution_convert_fusion.2 = bf16[2080,512]{1,0:T(8,128)(2,1)} fusion(bf16[2080,2048]{1,0:T(8,128)(2,1)} %bitcast.283, bf16[512,2048]{1,0:T(8,128)(2,1)S(1)} %assemble.13.refs_0_.refs_5_.wg), kind=kOutput, calls=%fused_computation.6 | convolution fusion | flops 4363141120 | bytes 12746752 | tf_op jit(solution)/shard_map/dot_general | solution.py:300
  160.8 10.9 %intra_forward.1.y = bf16[2048,512]{1,0:T(8,128)(2,1)S(1)} custom-call(bf16[2048,512]{1,0:T(8,128)(2,1)S(1)} %copy-done.12, bf16[2048,256]{1,0:T(8,128)(2,1)S(1)} %copy-done.8, f32[2,2,1024,4]{3,2,1,0:T(8,128)S(1)} %get-tuple-element.253.cum, f32[2,2,4,4,256]{4,3,2,1,0:T(4,128)S(1)} %get-tuple-element.254.row, f32[2,2,1024,4]{3,2,1,0:T(8,128)S(1)} %copy-done.16, ...), custom_call_target="tpu_custom_call" | custom-call | bytes 1024 | tf_op jit(solution)/shard_map/intra_forward/pallas_call | solution.py:367
  183.0 5.5 assemble.14
  188.5 8.3 %convolution_convert_fusion.3.og = bf16[2048,512]{1,0:T(8,128)(2,1)S(1)} fusion(bf16[2048,2048]{1,0:T(8,128)(2,1)} %bitcast.292, bf16[2048,512]{1,0:T(8,128)(2,1)S(1)} %assemble.15), kind=kOutput, calls=%fused_computation.35 | convolution fusion | flops 4296015872 | bytes 12582912 | tf_op jit(solution)/shard_map/dot_general | solution.py:300
  196.9 8.3 %join.1 = (bf16[2048,512]{1,0:T(8,128)(2,1)S(1)}, f32[2,8,1024]{2,1,0:T(8,128)S(1)}) custom-call(bf16[2048,512]{1,0:T(8,128)(2,1)S(1)} %copy-done.28, bf16[2048,256]{1,0:T(8,128)(2,1)S(1)} %copy-done.9, bf16[2,4,128,512]{3,2,1,0:T(8,128)(2,1)S(1)} %maximum_convert_fusion.enter, f32[2,2,1024,4]{3,2,1,0:T(8,128)S(1)} %get-tuple-element.253.cum, ...), custom_call_target="tpu_custom_call" | custom-call | bytes 1024 | tf_op jit(solution)/shard_map/join/pallas_call | solution.py:367
  212.5 12.0 %gates.1 = (bf16[2048,512]{1,0:T(8,128)(2,1)S(1)}, bf16[2,1040,512]{2,1,0:T(8,128)(2,1)}, bf16[2048,512]{1,0:T(8,128)(2,1)S(1)}, f32[1,512]{1,0:T(1,128)S(1)}, f32[2,4,128,512]{3,2,1,0:T(8,128)S(1)}) custom-call(bf16[2048,512]{1,0:T(8,128)(2,1)S(1)} %get-tuple-element.266.mixed, bf16[2,1040,512]{2,1,0:T(8,128)(2,1)} %bitcast.259, ...), custom_call_target="tpu_custom_call" | custom-call | bytes 1024 | tf_op jit(solution)/shard_map/gates/pallas_call | solution.py:367
  225.7 6.5 fusion.42
  245.1 6.7 %fusion.34.refs_6_ = bf16[512,1024]{1,0:T(8,128)(2,1)} fusion(bf16[2080,512]{1,0:T(8,128)(2,1)} %bitcast.269, bf16[2080,2048]{1,0:T(8,128)(2,1)} %bitcast.284), kind=kOutput, calls=%fused_computation.69 | convolution fusion | flops 2181562368 | bytes 7438336 | tf_op jit(solution)/shard_map/dot_general | solution.py:300
  251.9 37.9 %intra_backward.1 = (bf16[2048,512]{1,0:T(8,128)(2,1)S(1)}, f32[2,2,1024,4]{3,2,1,0:T(8,128)S(1)}, f32[2048,256]{1,0:T(8,128)S(1)}) custom-call(bf16[2048,512]{1,0:T(8,128)(2,1)S(1)} %copy-done.13, bf16[2048,256]{1,0:T(8,128)(2,1)S(1)} %copy-done.10, bf16[2048,512]{1,0:T(8,128)(2,1)S(1)} %copy-done.25, f32[2,2,1024,4]{3,2,1,0:T(8,128)} %copy-done.4, ...), custom_call_target="tpu_custom_call" | custom-call | bytes 1024 | tf_op jit(solution)/shard_map/intra_backward/pallas_call | solution.py:367
  289.8 8.0 %add_convert_fusion.7 = bf16[1024,512]{1,0:T(8,128)(2,1)} fusion(bf16[1024,512]{1,0:T(8,128)(2,1)} %collective-permute-done.28, bf16[2048,512]{1,0:T(8,128)(2,1)S(1)} %copy-done.64, bf16[2048,2048]{1,0:T(8,128)(2,1)} %bitcast.294), kind=kOutput, calls=%fused_computation.65 | convolution fusion | flops 2149056512 | bytes 8388608 | tf_op jit(solution)/shard_map/dot_general | solution.py:300
  308.5 5.3 fusion.10.refs_1_
  316.9 31.8 %finish.1 = (bf16[2,1040,768]{2,1,0:T(8,128)(2,1)}, bf16[2,1040,128]{2,1,0:T(8,128)(2,1)S(1)}, f32[2,8,768]{2,1,0:T(8,128)S(1)}, f32[2,2,8,4]{3,2,1,0:T(8,128)S(1)}) custom-call(bf16[2,1040,896]{2,1,0:T(8,128)(2,1)} %bitcast.252, bf16[2048,512]{1,0:T(8,128)(2,1)S(1)} %copy-done.14, bf16[2048,512]{1,0:T(8,128)(2,1)S(1)} %copy-done.26, ...), custom_call_target="tpu_custom_call" | custom-call | bytes 1024 | tf_op jit(solution)/shard_map/finish/pallas_call | solution.py:367
  355.9 6.7 %collective-permute-done.30 = bf16[1024,512]{1,0:T(8,128)(2,1)S(1)} collective-permute-done((bf16[1024,512]{1,0:T(8,128)(2,1)S(1)}, bf16[1024,512]{1,0:T(8,128)(2,1)S(1)}, u32[]{:S(2)}, u32[]{:S(2)}) %collective-permute-start.30) | collective-permute-done | bytes 1048608 | tf_op jit(solution)/shard_map/ppermute | solution.py:48
  382.4 29.0 %collective-permute-done.34 = bf16[256,2048]{1,0:T(8,128)(2,1)S(1)} collective-permute-done((bf16[256,2048]{1,0:T(8,128)(2,1)S(1)}, bf16[256,2048]{1,0:T(8,128)(2,1)S(1)}, u32[]{:S(2)}, u32[]{:S(2)}) %collective-permute-start.34) | collective-permute-done | bytes 1048608 | tf_op jit(solution)/shard_map/ppermute | solution.py:48
  419.4 16.6 %input_grad.1 = bf16[2,1024,2048]{2,1,0:T(8,128)(2,1)} custom-call(bf16[2080,512]{1,0:T(8,128)(2,1)S(1)} %bitcast.271, bf16[2080,768]{1,0:T(8,128)(2,1)S(1)} %bitcast.268, bf16[2080,128]{1,0:T(8,128)(2,1)S(1)} %bitcast.274, bf16[512,2048]{1,0:T(8,128)(2,1)S(1)} %copy-done.6, bf16[896,2048]{1,0:T(8,128)(2,1)S(1)} %copy-done.2, ...), custom_call_target="tpu_custom_call" | custom-call | bytes 1024 | tf_op jit(solution)/shard_map/input_grad/pallas_call | solution.py:367
  436.1 10.4 %collective-permute-done.37 = bf16[512,1024]{1,0:T(8,128)(2,1)} collective-permute-done((bf16[512,1024]{1,0:T(8,128)(2,1)}, bf16[512,1024]{1,0:T(8,128)(2,1)}, u32[]{:S(2)}, u32[]{:S(2)}) %collective-permute-start.37) | collective-permute-done | bytes 1048608 | tf_op jit(solution)/shard_map/ppermute | solution.py:48
  461.2 6.3 collective-permute-done.41
  472.0 6.9 %collective-permute-done.43 = bf16[96,1024]{1,0:T(8,128)(2,1)} collective-permute-done((bf16[96,1024]{1,0:T(8,128)(2,1)}, bf16[96,1024]{1,0:T(8,128)(2,1)}, u32[]{:S(2)}, u32[]{:S(2)}) %collective-permute-start.43) | collective-permute-done | bytes 196640 | tf_op jit(solution)/shard_map/ppermute | solution.py:48
  480.0 5.4 fusion
  489.8 28.7 %collective-permute-done.46 = bf16[512,1024]{1,0:T(8,128)(2,1)S(1)} collective-permute-done((bf16[512,1024]{1,0:T(8,128)(2,1)S(1)}, bf16[512,1024]{1,0:T(8,128)(2,1)S(1)}, u32[]{:S(2)}, u32[]{:S(2)}) %collective-permute-start.46) | collective-permute-done | bytes 1048608 | tf_op jit(solution)/shard_map/ppermute | solution.py:48
  518.5 5.7 collective-permute-done.45
  534.5 5.2 place.4
  539.7 33.0 %collective-permute-done.50 = bf16[48,1024]{1,0:T(8,128)(2,1)S(1)} collective-permute-done((bf16[48,1024]{1,0:T(8,128)(2,1)S(1)}, bf16[48,1024]{1,0:T(8,128)(2,1)S(1)}, u32[]{:S(2)}, u32[]{:S(2)}) %collective-permute-start.50) | collective-permute-done | bytes 98336 | tf_op jit(solution)/shard_map/ppermute | solution.py:48
  579.4 5.9 place.5.refs_2_
  585.3 16.4 %collective-permute-done.53 = bf16[48,1024]{1,0:T(8,128)(2,1)S(1)} collective-permute-done((bf16[48,1024]{1,0:T(8,128)(2,1)S(1)}, bf16[48,1024]{1,0:T(8,128)(2,1)S(1)}, u32[]{:S(2)}, u32[]{:S(2)}) %collective-permute-start.53) | collective-permute-done | bytes 98336 | tf_op jit(solution)/shard_map/ppermute | solution.py:48
  612.5 35.2 %collective-permute-done.55.refs_1_ = bf16[2048,512]{1,0:T(8,128)(2,1)} collective-permute-done((bf16[2048,512]{1,0:T(8,128)(2,1)S(1)}, bf16[2048,512]{1,0:T(8,128)(2,1)}, u32[]{:S(2)}, u32[]{:S(2)}) %collective-permute-start.55) | collective-permute-done | bytes 2097184 | tf_op jit(solution)/shard_map/ppermute | solution.py:48
  647.7 5.1 collective-permute-start.57
  652.9 5.2 place.6.refs_1_
  (497 shorter events, 230.3 us)
Async XLA Ops:
  12.3 29.3 %collective-permute-start.5 = (bf16[576,1024]{1,0:T(8,128)(2,1)}, bf16[576,1024]{1,0:T(8,128)(2,1)}, u32[]{:S(2)}, u32[]{:S(2)}) collective-permute-start(bf16[576,1024]{1,0:T(8,128)(2,1)} %slice.307), channel_id=1, source_target_pairs={{0,2},{1,3},{2,0},{3,1},{4,6},{5,7},{6,4},{7,5},{8,10},{9,11},{10,... | collective-permute-start | bytes 3538952 | tf_op jit(solution)/shard_map/ppermute | solution.py:48
  15.0 24.8 %collective-permute-start.1 = (bf16[256,2048]{1,0:T(8,128)(2,1)}, bf16[256,2048]{1,0:T(8,128)(2,1)}, u32[]{:S(2)}, u32[]{:S(2)}) collective-permute-start(bf16[256,2048]{1,0:T(8,128)(2,1)} %get-tuple-element.194), channel_id=1, source_target_pairs={{0,4},{1,5},{2,6},{3,7},{4,0},{5,1},{6,2},{7,3},{8,12},{9,13},{10,... | collective-permute-start | bytes 3145736 | tf_op jit(solution)/shard_map/ppermute | solution.py:48
  16.2 24.5 %collective-permute-start.2 = (bf16[256,2048]{1,0:T(8,128)(2,1)}, bf16[256,2048]{1,0:T(8,128)(2,1)}, u32[]{:S(2)}, u32[]{:S(2)}) collective-permute-start(bf16[256,2048]{1,0:T(8,128)(2,1)} %get-tuple-element.194), channel_id=1, source_target_pairs={{0,8},{1,9},{2,10},{3,11},{4,12},{5,13},{6,14},{7,15},{8,0},{9,1},... | collective-permute-start | bytes 3145736 | tf_op jit(solution)/shard_map/ppermute | solution.py:48
  49.1 26.8 %collective-permute-start.8 = (bf16[3,256,2048]{2,1,0:T(8,128)(2,1)}, bf16[3,256,2048]{2,1,0:T(8,128)(2,1)}, u32[]{:S(2)}, u32[]{:S(2)}) collective-permute-start(bf16[3,256,2048]{2,1,0:T(8,128)(2,1)} %pad_maximum_fusion), channel_id=1, source_target_pairs={{0,1},{1,0},{2,3},{3,2},{4,5},{5,4},{6,7},{7,6},{8,9},{9,8},{10,11... | collective-permute-start | bytes 9437192 | tf_op jit(solution)/shard_map/ppermute | solution.py:48
  82.0 25.1 %collective-permute-start.13 = (bf16[256,2048]{1,0:T(8,128)(2,1)}, bf16[256,2048]{1,0:T(8,128)(2,1)S(1)}, u32[]{:S(2)}, u32[]{:S(2)}) collective-permute-start(bf16[256,2048]{1,0:T(8,128)(2,1)} %pad_maximum_fusion.10), channel_id=1, source_target_pairs={{0,4},{1,5},{2,6},{3,7},{4,0},{5,1},{6,2},{7,3},{8,12},{9,13},{10,... | collective-permute-start | bytes 3145736 | tf_op jit(solution)/shard_map/ppermute | solution.py:48
  82.4 24.8 %collective-permute-start.14 = (bf16[256,2048]{1,0:T(8,128)(2,1)}, bf16[256,2048]{1,0:T(8,128)(2,1)S(1)}, u32[]{:S(2)}, u32[]{:S(2)}) collective-permute-start(bf16[256,2048]{1,0:T(8,128)(2,1)} %pad_maximum_fusion.10), channel_id=1, source_target_pairs={{0,8},{1,9},{2,10},{3,11},{4,12},{5,13},{6,14},{7,15},{8,0},{9,1},... | collective-permute-start | bytes 3145736 | tf_op jit(solution)/shard_map/ppermute | solution.py:48
  110.9 63.2 %collective-permute-start.18 = (bf16[3,256,2048]{2,1,0:T(8,128)(2,1)}, bf16[3,256,2048]{2,1,0:T(8,128)(2,1)}, u32[]{:S(2)}, u32[]{:S(2)}) collective-permute-start(bf16[3,256,2048]{2,1,0:T(8,128)(2,1)} %pad_maximum_fusion.1), channel_id=1, source_target_pairs={{0,1},{1,0},{2,3},{3,2},{4,5},{5,4},{6,7},{7,6},{8,9},{9,8},{10,11... | collective-permute-start | bytes 9437192 | tf_op jit(solution)/shard_map/ppermute | solution.py:48
  112.1 32.1 %collective-permute-start.19 = (bf16[512,1024]{1,0:T(8,128)(2,1)}, bf16[512,1024]{1,0:T(8,128)(2,1)}, u32[]{:S(2)}, u32[]{:S(2)}) collective-permute-start(bf16[512,1024]{1,0:T(8,128)(2,1)} %assemble.9.refs_0_), channel_id=1, source_target_pairs={{0,2},{1,3},{2,0},{3,1},{4,6},{5,7},{6,4},{7,5},{8,10},{9,11},{10,... | collective-permute-start | bytes 3145736 | tf_op jit(solution)/shard_map/ppermute | solution.py:48
  141.1 31.9 %collective-permute-start.16 = (bf16[128,2048]{1,0:T(8,128)(2,1)}, bf16[128,2048]{1,0:T(8,128)(2,1)S(1)}, u32[]{:S(2)}, u32[]{:S(2)}) collective-permute-start(bf16[128,2048]{1,0:T(8,128)(2,1)} %slice.256), channel_id=1, source_target_pairs={{0,8},{1,9},{2,10},{3,11},{4,12},{5,13},{6,14},{7,15},{8,0},{9,1},... | collective-permute-start | bytes 1572872 | tf_op jit(solution)/shard_map/ppermute | solution.py:48
  141.4 31.7 %collective-permute-start.17 = (bf16[128,2048]{1,0:T(8,128)(2,1)}, bf16[128,2048]{1,0:T(8,128)(2,1)S(1)}, u32[]{:S(2)}, u32[]{:S(2)}) collective-permute-start(bf16[128,2048]{1,0:T(8,128)(2,1)} %slice.257), channel_id=1, source_target_pairs={{0,4},{1,5},{2,6},{3,7},{4,0},{5,1},{6,2},{7,3},{8,12},{9,13},{10,... | collective-permute-start | bytes 1572872 | tf_op jit(solution)/shard_map/ppermute | solution.py:48
  144.2 28.8 %collective-permute-start.20 = (bf16[1024,512]{1,0:T(8,128)(2,1)S(1)}, bf16[1024,512]{1,0:T(8,128)(2,1)S(1)}, u32[]{:S(2)}, u32[]{:S(2)}) collective-permute-start(bf16[1024,512]{1,0:T(8,128)(2,1)S(1)} %copy-done.40), channel_id=1, source_target_pairs={{0,2},{1,3},{2,0},{3,1},{4,6},{5,7},{6,4},{7,5},{8,10},{9,11},{10,... | collective-permute-start | bytes 3145736 | tf_op jit(solution)/shard_map/ppermute | solution.py:48
  144.5 28.5 %collective-permute-start.21 = (bf16[2,128,512]{2,1,0:T(8,128)(2,1)S(1)}, bf16[2,128,512]{2,1,0:T(8,128)(2,1)S(1)}, u32[]{:S(2)}, u32[]{:S(2)}) collective-permute-start(bf16[2,128,512]{2,1,0:T(8,128)(2,1)S(1)} %fusion.50), channel_id=1, source_target_pairs={{0,16},{1,17},{2,18},{3,19},{4,20},{5,21},{6,22},{7,23},{8,24},{9,... | collective-permute-start | bytes 786440 | tf_op jit(solution)/shard_map/ppermute | solution.py:48
  240.6 49.2 %collective-permute-start.29 = (bf16[4,256,2048]{2,1,0:T(8,128)(2,1)}, bf16[4,256,2048]{2,1,0:T(8,128)(2,1)}, u32[]{:S(2)}, u32[]{:S(2)}) collective-permute-start(bf16[4,256,2048]{2,1,0:T(8,128)(2,1)} %bitcast.62), channel_id=1, source_target_pairs={{0,1},{1,0},{2,3},{3,2},{4,5},{5,4},{6,7},{7,6},{8,9},{9,8},{10,11... | collective-permute-start | bytes 12582920 | tf_op jit(solution)/shard_map/ppermute | solution.py:48
  242.3 47.5 %collective-permute-start.28 = (bf16[1024,512]{1,0:T(8,128)(2,1)}, bf16[1024,512]{1,0:T(8,128)(2,1)}, u32[]{:S(2)}, u32[]{:S(2)}) collective-permute-start(bf16[1024,512]{1,0:T(8,128)(2,1)} %fusion.42), channel_id=1, source_target_pairs={{0,2},{1,3},{2,0},{3,1},{4,6},{5,7},{6,4},{7,5},{8,10},{9,11},{10,... | collective-permute-start | bytes 3145736 | tf_op jit(solution)/shard_map/ppermute | solution.py:48
  243.6 46.2 %collective-permute-start.27 = (bf16[2,128,512]{2,1,0:T(8,128)(2,1)}, bf16[2,128,512]{2,1,0:T(8,128)(2,1)S(1)}, u32[]{:S(2)}, u32[]{:S(2)}) collective-permute-start(bf16[2,128,512]{2,1,0:T(8,128)(2,1)} %fusion.49), channel_id=1, source_target_pairs={{16,0},{17,1},{18,2},{19,3},{20,4},{21,5},{22,6},{23,7},{24,8},{25... | collective-permute-start | bytes 786440 | tf_op jit(solution)/shard_map/ppermute | solution.py:48
  307.3 55.3 %collective-permute-start.31 = (bf16[2,256,2048]{2,1,0:T(8,128)(2,1)}, bf16[2,256,2048]{2,1,0:T(8,128)(2,1)}, u32[]{:S(2)}, u32[]{:S(2)}) collective-permute-start(bf16[2,256,2048]{2,1,0:T(8,128)(2,1)} %pad_maximum_fusion.2), channel_id=1, source_target_pairs={{0,4},{1,5},{2,6},{3,7},{4,0},{5,1},{6,2},{7,3},{8,12},{9,13},{10,... | collective-permute-start | bytes 6291464 | tf_op jit(solution)/shard_map/ppermute | solution.py:48
  313.8 48.8 %collective-permute-start.30 = (bf16[1024,512]{1,0:T(8,128)(2,1)S(1)}, bf16[1024,512]{1,0:T(8,128)(2,1)S(1)}, u32[]{:S(2)}, u32[]{:S(2)}) collective-permute-start(bf16[1024,512]{1,0:T(8,128)(2,1)S(1)} %copy-done.78), channel_id=1, source_target_pairs={{0,16},{1,17},{2,18},{3,19},{4,20},{5,21},{6,22},{7,23},{8,24},{9,... | collective-permute-start | bytes 3145736 | tf_op jit(solution)/shard_map/ppermute | solution.py:48
  316.6 46.0 %collective-permute-start.32 = (bf16[512,1024]{1,0:T(8,128)(2,1)S(1)}, bf16[512,1024]{1,0:T(8,128)(2,1)S(1)}, u32[]{:S(2)}, u32[]{:S(2)}) collective-permute-start(bf16[512,1024]{1,0:T(8,128)(2,1)S(1)} %copy-done.50), channel_id=1, source_target_pairs={{0,2},{1,3},{2,0},{3,1},{4,6},{5,7},{6,4},{7,5},{8,10},{9,11},{10,... | collective-permute-start | bytes 3145736 | tf_op jit(solution)/shard_map/ppermute | solution.py:48
  369.6 41.8 %collective-permute-start.34 = (bf16[256,2048]{1,0:T(8,128)(2,1)S(1)}, bf16[256,2048]{1,0:T(8,128)(2,1)S(1)}, u32[]{:S(2)}, u32[]{:S(2)}) collective-permute-start(bf16[256,2048]{1,0:T(8,128)(2,1)S(1)} %fusion.45), channel_id=1, source_target_pairs={{0,8},{1,9},{2,10},{3,11},{4,12},{5,13},{6,14},{7,15},{8,0},{9,1},... | collective-permute-start | bytes 3145736 | tf_op jit(solution)/shard_map/ppermute | solution.py:48
  369.6 41.8 %collective-permute-start.35 = (bf16[512,1024]{1,0:T(8,128)(2,1)S(1)}, bf16[512,1024]{1,0:T(8,128)(2,1)S(1)}, u32[]{:S(2)}, u32[]{:S(2)}) collective-permute-start(bf16[512,1024]{1,0:T(8,128)(2,1)S(1)} %fusion.37.refs_8_), channel_id=1, source_target_pairs={{0,2},{1,3},{2,0},{3,1},{4,6},{5,7},{6,4},{7,5},{8,10},{9,11},{10,... | collective-permute-start | bytes 3145736 | tf_op jit(solution)/shard_map/ppermute | solution.py:48
  374.5 61.5 %collective-permute-start.38 = (bf16[512,1024]{1,0:T(8,128)(2,1)}, bf16[512,1024]{1,0:T(8,128)(2,1)}, u32[]{:S(2)}, u32[]{:S(2)}) collective-permute-start(bf16[512,1024]{1,0:T(8,128)(2,1)} %add_convert_fusion.4), channel_id=1, source_target_pairs={{0,16},{1,17},{2,18},{3,19},{4,20},{5,21},{6,22},{7,23},{8,24},{9,... | collective-permute-start | bytes 3145736 | tf_op jit(solution)/shard_map/ppermute | solution.py:48
  413.9 32.5 %collective-permute-start.37 = (bf16[512,1024]{1,0:T(8,128)(2,1)}, bf16[512,1024]{1,0:T(8,128)(2,1)}, u32[]{:S(2)}, u32[]{:S(2)}) collective-permute-start(bf16[512,1024]{1,0:T(8,128)(2,1)} %pad_maximum_fusion.13), channel_id=1, source_target_pairs={{0,8},{1,9},{2,10},{3,11},{4,12},{5,13},{6,14},{7,15},{8,0},{9,1},... | collective-permute-start | bytes 3145736 | tf_op jit(solution)/shard_map/ppermute | solution.py:48
  460.8 57.7 %collective-permute-start.44 = (bf16[512,2048]{1,0:T(8,128)(2,1)S(1)}, bf16[512,2048]{1,0:T(8,128)(2,1)}, u32[]{:S(2)}, u32[]{:S(2)}) collective-permute-start(bf16[512,2048]{1,0:T(8,128)(2,1)S(1)} %pad_maximum_fusion.3.refs_0_), channel_id=1, source_target_pairs={{0,4},{1,5},{2,6},{3,7},{4,0},{5,1},{6,2},{7,3},{8,12},{9,13},{10,... | collective-permute-start | bytes 6291464 | tf_op jit(solution)/shard_map/ppermute | solution.py:48
  470.7 47.8 %collective-permute-start.46 = (bf16[512,1024]{1,0:T(8,128)(2,1)S(1)}, bf16[512,1024]{1,0:T(8,128)(2,1)S(1)}, u32[]{:S(2)}, u32[]{:S(2)}) collective-permute-start(bf16[512,1024]{1,0:T(8,128)(2,1)S(1)} %copy-done.73), channel_id=1, source_target_pairs={{0,16},{1,17},{2,18},{3,19},{4,20},{5,21},{6,22},{7,23},{8,24},{9,... | collective-permute-start | bytes 3145736 | tf_op jit(solution)/shard_map/ppermute | solution.py:48
  479.9 44.3 %collective-permute-start.45 = (bf16[1024,512]{1,0:T(8,128)(2,1)S(1)}, bf16[1024,512]{1,0:T(8,128)(2,1)S(1)}, u32[]{:S(2)}, u32[]{:S(2)}) collective-permute-start(bf16[1024,512]{1,0:T(8,128)(2,1)S(1)} %pad_maximum_fusion.14), channel_id=1, source_target_pairs={{0,8},{1,9},{2,10},{3,11},{4,12},{5,13},{6,14},{7,15},{8,0},{9,1},... | collective-permute-start | bytes 3145736 | tf_op jit(solution)/shard_map/ppermute | solution.py:48
  487.4 31.1 %collective-permute-start.47 = (bf16[48,1024]{1,0:T(8,128)(2,1)S(1)}, bf16[48,1024]{1,0:T(8,128)(2,1)S(1)}, u32[]{:S(2)}, u32[]{:S(2)}) collective-permute-start(bf16[48,1024]{1,0:T(8,128)(2,1)S(1)} %constant_dynamic-slice_fusion.12), channel_id=1, source_target_pairs={{0,4},{1,5},{2,6},{3,7},{4,0},{5,1},{6,2},{7,3},{8,12},{9,13},{10,... | collective-permute-start | bytes 294920 | tf_op jit(solution)/shard_map/ppermute | solution.py:48
  527.1 45.6 %collective-permute-start.48 = (bf16[2048,512]{1,0:T(8,128)(2,1)}, bf16[2048,512]{1,0:T(8,128)(2,1)}, u32[]{:S(2)}, u32[]{:S(2)}) collective-permute-start(bf16[2048,512]{1,0:T(8,128)(2,1)} %pad_maximum_fusion.4.refs_0_), channel_id=1, source_target_pairs={{0,4},{1,5},{2,6},{3,7},{4,0},{5,1},{6,2},{7,3},{8,12},{9,13},{10,... | collective-permute-start | bytes 6291464 | tf_op jit(solution)/shard_map/ppermute | solution.py:48
  527.6 47.2 %collective-permute-start.51 = (bf16[2,256,2048]{2,1,0:T(8,128)(2,1)}, bf16[2,256,2048]{2,1,0:T(8,128)(2,1)}, u32[]{:S(2)}, u32[]{:S(2)}) collective-permute-start(bf16[2,256,2048]{2,1,0:T(8,128)(2,1)} %pad_maximum_fusion.5), channel_id=1, source_target_pairs={{0,8},{1,9},{2,10},{3,11},{4,12},{5,13},{6,14},{7,15},{8,0},{9,1},... | collective-permute-start | bytes 6291464 | tf_op jit(solution)/shard_map/ppermute | solution.py:48
  529.8 42.9 %collective-permute-start.49 = (bf16[512,512]{1,0:T(8,128)(2,1)S(1)}, bf16[512,512]{1,0:T(8,128)(2,1)S(1)}, u32[]{:S(2)}, u32[]{:S(2)}) collective-permute-start(bf16[512,512]{1,0:T(8,128)(2,1)S(1)} %copy-done.86), channel_id=1, source_target_pairs={{0,1},{1,0},{2,3},{3,2},{4,5},{5,4},{6,7},{7,6},{8,9},{9,8},{10,11... | collective-permute-start | bytes 1572872 | tf_op jit(solution)/shard_map/ppermute | solution.py:48
  532.5 40.2 %collective-permute-start.50 = (bf16[48,1024]{1,0:T(8,128)(2,1)S(1)}, bf16[48,1024]{1,0:T(8,128)(2,1)S(1)}, u32[]{:S(2)}, u32[]{:S(2)}) collective-permute-start(bf16[48,1024]{1,0:T(8,128)(2,1)S(1)} %add_convert_fusion.13), channel_id=1, source_target_pairs={{0,16},{1,17},{2,18},{3,19},{4,20},{5,21},{6,22},{7,23},{8,24},{9,... | collective-permute-start | bytes 294920 | tf_op jit(solution)/shard_map/ppermute | solution.py:48
  577.9 24.8 %collective-permute-start.54 = (bf16[256,2048]{1,0:T(8,128)(2,1)}, bf16[256,2048]{1,0:T(8,128)(2,1)}, u32[]{:S(2)}, u32[]{:S(2)}) collective-permute-start(bf16[256,2048]{1,0:T(8,128)(2,1)} %fusion.46), channel_id=1, source_target_pairs={{0,4},{1,5},{2,6},{3,7},{4,0},{5,1},{6,2},{7,3},{8,12},{9,13},{10,... | collective-permute-start | bytes 3145736 | tf_op jit(solution)/shard_map/ppermute | solution.py:48
  604.5 43.2 %collective-permute-start.55 = (bf16[2048,512]{1,0:T(8,128)(2,1)S(1)}, bf16[2048,512]{1,0:T(8,128)(2,1)}, u32[]{:S(2)}, u32[]{:S(2)}) collective-permute-start(bf16[2048,512]{1,0:T(8,128)(2,1)S(1)} %pad_maximum_fusion.6.refs_0_), channel_id=1, source_target_pairs={{0,4},{1,5},{2,6},{3,7},{4,0},{5,1},{6,2},{7,3},{8,12},{9,13},{10,... | collective-permute-start | bytes 6291464 | tf_op jit(solution)/shard_map/ppermute | solution.py:48
  (134 other events, 944.3 us)
